TPU v7x, 32 devices: a whole 2x2x4 slice. The times are simulated.
32 devices in a mesh: fsdp: 32 (over z, y, x, core).
Axes of the slice: x: 2, y: 2, z: 4, core: 2. Of those that a mesh axis runs over, the one named last changes fastest.
Arguments:
- inputs: bfloat16 [256, 4096], P('fsdp'), may hold values from -6 to 6
- norm_gain: bfloat16 [4096], replicated, may hold values from 0.099609375 to 1.8984375
- lengths: int32 [2], replicated, may hold values from 1 to 128, 192 in all
- gate_rows: bfloat16 [10240, 4096], P('fsdp'), may hold values from -0.09375 to 0.09375
- up_rows: bfloat16 [10240, 4096], P('fsdp'), may hold values from -0.09375 to 0.09375
- down_rows: bfloat16 [10240, 4096], P('fsdp'), may hold values from -0.109375 to 0.109375
- krylov_gate: bfloat16 [8, 10240, 4096], P(None, 'fsdp'), may hold values from -30 to 30
- krylov_up: bfloat16 [8, 10240, 4096], P(None, 'fsdp'), may hold values from -30 to 30
- krylov_down: bfloat16 [8, 10240, 4096], P(None, 'fsdp'), may hold values from -30 to 30
Outputs:
- new_gate: bfloat16 [10240, 4096], P('fsdp')
- new_up: bfloat16 [10240, 4096], P('fsdp')
- new_down: bfloat16 [10240, 4096], P('fsdp')
- coefficients: float32 [9], replicated
Inputs may be any that keep to these rules, and one draw needn't show every extreme that they name: The lengths sum to exactly 192.
All inputs are finite; a program needn't handle non-finite values.
Results may differ from a plain program's by a relative error of at most 0.0051.
The roundings to bfloat16 on the way count: a program that leaves them out, or rounds other values in their place, can miss the bound.
Values may be sent and summed in bfloat16 or wider, within the bound.
No kernel may reach another device: no remote copies, remote signals or barrier semaphores. Data moves between devices by JAX's collectives and lax.ppermute only.
A program may use at most 192 MiB of HBM per device.

v0:
```python
import math

import jax
import jax.numpy as jnp
from jax import lax
from jax.sharding import PartitionSpec as P

LEN = 128


def gelu_pair(gate_pre):
    coef = math.sqrt(2.0 / math.pi)
    cube = gate_pre * gate_pre * gate_pre
    tanh_val = jnp.tanh(coef * (gate_pre + 0.044715 * cube))
    act = 0.5 * gate_pre * (1.0 + tanh_val)
    slope = 0.5 * (1.0 + tanh_val) + 0.5 * gate_pre * (1.0 - tanh_val * tanh_val) * coef * (
        1.0 + 3.0 * 0.044715 * gate_pre * gate_pre
    )
    return (act, slope)


def contract_first(left, right):
    return lax.dot_general(
        left, right, (((0,), (0,)), ((), ())), preferred_element_type=jnp.float32
    )


def contract_last(left, right):
    return lax.dot_general(
        left, right, (((1,), (1,)), ((), ())), preferred_element_type=jnp.float32
    )


def live_mask(positions, lengths):
    seq_ids = positions // LEN
    table = jnp.arange(lengths.shape[0], dtype=jnp.int32)
    limits = jnp.sum(jnp.where(seq_ids[:, None] == table[None, :], lengths[None, :], 0), axis=1)
    return (positions % LEN < limits).astype(jnp.float32)


def local_dots(parts, grads):
    total = jnp.zeros((parts[0].shape[0],), jnp.float32)
    for krylov, grad in zip(parts, grads):
        total = total + jnp.einsum(
            "jfd,fd->j", krylov.astype(jnp.float32), grad, precision=lax.Precision.HIGHEST
        )
    return total


def per_device(
    inputs, norm_gain, lengths, gate_rows, up_rows, down_rows, krylov_gate, krylov_up, krylov_down
):
    parts = (krylov_gate, krylov_up, krylov_down)
    basis_count = krylov_gate.shape[0]
    width = inputs.shape[1]
    devices = lax.axis_size("fsdp")
    hidden_all = gate_rows.shape[0] * devices
    count = 3.0 * width * hidden_all
    wide = inputs.astype(jnp.float32)
    normed_own = (
        wide
        * lax.rsqrt(jnp.mean(wide * wide, axis=1, keepdims=True) + 1e-06)
        * norm_gain.astype(jnp.float32)
    ).astype(jnp.bfloat16)
    normed = lax.all_gather(normed_own, "fsdp", axis=0, tiled=True)
    token_count = normed.shape[0]
    inv_d = 1.0 / math.sqrt(width)
    inv_ff = 1.0 / math.sqrt(hidden_all)
    probe_gate = krylov_gate[basis_count - 1]
    probe_up = krylov_up[basis_count - 1]
    probe_down = krylov_down[basis_count - 1]
    gate_pre = contract_last(gate_rows, normed)
    up_pre = contract_last(up_rows, normed)
    tan_gate = contract_last(probe_gate, normed) * inv_d
    tan_up = contract_last(probe_up, normed) * inv_d
    act, slope = gelu_pair(gate_pre)
    hidden = (act * up_pre).astype(jnp.bfloat16)
    tangent = (slope * tan_gate * up_pre + act * tan_up).astype(jnp.bfloat16)
    jvp_own = lax.psum_scatter(
        contract_first(down_rows, tangent) + contract_first(probe_down, hidden) * inv_ff,
        "fsdp",
        scatter_dimension=0,
        tiled=True,
    )
    live = live_mask(jnp.arange(token_count, dtype=jnp.int32), lengths)
    loss_own = (jvp_own * live[None, :]).astype(jnp.bfloat16)
    loss_t = lax.all_gather(loss_own, "fsdp", axis=0, tiled=True)
    back = jnp.dot(down_rows, loss_t, preferred_element_type=jnp.float32)
    grad_down = contract_last(hidden, loss_t) * inv_ff
    s_term = (back * up_pre * slope).astype(jnp.bfloat16)
    r_term = (back * act).astype(jnp.bfloat16)
    grad_gate = jnp.dot(s_term, normed, preferred_element_type=jnp.float32) * inv_d
    grad_up = jnp.dot(r_term, normed, preferred_element_type=jnp.float32) * inv_d
    grads = (grad_gate, grad_up, grad_down)
    dots_own = local_dots(parts, grads)
    proj = lax.psum(dots_own, "fsdp") / count
    residuals = []
    for krylov, grad in zip(parts, grads):
        residuals.append(
            grad
            - jnp.einsum(
                "j,jfd->fd", proj, krylov.astype(jnp.float32), precision=lax.Precision.HIGHEST
            )
        )
    own_left = (
        jnp.sum(residuals[0] * residuals[0])
        + jnp.sum(residuals[1] * residuals[1])
        + jnp.sum(residuals[2] * residuals[2])
    )
    squares = lax.psum(own_left, "fsdp") / count
    norm = jnp.sqrt(squares + 1e-06)
    new_gate = (residuals[0] / norm).astype(jnp.bfloat16)
    new_up = (residuals[1] / norm).astype(jnp.bfloat16)
    new_down = (residuals[2] / norm).astype(jnp.bfloat16)
    coefficients = jnp.concatenate([proj, norm[None]])
    return (new_gate, new_up, new_down, coefficients)


def solution(mesh):
    placed = (
        P("fsdp", None),
        P(),
        P(),
        P("fsdp", None),
        P("fsdp", None),
        P("fsdp", None),
        P(None, "fsdp", None),
        P(None, "fsdp", None),
        P(None, "fsdp", None),
    )
    return jax.shard_map(
        per_device,
        mesh=mesh,
        in_specs=placed,
        out_specs=(P("fsdp", None), P("fsdp", None), P("fsdp", None), P()),
        check_vma=False,
    )
```

profile of v0, /device:TPU:0, one launch (start us, length us, event | category | flops | bytes accessed | tf_op | source)
XLA Modules:
  0.0 818.3 jit_solution(6704923044619524791)
XLA Ops:
  7.2 0.0 copy-start
  7.2 0.0 all-gather.3.cloned.1.call-start
  7.2 1.1 fusion.88
  8.4 0.7 convert_element_type.47
  9.1 1.5 fusion.90
  10.6 0.0 all-gather.3.cloned.1.call-update
  10.7 0.0 reduce-scatter.2.cloned.1.call-start
  10.7 59.8 %all-gather.3.cloned.1.call-done = bf16[256,4096]{1,0:T(8,128)(2,1)} async-done(((bf16[8,4096]{1,0:T(8,128)(2,1)}), bf16[256,4096]{1,0:T(8,128)(2,1)}) %all-gather.3.cloned.1.call-update) | async-done | bytes 2097168 | tf_op jit(solution)/shard_map/all_gather | solution.py:65
  70.6 3.4 convolution_bitcast_fusion.2
  74.0 4.0 fusion.37
  77.9 0.9 multiply_convert_fusion.2
  78.8 7.9 fusion.53
  86.7 6.2 fusion.13
  93.0 0.0 reduce-scatter.2.cloned.1.call-update
  93.0 0.2 all-gather.5.cloned.1.call-start
  93.2 0.1 fusion.91
  93.3 139.5 %reduce-scatter.2.cloned.1.call-done = f32[128,256]{0,1:T(8,128)} async-done(((f32[4096,256]{0,1:T(8,128)}), f32[128,256]{0,1:T(8,128)}) %reduce-scatter.2.cloned.1.call-update) | async-done | bytes 131088 | tf_op jit(solution)/shard_map/reduce_scatter | solution.py:79
  232.8 1.6 multiply_convert_fusion.5
  234.4 0.0 all-gather.5.cloned.1.call-update
  234.4 50.9 %all-gather.5.cloned.1.call-done = bf16[4096,256]{0,1:T(8,128)(2,1)} async-done(((bf16[128,256]{0,1:T(8,128)(2,1)}), bf16[4096,256]{0,1:T(8,128)(2,1)}) %all-gather.5.cloned.1.call-update) | async-done | bytes 2097168 | tf_op jit(solution)/shard_map/all_gather | solution.py:87
  285.4 2.6 convolution_bitcast_fusion
  288.0 1.0 convolution_multiply_fusion.2
  289.0 80.7 %fusion.55 = f32[8]{0:T(128)S(1)} fusion(bf16[8,320,4096]{2,1,0:T(8,128)(2,1)} %param.15, f32[320,4096,1]{1,0,2:T(8,128)S(1)} %bitcast.108), kind=kOutput, calls=%fused_computation.51 | convolution fusion | flops 125829120 | bytes 26214432 | tf_op jit(solution)/shard_map/jfd,fd->j/dot_general | solution.py:44
  369.8 0.0 copy-done.2
  369.8 0.0 slice-start.6
  369.8 0.9 convolution_multiply_fusion.1
  370.7 0.0 slice-start.7
  370.7 0.0 slice-start.8
  370.7 0.0 slice-start.9
  370.7 0.0 slice-start.10
  370.8 81.9 %fusion.75 = f32[8]{0:T(128)S(1)} fusion(f32[8]{0:T(128)S(1)} %fusion.55, bf16[8,320,4096]{2,1,0:T(8,128)(2,1)} %param.16, f32[320,4096,1]{1,0,2:T(8,128)S(1)} %bitcast.113), kind=kOutput, calls=%fused_computation.55 | convolution fusion | flops 125829128 | bytes 26214464 | tf_op jit(solution)/shard_map/jfd,fd->j/dot_general | solution.py:44
  452.7 0.0 copy-done.9
  452.7 0.9 convolution_multiply_fusion
  453.6 2.2 copy-done.4
  455.9 78.6 %fusion.70 = f32[8]{0:T(128)S(1)} fusion(f32[8]{0:T(128)S(1)} %fusion.75, bf16[8,320,4096]{2,1,0:T(8,128)(2,1)S(1)} %bitcast.118, f32[320,4096,1]{1,0,2:T(8,128)S(1)} %bitcast.114), kind=kOutput, calls=%fused_computation.54 | convolution fusion | flops 125829128 | bytes 26214464 | tf_op jit(solution)/shard_map/jfd,fd->j/dot_general | solution.py:44
  534.5 39.6 %psum.14 = f32[8]{0:T(128)S(1)} all-reduce(f32[8]{0:T(128)S(1)} %fusion.70), channel_id=1, replica_groups=mesh['fsdp'=32] {'fsdp'}, use_global_device_ids=true, to_apply=%region_3.4 | all-reduce | flops 8 | bytes 64 | tf_op jit(solution)/shard_map/psum | solution.py:96
  574.1 49.1 %fusion.8 = f32[1,320,4096]{2,0,1:T(1,128)} fusion(bf16[8,320,4096]{2,1,0:T(8,128)(2,1)} %param.15, f32[8]{0:T(128)S(1)} %psum.14), kind=kOutput, calls=%fused_computation.8 | convolution fusion | flops 125829128 | bytes 26214432 | tf_op jit(solution)/shard_map/j,jfd->fd/dot_general | solution.py:101
  623.2 49.6 %fusion = f32[1,320,4096]{2,0,1:T(1,128)} fusion(bf16[8,320,4096]{2,1,0:T(8,128)(2,1)} %param.17, f32[8]{0:T(128)S(1)} %psum.14), kind=kOutput, calls=%fused_computation | convolution fusion | flops 125829128 | bytes 26214432 | tf_op jit(solution)/shard_map/j,jfd->fd/dot_general | solution.py:101
  672.9 49.6 %fusion.4 = f32[1,320,4096]{2,0,1:T(1,128)} fusion(bf16[8,320,4096]{2,1,0:T(8,128)(2,1)} %param.16, f32[8]{0:T(128)S(1)} %psum.14), kind=kOutput, calls=%fused_computation.4 | convolution fusion | flops 125829128 | bytes 26214432 | tf_op jit(solution)/shard_map/j,jfd->fd/dot_general | solution.py:101
  722.5 10.0 %multiply_reduce_fusion = f32[]{:T(128)} fusion(f32[320,4096]{1,0:T(8,128)} %copy-done.4, f32[1,320,4096]{2,0,1:T(1,128)} %fusion), kind=kLoop, calls=%fused_computation.27 | loop fusion | flops 3932159 | bytes 10485764 | tf_op jit(solution)/shard_map/reduce_sum | solution.py:108
  732.5 13.1 %multiply_reduce_fusion.1 = (f32[]{:T(128)}, f32[]{:T(128)}) fusion(f32[320,4096]{1,0:T(8,128)} %copy-done.3, f32[1,320,4096]{2,0,1:T(1,128)S(1)} %copy-done.6, f32[320,4096]{1,0:T(8,128)S(1)} %bitcast.110, f32[1,320,4096]{2,0,1:T(1,128)S(1)} %copy-done.5), kind=kLoop, calls=%fused_computation.28 | loop fusion | flops 7864318 | bytes 20971528 | tf_op jit(solution)/shard_map/reduce_sum | solution.py:107
  747.5 39.7 %psum.15 = f32[]{:T(128)} all-reduce(f32[]{:T(128)S(6)} %add.78), channel_id=1, replica_groups=mesh['fsdp'=32] {'fsdp'}, use_global_device_ids=true, to_apply=%region_7.8 | all-reduce | flops 1 | bytes 8 | tf_op jit(solution)/shard_map/psum | solution.py:110
  787.9 0.0 slice-start.2
  788.0 0.0 slice-start.4
  788.0 9.1 %divide_convert_fusion.1 = bf16[320,4096]{1,0:T(8,128)(2,1)} fusion(f32[]{:T(128)} %sqrt.3, f32[320,4096]{1,0:T(8,128)} %copy-done.3, f32[1,320,4096]{2,0,1:T(1,128)} %fusion.4), kind=kLoop, calls=%fused_computation.25 | loop fusion | flops 3932160 | bytes 13107204 | tf_op jit(solution)/shard_map/convert_element_type | solution.py:113
  797.1 9.1 %divide_convert_fusion = bf16[320,4096]{1,0:T(8,128)(2,1)} fusion(f32[]{:T(128)} %sqrt.3, f32[320,4096]{1,0:T(8,128)} %copy-done.4, f32[1,320,4096]{2,0,1:T(1,128)} %fusion), kind=kLoop, calls=%fused_computation.24 | loop fusion | flops 3932160 | bytes 13107204 | tf_op jit(solution)/shard_map/convert_element_type | solution.py:114
  806.2 4.9 divide_convert_fusion.2
  811.0 0.6 pad_maximum_fusion
  (43 shorter events, 0.1 us)
Async XLA Ops:
  7.2 71.7 %copy-start = (bf16[320,4096]{1,0:T(8,128)(2,1)S(1)}, bf16[320,4096]{1,0:T(8,128)(2,1)}, u32[]{:S(2)}) copy-start(bf16[320,4096]{1,0:T(8,128)(2,1)} %param.14) | copy-start | bytes 7864324
  7.2 63.4 %all-gather.3.cloned.1.call-start = ((), (), s32[]{:S(2)}) async-start(), calls=%async_computation.1 | async-start | bytes 2162688 | tf_op jit(solution)/shard_map/all_gather | solution.py:65
  10.7 222.1 %reduce-scatter.2.cloned.1.call-start = ((), (), s32[]{:S(2)}) async-start(), calls=%async_computation.2 | async-start | bytes 4325376 | tf_op jit(solution)/shard_map/reduce_scatter | solution.py:79
  70.6 7.4 copy-start.7
  70.6 7.4 copy-start.11
  86.7 6.5 copy-start.10
  93.0 192.4 %all-gather.5.cloned.1.call-start = ((), (), s32[]{:S(2)}) async-start(), calls=%async_computation.3 | async-start | bytes 2162688 | tf_op jit(solution)/shard_map/all_gather | solution.py:87
  285.4 2.6 copy-start.8
  289.0 80.8 %copy-start.2 = (f32[320,4096]{1,0:T(8,128)}, f32[320,4096]{1,0:T(8,128)S(1)}, u32[]{:S(2)}) copy-start(f32[320,4096]{1,0:T(8,128)S(1)} %convolution_multiply_fusion.2) | copy-start | bytes 15728644
  369.8 86.1 %slice-start.6 = ((s8[20971520]{0:T(1024)(128)(4,1)}), s8[4194304]{0:T(1024)(128)(4,1)S(1)}, s32[]{:S(2)}) async-start(s8[20971520]{0:T(1024)(128)(4,1)} %bitcast.117), calls=%async_computation.10 | async-start | bytes 8388608
  370.7 82.0 %copy-start.3 = (f32[320,4096]{1,0:T(8,128)}, f32[320,4096]{1,0:T(8,128)S(1)}, u32[]{:S(2)}) copy-start(f32[320,4096]{1,0:T(8,128)S(1)} %convolution_multiply_fusion.1) | copy-start | bytes 15728644
  370.7 82.0 %copy-start.9 = (bf16[4096,256]{0,1:T(8,128)(2,1)S(1)}, bf16[4096,256]{0,1:T(8,128)(2,1)}, u32[]{:S(2)}) copy-start(bf16[4096,256]{0,1:T(8,128)(2,1)} %all-gather.5.cloned.1.call-done) | copy-start | bytes 6291460
  370.7 85.1 %slice-start.7 = ((s8[20971520]{0:T(1024)(128)(4,1)}), s8[4194304]{0:T(1024)(128)(4,1)S(1)}, s32[]{:S(2)}) async-start(s8[20971520]{0:T(1024)(128)(4,1)} %bitcast.117), calls=%async_computation.11 | async-start | bytes 8388608
  370.7 85.1 %slice-start.8 = ((s8[20971520]{0:T(1024)(128)(4,1)}), s8[4194304]{0:T(1024)(128)(4,1)S(1)}, s32[]{:S(2)}) async-start(s8[20971520]{0:T(1024)(128)(4,1)} %bitcast.117), calls=%async_computation.12 | async-start | bytes 8388608
  370.7 85.1 %slice-start.9 = ((s8[20971520]{0:T(1024)(128)(4,1)}), s8[4194304]{0:T(1024)(128)(4,1)S(1)}, s32[]{:S(2)}) async-start(s8[20971520]{0:T(1024)(128)(4,1)} %bitcast.117), calls=%async_computation.13 | async-start | bytes 8388608
  370.7 85.1 %slice-start.10 = ((s8[20971520]{0:T(1024)(128)(4,1)}), s8[4194304]{0:T(1024)(128)(4,1)S(1)}, s32[]{:S(2)}) async-start(s8[20971520]{0:T(1024)(128)(4,1)} %bitcast.117), calls=%async_computation.14 | async-start | bytes 8388608
  453.6 2.2 copy-start.4
  623.2 109.2 %slice-start = ((s8[5242880]{0:T(1024)(128)(4,1)}), s8[4194304]{0:T(1024)(128)(4,1)S(1)}, s32[]{:S(2)}) async-start(s8[5242880]{0:T(1024)(128)(4,1)} %bitcast.109), calls=%async_computation.4 | async-start | bytes 8388608
  672.9 59.6 %slice-start.1 = ((s8[5242880]{0:T(1024)(128)(4,1)}), s8[1048576]{0:T(1024)(128)(4,1)S(1)}, s32[]{:S(2)}) async-start(s8[5242880]{0:T(1024)(128)(4,1)} %bitcast.109), calls=%async_computation.5 | async-start | bytes 2097152
  722.4 10.0 %copy-start.5 = (f32[1,320,4096]{2,0,1:T(1,128)S(1)}, f32[1,320,4096]{2,0,1:T(1,128)}, u32[]{:S(2)}) copy-start(f32[1,320,4096]{2,0,1:T(1,128)} %fusion.8) | copy-start | bytes 15728644
  722.4 10.0 %copy-start.6 = (f32[1,320,4096]{2,0,1:T(1,128)S(1)}, f32[1,320,4096]{2,0,1:T(1,128)}, u32[]{:S(2)}) copy-start(f32[1,320,4096]{2,0,1:T(1,128)} %fusion.4) | copy-start | bytes 15728644
  787.9 18.2 %slice-start.2 = ((s8[5242880]{0:T(1024)(128)(4,1)}), s8[4194304]{0:T(1024)(128)(4,1)S(1)}, s32[]{:S(2)}) async-start(s8[5242880]{0:T(1024)(128)(4,1)} %bitcast.111), calls=%async_computation.6 | async-start | bytes 8388608
  788.0 18.2 %slice-start.4 = ((s8[5242880]{0:T(1024)(128)(4,1)}), s8[4194304]{0:T(1024)(128)(4,1)S(1)}, s32[]{:S(2)}) async-start(s8[5242880]{0:T(1024)(128)(4,1)} %bitcast.115), calls=%async_computation.8 | async-start | bytes 8388608
  797.1 9.1 %slice-start.3 = ((s8[5242880]{0:T(1024)(128)(4,1)}), s8[1048576]{0:T(1024)(128)(4,1)S(1)}, s32[]{:S(2)}) async-start(s8[5242880]{0:T(1024)(128)(4,1)} %bitcast.111), calls=%async_computation.7 | async-start | bytes 2097152
  797.1 9.1 %slice-start.5 = ((s8[5242880]{0:T(1024)(128)(4,1)}), s8[1048576]{0:T(1024)(128)(4,1)S(1)}, s32[]{:S(2)}) async-start(s8[5242880]{0:T(1024)(128)(4,1)} %bitcast.115), calls=%async_computation.9 | async-start | bytes 2097152
  797.1 14.5 %copy-start.1 = (bf16[320,4096]{1,0:T(8,128)(2,1)S(1)}, bf16[320,4096]{1,0:T(8,128)(2,1)}, u32[]{:S(2)}) copy-start(bf16[320,4096]{1,0:T(8,128)(2,1)} %param.14) | copy-start | bytes 7864324
Sparse Core Ops, SparseCore 0:
  11.4 59.0 all-gather.2
  93.1 139.6 reduce-scatter.1
  236.2 49.1 all-gather.4
where the time goes:
time: 824 us; the launch traced here: 818 us
  matrix products  417 us (51%)
  waiting for transfers between devices  250 us (30%)
  blocking collectives  79.3 us (10%)
  other arithmetic  51.8 us (6%)
  between operations  16.9 us (2%)
    dot_general x3, matrix products, local_dots(): jnp.einsum('jfd,fd->j', krylov.astype(jnp.float32), grad, precision=lax.P...  241 us
    dot_general x3, matrix products, per_device(): jnp.einsum('j,jfd->fd', proj, krylov.astype(jnp.float32), precision=lax.P...  148 us
    reduce_scatter x1, waiting for transfers between devices, per_device(): lax.psum_scatter(contract_first(down_rows, tangent) + contract_first(prob...  139 us
    all_gather x1, waiting for transfers between devices, per_device(): normed = lax.all_gather(normed_own, 'fsdp', axis=0, tiled=True)  59.8 us
    all_gather x1, waiting for transfers between devices, per_device(): loss_t = lax.all_gather(loss_own, 'fsdp', axis=0, tiled=True)  50.9 us
    psum x1, blocking collectives, per_device(): squares = lax.psum(own_left, 'fsdp') / count  39.7 us
    psum x1, blocking collectives, per_device(): proj = lax.psum(dots_own, 'fsdp') / count  39.6 us
  transfers between devices with their start and end apart: 3, of which 3 were waited for; matrix products, arithmetic and copies ran while one was open for 0% of the time, Pallas kernels for 0%

commit v1 on v0

v1 whole, which is shorter than its diff:
```python
import functools
import math

import jax
import jax.numpy as jnp
from jax import lax
from jax.experimental import pallas as pl
from jax.experimental.pallas import tpu as pltpu
from jax.sharding import PartitionSpec as P

LEN = 128
LIVE = 192
GROUP = 8
LANES = 128
F32 = jnp.float32
BF16 = jnp.bfloat16


def gelu_pair(gate_pre):
    coef = math.sqrt(2.0 / math.pi)
    cube = gate_pre * gate_pre * gate_pre
    tanh_val = jnp.tanh(coef * (gate_pre + 0.044715 * cube))
    act = 0.5 * gate_pre * (1.0 + tanh_val)
    slope = 0.5 * (1.0 + tanh_val) + 0.5 * gate_pre * (1.0 - tanh_val * tanh_val) * coef * (
        1.0 + 3.0 * 0.044715 * gate_pre * gate_pre
    )
    return (act, slope)


def dot_nn(left, right):
    return jnp.dot(left, right, preferred_element_type=F32)


def dot_nt(left, right):
    return lax.dot_general(left, right, (((1,), (1,)), ((), ())), preferred_element_type=F32)


def dot_tn(left, right):
    return lax.dot_general(left, right, (((0,), (0,)), ((), ())), preferred_element_type=F32)


def total(values):
    return jnp.sum(jnp.sum(values, axis=0, keepdims=True), axis=1, keepdims=True)


def reverse_bits(value, bits):
    out = value * 0
    for bit in range(bits):
        out = out | (((value >> bit) & 1) << (bits - 1 - bit))
    return out


def exchange(block, bit):
    count = lax.axis_size("fsdp")
    return lax.ppermute(block, "fsdp", [(one, one ^ (1 << bit)) for one in range(count)])


def gather_blocks(block, bits):
    for bit in reversed(range(bits)):
        block = jnp.concatenate([block, exchange(block, bit)], axis=0)
    return block


def params(mib, grid=1):
    return pltpu.CompilerParams(
        vmem_limit_bytes=mib << 20, dimension_semantics=("arbitrary",) * grid
    )


def whole(shape):
    return pl.BlockSpec(shape, lambda *_: (0,) * len(shape))


def live_tokens(info, gathered, gain, normed, spots):
    spare = info[1] - (LIVE - LEN)
    shift = lax.rem(spare, GROUP)
    half = (LIVE - LEN) // GROUP
    per = LEN // GROUP
    scale = gain[...].astype(F32)
    row_ids = lax.broadcasted_iota(jnp.int32, (GROUP, 1), 0)

    def load(group):
        return gathered[spots(info[0], group)].astype(F32)

    def tokens(slot):
        if slot < half:
            return load(slot)
        if slot < 2 * half:
            at = slot - half
            first = load(half + at)
            second = pltpu.roll(load(per + 2 * half - 1 - at), shift, 0)
            return jnp.where(GROUP * at + row_ids < spare, first, second)
        return load(per + slot - 2 * half)

    def norm(wide):
        mean = jnp.mean(wide * wide, axis=1, keepdims=True)
        return wide * lax.rsqrt(mean + 1e-06) * scale

    for pair in range(LIVE // (2 * GROUP)):
        both = [norm(tokens(2 * pair + side)) for side in range(2)]
        normed[2 * GROUP * pair : 2 * GROUP * (pair + 1), :] = jnp.concatenate(both, 0).astype(BF16)


def jvp_columns(info, tangent, hidden, down, probe, out, inv_ff, splits, places):
    values = dot_tn(tangent, down) + dot_tn(hidden, probe) * inv_ff
    rows = LIVE // splits
    for chunk in range(places):
        column, part = chunk // splits, chunk % splits
        piece = values[part * rows : (part + 1) * rows, column * LANES : (column + 1) * LANES]
        out[chunk ^ (info[0] & (places - 1))] = piece.astype(out.dtype)


def forward_kernel(
    blocks, inv_d, inv_ff, spots, splits, places,
    info, gathered, gain, gate, up, probe_gate, probe_up, down, probe_down,
    normed, normed_t, hidden, tangent, weight, act_out, send,
    sums,
):
    step = pl.program_id(0)
    width = gate.shape[1]

    @pl.when(step == 0)
    def _():
        live_tokens(info, gathered, gain, normed, spots)
        sums[...] = jnp.zeros_like(sums)

    @pl.when(step < blocks)
    def _():
        columns = normed[:, pl.ds(pl.multiple_of(step * width, width), width)]
        turned = columns.T
        normed_t[pl.ds(pl.multiple_of(step * width, width), width), :] = turned
        for at, rows in enumerate((gate, up, probe_gate, probe_up)):
            sums[at] += dot_nn(rows[...], turned)

    @pl.when(step == blocks - 1)
    def _():
        up_pre = sums[1]
        act, slope = gelu_pair(sums[0])
        hidden[...] = (act * up_pre).astype(BF16)
        tangent[...] = (
            slope * (sums[2] * inv_d) * up_pre + act * (sums[3] * inv_d)
        ).astype(BF16)
        weight[...] = up_pre * slope
        act_out[...] = act

    @pl.when(step >= blocks)
    def _():
        jvp_columns(
            info, tangent[...], hidden[...], down[...], probe_down[...], send, inv_ff, splits, places
        )


def keep_kernel(inv_ff, splits, places, info, tangent, hidden, down, probe_down, keep):
    jvp_columns(
        info, tangent[...], hidden[...], down[...], probe_down[...], keep, inv_ff, splits, places
    )


def gram_kernel(blocks, krylov, out, sums):
    step = pl.program_id(0)
    basis, rows, width = krylov.shape
    stack = krylov[...]
    if rows % 16:
        stack = stack.astype(F32).reshape(basis * rows, width).astype(BF16)
    else:
        stack = stack.reshape(basis * rows, width)

    @pl.when(step == 0)
    def _():
        sums[...] = jnp.zeros_like(sums)

    sums[...] += dot_nt(stack, stack)

    @pl.when(step == blocks - 1)
    def _():
        size = basis * rows
        own = lax.broadcasted_iota(jnp.int32, (size, size), 0)
        other = lax.broadcasted_iota(jnp.int32, (size, size), 1)
        same = jnp.where(lax.rem(own, rows) == lax.rem(other, rows), sums[...], 0.0)
        lane = lax.broadcasted_iota(jnp.int32, (1, LANES), 1)
        group = lax.broadcasted_iota(jnp.int32, (1, size), 1) // rows
        for one in range(basis):
            line = jnp.sum(same[one * rows : (one + 1) * rows], axis=0, keepdims=True)
            entry = jnp.zeros((1, LANES), F32)
            for two in range(basis):
                value = jnp.sum(jnp.where(group == two, line, 0.0), axis=1, keepdims=True)
                entry = entry + jnp.where(lane == two, value, 0.0)
            out[one : one + 1, :] = entry


def product_kernel(krylov, normed, normed_t, out, square):
    step = pl.program_id(0)

    @pl.when(step == 0)
    def _():
        out[...] = jnp.zeros_like(out)
        square[...] = jnp.zeros_like(square)

    turned = normed_t[...]
    for one in range(krylov.shape[0]):
        out[one] += dot_nn(krylov[one], turned)
    square[...] += dot_nn(normed[...], turned)


def back_kernel(
    blocks, inv_d, inv_ff, splits,
    info, gathered, down, krylov, hidden, weight, act, prod_gate, prod_up, square,
    gram_gate, gram_up, gram_down,
    loss, s_out, r_out, stats,
    sums, loss_square,
):
    step = pl.program_id(0)
    basis, rows, width = krylov.shape

    @pl.when(step == 0)
    def _():
        for column in range(loss.shape[1] // LANES):
            pieces = [
                gathered[(column * splits + part) ^ info[0]] for part in range(splits)
            ]
            if splits > 1:
                piece = jnp.concatenate([one.astype(F32) for one in pieces], 0).astype(BF16)
            else:
                piece = pieces[0]
            loss[:, column * LANES : (column + 1) * LANES] = piece
        sums[...] = jnp.zeros_like(sums)
        loss_square[...] = jnp.zeros_like(loss_square)

    columns = loss[:, pl.ds(pl.multiple_of(step * width, width), width)]
    turned = columns.T
    for one in range(basis):
        sums[one] += dot_nn(krylov[one], turned)
    sums[basis] += dot_nn(down[...], turned)
    loss_square[...] += dot_nn(columns, turned)

    @pl.when(step == blocks - 1)
    def _():
        back = sums[basis]
        s_term = (back * weight[...]).astype(BF16)
        r_term = (back * act[...]).astype(BF16)
        s_out[...] = s_term
        r_out[...] = r_term
        held = hidden[...]
        wide_s, wide_r, wide_h = s_term.astype(F32), r_term.astype(F32), held.astype(F32)
        for one in range(basis):
            value = inv_d * (wide_s * prod_gate[one] + wide_r * prod_up[one])
            value = total(value + inv_ff * (wide_h * sums[one]))
            stats[one : one + 1, :] = jnp.broadcast_to(value, (1, LANES))
        squares = inv_d * inv_d * ((dot_tn(s_term, s_term) + dot_tn(r_term, r_term)) * square[...])
        squares = total(squares + inv_ff * inv_ff * (dot_tn(held, held) * loss_square[...]))
        stats[basis : 2 * basis, :] = jnp.broadcast_to(squares, (basis, LANES))
        stats[2 * basis : 3 * basis, :] = gram_gate[...] + gram_up[...] + gram_down[...]


def new_kernel(
    basis, count, inv_d, inv_ff,
    stats, s_term, r_term, hidden, normed, loss, krylov_gate, krylov_up, krylov_down,
    new_gate, new_up, new_down, coefficients,
    scales, wide,
):
    @pl.when(pl.program_id(0) == 0)
    def _():
        proj = [stats[one, 0] / count for one in range(basis)]
        squares = stats[basis, 0]
        for one in range(basis):
            line = stats[2 * basis + one, 0] * proj[0]
            for two in range(1, basis):
                line = line + stats[2 * basis + one, two] * proj[two]
            squares = squares + proj[one] * (line - 2.0 * stats[one, 0])
        mean = jnp.maximum(jnp.full((8, LANES), squares / count, F32), 0.0)
        norm = jnp.sqrt(mean + 1e-06)
        inverse = jnp.max(1.0 / norm)
        for one in range(basis):
            coefficients[one] = proj[one]
            scales[one] = proj[one] * inverse
        coefficients[basis] = jnp.max(norm)
        scales[basis] = inverse

    weights = [scales[one] for one in range(basis)]
    inverse = scales[basis]
    rows = s_term.shape[0]
    tile = 16 if rows % 16 == 0 else rows
    for left, right, scale, krylov, out in (
        (s_term, normed, inv_d, krylov_gate, new_gate),
        (r_term, normed, inv_d, krylov_up, new_up),
        (hidden, loss, inv_ff, krylov_down, new_down),
    ):
        wide[...] = dot_nn(left[...], right[...]) * (scale * inverse)

        def body(at, carry, krylov=krylov, out=out):
            here = pl.ds(pl.multiple_of(at * tile, tile), tile)
            value = wide[here, :]
            for one in range(basis):
                value = value - weights[one] * krylov[one, here, :].astype(F32)
            out[here, :] = value.astype(BF16)
            return carry

        lax.fori_loop(0, rows // tile, body, 0, unroll=2 if (rows // tile) % 2 == 0 else 1)


def per_device(
    inputs, norm_gain, lengths, gate_rows, up_rows, down_rows, krylov_gate, krylov_up, krylov_down
):
    basis, rows, width = krylov_gate.shape
    devices = lax.axis_size("fsdp")
    bits = devices.bit_length() - 1
    hidden_all = rows * devices
    count = 3.0 * width * hidden_all
    inv_d = 1.0 / math.sqrt(width)
    inv_ff = 1.0 / math.sqrt(hidden_all)
    me = lax.axis_index("fsdp").astype(jnp.int32)
    mirror = reverse_bits(me, bits)
    info = jnp.stack([mirror, lengths[0]])

    own_tokens = inputs.shape[0]
    tokens = own_tokens * devices
    if own_tokens % GROUP == 0:
        sub = own_tokens // GROUP
        gathered = gather_blocks(inputs.reshape(sub, GROUP, width), bits)

        def spots(flip, group):
            return (reverse_bits(group // sub, bits) ^ flip) * sub + group % sub

    else:
        gathered = lax.all_gather(inputs, "fsdp", axis=0, tiled=True)
        gathered = gathered.reshape(tokens // GROUP, GROUP, width)

        def spots(flip, group):
            return group

    splits = devices // (width // LANES)
    chunk_rows = LIVE // splits
    cols = min(512, width // 2)
    blocks = width // cols
    places = devices // blocks
    half = blocks // 2
    gain = norm_gain.reshape(1, width)

    def fwd_spec(block, at):
        return pl.BlockSpec(block, at)

    def col(step):
        return jnp.minimum(step, blocks - 1)

    def send_col(step, info):
        return (half + jnp.maximum(step - blocks, 0)) ^ (info[0] // places)

    weights = pl.BlockSpec((rows, cols), lambda step, info: (0, col(step)))
    probe = pl.BlockSpec((None, rows, cols), lambda step, info: (basis - 1, 0, col(step)))
    normed, normed_t, hidden, tangent, weight, act, send = pl.pallas_call(
        functools.partial(
            forward_kernel, blocks, inv_d, inv_ff, spots, splits, places
        ),
        grid_spec=pltpu.PrefetchScalarGridSpec(
            num_scalar_prefetch=1,
            grid=(blocks + half,),
            in_specs=[
                whole(gathered.shape),
                whole(gain.shape),
                weights,
                weights,
                probe,
                probe,
                pl.BlockSpec((rows, cols), lambda step, info: (0, send_col(step, info))),
                pl.BlockSpec(
                    (None, rows, cols), lambda step, info: (basis - 1, 0, send_col(step, info))
                ),
            ],
            out_specs=[
                whole((LIVE, width)),
                whole((width, LIVE)),
                whole((rows, LIVE)),
                whole((rows, LIVE)),
                whole((rows, LIVE)),
                whole((rows, LIVE)),
                pl.BlockSpec(
                    (places, chunk_rows, LANES),
                    lambda step, info: (jnp.maximum(step - blocks, 0), 0, 0),
                ),
            ],
            scratch_shapes=[pltpu.VMEM((4, rows, LIVE), F32)],
        ),
        out_shape=[
            jax.ShapeDtypeStruct((LIVE, width), BF16),
            jax.ShapeDtypeStruct((width, LIVE), BF16),
            jax.ShapeDtypeStruct((rows, LIVE), BF16),
            jax.ShapeDtypeStruct((rows, LIVE), BF16),
            jax.ShapeDtypeStruct((rows, LIVE), F32),
            jax.ShapeDtypeStruct((rows, LIVE), F32),
            jax.ShapeDtypeStruct((devices // 2, chunk_rows, LANES), BF16),
        ],
        compiler_params=params(32),
        cost_estimate=pl.CostEstimate(
            flops=10 * rows * width * LIVE,
            bytes_accessed=10 * rows * width + 6 * LIVE * width,
            transcendentals=rows * LIVE,
        ),
        name="forward",
    )(info, gathered, gain, gate_rows, up_rows, krylov_gate, krylov_up, down_rows, krylov_down)

    got = exchange(send, 0)

    def keep_col(step, info):
        return step ^ (info[0] // places)

    keep = pl.pallas_call(
        functools.partial(keep_kernel, inv_ff, splits, places),
        grid_spec=pltpu.PrefetchScalarGridSpec(
            num_scalar_prefetch=1,
            grid=(half,),
            in_specs=[
                whole((rows, LIVE)),
                whole((rows, LIVE)),
                pl.BlockSpec((rows, cols), lambda step, info: (0, keep_col(step, info))),
                pl.BlockSpec(
                    (None, rows, cols), lambda step, info: (basis - 1, 0, keep_col(step, info))
                ),
            ],
            out_specs=pl.BlockSpec((places, chunk_rows, LANES), lambda step, info: (step, 0, 0)),
        ),
        out_shape=jax.ShapeDtypeStruct((devices // 2, chunk_rows, LANES), F32),
        compiler_params=params(16),
        cost_estimate=pl.CostEstimate(
            flops=2 * rows * width * LIVE,
            bytes_accessed=2 * rows * width + 2 * LIVE * width,
            transcendentals=0,
        ),
        name="keep",
    )(info, tangent, hidden, down_rows, krylov_down)

    for bit in range(1, bits):
        part = keep.shape[0] // 2
        send = (keep[part:] + got[part:].astype(F32)).astype(BF16)
        keep = keep[:part] + got[:part].astype(F32)
        got = exchange(send, bit)
    loss_own = (keep + got.astype(F32)).astype(BF16)
    loss_all = gather_blocks(loss_own, bits)

    lines = 32 if rows % 32 == 0 else rows
    pieces = rows // lines

    def gram(krylov):
        return pl.pallas_call(
            functools.partial(gram_kernel, pieces),
            grid=(pieces,),
            in_specs=[pl.BlockSpec((basis, lines, width), lambda step: (0, step, 0))],
            out_specs=whole((basis, LANES)),
            out_shape=jax.ShapeDtypeStruct((basis, LANES), F32),
            scratch_shapes=[pltpu.VMEM((basis * lines, basis * lines), F32)],
            compiler_params=params(24),
            cost_estimate=pl.CostEstimate(
                flops=2 * basis * basis * lines * rows * width,
                bytes_accessed=2 * basis * rows * width,
                transcendentals=0,
            ),
            name="gram",
        )(krylov)

    def product(krylov):
        return pl.pallas_call(
            product_kernel,
            grid=(blocks,),
            in_specs=[
                pl.BlockSpec((basis, rows, cols), lambda step: (0, 0, step)),
                pl.BlockSpec((LIVE, cols), lambda step: (0, step)),
                pl.BlockSpec((cols, LIVE), lambda step: (step, 0)),
            ],
            out_specs=[whole((basis, rows, LIVE)), whole((LIVE, LIVE))],
            out_shape=[
                jax.ShapeDtypeStruct((basis, rows, LIVE), F32),
                jax.ShapeDtypeStruct((LIVE, LIVE), F32),
            ],
            compiler_params=params(24),
            cost_estimate=pl.CostEstimate(
                flops=2 * basis * rows * width * LIVE,
                bytes_accessed=2 * basis * rows * width + 4 * basis * rows * LIVE,
                transcendentals=0,
            ),
            name="product",
        )(krylov, normed, normed_t)

    gram_gate, gram_up, gram_down = gram(krylov_gate), gram(krylov_up), gram(krylov_down)
    prod_gate, square = product(krylov_gate)
    prod_up, _ = product(krylov_up)

    loss, s_term, r_term, stats = pl.pallas_call(
        functools.partial(back_kernel, blocks, inv_d, inv_ff, splits),
        grid_spec=pltpu.PrefetchScalarGridSpec(
            num_scalar_prefetch=1,
            grid=(blocks,),
            in_specs=[
                whole(loss_all.shape),
                pl.BlockSpec((rows, cols), lambda step, info: (0, step)),
                pl.BlockSpec((basis, rows, cols), lambda step, info: (0, 0, step)),
                whole((rows, LIVE)),
                whole((rows, LIVE)),
                whole((rows, LIVE)),
                whole((basis, rows, LIVE)),
                whole((basis, rows, LIVE)),
                whole((LIVE, LIVE)),
                whole((basis, LANES)),
                whole((basis, LANES)),
                whole((basis, LANES)),
            ],
            out_specs=[
                whole((LIVE, width)),
                whole((rows, LIVE)),
                whole((rows, LIVE)),
                whole((3 * basis, LANES)),
            ],
            scratch_shapes=[
                pltpu.VMEM((basis + 1, rows, LIVE), F32),
                pltpu.VMEM((LIVE, LIVE), F32),
            ],
        ),
        out_shape=[
            jax.ShapeDtypeStruct((LIVE, width), BF16),
            jax.ShapeDtypeStruct((rows, LIVE), BF16),
            jax.ShapeDtypeStruct((rows, LIVE), BF16),
            jax.ShapeDtypeStruct((3 * basis, LANES), F32),
        ],
        compiler_params=params(40),
        cost_estimate=pl.CostEstimate(
            flops=2 * (basis + 1) * rows * width * LIVE,
            bytes_accessed=2 * (basis + 1) * rows * width + 8 * basis * rows * LIVE,
            transcendentals=0,
        ),
        name="back",
    )(
        info, loss_all, down_rows, krylov_down, hidden, weight, act, prod_gate, prod_up, square,
        gram_gate, gram_up, gram_down,
    )

    for bit in range(bits):
        stats = stats + exchange(stats, bit)

    narrow = min(256, cols)
    krylov_spec = pl.BlockSpec((basis, rows, narrow), lambda step: (0, 0, step))
    token_spec = pl.BlockSpec((LIVE, narrow), lambda step: (0, step))
    out_spec = pl.BlockSpec((rows, narrow), lambda step: (0, step))
    out_shape = jax.ShapeDtypeStruct((rows, width), BF16)
    new_gate, new_up, new_down, coefficients = pl.pallas_call(
        functools.partial(new_kernel, basis, count, inv_d, inv_ff),
        grid=(width // narrow,),
        in_specs=[
            pl.BlockSpec(memory_space=pltpu.SMEM),
            whole((rows, LIVE)),
            whole((rows, LIVE)),
            whole((rows, LIVE)),
            token_spec,
            token_spec,
            krylov_spec,
            krylov_spec,
            krylov_spec,
        ],
        out_specs=[out_spec, out_spec, out_spec, pl.BlockSpec(memory_space=pltpu.SMEM)],
        out_shape=[
            out_shape,
            out_shape,
            out_shape,
            jax.ShapeDtypeStruct((basis + 1,), F32),
        ],
        scratch_shapes=[pltpu.SMEM((basis + 1,), F32), pltpu.VMEM((rows, narrow), F32)],
        compiler_params=params(32),
        cost_estimate=pl.CostEstimate(
            flops=6 * rows * width * LIVE,
            bytes_accessed=6 * (basis + 1) * rows * width,
            transcendentals=0,
        ),
        name="new",
    )(stats, s_term, r_term, hidden, normed, loss, krylov_gate, krylov_up, krylov_down)
    return (new_gate, new_up, new_down, coefficients)


def solution(mesh):
    placed = (
        P("fsdp", None),
        P(),
        P(),
        P("fsdp", None),
        P("fsdp", None),
        P("fsdp", None),
        P(None, "fsdp", None),
        P(None, "fsdp", None),
        P(None, "fsdp", None),
    )
    return jax.shard_map(
        per_device,
        mesh=mesh,
        in_specs=placed,
        out_specs=(P("fsdp", None), P("fsdp", None), P("fsdp", None), P()),
        check_vma=False,
    )
```

time: 824 us -> 268 us (0.33)
  matrix products: 417 us -> 0 us
  waiting for transfers between devices: 250 us -> 60.8 us
  Pallas kernels: 0 us -> 117 us
  blocking collectives: 79.3 us -> 0 us
  local copies, waits for them, and re-layouts: 2.35 us -> 52.8 us
  other arithmetic: 51.8 us -> 3.15 us
  starting transfers between devices: 0.3 us -> 31.5 us
  between operations: 16.9 us -> 0.91 us
    dot_general x15 -> x0, matrix products: 417 us -> none  [the longest x3 241 us: local_dots(): jnp.einsum('jfd,fd->j', krylov.astype(jnp.float32), grad, precision=lax.P...]
    reduce_scatter x1 -> x0, waiting for transfers between devices: 139 us -> none  [per_device(): lax.psum_scatter(contract_first(down_rows, tangent) + contract_first(prob...]
    pallas_call x0 -> x9, Pallas kernels: none -> 117 us  [the longest x1 35 us: per_device(): pl.pallas_call(functools.partial(new_kernel, basis, count, inv_d, inv_ff)...]
    all_gather x2 -> x0, waiting for transfers between devices: 111 us -> none  [the longest x1 59.8 us: per_device(): normed = lax.all_gather(normed_own, 'fsdp', axis=0, tiled=True)]
    psum x2 -> x0, blocking collectives: 79.3 us -> none  [the longest x1 39.7 us: per_device(): squares = lax.psum(own_left, 'fsdp') / count]
    ppermute x0 -> x20, waiting for transfers between devices: none -> 60.8 us  [exchange(): lax.ppermute(block, 'fsdp', [(one, one ^ 1 << bit) for one in range(count)])]
    unnamed x46 -> x30, local copies, waits for them, and re-layouts: 2.35 us -> 49.1 us
    ppermute x0 -> x20, starting transfers between devices: none -> 31.5 us  [exchange(): lax.ppermute(block, 'fsdp', [(one, one ^ 1 << bit) for one in range(count)])]
  transfers between devices with their start and end apart: 3 -> 20, of which waited for: 3 -> 16; matrix products, arithmetic and copies ran while one was open for 0% -> 1% of each run, Pallas kernels for 0% -> 20%
where the time goes in v1:
time: 268 us; the launch traced here: 267 us
  Pallas kernels  117 us (44%)
  waiting for transfers between devices  60.8 us (23%)
  local copies, waits for them, and re-layouts  52.8 us (20%)
  starting transfers between devices  31.5 us (12%)
  other arithmetic  3.15 us (1%)
    ppermute x20, waiting for transfers between devices, exchange(): lax.ppermute(block, 'fsdp', [(one, one ^ 1 << bit) for one in range(count)])  60.8 us
    unnamed x30, local copies, waits for them, and re-layouts  49.1 us
    pallas_call x1, Pallas kernels, per_device(): pl.pallas_call(functools.partial(new_kernel, basis, count, inv_d, inv_ff)...  35 us
    ppermute x20, starting transfers between devices, exchange(): lax.ppermute(block, 'fsdp', [(one, one ^ 1 << bit) for one in range(count)])  31.5 us
    pallas_call x3, Pallas kernels, gram(): pl.pallas_call(functools.partial(gram_kernel, pieces), grid=(pieces,), in...  31 us
    pallas_call x2, Pallas kernels, product(): pl.pallas_call(product_kernel, grid=(blocks,), in_specs=[pl.BlockSpec((ba...  20.1 us
    pallas_call x1, Pallas kernels, per_device(): pl.pallas_call(functools.partial(back_kernel, blocks, inv_d, inv_ff, spli...  15.4 us
    pallas_call x1, Pallas kernels, per_device(): pl.pallas_call(functools.partial(forward_kernel, blocks, inv_d, inv_ff, s...  13.4 us
  transfers between devices with their start and end apart: 20, of which 16 were waited for; matrix products, arithmetic and copies ran while one was open for 1% of the time, Pallas kernels for 20%

profile of v1, /device:TPU:0, one launch (start us, length us, event | category | flops | bytes accessed | tf_op | source)
XLA Modules:
  0.0 266.6 jit_solution(2586167096070654922)
XLA Ops:
  0.6 4.1 %collective-permute-start = (bf16[1,8,4096]{2,1,0:T(8,128)(2,1)}, bf16[1,8,4096]{2,1,0:T(8,128)(2,1)S(1)}, u32[]{:S(2)}, u32[]{:S(2)}) collective-permute-start(bf16[1,8,4096]{2,1,0:T(8,128)(2,1)} %bitcast.5), channel_id=1, source_target_pairs={{0,16},{1,17},{2,18},{3,19},{4,20},{5,21},{6,22},{7,23},{8,24},{9,... | collective-permute-start | bytes 196616 | tf_op jit(solution)/shard_map/ppermute | solution.py:55
  4.7 3.9 %collective-permute-done = bf16[1,8,4096]{2,1,0:T(8,128)(2,1)S(1)} collective-permute-done((bf16[1,8,4096]{2,1,0:T(8,128)(2,1)}, bf16[1,8,4096]{2,1,0:T(8,128)(2,1)S(1)}, u32[]{:S(2)}, u32[]{:S(2)}) %collective-permute-start) | collective-permute-done | bytes 65568 | tf_op jit(solution)/shard_map/ppermute | solution.py:55
  10.2 1.5 constant_dynamic-update-slice_fusion.4
  11.7 2.8 %collective-permute-done.1 = bf16[2,8,4096]{2,1,0:T(8,128)(2,1)S(1)} collective-permute-done((bf16[2,8,4096]{2,1,0:T(8,128)(2,1)S(1)}, bf16[2,8,4096]{2,1,0:T(8,128)(2,1)S(1)}, u32[]{:S(2)}, u32[]{:S(2)}) %collective-permute-start.1) | collective-permute-done | bytes 131104 | tf_op jit(solution)/shard_map/ppermute | solution.py:55
  15.4 1.8 collective-permute-start.2
  17.8 4.0 %collective-permute-done.2 = bf16[4,8,4096]{2,1,0:T(8,128)(2,1)S(1)} collective-permute-done((bf16[4,8,4096]{2,1,0:T(8,128)(2,1)S(1)}, bf16[4,8,4096]{2,1,0:T(8,128)(2,1)S(1)}, u32[]{:S(2)}, u32[]{:S(2)}) %collective-permute-start.2) | collective-permute-done | bytes 262176 | tf_op jit(solution)/shard_map/ppermute | solution.py:55
  22.7 1.8 collective-permute-start.3
  26.0 6.7 %collective-permute-done.3 = bf16[8,8,4096]{2,1,0:T(8,128)(2,1)S(1)} collective-permute-done((bf16[8,8,4096]{2,1,0:T(8,128)(2,1)S(1)}, bf16[8,8,4096]{2,1,0:T(8,128)(2,1)S(1)}, u32[]{:S(2)}, u32[]{:S(2)}) %collective-permute-start.3) | collective-permute-done | bytes 524320 | tf_op jit(solution)/shard_map/ppermute | solution.py:55
  32.8 1.1 constant_dynamic-update-slice_fusion
  34.0 2.8 %collective-permute-done.4 = bf16[16,8,4096]{2,1,0:T(8,128)(2,1)} collective-permute-done((bf16[16,8,4096]{2,1,0:T(8,128)(2,1)}, bf16[16,8,4096]{2,1,0:T(8,128)(2,1)}, u32[]{:S(2)}, u32[]{:S(2)}) %collective-permute-start.4) | collective-permute-done | bytes 1048608 | tf_op jit(solution)/shard_map/ppermute | solution.py:55
  36.8 2.3 constant_dynamic-update-slice_fusion.5.gathered
  39.1 1.7 copy-done.7
  40.9 1.7 copy-done.8
  42.6 13.4 %forward.1 = (bf16[192,4096]{1,0:T(8,128)(2,1)S(1)}, bf16[4096,192]{1,0:T(8,128)(2,1)S(1)}, bf16[320,192]{1,0:T(8,128)(2,1)S(1)}, bf16[320,192]{1,0:T(8,128)(2,1...) custom-call(s32[2]{0:T(128)S(1)} %pad_add_fusion.info, ...), custom_call_target="tpu_custom_call" | custom-call | flops 2516582400 | bytes 17825792 | tf_op jit(solution)/shard_map/forward/pallas_call | solution.py:350
  56.3 7.0 %copy-done = bf16[8,320,4096]{2,1,0:T(8,128)(2,1)S(1)} copy-done((bf16[8,320,4096]{2,1,0:T(8,128)(2,1)S(1)}, bf16[8,320,4096]{2,1,0:T(8,128)(2,1)}, u32[]{:S(2)}) %copy-start) | copy-done | bytes 20971544
  63.2 2.6 keep.1
  66.0 1.6 collective-permute-start.6
  67.6 9.9 %collective-permute-done.6 = bf16[8,192,128]{2,1,0:T(8,128)(2,1)S(1)} collective-permute-done((bf16[8,192,128]{2,1,0:T(8,128)(2,1)S(1)}, bf16[8,192,128]{2,1,0:T(8,128)(2,1)S(1)}, u32[]{:S(2)}, u32[]{:S(2)}) %collective-permute-start.6) | collective-permute-done | bytes 393248 | tf_op jit(solution)/shard_map/ppermute | solution.py:55
  77.5 1.6 collective-permute-start.7
  79.1 4.8 %collective-permute-done.7 = bf16[4,192,128]{2,1,0:T(8,128)(2,1)S(1)} collective-permute-done((bf16[4,192,128]{2,1,0:T(8,128)(2,1)S(1)}, bf16[4,192,128]{2,1,0:T(8,128)(2,1)S(1)}, u32[]{:S(2)}, u32[]{:S(2)}) %collective-permute-start.7) | collective-permute-done | bytes 196640 | tf_op jit(solution)/shard_map/ppermute | solution.py:55
  84.0 2.2 collective-permute-start.8
  86.3 2.6 collective-permute-done.8
  88.9 5.7 %collective-permute-start.9 = (bf16[1,192,128]{2,1,0:T(8,128)(2,1)S(1)}, bf16[1,192,128]{2,1,0:T(8,128)(2,1)S(1)}, u32[]{:S(2)}, u32[]{:S(2)}) collective-permute-start(bf16[1,192,128]{2,1,0:T(8,128)(2,1)S(1)} %fusion.3), channel_id=1, source_target_pairs={{0,16},{1,17},{2,18},{3,19},{4,20},{5,21},{6,22},{7,23},{8,24},{9,... | collective-permute-start | bytes 147464 | tf_op jit(solution)/shard_map/ppermute | solution.py:55
  94.5 3.5 %collective-permute-done.9 = bf16[1,192,128]{2,1,0:T(8,128)(2,1)S(1)} collective-permute-done((bf16[1,192,128]{2,1,0:T(8,128)(2,1)S(1)}, bf16[1,192,128]{2,1,0:T(8,128)(2,1)S(1)}, u32[]{:S(2)}, u32[]{:S(2)}) %collective-permute-start.9) | collective-permute-done | bytes 49184 | tf_op jit(solution)/shard_map/ppermute | solution.py:55
  98.1 2.1 collective-permute-start.10
  100.2 2.9 %collective-permute-done.10 = bf16[1,192,128]{2,1,0:T(8,128)(2,1)S(1)} collective-permute-done((bf16[1,192,128]{2,1,0:T(8,128)(2,1)S(1)}, bf16[1,192,128]{2,1,0:T(8,128)(2,1)S(1)}, u32[]{:S(2)}, u32[]{:S(2)}) %collective-permute-start.10) | collective-permute-done | bytes 49184 | tf_op jit(solution)/shard_map/ppermute | solution.py:55
  103.3 7.0 %copy-done.2 = bf16[8,320,4096]{2,1,0:T(8,128)(2,1)S(1)} copy-done((bf16[8,320,4096]{2,1,0:T(8,128)(2,1)S(1)}, bf16[8,320,4096]{2,1,0:T(8,128)(2,1)}, u32[]{:S(2)}) %copy-start.2) | copy-done | bytes 20971544
  110.2 10.3 %gram.3.gram_gate = f32[8,128]{1,0:T(8,128)S(1)} custom-call(bf16[8,320,4096]{2,1,0:T(8,128)(2,1)S(1)} %copy-done.2), custom_call_target="tpu_custom_call" | custom-call | flops 5368709120 | bytes 20971520 | tf_op jit(solution)/shard_map/gram/pallas_call | solution.py:443
  120.6 1.6 collective-permute-start.12
  122.2 7.0 %copy-done.4 = bf16[8,320,4096]{2,1,0:T(8,128)(2,1)S(1)} copy-done((bf16[8,320,4096]{2,1,0:T(8,128)(2,1)S(1)}, bf16[8,320,4096]{2,1,0:T(8,128)(2,1)}, u32[]{:S(2)}) %copy-start.4) | copy-done | bytes 20971544
  129.2 10.3 %gram.4.gram_up = f32[8,128]{1,0:T(8,128)S(1)} custom-call(bf16[8,320,4096]{2,1,0:T(8,128)(2,1)S(1)} %copy-done.4), custom_call_target="tpu_custom_call" | custom-call | flops 5368709120 | bytes 20971520 | tf_op jit(solution)/shard_map/gram/pallas_call | solution.py:443
  139.6 1.5 collective-permute-start.13
  141.3 6.2 %collective-permute-done.13 = bf16[8,192,128]{2,1,0:T(8,128)(2,1)S(1)} collective-permute-done((bf16[8,192,128]{2,1,0:T(8,128)(2,1)S(1)}, bf16[8,192,128]{2,1,0:T(8,128)(2,1)S(1)}, u32[]{:S(2)}, u32[]{:S(2)}) %collective-permute-start.13) | collective-permute-done | bytes 393248 | tf_op jit(solution)/shard_map/ppermute | solution.py:55
  147.7 7.0 %copy-done.1 = bf16[8,320,4096]{2,1,0:T(8,128)(2,1)S(1)} copy-done((bf16[8,320,4096]{2,1,0:T(8,128)(2,1)S(1)}, bf16[8,320,4096]{2,1,0:T(8,128)(2,1)}, u32[]{:S(2)}) %copy-start.1) | copy-done | bytes 20971544
  154.7 10.3 %gram.5.gram_down = f32[8,128]{1,0:T(8,128)S(1)} custom-call(bf16[8,320,4096]{2,1,0:T(8,128)(2,1)S(1)} %copy-done.1), custom_call_target="tpu_custom_call" | custom-call | flops 5368709120 | bytes 20971520 | tf_op jit(solution)/shard_map/gram/pallas_call | solution.py:443
  165.1 7.0 %copy-done.3 = bf16[8,320,4096]{2,1,0:T(8,128)(2,1)S(1)} copy-done((bf16[8,320,4096]{2,1,0:T(8,128)(2,1)S(1)}, bf16[8,320,4096]{2,1,0:T(8,128)(2,1)}, u32[]{:S(2)}) %copy-start.3) | copy-done | bytes 20971544
  172.0 9.6 %product.2 = (f32[8,320,192]{2,1,0:T(8,128)S(1)}, f32[192,192]{1,0:T(8,128)S(1)}) custom-call(bf16[8,320,4096]{2,1,0:T(8,128)(2,1)S(1)} %copy-done.3, bf16[192,4096]{1,0:T(8,128)(2,1)S(1)} %get-tuple-element.23.normed, bf16[4096,192]{1,0:T(8,128)(2,1)S(1)} %get-tuple-element.24.normed_t), custom_call_target="tpu_custom_call" | custom-call | flops 4026531840 | bytes 22937600 | tf_op jit(solution)/shard_map/product/pallas_call | solution.py:460
  181.7 7.0 %copy-done.5 = bf16[8,320,4096]{2,1,0:T(8,128)(2,1)S(1)} copy-done((bf16[8,320,4096]{2,1,0:T(8,128)(2,1)S(1)}, bf16[8,320,4096]{2,1,0:T(8,128)(2,1)}, u32[]{:S(2)}) %copy-start.5) | copy-done | bytes 20971544
  188.6 10.5 %product.3 = (f32[8,320,192]{2,1,0:T(8,128)S(1)}, f32[192,192]{1,0:T(8,128)}) custom-call(bf16[8,320,4096]{2,1,0:T(8,128)(2,1)S(1)} %copy-done.5, bf16[192,4096]{1,0:T(8,128)(2,1)S(1)} %get-tuple-element.23.normed, bf16[4096,192]{1,0:T(8,128)(2,1)S(1)} %get-tuple-element.24.normed_t), custom_call_target="tpu_custom_call" | custom-call | flops 4026531840 | bytes 22937600 | tf_op jit(solution)/shard_map/product/pallas_call | solution.py:460
  199.2 15.4 %back.1 = (bf16[192,4096]{1,0:T(8,128)(2,1)S(1)}, bf16[320,192]{1,0:T(8,128)(2,1)S(1)}, bf16[320,192]{1,0:T(8,128)(2,1)S(1)}, f32[24,128]{1,0:T(8,128)S(1)}) custom-call(s32[2]{0:T(128)S(1)} %pad_add_fusion.info, bf16[32,192,128]{2,1,0:T(8,128)(2,1)S(1)} %constant_dynamic-update-slice_fusion.16.gathered, bf16[320,4096]{1,0:T(8,128)(2,1)S(1)} %copy-done.6, ...), custom_call_target="tpu_custom_call" | custom-call | flops 4529848320 | bytes 27525120 | tf_op jit(solution)/shard_map/back/pallas_call | solution.py:486
  215.9 1.4 collective-permute-start.16
  217.4 2.3 collective-permute-done.16
  220.1 3.2 %collective-permute-done.17 = f32[24,128]{1,0:T(8,128)S(1)} collective-permute-done((f32[24,128]{1,0:T(8,128)S(1)}, f32[24,128]{1,0:T(8,128)S(1)}, u32[]{:S(2)}, u32[]{:S(2)}) %collective-permute-start.17) | collective-permute-done | bytes 12320 | tf_op jit(solution)/shard_map/ppermute | solution.py:55
  223.3 2.0 collective-permute-start.18
  225.3 1.7 collective-permute-done.18
  227.0 2.1 collective-permute-start.19
  229.1 2.5 collective-permute-done.19
  231.6 35.0 %new.1 = (bf16[320,4096]{1,0:T(8,128)(2,1)}, bf16[320,4096]{1,0:T(8,128)(2,1)}, bf16[320,4096]{1,0:T(8,128)(2,1)}, f32[9]{0:T(128)}) custom-call(f32[24,128]{1,0:T(8,128)S(1)} %add.55.stats, bf16[320,192]{1,0:T(8,128)(2,1)S(1)} %get-tuple-element.29.s_term, bf16[320,192]{1,0:T(8,128)(2,1)S(1)} %get-tuple-element.30.r_term, ...), custom_call_target="tpu_custom_call" | custom-call | flops 1509949440 | bytes 70778880 | tf_op jit(solution)/shard_map/new/pallas_call | solution.py:542
  (53 shorter events, 8.7 us)
Async XLA Ops:
  0.6 8.0 %collective-permute-start = (bf16[1,8,4096]{2,1,0:T(8,128)(2,1)}, bf16[1,8,4096]{2,1,0:T(8,128)(2,1)S(1)}, u32[]{:S(2)}, u32[]{:S(2)}) collective-permute-start(bf16[1,8,4096]{2,1,0:T(8,128)(2,1)} %bitcast.5), channel_id=1, source_target_pairs={{0,16},{1,17},{2,18},{3,19},{4,20},{5,21},{6,22},{7,23},{8,24},{9,... | collective-permute-start | bytes 196616 | tf_op jit(solution)/shard_map/ppermute | solution.py:55
  9.4 5.0 %collective-permute-start.1 = (bf16[2,8,4096]{2,1,0:T(8,128)(2,1)S(1)}, bf16[2,8,4096]{2,1,0:T(8,128)(2,1)S(1)}, u32[]{:S(2)}, u32[]{:S(2)}) collective-permute-start(bf16[2,8,4096]{2,1,0:T(8,128)(2,1)S(1)} %pad_maximum_fusion.4), channel_id=1, source_target_pairs={{0,8},{1,9},{2,10},{3,11},{4,12},{5,13},{6,14},{7,15},{8,0},{9,1},... | collective-permute-start | bytes 393224 | tf_op jit(solution)/shard_map/ppermute | solution.py:55
  15.4 18.5 %copy-start.9 = (bf16[4096]{0:T(1024)(128)(2,1)S(1)}, bf16[4096]{0:T(1024)(128)(2,1)}, u32[]{:S(2)}) copy-start(bf16[4096]{0:T(1024)(128)(2,1)} %param.10) | copy-start | bytes 24580
  15.4 18.5 %copy-start.10 = (s32[2]{0:T(128)S(1)}, s32[2]{0:T(128)}, u32[]{:S(2)}) copy-start(s32[2]{0:T(128)} %param.11) | copy-start | bytes 28
  15.4 6.4 %collective-permute-start.2 = (bf16[4,8,4096]{2,1,0:T(8,128)(2,1)S(1)}, bf16[4,8,4096]{2,1,0:T(8,128)(2,1)S(1)}, u32[]{:S(2)}, u32[]{:S(2)}) collective-permute-start(bf16[4,8,4096]{2,1,0:T(8,128)(2,1)S(1)} %pad_maximum_fusion.2), channel_id=1, source_target_pairs={{0,4},{1,5},{2,6},{3,7},{4,0},{5,1},{6,2},{7,3},{8,12},{9,13},{10,... | collective-permute-start | bytes 786440 | tf_op jit(solution)/shard_map/ppermute | solution.py:55
  22.7 10.1 %collective-permute-start.3 = (bf16[8,8,4096]{2,1,0:T(8,128)(2,1)S(1)}, bf16[8,8,4096]{2,1,0:T(8,128)(2,1)S(1)}, u32[]{:S(2)}, u32[]{:S(2)}) collective-permute-start(bf16[8,8,4096]{2,1,0:T(8,128)(2,1)S(1)} %pad_maximum_fusion), channel_id=1, source_target_pairs={{0,2},{1,3},{2,0},{3,1},{4,6},{5,7},{6,4},{7,5},{8,10},{9,11},{10,... | collective-permute-start | bytes 1572872 | tf_op jit(solution)/shard_map/ppermute | solution.py:55
  25.2 13.9 %copy-start.6 = (bf16[320,4096]{1,0:T(8,128)(2,1)S(1)}, bf16[320,4096]{1,0:T(8,128)(2,1)}, u32[]{:S(2)}) copy-start(bf16[320,4096]{1,0:T(8,128)(2,1)} %down.5) | copy-start | bytes 7864324
  33.8 3.0 %collective-permute-start.4 = (bf16[16,8,4096]{2,1,0:T(8,128)(2,1)}, bf16[16,8,4096]{2,1,0:T(8,128)(2,1)}, u32[]{:S(2)}, u32[]{:S(2)}) collective-permute-start(bf16[16,8,4096]{2,1,0:T(8,128)(2,1)} %get-tuple-element.40), channel_id=1, source_target_pairs={{0,1},{1,0},{2,3},{3,2},{4,5},{5,4},{6,7},{7,6},{8,9},{9,8},{10,11... | collective-permute-start | bytes 3145736 | tf_op jit(solution)/shard_map/ppermute | solution.py:55
  39.1 1.7 copy-start.7
  40.9 1.7 copy-start.8
  56.0 9.8 %collective-permute-start.5 = (bf16[16,192,128]{2,1,0:T(8,128)(2,1)S(1)}, bf16[16,192,128]{2,1,0:T(8,128)(2,1)S(1)}, u32[]{:S(2)}, u32[]{:S(2)}) collective-permute-start(bf16[16,192,128]{2,1,0:T(8,128)(2,1)S(1)} %get-tuple-element.20), channel_id=1, source_target_pairs={{0,1},{1,0},{2,3},{3,2},{4,5},{5,4},{6,7},{7,6},{8,9},{9,8},{10,11... | collective-permute-start | bytes 2359304 | tf_op jit(solution)/shard_map/ppermute | solution.py:55
  56.3 7.0 %copy-start = (bf16[8,320,4096]{2,1,0:T(8,128)(2,1)S(1)}, bf16[8,320,4096]{2,1,0:T(8,128)(2,1)}, u32[]{:S(2)}) copy-start(bf16[8,320,4096]{2,1,0:T(8,128)(2,1)} %krylov_down.1) | copy-start | bytes 62914564
  66.0 11.5 %collective-permute-start.6 = (bf16[8,192,128]{2,1,0:T(8,128)(2,1)S(1)}, bf16[8,192,128]{2,1,0:T(8,128)(2,1)S(1)}, u32[]{:S(2)}, u32[]{:S(2)}) collective-permute-start(bf16[8,192,128]{2,1,0:T(8,128)(2,1)S(1)} %get-tuple-element.34), channel_id=1, source_target_pairs={{0,2},{1,3},{2,0},{3,1},{4,6},{5,7},{6,4},{7,5},{8,10},{9,11},{10,... | collective-permute-start | bytes 1179656 | tf_op jit(solution)/shard_map/ppermute | solution.py:55
  77.5 6.4 %collective-permute-start.7 = (bf16[4,192,128]{2,1,0:T(8,128)(2,1)S(1)}, bf16[4,192,128]{2,1,0:T(8,128)(2,1)S(1)}, u32[]{:S(2)}, u32[]{:S(2)}) collective-permute-start(bf16[4,192,128]{2,1,0:T(8,128)(2,1)S(1)} %get-tuple-element.36), channel_id=1, source_target_pairs={{0,4},{1,5},{2,6},{3,7},{4,0},{5,1},{6,2},{7,3},{8,12},{9,13},{10,... | collective-permute-start | bytes 589832 | tf_op jit(solution)/shard_map/ppermute | solution.py:55
  84.0 4.8 %collective-permute-start.8 = (bf16[2,192,128]{2,1,0:T(8,128)(2,1)S(1)}, bf16[2,192,128]{2,1,0:T(8,128)(2,1)S(1)}, u32[]{:S(2)}, u32[]{:S(2)}) collective-permute-start(bf16[2,192,128]{2,1,0:T(8,128)(2,1)S(1)} %get-tuple-element.38), channel_id=1, source_target_pairs={{0,8},{1,9},{2,10},{3,11},{4,12},{5,13},{6,14},{7,15},{8,0},{9,1},... | collective-permute-start | bytes 294920 | tf_op jit(solution)/shard_map/ppermute | solution.py:55
  88.9 9.2 %collective-permute-start.9 = (bf16[1,192,128]{2,1,0:T(8,128)(2,1)S(1)}, bf16[1,192,128]{2,1,0:T(8,128)(2,1)S(1)}, u32[]{:S(2)}, u32[]{:S(2)}) collective-permute-start(bf16[1,192,128]{2,1,0:T(8,128)(2,1)S(1)} %fusion.3), channel_id=1, source_target_pairs={{0,16},{1,17},{2,18},{3,19},{4,20},{5,21},{6,22},{7,23},{8,24},{9,... | collective-permute-start | bytes 147464 | tf_op jit(solution)/shard_map/ppermute | solution.py:55
  98.1 5.1 %collective-permute-start.10 = (bf16[1,192,128]{2,1,0:T(8,128)(2,1)S(1)}, bf16[1,192,128]{2,1,0:T(8,128)(2,1)S(1)}, u32[]{:S(2)}, u32[]{:S(2)}) collective-permute-start(bf16[1,192,128]{2,1,0:T(8,128)(2,1)S(1)} %get-tuple-element.33), channel_id=1, source_target_pairs={{0,16},{1,17},{2,18},{3,19},{4,20},{5,21},{6,22},{7,23},{8,24},{9,... | collective-permute-start | bytes 147464 | tf_op jit(solution)/shard_map/ppermute | solution.py:55
  103.2 17.4 %collective-permute-start.11 = (bf16[2,192,128]{2,1,0:T(8,128)(2,1)S(1)}, bf16[2,192,128]{2,1,0:T(8,128)(2,1)S(1)}, u32[]{:S(2)}, u32[]{:S(2)}) collective-permute-start(bf16[2,192,128]{2,1,0:T(8,128)(2,1)S(1)} %pad_maximum_fusion.5), channel_id=1, source_target_pairs={{0,8},{1,9},{2,10},{3,11},{4,12},{5,13},{6,14},{7,15},{8,0},{9,1},... | collective-permute-start | bytes 294920 | tf_op jit(solution)/shard_map/ppermute | solution.py:55
  103.3 7.0 %copy-start.2 = (bf16[8,320,4096]{2,1,0:T(8,128)(2,1)S(1)}, bf16[8,320,4096]{2,1,0:T(8,128)(2,1)}, u32[]{:S(2)}) copy-start(bf16[8,320,4096]{2,1,0:T(8,128)(2,1)} %krylov_gate.1) | copy-start | bytes 62914564
  120.6 19.0 %collective-permute-start.12 = (bf16[4,192,128]{2,1,0:T(8,128)(2,1)S(1)}, bf16[4,192,128]{2,1,0:T(8,128)(2,1)S(1)}, u32[]{:S(2)}, u32[]{:S(2)}) collective-permute-start(bf16[4,192,128]{2,1,0:T(8,128)(2,1)S(1)} %pad_maximum_fusion.3), channel_id=1, source_target_pairs={{0,4},{1,5},{2,6},{3,7},{4,0},{5,1},{6,2},{7,3},{8,12},{9,13},{10,... | collective-permute-start | bytes 589832 | tf_op jit(solution)/shard_map/ppermute | solution.py:55
  122.2 7.0 %copy-start.4 = (bf16[8,320,4096]{2,1,0:T(8,128)(2,1)S(1)}, bf16[8,320,4096]{2,1,0:T(8,128)(2,1)}, u32[]{:S(2)}) copy-start(bf16[8,320,4096]{2,1,0:T(8,128)(2,1)} %krylov_up.1) | copy-start | bytes 62914564
  139.6 7.8 %collective-permute-start.13 = (bf16[8,192,128]{2,1,0:T(8,128)(2,1)S(1)}, bf16[8,192,128]{2,1,0:T(8,128)(2,1)S(1)}, u32[]{:S(2)}, u32[]{:S(2)}) collective-permute-start(bf16[8,192,128]{2,1,0:T(8,128)(2,1)S(1)} %pad_maximum_fusion.1), channel_id=1, source_target_pairs={{0,2},{1,3},{2,0},{3,1},{4,6},{5,7},{6,4},{7,5},{8,10},{9,11},{10,... | collective-permute-start | bytes 1179656 | tf_op jit(solution)/shard_map/ppermute | solution.py:55
  147.7 51.5 %collective-permute-start.14 = (bf16[16,192,128]{2,1,0:T(8,128)(2,1)S(1)}, bf16[16,192,128]{2,1,0:T(8,128)(2,1)S(1)}, u32[]{:S(2)}, u32[]{:S(2)}) collective-permute-start(bf16[16,192,128]{2,1,0:T(8,128)(2,1)S(1)} %get-tuple-element.42), channel_id=1, source_target_pairs={{0,1},{1,0},{2,3},{3,2},{4,5},{5,4},{6,7},{7,6},{8,9},{9,8},{10,11... | collective-permute-start | bytes 2359304 | tf_op jit(solution)/shard_map/ppermute | solution.py:55
  147.7 7.0 %copy-start.1 = (bf16[8,320,4096]{2,1,0:T(8,128)(2,1)S(1)}, bf16[8,320,4096]{2,1,0:T(8,128)(2,1)}, u32[]{:S(2)}) copy-start(bf16[8,320,4096]{2,1,0:T(8,128)(2,1)} %krylov_down.1) | copy-start | bytes 62914564
  165.1 7.0 %copy-start.3 = (bf16[8,320,4096]{2,1,0:T(8,128)(2,1)S(1)}, bf16[8,320,4096]{2,1,0:T(8,128)(2,1)}, u32[]{:S(2)}) copy-start(bf16[8,320,4096]{2,1,0:T(8,128)(2,1)} %krylov_gate.1) | copy-start | bytes 62914564
  181.7 7.0 %copy-start.5 = (bf16[8,320,4096]{2,1,0:T(8,128)(2,1)S(1)}, bf16[8,320,4096]{2,1,0:T(8,128)(2,1)}, u32[]{:S(2)}) copy-start(bf16[8,320,4096]{2,1,0:T(8,128)(2,1)} %krylov_up.1) | copy-start | bytes 62914564
  214.6 1.3 collective-permute-start.15
  215.9 3.7 %collective-permute-start.16 = (f32[24,128]{1,0:T(8,128)S(1)}, f32[24,128]{1,0:T(8,128)S(1)}, u32[]{:S(2)}, u32[]{:S(2)}) collective-permute-start(f32[24,128]{1,0:T(8,128)S(1)} %add.51), channel_id=1, source_target_pairs={{0,2},{1,3},{2,0},{3,1},{4,6},{5,7},{6,4},{7,5},{8,10},{9,11},{10,... | collective-permute-start | bytes 36872 | tf_op jit(solution)/shard_map/ppermute | solution.py:55
  219.6 3.7 %collective-permute-start.17 = (f32[24,128]{1,0:T(8,128)S(1)}, f32[24,128]{1,0:T(8,128)S(1)}, u32[]{:S(2)}, u32[]{:S(2)}) collective-permute-start(f32[24,128]{1,0:T(8,128)S(1)} %add.52), channel_id=1, source_target_pairs={{0,4},{1,5},{2,6},{3,7},{4,0},{5,1},{6,2},{7,3},{8,12},{9,13},{10,... | collective-permute-start | bytes 36872 | tf_op jit(solution)/shard_map/ppermute | solution.py:55
  223.3 3.7 %collective-permute-start.18 = (f32[24,128]{1,0:T(8,128)S(1)}, f32[24,128]{1,0:T(8,128)S(1)}, u32[]{:S(2)}, u32[]{:S(2)}) collective-permute-start(f32[24,128]{1,0:T(8,128)S(1)} %add.53), channel_id=1, source_target_pairs={{0,8},{1,9},{2,10},{3,11},{4,12},{5,13},{6,14},{7,15},{8,0},{9,1},... | collective-permute-start | bytes 36872 | tf_op jit(solution)/shard_map/ppermute | solution.py:55
  227.0 4.6 %collective-permute-start.19 = (f32[24,128]{1,0:T(8,128)S(1)}, f32[24,128]{1,0:T(8,128)S(1)}, u32[]{:S(2)}, u32[]{:S(2)}) collective-permute-start(f32[24,128]{1,0:T(8,128)S(1)} %add.54), channel_id=1, source_target_pairs={{0,16},{1,17},{2,18},{3,19},{4,20},{5,21},{6,22},{7,23},{8,24},{9,... | collective-permute-start | bytes 36872 | tf_op jit(solution)/shard_map/ppermute | solution.py:55

commit v2 on v1

v2 whole, which is shorter than its diff:
```python
import functools
import math

import jax
import jax.numpy as jnp
from jax import lax
from jax.experimental import pallas as pl
from jax.experimental.pallas import tpu as pltpu
from jax.sharding import PartitionSpec as P

LEN = 128
LIVE = 192
GROUP = 8
LANES = 128
F32 = jnp.float32
BF16 = jnp.bfloat16


def gelu_pair(gate_pre):
    coef = math.sqrt(2.0 / math.pi)
    cube = gate_pre * gate_pre * gate_pre
    tanh_val = jnp.tanh(coef * (gate_pre + 0.044715 * cube))
    act = 0.5 * gate_pre * (1.0 + tanh_val)
    slope = 0.5 * (1.0 + tanh_val) + 0.5 * gate_pre * (1.0 - tanh_val * tanh_val) * coef * (
        1.0 + 3.0 * 0.044715 * gate_pre * gate_pre
    )
    return (act, slope)


def dot_nn(left, right):
    return jnp.dot(left, right, preferred_element_type=F32)


def dot_nt(left, right):
    return lax.dot_general(left, right, (((1,), (1,)), ((), ())), preferred_element_type=F32)


def dot_tn(left, right):
    return lax.dot_general(left, right, (((0,), (0,)), ((), ())), preferred_element_type=F32)


def total(values):
    return jnp.sum(jnp.sum(values, axis=0, keepdims=True), axis=1, keepdims=True)


def reverse_bits(value, bits):
    out = value * 0
    for bit in range(bits):
        out = out | (((value >> bit) & 1) << (bits - 1 - bit))
    return out


def exchange(block, bit):
    count = lax.axis_size("fsdp")
    return lax.ppermute(block, "fsdp", [(one, one ^ (1 << bit)) for one in range(count)])


def gather_blocks(block, bits, beside):
    made = []
    for bit in reversed(range(bits)):
        other = exchange(block, bit)
        if bit in beside:
            extra = beside[bit](block)
            other, extra = lax.optimization_barrier((other, extra))
            made.append(extra)
        if bit:
            block = jnp.concatenate([block, other], axis=0)
    return block, other, made


def after(value, earlier):
    return lax.optimization_barrier((value, earlier))[0]


def stacked(krylov):
    basis, rows, width = krylov.shape
    if rows % 16:
        return krylov.astype(F32).reshape(basis * rows, width).astype(BF16)
    return krylov.reshape(basis * rows, width)


def params(mib, grid=1):
    return pltpu.CompilerParams(
        vmem_limit_bytes=mib << 20, dimension_semantics=("arbitrary",) * grid
    )


def whole(shape):
    return pl.BlockSpec(shape, lambda *_: (0,) * len(shape))


def live_tokens(info, lower, upper, gain, normed, spots):
    spare = info[1] - (LIVE - LEN)
    shift = lax.rem(spare, GROUP)
    half = (LIVE - LEN) // GROUP
    per = LEN // GROUP
    scale = gain[...].astype(F32)
    row_ids = lax.broadcasted_iota(jnp.int32, (GROUP, 1), 0)

    half_groups = lower.shape[0]

    def load(group):
        spot = spots(info[0], group)
        place = lax.rem(spot, half_groups)
        return jnp.where(spot < half_groups, lower[place], upper[place]).astype(F32)

    def tokens(slot):
        if slot < half:
            return load(slot)
        if slot < 2 * half:
            at = slot - half
            first = load(half + at)
            second = pltpu.roll(load(per + 2 * half - 1 - at), shift, 0)
            return jnp.where(GROUP * at + row_ids < spare, first, second)
        return load(per + slot - 2 * half)

    def norm(wide):
        mean = jnp.mean(wide * wide, axis=1, keepdims=True)
        return wide * lax.rsqrt(mean + 1e-06) * scale

    for pair in range(LIVE // (2 * GROUP)):
        both = [norm(tokens(2 * pair + side)) for side in range(2)]
        normed[2 * GROUP * pair : 2 * GROUP * (pair + 1), :] = jnp.concatenate(both, 0).astype(BF16)


def jvp_columns(info, tangent, hidden, down, probe, out, inv_ff, splits, places):
    values = dot_tn(tangent, down) + dot_tn(hidden, probe) * inv_ff
    rows = LIVE // splits
    for chunk in range(places):
        column, part = chunk // splits, chunk % splits
        piece = values[part * rows : (part + 1) * rows, column * LANES : (column + 1) * LANES]
        out[chunk ^ (info[0] & (places - 1))] = piece.astype(out.dtype)


def forward_kernel(
    blocks, inv_d, inv_ff, spots, splits, places,
    info, lower, upper, gain, gate, up, probe_gate, probe_up, down, probe_down,
    normed_out, hidden, tangent, weight, act_out, send,
    normed, sums,
):
    step = pl.program_id(0)
    width = gate.shape[1]

    @pl.when(step == 0)
    def _():
        live_tokens(info, lower, upper, gain, normed, spots)
        sums[...] = jnp.zeros_like(sums)

    @pl.when(step < blocks)
    def _():
        columns = normed[:, pl.ds(pl.multiple_of(step * width, width), width)]
        normed_out[...] = columns
        turned = columns.T
        for at, rows in enumerate((gate, up, probe_gate, probe_up)):
            sums[at] += dot_nn(rows[...], turned)

    @pl.when(step == blocks - 1)
    def _():
        up_pre = sums[1]
        act, slope = gelu_pair(sums[0])
        hidden[...] = (act * up_pre).astype(BF16)
        tangent[...] = (
            slope * (sums[2] * inv_d) * up_pre + act * (sums[3] * inv_d)
        ).astype(BF16)
        weight[...] = up_pre * slope
        act_out[...] = act

    @pl.when(step >= blocks)
    def _():
        jvp_columns(
            info, tangent[...], hidden[...], down[...], probe_down[...], send, inv_ff, splits, places
        )


def keep_kernel(inv_ff, splits, places, info, tangent, hidden, down, probe_down, keep):
    jvp_columns(
        info, tangent[...], hidden[...], down[...], probe_down[...], keep, inv_ff, splits, places
    )


def gram_kernel(blocks, krylov, out, sums):
    step = pl.program_id(0)
    basis, rows, width = krylov.shape
    stack = stacked(krylov[...])

    @pl.when(step == 0)
    def _():
        sums[...] = jnp.zeros_like(sums)

    sums[...] += dot_nt(stack, stack)

    @pl.when(step == blocks - 1)
    def _():
        size = basis * rows
        own = lax.broadcasted_iota(jnp.int32, (size, size), 0)
        other = lax.broadcasted_iota(jnp.int32, (size, size), 1)
        same = jnp.where(lax.rem(own, rows) == lax.rem(other, rows), sums[...], 0.0)
        lane = lax.broadcasted_iota(jnp.int32, (1, LANES), 1)
        group = lax.broadcasted_iota(jnp.int32, (1, size), 1) // rows
        for one in range(basis):
            line = jnp.sum(same[one * rows : (one + 1) * rows], axis=0, keepdims=True)
            entry = jnp.zeros((1, LANES), F32)
            for two in range(basis):
                value = jnp.sum(jnp.where(group == two, line, 0.0), axis=1, keepdims=True)
                entry = entry + jnp.where(lane == two, value, 0.0)
            out[one : one + 1, :] = entry


def product_kernel(krylov, normed, out, square):
    basis, rows, width = krylov.shape
    columns = normed[...]
    turned = columns.T
    made = dot_nn(stacked(krylov[...]), turned).reshape(basis, rows, LIVE)
    made_square = dot_nn(columns, turned)
    first = pl.program_id(0) == 0

    @pl.when(first)
    def _():
        out[...] = made
        square[...] = made_square

    @pl.when(jnp.logical_not(first))
    def _():
        out[...] += made
        square[...] += made_square


def loss_columns(flip, load, places, splits):
    made = []
    for column in range(places // splits):
        pieces = [
            load((column * splits + part) ^ (flip & (places - 1))) for part in range(splits)
        ]
        if splits > 1:
            pieces = [jnp.concatenate([one.astype(F32) for one in pieces], 0).astype(BF16)]
        made.append(pieces[0])
    return jnp.concatenate(made, axis=1)


def back_columns(info, chunks, down, krylov, sums, square, splits, start):
    basis, rows, width = krylov.shape
    columns = loss_columns(info[0], lambda at: chunks[at], chunks.shape[0], splits)
    turned = columns.T
    size = basis * rows
    made = dot_nn(stacked(krylov[...]), turned)
    made_down = dot_nn(down[...], turned)
    made_square = dot_nn(columns, turned)

    @pl.when(start)
    def _():
        sums[0:size, :] = made
        sums[size : size + rows, :] = made_down
        square[...] = made_square

    @pl.when(jnp.logical_not(start))
    def _():
        sums[0:size, :] += made
        sums[size : size + rows, :] += made_down
        square[...] += made_square


def back_half_kernel(splits, info, chunks, down, krylov, sums, square):
    back_columns(info, chunks, down, krylov, sums, square, splits, pl.program_id(0) == 0)


def back_kernel(
    blocks, inv_d, inv_ff, splits, parts,
    info, chunks, down, krylov, hidden, weight, act, square, loss_square_half, grams,
    sums_half, *rest,
):
    prods = rest[: 2 * parts]
    s_out, r_out, stats, sums, loss_square, half_held, gate_held, up_held, sems = rest[2 * parts :]
    step = pl.program_id(0)
    basis, rows, width = krylov.shape
    size = basis * rows
    share = basis // parts

    copies = [pltpu.make_async_copy(sums_half, half_held, sems.at[0])]
    for part in range(parts):
        here = pl.ds(part * share, share)
        copies.append(
            pltpu.make_async_copy(prods[part], gate_held.at[here], sems.at[1 + part])
        )
        copies.append(
            pltpu.make_async_copy(
                prods[parts + part], up_held.at[here], sems.at[1 + parts + part]
            )
        )

    @pl.when(step == 0)
    def _():
        for copy in copies:
            copy.start()

    back_columns(info, chunks, down, krylov, sums, loss_square, splits, step == 0)

    @pl.when(step == blocks - 1)
    def _():
        for copy in copies:
            copy.wait()
        back = sums[size : size + rows, :] + half_held[size : size + rows, :]
        s_term = (back * weight[...]).astype(BF16)
        r_term = (back * act[...]).astype(BF16)
        s_out[...] = s_term
        r_out[...] = r_term
        held = hidden[...]
        wide_s = s_term.astype(F32) * inv_d
        wide_r = r_term.astype(F32) * inv_d
        wide_h = held.astype(F32) * inv_ff
        for one in range(basis):
            here = slice(one * rows, (one + 1) * rows)
            value = wide_s * gate_held[one] + wide_r * up_held[one]
            value = total(value + wide_h * (sums[here, :] + half_held[here, :]))
            stats[one : one + 1, :] = jnp.broadcast_to(value, (1, LANES))
        squares = inv_d * inv_d * ((dot_tn(s_term, s_term) + dot_tn(r_term, r_term)) * square[...])
        other = loss_square[...] + loss_square_half[...]
        squares = total(squares + inv_ff * inv_ff * (dot_tn(held, held) * other))
        stats[basis : 2 * basis, :] = jnp.broadcast_to(squares, (basis, LANES))
        stats[2 * basis : 3 * basis, :] = jnp.sum(grams[...], axis=0)


def split_three(value):
    first = value.astype(BF16)
    rest = value - first.astype(F32)
    second = rest.astype(BF16)
    return first, second, (rest - second.astype(F32)).astype(BF16)


def new_kernel(
    basis, count, inv_d, inv_ff, splits, lines,
    info, stats, s_term, r_term, hidden, normed, lower, upper,
    krylov_gate, krylov_up, krylov_down,
    new_gate, new_up, new_down, coefficients,
    scale_held, mixer, wide,
):
    step = pl.program_id(0)
    size = basis * lines

    @pl.when(step == 0)
    def _():
        proj = [stats[one, 0] / count for one in range(basis)]
        squares = stats[basis, 0]
        for one in range(basis):
            line = stats[2 * basis + one, 0] * proj[0]
            for two in range(1, basis):
                line = line + stats[2 * basis + one, two] * proj[two]
            squares = squares + proj[one] * (line - 2.0 * stats[one, 0])
        mean = jnp.maximum(jnp.full((8, LANES), squares / count, F32), 0.0)
        norm = jnp.sqrt(mean + 1e-06)
        inverse = jnp.max(1.0 / norm)
        for one in range(basis):
            coefficients[one] = proj[one]
        coefficients[basis] = jnp.max(norm)
        scale_held[0] = inverse
        lane = lax.broadcasted_iota(jnp.int32, (lines, size), 1)
        row = lax.broadcasted_iota(jnp.int32, (lines, size), 0)
        values = jnp.zeros((lines, size), F32)
        for one in range(basis):
            values = jnp.where(lane == one * lines + row, proj[one] * inverse, values)
        terms = [term.astype(F32) for term in split_three(values)]
        mixer[...] = jnp.concatenate(terms, axis=0).astype(BF16)

    inverse = scale_held[0]
    rows = s_term.shape[0]
    low = step < pl.num_programs(0) // 2
    loss = loss_columns(
        info[0], lambda at: jnp.where(low, lower[at], upper[at]), lower.shape[0], splits
    )
    mix = mixer[...]
    for left, right, scale, krylov, out in (
        (s_term, normed[...], inv_d, krylov_gate, new_gate),
        (r_term, normed[...], inv_d, krylov_up, new_up),
        (hidden, loss, inv_ff, krylov_down, new_down),
    ):
        wide[...] = dot_nn(left[...], right) * (scale * inverse)
        for at in range(rows // lines):
            here = slice(at * lines, (at + 1) * lines)
            mixed = dot_nn(mix, stacked(krylov[:, here, :]))
            mixed = mixed[:lines] + (mixed[lines : 2 * lines] + mixed[2 * lines :])
            out[here, :] = (wide[here, :] - mixed).astype(BF16)


def per_device(
    inputs, norm_gain, lengths, gate_rows, up_rows, down_rows, krylov_gate, krylov_up, krylov_down
):
    basis, rows, width = krylov_gate.shape
    devices = lax.axis_size("fsdp")
    bits = devices.bit_length() - 1
    hidden_all = rows * devices
    count = 3.0 * width * hidden_all
    inv_d = 1.0 / math.sqrt(width)
    inv_ff = 1.0 / math.sqrt(hidden_all)
    me = lax.axis_index("fsdp").astype(jnp.int32)
    mirror = reverse_bits(me, bits)
    info = jnp.stack([mirror, lengths[0]])

    splits = devices // (width // LANES)
    chunk_rows = LIVE // splits
    cols = min(512, width // 2)
    blocks = width // cols
    places = devices // blocks
    half = blocks // 2
    lines = 32 if rows % 32 == 0 else rows
    pieces = rows // lines
    parts = 2 if basis % 2 == 0 else 1
    share = basis // parts

    def gram(krylov, first, number, earlier):
        return pl.pallas_call(
            functools.partial(gram_kernel, number),
            grid=(number,),
            in_specs=[pl.BlockSpec((basis, lines, width), lambda step: (0, first + step, 0))],
            out_specs=whole((basis, LANES)),
            out_shape=jax.ShapeDtypeStruct((basis, LANES), F32),
            scratch_shapes=[pltpu.VMEM((basis * lines, basis * lines), F32)],
            compiler_params=params(60),
            cost_estimate=pl.CostEstimate(
                flops=4 * basis * basis * lines * lines * number * width,
                bytes_accessed=2 * basis * lines * number * width,
                transcendentals=0,
            ),
            name="gram",
        )(after(krylov, earlier))

    cut = (pieces + 1) // 2
    gate_low = lambda earlier: gram(krylov_gate, 0, cut, earlier)
    gate_high = lambda earlier: gram(krylov_gate, cut, pieces - cut, earlier)
    up_low = lambda earlier: gram(krylov_up, 0, cut, earlier)
    up_high = lambda earlier: gram(krylov_up, cut, pieces - cut, earlier)
    down_low = lambda earlier: gram(krylov_down, 0, cut, earlier)
    down_high = lambda earlier: gram(krylov_down, cut, pieces - cut, earlier)

    own_tokens = inputs.shape[0]
    tokens = own_tokens * devices
    if own_tokens % GROUP == 0 and pieces > 1:
        sub = own_tokens // GROUP
        work = (down_low, up_high, up_low, gate_high, gate_low)
        lower, upper, grams = gather_blocks(
            inputs.reshape(sub, GROUP, width), bits, dict(enumerate(work))
        )
        grams.append(None)

        def spots(flip, group):
            return (reverse_bits(group // sub, bits) ^ flip) * sub + group % sub

    else:
        gathered = lax.all_gather(inputs, "fsdp", axis=0, tiled=True)
        gathered = gathered.reshape(tokens // GROUP, GROUP, width)
        lower, upper = jnp.split(gathered, 2)
        grams = [
            gram(one, 0, pieces, info) for one in (krylov_gate, krylov_up, krylov_down)
        ]

        def spots(flip, group):
            return group

    gain = norm_gain.reshape(1, width)

    def col(step):
        return jnp.minimum(step, blocks - 1)

    def send_col(step, info):
        return (half + jnp.maximum(step - blocks, 0)) ^ (info[0] // places)

    weights = pl.BlockSpec((rows, cols), lambda step, info: (0, col(step)))
    probe = pl.BlockSpec((None, rows, cols), lambda step, info: (basis - 1, 0, col(step)))
    normed, hidden, tangent, weight, act, send = pl.pallas_call(
        functools.partial(forward_kernel, blocks, inv_d, inv_ff, spots, splits, places),
        grid_spec=pltpu.PrefetchScalarGridSpec(
            num_scalar_prefetch=1,
            grid=(blocks + half,),
            in_specs=[
                whole(lower.shape),
                whole(upper.shape),
                whole(gain.shape),
                weights,
                weights,
                probe,
                probe,
                pl.BlockSpec((rows, cols), lambda step, info: (0, send_col(step, info))),
                pl.BlockSpec(
                    (None, rows, cols), lambda step, info: (basis - 1, 0, send_col(step, info))
                ),
            ],
            out_specs=[
                pl.BlockSpec((LIVE, cols), lambda step, info: (0, col(step))),
                whole((rows, LIVE)),
                whole((rows, LIVE)),
                whole((rows, LIVE)),
                whole((rows, LIVE)),
                pl.BlockSpec(
                    (places, chunk_rows, LANES),
                    lambda step, info: (jnp.maximum(step - blocks, 0), 0, 0),
                ),
            ],
            scratch_shapes=[pltpu.VMEM((LIVE, width), BF16), pltpu.VMEM((4, rows, LIVE), F32)],
        ),
        out_shape=[
            jax.ShapeDtypeStruct((LIVE, width), BF16),
            jax.ShapeDtypeStruct((rows, LIVE), BF16),
            jax.ShapeDtypeStruct((rows, LIVE), BF16),
            jax.ShapeDtypeStruct((rows, LIVE), F32),
            jax.ShapeDtypeStruct((rows, LIVE), F32),
            jax.ShapeDtypeStruct((devices // 2, chunk_rows, LANES), BF16),
        ],
        compiler_params=params(60),
        cost_estimate=pl.CostEstimate(
            flops=10 * rows * width * LIVE,
            bytes_accessed=10 * rows * width + 6 * LIVE * width,
            transcendentals=rows * LIVE,
        ),
        name="forward",
    )(
        info, lower, upper, gain, gate_rows, up_rows, krylov_gate, krylov_up, down_rows,
        krylov_down,
    )

    def product(krylov, part, earlier):
        return pl.pallas_call(
            product_kernel,
            grid=(blocks,),
            in_specs=[
                pl.BlockSpec((share, rows, cols), lambda step: (part, 0, step)),
                pl.BlockSpec((LIVE, cols), lambda step: (0, step)),
            ],
            out_specs=[whole((share, rows, LIVE)), whole((LIVE, LIVE))],
            out_shape=[
                jax.ShapeDtypeStruct((share, rows, LIVE), F32),
                jax.ShapeDtypeStruct((LIVE, LIVE), F32),
            ],
            compiler_params=params(60),
            cost_estimate=pl.CostEstimate(
                flops=2 * share * rows * width * LIVE,
                bytes_accessed=2 * share * rows * width + 4 * share * rows * LIVE,
                transcendentals=0,
            ),
            name="product",
        )(after(krylov, earlier), normed)

    got = exchange(send, 0)

    def keep_col(step, info):
        return step ^ (info[0] // places)

    keep = pl.pallas_call(
        functools.partial(keep_kernel, inv_ff, splits, places),
        grid_spec=pltpu.PrefetchScalarGridSpec(
            num_scalar_prefetch=1,
            grid=(half,),
            in_specs=[
                whole((rows, LIVE)),
                whole((rows, LIVE)),
                pl.BlockSpec((rows, cols), lambda step, info: (0, keep_col(step, info))),
                pl.BlockSpec(
                    (None, rows, cols), lambda step, info: (basis - 1, 0, keep_col(step, info))
                ),
            ],
            out_specs=pl.BlockSpec((places, chunk_rows, LANES), lambda step, info: (step, 0, 0)),
        ),
        out_shape=jax.ShapeDtypeStruct((devices // 2, chunk_rows, LANES), F32),
        compiler_params=params(60),
        cost_estimate=pl.CostEstimate(
            flops=2 * rows * width * LIVE,
            bytes_accessed=2 * rows * width + 2 * LIVE * width,
            transcendentals=0,
        ),
        name="keep",
    )(info, tangent, hidden, down_rows, krylov_down)

    jobs = [(krylov_gate, part) for part in range(parts)]
    jobs += [(krylov_up, part) for part in range(parts)]
    plan = {1: 2, 2: 1, 3: 1}
    prods = []
    for bit in range(1, bits):
        part = keep.shape[0] // 2
        send = (keep[part:] + got[part:].astype(F32)).astype(BF16)
        keep = keep[:part] + got[:part].astype(F32)
        got = exchange(send, bit)
        for _ in range(plan.get(bit, 0)):
            krylov, at = jobs[len(prods)]
            prods.append(product(krylov, at, prods[-1][0] if prods else send))
        if plan.get(bit, 0):
            got, last = lax.optimization_barrier((got, prods[-1]))
            prods[-1] = last
    square = prods[0][1]
    prods = [one for one, _ in prods]
    loss_own = (keep + got.astype(F32)).astype(BF16)

    def half_call(lower):
        return pl.pallas_call(
            functools.partial(back_half_kernel, splits),
            grid_spec=pltpu.PrefetchScalarGridSpec(
                num_scalar_prefetch=1,
                grid=(half,),
                in_specs=[
                    pl.BlockSpec((places, chunk_rows, LANES), lambda step, info: (step, 0, 0)),
                    pl.BlockSpec((rows, cols), lambda step, info: (0, keep_col(step, info))),
                    pl.BlockSpec(
                        (basis, rows, cols), lambda step, info: (0, 0, keep_col(step, info))
                    ),
                ],
                out_specs=[whole(((basis + 1) * rows, LIVE)), whole((LIVE, LIVE))],
            ),
            out_shape=[
                jax.ShapeDtypeStruct(((basis + 1) * rows, LIVE), F32),
                jax.ShapeDtypeStruct((LIVE, LIVE), F32),
            ],
            compiler_params=params(60),
            cost_estimate=pl.CostEstimate(
                flops=(basis + 1) * rows * width * LIVE,
                bytes_accessed=(basis + 1) * rows * width + 4 * (basis + 1) * rows * LIVE,
                transcendentals=0,
            ),
            name="back_half",
        )(info, lower, down_rows, krylov_down)

    beside = {0: half_call}
    if grams[-1] is None:
        beside[1] = down_high
    lower, upper, made = gather_blocks(loss_own, bits, beside)
    sums_half, loss_square_half = made[-1]
    if grams[-1] is None:
        grams[-1] = made[0]
    grams = jnp.stack(grams)

    def back_col(step, info):
        return (half + step) ^ (info[0] // places)

    anywhere = pl.BlockSpec(memory_space=pl.ANY)
    s_term, r_term, stats = pl.pallas_call(
        functools.partial(back_kernel, half, inv_d, inv_ff, splits, parts),
        grid_spec=pltpu.PrefetchScalarGridSpec(
            num_scalar_prefetch=1,
            grid=(half,),
            in_specs=[
                pl.BlockSpec((places, chunk_rows, LANES), lambda step, info: (step, 0, 0)),
                pl.BlockSpec((rows, cols), lambda step, info: (0, back_col(step, info))),
                pl.BlockSpec((basis, rows, cols), lambda step, info: (0, 0, back_col(step, info))),
                whole((rows, LIVE)),
                whole((rows, LIVE)),
                whole((rows, LIVE)),
                whole((LIVE, LIVE)),
                whole((LIVE, LIVE)),
                whole(grams.shape),
                anywhere,
            ]
            + [anywhere] * (2 * parts),
            out_specs=[
                whole((rows, LIVE)),
                whole((rows, LIVE)),
                whole((3 * basis, LANES)),
            ],
            scratch_shapes=[
                pltpu.VMEM(((basis + 1) * rows, LIVE), F32),
                pltpu.VMEM((LIVE, LIVE), F32),
                pltpu.VMEM(((basis + 1) * rows, LIVE), F32),
                pltpu.VMEM((basis, rows, LIVE), F32),
                pltpu.VMEM((basis, rows, LIVE), F32),
                pltpu.SemaphoreType.DMA((1 + 2 * parts,)),
            ],
        ),
        out_shape=[
            jax.ShapeDtypeStruct((rows, LIVE), BF16),
            jax.ShapeDtypeStruct((rows, LIVE), BF16),
            jax.ShapeDtypeStruct((3 * basis, LANES), F32),
        ],
        compiler_params=params(60),
        cost_estimate=pl.CostEstimate(
            flops=(basis + 1) * rows * width * LIVE,
            bytes_accessed=(basis + 1) * rows * width + 12 * basis * rows * LIVE,
            transcendentals=0,
        ),
        name="back",
    )(
        info, upper, down_rows, krylov_down, hidden, weight, act, square, loss_square_half, grams,
        sums_half, *prods,
    )

    for bit in range(bits):
        stats = stats + exchange(stats, bit)

    narrow = min(256, cols)
    steps = width // narrow
    near = devices // steps

    def new_col(step, info):
        return step ^ (info[0] // near)

    krylov_spec = pl.BlockSpec(
        (basis, rows, narrow), lambda step, info: (0, 0, new_col(step, info))
    )
    out_spec = pl.BlockSpec((rows, narrow), lambda step, info: (0, new_col(step, info)))
    out_shape = jax.ShapeDtypeStruct((rows, width), BF16)
    new_gate, new_up, new_down, coefficients = pl.pallas_call(
        functools.partial(new_kernel, basis, count, inv_d, inv_ff, splits, lines),
        grid_spec=pltpu.PrefetchScalarGridSpec(
            num_scalar_prefetch=1,
            grid=(steps,),
            in_specs=[
                pl.BlockSpec(memory_space=pltpu.SMEM),
                whole((rows, LIVE)),
                whole((rows, LIVE)),
                whole((rows, LIVE)),
                pl.BlockSpec((LIVE, narrow), lambda step, info: (0, new_col(step, info))),
                pl.BlockSpec(
                    (near, chunk_rows, LANES),
                    lambda step, info: (jnp.minimum(step, steps // 2 - 1), 0, 0),
                ),
                pl.BlockSpec(
                    (near, chunk_rows, LANES),
                    lambda step, info: (jnp.maximum(step - steps // 2, 0), 0, 0),
                ),
                krylov_spec,
                krylov_spec,
                krylov_spec,
            ],
            out_specs=[out_spec, out_spec, out_spec, pl.BlockSpec(memory_space=pltpu.SMEM)],
            scratch_shapes=[
                pltpu.SMEM((1,), F32),
                pltpu.VMEM((3 * lines, basis * lines), BF16),
                pltpu.VMEM((rows, narrow), F32),
            ],
        ),
        out_shape=[
            out_shape,
            out_shape,
            out_shape,
            jax.ShapeDtypeStruct((basis + 1,), F32),
        ],
        compiler_params=params(60),
        cost_estimate=pl.CostEstimate(
            flops=6 * rows * width * LIVE,
            bytes_accessed=6 * (basis + 1) * rows * width,
            transcendentals=0,
        ),
        name="new",
    )(
        info, stats, s_term, r_term, hidden, normed, lower, upper, krylov_gate, krylov_up,
        krylov_down,
    )
    return (new_gate, new_up, new_down, coefficients)


def solution(mesh):
    placed = (
        P("fsdp", None),
        P(),
        P(),
        P("fsdp", None),
        P("fsdp", None),
        P("fsdp", None),
        P(None, "fsdp", None),
        P(None, "fsdp", None),
        P(None, "fsdp", None),
    )
    return jax.shard_map(
        per_device,
        mesh=mesh,
        in_specs=placed,
        out_specs=(P("fsdp", None), P("fsdp", None), P("fsdp", None), P()),
        check_vma=False,
    )
```

time: 268 us -> 230 us (0.86)
  local copies, waits for them, and re-layouts: 52.8 us -> 4.49 us
  Pallas kernels: 117 us -> 165 us
  waiting for transfers between devices: 60.8 us -> 31.2 us
  starting transfers between devices: 31.5 us -> 22.2 us
    unnamed x30 -> x40, local copies, waits for them, and re-layouts: 49.1 us -> 3.64 us
    pallas_call x7 -> x13, Pallas kernels: 101 us -> 144 us  [the longest x6 49.3 us: gram(): pl.pallas_call(functools.partial(gram_kernel, number), grid=(number,), in...]
    ppermute x20, waiting for transfers between devices: 60.8 us -> 31.2 us  [exchange(): lax.ppermute(block, 'fsdp', [(one, one ^ 1 << bit) for one in range(count)])]
    ppermute x20, starting transfers between devices: 31.5 us -> 22.2 us  [exchange(): lax.ppermute(block, 'fsdp', [(one, one ^ 1 << bit) for one in range(count)])]
    concatenate x4 -> x2, local copies, waits for them, and re-layouts: 3.66 us -> 0.09 us  [gather_blocks(): block = jnp.concatenate([block, other], axis=0)]
    pallas_call x1, Pallas kernels: 2.58 us -> 5.31 us  [per_device(): pl.pallas_call(functools.partial(keep_kernel, inv_ff, splits, places), gr...]
  transfers between devices with their start and end apart: 20 -> 20, of which waited for: 16 -> 10; matrix products, arithmetic and copies ran while one was open for 1% -> 1% of each run, Pallas kernels for 20% -> 47%
where the time goes in v2:
time: 230 us; the launch traced here: 228 us
  Pallas kernels  165 us (72%)
  waiting for transfers between devices  31.2 us (14%)
  starting transfers between devices  22.2 us (10%)
  local copies, waits for them, and re-layouts  4.49 us (2%)
  other arithmetic  3.73 us (2%)
    pallas_call x6, Pallas kernels, gram(): pl.pallas_call(functools.partial(gram_kernel, number), grid=(number,), in...  49.3 us
    pallas_call x4, Pallas kernels, product(): pl.pallas_call(product_kernel, grid=(blocks,), in_specs=[pl.BlockSpec((sh...  41.6 us
    ppermute x20, waiting for transfers between devices, exchange(): lax.ppermute(block, 'fsdp', [(one, one ^ 1 << bit) for one in range(count)])  31.2 us
    pallas_call x1, Pallas kernels, per_device(): pl.pallas_call(functools.partial(new_kernel, basis, count, inv_d, inv_ff,...  30.2 us
    ppermute x20, starting transfers between devices, exchange(): lax.ppermute(block, 'fsdp', [(one, one ^ 1 << bit) for one in range(count)])  22.2 us
    pallas_call x1, Pallas kernels, per_device(): pl.pallas_call(functools.partial(forward_kernel, blocks, inv_d, inv_ff, s...  15.9 us
    pallas_call x1, Pallas kernels, per_device(): pl.pallas_call(functools.partial(back_kernel, half, inv_d, inv_ff, splits...  12.4 us
    pallas_call x1, Pallas kernels, half_call(): pl.pallas_call(functools.partial(back_half_kernel, splits), grid_spec=plt...  10.6 us
  transfers between devices with their start and end apart: 20, of which 10 were waited for; matrix products, arithmetic and copies ran while one was open for 1% of the time, Pallas kernels for 47%

profile of v2, /device:TPU:0, one launch (start us, length us, event | category | flops | bytes accessed | tf_op | source)
XLA Modules:
  0.0 228.0 jit_solution(1034538454828343104)
XLA Ops:
  0.6 4.1 %collective-permute-start = (bf16[1,8,4096]{2,1,0:T(8,128)(2,1)}, bf16[1,8,4096]{2,1,0:T(8,128)(2,1)S(1)}, u32[]{:S(2)}, u32[]{:S(2)}) collective-permute-start(bf16[1,8,4096]{2,1,0:T(8,128)(2,1)} %bitcast.16), channel_id=1, source_target_pairs={{0,16},{1,17},{2,18},{3,19},{4,20},{5,21},{6,22},{7,23},{8,24},{9,... | collective-permute-start | bytes 196616 | tf_op jit(solution)/shard_map/ppermute | solution.py:55
  4.7 0.9 constant_dynamic-update-slice_fusion.4
  5.6 8.3 %gram.6 = f32[8,128]{1,0:T(8,128)} custom-call(bf16[8,320,4096]{2,1,0:T(8,128)(2,1)} %krylov_gate.1), custom_call_target="tpu_custom_call" | custom-call | flops 5368709120 | bytes 10485760 | tf_op jit(solution)/shard_map/gram/pallas_call | solution.py:409
  13.9 1.6 collective-permute-start.1
  15.5 8.2 %gram.7 = f32[8,128]{1,0:T(8,128)} custom-call(bf16[8,320,4096]{2,1,0:T(8,128)(2,1)} %krylov_gate.1), custom_call_target="tpu_custom_call" | custom-call | flops 5368709120 | bytes 10485760 | tf_op jit(solution)/shard_map/gram/pallas_call | solution.py:409
  23.8 1.6 collective-permute-start.2
  25.4 8.2 %gram.8 = f32[8,128]{1,0:T(8,128)} custom-call(bf16[8,320,4096]{2,1,0:T(8,128)(2,1)} %krylov_up.1), custom_call_target="tpu_custom_call" | custom-call | flops 5368709120 | bytes 10485760 | tf_op jit(solution)/shard_map/gram/pallas_call | solution.py:409
  33.7 1.5 collective-permute-start.3
  35.3 8.2 %gram.9 = f32[8,128]{1,0:T(8,128)} custom-call(bf16[8,320,4096]{2,1,0:T(8,128)(2,1)} %krylov_up.1), custom_call_target="tpu_custom_call" | custom-call | flops 5368709120 | bytes 10485760 | tf_op jit(solution)/shard_map/gram/pallas_call | solution.py:409
  43.5 3.1 %collective-permute-done.3 = bf16[8,8,4096]{2,1,0:T(8,128)(2,1)S(1)} collective-permute-done((bf16[8,8,4096]{2,1,0:T(8,128)(2,1)S(1)}, bf16[8,8,4096]{2,1,0:T(8,128)(2,1)S(1)}, u32[]{:S(2)}, u32[]{:S(2)}) %collective-permute-start.3) | collective-permute-done | bytes 524320 | tf_op jit(solution)/shard_map/ppermute | solution.py:55
  46.7 0.8 reshape.15.gain
  47.5 0.6 pad_add_fusion.info
  48.1 8.2 %gram.10 = f32[8,128]{1,0:T(8,128)} custom-call(bf16[8,320,4096]{2,1,0:T(8,128)(2,1)} %krylov_down.1), custom_call_target="tpu_custom_call" | custom-call | flops 5368709120 | bytes 10485760 | tf_op jit(solution)/shard_map/gram/pallas_call | solution.py:409
  56.3 1.0 copy-done.3
  57.3 15.9 %forward.1 = (bf16[192,4096]{1,0:T(8,128)(2,1)}, bf16[320,192]{1,0:T(8,128)(2,1)}, bf16[320,192]{1,0:T(8,128)(2,1)}, f32[320,192]{1,0:T(8,128)}, f32[320,192]{1,0:T(8,128)}, /*index=5*/bf16[16,192,128]{2,1,0:T(8,128)(2,1)}) custom-call(s32[2]{0:T(128)} %pad_add_fusion.info, bf16[16,8,4096]{2,1,0:T(8,128)(2,1)} %copy-done.2, bf16[16,8,4096]{2,1,0:T(8,128)(2,1)} %copy-done.3, ...), custom_call_target="tpu_custom_call" | custom-call | flops 2516582400 | bytes 17825792 | tf_op jit(solution)/shard_map/forward/pallas_call | solution.py:467
  73.5 5.3 %keep.1 = f32[16,192,128]{2,1,0:T(8,128)} custom-call(s32[2]{0:T(128)} %pad_add_fusion.info, bf16[320,192]{1,0:T(8,128)(2,1)} %get-tuple-element.61.tangent, bf16[320,192]{1,0:T(8,128)(2,1)} %get-tuple-element.62.hidden, bf16[320,4096]{1,0:T(8,128)(2,1)} %down.7, bf16[8,320,4096]{2,1,0:T(8,128)(2,1)} %krylov_down.1), custom_call_target="tpu_custom_call" | custom-call | flops 503316480 | bytes 4194304 | tf_op jit(solution)/shard_map/keep/pallas_call | solution.py:545
  78.8 1.5 fusion
  80.4 1.6 collective-permute-start.6
  82.0 10.4 %product.4 = (f32[4,320,192]{2,1,0:T(8,128)}, f32[192,192]{1,0:T(8,128)}) custom-call(bf16[8,320,4096]{2,1,0:T(8,128)(2,1)} %krylov_gate.1, bf16[192,4096]{1,0:T(8,128)(2,1)} %get-tuple-element.65.normed), custom_call_target="tpu_custom_call" | custom-call | flops 2013265920 | bytes 11468800 | tf_op jit(solution)/shard_map/product/pallas_call | solution.py:519
  92.4 10.4 %product.5 = (f32[4,320,192]{2,1,0:T(8,128)}, f32[192,192]{1,0:T(8,128)}) custom-call(bf16[8,320,4096]{2,1,0:T(8,128)(2,1)} %krylov_gate.1, bf16[192,4096]{1,0:T(8,128)(2,1)} %get-tuple-element.65.normed), custom_call_target="tpu_custom_call" | custom-call | flops 2013265920 | bytes 11468800 | tf_op jit(solution)/shard_map/product/pallas_call | solution.py:519
  102.9 0.5 collective-permute-start.7
  103.3 10.4 %product.6 = (f32[4,320,192]{2,1,0:T(8,128)}, f32[192,192]{1,0:T(8,128)}) custom-call(bf16[8,320,4096]{2,1,0:T(8,128)(2,1)} %krylov_up.1, bf16[192,4096]{1,0:T(8,128)(2,1)} %get-tuple-element.65.normed), custom_call_target="tpu_custom_call" | custom-call | flops 2013265920 | bytes 11468800 | tf_op jit(solution)/shard_map/product/pallas_call | solution.py:519
  113.8 0.5 collective-permute-start.8
  114.3 10.4 %product.7 = (f32[4,320,192]{2,1,0:T(8,128)}, f32[192,192]{1,0:T(8,128)}) custom-call(bf16[8,320,4096]{2,1,0:T(8,128)(2,1)} %krylov_up.1, bf16[192,4096]{1,0:T(8,128)(2,1)} %get-tuple-element.65.normed), custom_call_target="tpu_custom_call" | custom-call | flops 2013265920 | bytes 11468800 | tf_op jit(solution)/shard_map/product/pallas_call | solution.py:519
  125.2 4.7 %collective-permute-done.9 = bf16[1,192,128]{2,1,0:T(8,128)(2,1)S(1)} collective-permute-done((bf16[1,192,128]{2,1,0:T(8,128)(2,1)S(1)}, bf16[1,192,128]{2,1,0:T(8,128)(2,1)S(1)}, u32[]{:S(2)}, u32[]{:S(2)}) %collective-permute-start.9) | collective-permute-done | bytes 49184 | tf_op jit(solution)/shard_map/ppermute | solution.py:55
  129.9 0.4 collective-permute-start.10
  130.3 4.7 %collective-permute-done.10 = bf16[1,192,128]{2,1,0:T(8,128)(2,1)S(1)} collective-permute-done((bf16[1,192,128]{2,1,0:T(8,128)(2,1)S(1)}, bf16[1,192,128]{2,1,0:T(8,128)(2,1)S(1)}, u32[]{:S(2)}, u32[]{:S(2)}) %collective-permute-start.10) | collective-permute-done | bytes 49184 | tf_op jit(solution)/shard_map/ppermute | solution.py:55
  135.0 1.9 collective-permute-start.11
  136.9 2.8 %collective-permute-done.11 = bf16[2,192,128]{2,1,0:T(8,128)(2,1)S(1)} collective-permute-done((bf16[2,192,128]{2,1,0:T(8,128)(2,1)S(1)}, bf16[2,192,128]{2,1,0:T(8,128)(2,1)S(1)}, u32[]{:S(2)}, u32[]{:S(2)}) %collective-permute-start.11) | collective-permute-done | bytes 98336 | tf_op jit(solution)/shard_map/ppermute | solution.py:55
  139.7 1.6 collective-permute-start.12
  141.4 4.1 %collective-permute-done.12 = bf16[4,192,128]{2,1,0:T(8,128)(2,1)S(1)} collective-permute-done((bf16[4,192,128]{2,1,0:T(8,128)(2,1)S(1)}, bf16[4,192,128]{2,1,0:T(8,128)(2,1)S(1)}, u32[]{:S(2)}, u32[]{:S(2)}) %collective-permute-start.12) | collective-permute-done | bytes 196640 | tf_op jit(solution)/shard_map/ppermute | solution.py:55
  145.5 0.6 collective-permute-start.13
  146.1 8.2 %gram.11 = f32[8,128]{1,0:T(8,128)} custom-call(bf16[8,320,4096]{2,1,0:T(8,128)(2,1)} %krylov_down.1), custom_call_target="tpu_custom_call" | custom-call | flops 5368709120 | bytes 10485760 | tf_op jit(solution)/shard_map/gram/pallas_call | solution.py:409
  154.5 0.8 copy-done
  155.3 10.6 %back_half.1 = (f32[2880,192]{1,0:T(8,128)}, f32[192,192]{1,0:T(8,128)}) custom-call(s32[2]{0:T(128)} %pad_add_fusion.info, bf16[16,192,128]{2,1,0:T(8,128)(2,1)} %copy-done, bf16[320,4096]{1,0:T(8,128)(2,1)} %down.7, bf16[8,320,4096]{2,1,0:T(8,128)(2,1)} %krylov_down.1), custom_call_target="tpu_custom_call" | custom-call | flops 2264924160 | bytes 14008320 | tf_op jit(solution)/shard_map/back_half/pallas_call | solution.py:590
  165.9 0.6 copy-done.5
  166.8 12.4 %back.1 = (bf16[320,192]{1,0:T(8,128)(2,1)}, bf16[320,192]{1,0:T(8,128)(2,1)}, f32[24,128]{1,0:T(8,128)}) custom-call(s32[2]{0:T(128)} %pad_add_fusion.info, bf16[16,192,128]{2,1,0:T(8,128)(2,1)} %copy-done.1, bf16[320,4096]{1,0:T(8,128)(2,1)} %down.7, bf16[8,320,4096]{2,1,0:T(8,128)(2,1)} %krylov_down.1, bf16[320,192]{1,0:T(8,128)(2,1)} %get-tuple-element.62.hidden, ...), custom_call_target="tpu_custom_call" | custom-call | flops 2264924160 | bytes 17694720 | tf_op jit(solution)/shard_map/back/pallas_call | solution.py:630
  179.3 1.4 collective-permute-done.15
  180.6 0.7 add.51
  181.3 1.5 collective-permute-start.16
  182.9 2.2 collective-permute-done.16
  185.0 1.5 collective-permute-start.17
  186.5 2.2 collective-permute-done.17
  188.7 1.8 collective-permute-start.18
  190.6 1.9 collective-permute-done.18
  192.8 4.2 %collective-permute-done.19 = f32[24,128]{1,0:T(8,128)S(1)} collective-permute-done((f32[24,128]{1,0:T(8,128)S(1)}, f32[24,128]{1,0:T(8,128)S(1)}, u32[]{:S(2)}, u32[]{:S(2)}) %collective-permute-start.19) | collective-permute-done | bytes 12320 | tf_op jit(solution)/shard_map/ppermute | solution.py:55
  197.0 0.6 add.55.stats
  197.6 30.2 %new.1 = (bf16[320,4096]{1,0:T(8,128)(2,1)}, bf16[320,4096]{1,0:T(8,128)(2,1)}, bf16[320,4096]{1,0:T(8,128)(2,1)}, f32[9]{0:T(128)}) custom-call(s32[2]{0:T(128)} %pad_add_fusion.info, f32[24,128]{1,0:T(8,128)} %add.55.stats, bf16[320,192]{1,0:T(8,128)(2,1)} %get-tuple-element.96.s_term, bf16[320,192]{1,0:T(8,128)(2,1)} %get-tuple-element.97.r_term, ...), custom_call_target="tpu_custom_call" | custom-call | flops 1509949440 | bytes 70778880 | tf_op jit(solution)/shard_map/new/pallas_call | solution.py:694
  (68 shorter events, 2.2 us)
Async XLA Ops:
  0.6 13.2 %collective-permute-start = (bf16[1,8,4096]{2,1,0:T(8,128)(2,1)}, bf16[1,8,4096]{2,1,0:T(8,128)(2,1)S(1)}, u32[]{:S(2)}, u32[]{:S(2)}) collective-permute-start(bf16[1,8,4096]{2,1,0:T(8,128)(2,1)} %bitcast.16), channel_id=1, source_target_pairs={{0,16},{1,17},{2,18},{3,19},{4,20},{5,21},{6,22},{7,23},{8,24},{9,... | collective-permute-start | bytes 196616 | tf_op jit(solution)/shard_map/ppermute | solution.py:55
  5.6 8.3 %copy-start.4 = (bf16[8,4096]{1,0:T(8,128)(2,1)S(1)}, bf16[8,4096]{1,0:T(8,128)(2,1)}, u32[]{:S(2)}) copy-start(bf16[8,4096]{1,0:T(8,128)(2,1)} %param.9) | copy-start | bytes 196612
  13.9 9.9 %collective-permute-start.1 = (bf16[2,8,4096]{2,1,0:T(8,128)(2,1)S(1)}, bf16[2,8,4096]{2,1,0:T(8,128)(2,1)S(1)}, u32[]{:S(2)}, u32[]{:S(2)}) collective-permute-start(bf16[2,8,4096]{2,1,0:T(8,128)(2,1)S(1)} %pad_maximum_fusion.4), channel_id=1, source_target_pairs={{0,8},{1,9},{2,10},{3,11},{4,12},{5,13},{6,14},{7,15},{8,0},{9,1},... | collective-permute-start | bytes 393224 | tf_op jit(solution)/shard_map/ppermute | solution.py:55
  23.8 9.8 %collective-permute-start.2 = (bf16[4,8,4096]{2,1,0:T(8,128)(2,1)S(1)}, bf16[4,8,4096]{2,1,0:T(8,128)(2,1)S(1)}, u32[]{:S(2)}, u32[]{:S(2)}) collective-permute-start(bf16[4,8,4096]{2,1,0:T(8,128)(2,1)S(1)} %pad_maximum_fusion.2), channel_id=1, source_target_pairs={{0,4},{1,5},{2,6},{3,7},{4,0},{5,1},{6,2},{7,3},{8,12},{9,13},{10,... | collective-permute-start | bytes 786440 | tf_op jit(solution)/shard_map/ppermute | solution.py:55
  33.7 12.9 %collective-permute-start.3 = (bf16[8,8,4096]{2,1,0:T(8,128)(2,1)S(1)}, bf16[8,8,4096]{2,1,0:T(8,128)(2,1)S(1)}, u32[]{:S(2)}, u32[]{:S(2)}) collective-permute-start(bf16[8,8,4096]{2,1,0:T(8,128)(2,1)S(1)} %pad_maximum_fusion), channel_id=1, source_target_pairs={{0,2},{1,3},{2,0},{3,1},{4,6},{5,7},{6,4},{7,5},{8,10},{9,11},{10,... | collective-permute-start | bytes 1572872 | tf_op jit(solution)/shard_map/ppermute | solution.py:55
  35.2 11.5 %copy-start.12 = (bf16[4096]{0:T(1024)(128)(2,1)S(1)}, bf16[4096]{0:T(1024)(128)(2,1)}, u32[]{:S(2)}) copy-start(bf16[4096]{0:T(1024)(128)(2,1)} %param.10) | copy-start | bytes 24580
  35.3 12.2 %copy-start.13 = (s32[2]{0:T(128)S(1)}, s32[2]{0:T(128)}, u32[]{:S(2)}) copy-start(s32[2]{0:T(128)} %param.11) | copy-start | bytes 28
  46.6 9.7 %copy-start.2 = (bf16[16,8,4096]{2,1,0:T(8,128)(2,1)}, bf16[16,8,4096]{2,1,0:T(8,128)(2,1)S(1)}, u32[]{:S(2)}) copy-start(bf16[16,8,4096]{2,1,0:T(8,128)(2,1)S(1)} %constant_dynamic-update-slice_fusion.lower) | copy-start | bytes 3145732
  46.6 9.7 %collective-permute-start.4 = (bf16[16,8,4096]{2,1,0:T(8,128)(2,1)S(1)}, bf16[16,8,4096]{2,1,0:T(8,128)(2,1)S(1)}, u32[]{:S(2)}, u32[]{:S(2)}) collective-permute-start(bf16[16,8,4096]{2,1,0:T(8,128)(2,1)S(1)} %constant_dynamic-update-slice_fusion.lower), channel_id=1, source_target_pairs={{0,1},{1,0},{2,3},{3,2},{4,5},{5,4},{6,7},{7,6},{8,9},{9,8},{10,11... | collective-permute-start | bytes 3145736 | tf_op jit(solution)/shard_map/ppermute | solution.py:55
  56.3 1.0 copy-start.3
  73.1 5.7 %collective-permute-start.5 = (bf16[16,192,128]{2,1,0:T(8,128)(2,1)}, bf16[16,192,128]{2,1,0:T(8,128)(2,1)S(1)}, u32[]{:S(2)}, u32[]{:S(2)}) collective-permute-start(bf16[16,192,128]{2,1,0:T(8,128)(2,1)} %get-tuple-element.63), channel_id=1, source_target_pairs={{0,1},{1,0},{2,3},{3,2},{4,5},{5,4},{6,7},{7,6},{8,9},{9,8},{10,11... | collective-permute-start | bytes 2359304 | tf_op jit(solution)/shard_map/ppermute | solution.py:55
  80.4 22.4 %collective-permute-start.6 = (bf16[8,192,128]{2,1,0:T(8,128)(2,1)S(1)}, bf16[8,192,128]{2,1,0:T(8,128)(2,1)S(1)}, u32[]{:S(2)}, u32[]{:S(2)}) collective-permute-start(bf16[8,192,128]{2,1,0:T(8,128)(2,1)S(1)} %get-tuple-element.100), channel_id=1, source_target_pairs={{0,2},{1,3},{2,0},{3,1},{4,6},{5,7},{6,4},{7,5},{8,10},{9,11},{10,... | collective-permute-start | bytes 1179656 | tf_op jit(solution)/shard_map/ppermute | solution.py:55
  102.9 10.8 %collective-permute-start.7 = (bf16[4,192,128]{2,1,0:T(8,128)(2,1)S(1)}, bf16[4,192,128]{2,1,0:T(8,128)(2,1)S(1)}, u32[]{:S(2)}, u32[]{:S(2)}) collective-permute-start(bf16[4,192,128]{2,1,0:T(8,128)(2,1)S(1)} %get-tuple-element.102), channel_id=1, source_target_pairs={{0,4},{1,5},{2,6},{3,7},{4,0},{5,1},{6,2},{7,3},{8,12},{9,13},{10,... | collective-permute-start | bytes 589832 | tf_op jit(solution)/shard_map/ppermute | solution.py:55
  113.7 11.4 %copy-start.9 = (f32[8,128]{1,0:T(8,128)S(1)}, f32[8,128]{1,0:T(8,128)}, u32[]{:S(2)}) copy-start(f32[8,128]{1,0:T(8,128)} %gram.6) | copy-start | bytes 12292
  113.8 16.5 %copy-start.7 = (f32[8,128]{1,0:T(8,128)S(1)}, f32[8,128]{1,0:T(8,128)}, u32[]{:S(2)}) copy-start(f32[8,128]{1,0:T(8,128)} %gram.7) | copy-start | bytes 12292
  113.8 23.1 %copy-start.8 = (f32[8,128]{1,0:T(8,128)S(1)}, f32[8,128]{1,0:T(8,128)}, u32[]{:S(2)}) copy-start(f32[8,128]{1,0:T(8,128)} %gram.8) | copy-start | bytes 12292
  113.8 11.0 %collective-permute-start.8 = (bf16[2,192,128]{2,1,0:T(8,128)(2,1)S(1)}, bf16[2,192,128]{2,1,0:T(8,128)(2,1)S(1)}, u32[]{:S(2)}, u32[]{:S(2)}) collective-permute-start(bf16[2,192,128]{2,1,0:T(8,128)(2,1)S(1)} %get-tuple-element.104), channel_id=1, source_target_pairs={{0,8},{1,9},{2,10},{3,11},{4,12},{5,13},{6,14},{7,15},{8,0},{9,1},... | collective-permute-start | bytes 294920 | tf_op jit(solution)/shard_map/ppermute | solution.py:55
  124.8 5.1 %collective-permute-start.9 = (bf16[1,192,128]{2,1,0:T(8,128)(2,1)S(1)}, bf16[1,192,128]{2,1,0:T(8,128)(2,1)S(1)}, u32[]{:S(2)}, u32[]{:S(2)}) collective-permute-start(bf16[1,192,128]{2,1,0:T(8,128)(2,1)S(1)} %fusion.3), channel_id=1, source_target_pairs={{0,16},{1,17},{2,18},{3,19},{4,20},{5,21},{6,22},{7,23},{8,24},{9,... | collective-permute-start | bytes 147464 | tf_op jit(solution)/shard_map/ppermute | solution.py:55
  129.9 5.1 %collective-permute-start.10 = (bf16[1,192,128]{2,1,0:T(8,128)(2,1)S(1)}, bf16[1,192,128]{2,1,0:T(8,128)(2,1)S(1)}, u32[]{:S(2)}, u32[]{:S(2)}) collective-permute-start(bf16[1,192,128]{2,1,0:T(8,128)(2,1)S(1)} %get-tuple-element.99), channel_id=1, source_target_pairs={{0,16},{1,17},{2,18},{3,19},{4,20},{5,21},{6,22},{7,23},{8,24},{9,... | collective-permute-start | bytes 147464 | tf_op jit(solution)/shard_map/ppermute | solution.py:55
  135.0 4.7 %collective-permute-start.11 = (bf16[2,192,128]{2,1,0:T(8,128)(2,1)S(1)}, bf16[2,192,128]{2,1,0:T(8,128)(2,1)S(1)}, u32[]{:S(2)}, u32[]{:S(2)}) collective-permute-start(bf16[2,192,128]{2,1,0:T(8,128)(2,1)S(1)} %pad_maximum_fusion.5), channel_id=1, source_target_pairs={{0,8},{1,9},{2,10},{3,11},{4,12},{5,13},{6,14},{7,15},{8,0},{9,1},... | collective-permute-start | bytes 294920 | tf_op jit(solution)/shard_map/ppermute | solution.py:55
  139.7 5.7 %collective-permute-start.12 = (bf16[4,192,128]{2,1,0:T(8,128)(2,1)S(1)}, bf16[4,192,128]{2,1,0:T(8,128)(2,1)S(1)}, u32[]{:S(2)}, u32[]{:S(2)}) collective-permute-start(bf16[4,192,128]{2,1,0:T(8,128)(2,1)S(1)} %pad_maximum_fusion.3), channel_id=1, source_target_pairs={{0,4},{1,5},{2,6},{3,7},{4,0},{5,1},{6,2},{7,3},{8,12},{9,13},{10,... | collective-permute-start | bytes 589832 | tf_op jit(solution)/shard_map/ppermute | solution.py:55
  145.5 8.9 %collective-permute-start.13 = (bf16[8,192,128]{2,1,0:T(8,128)(2,1)S(1)}, bf16[8,192,128]{2,1,0:T(8,128)(2,1)S(1)}, u32[]{:S(2)}, u32[]{:S(2)}) collective-permute-start(bf16[8,192,128]{2,1,0:T(8,128)(2,1)S(1)} %pad_maximum_fusion.1), channel_id=1, source_target_pairs={{0,2},{1,3},{2,0},{3,1},{4,6},{5,7},{6,4},{7,5},{8,10},{9,11},{10,... | collective-permute-start | bytes 1179656 | tf_op jit(solution)/shard_map/ppermute | solution.py:55
  146.1 8.4 %copy-start.6 = (f32[8,128]{1,0:T(8,128)S(1)}, f32[8,128]{1,0:T(8,128)}, u32[]{:S(2)}) copy-start(f32[8,128]{1,0:T(8,128)} %gram.9) | copy-start | bytes 12292
  146.1 8.4 %copy-start.10 = (f32[8,128]{1,0:T(8,128)S(1)}, f32[8,128]{1,0:T(8,128)}, u32[]{:S(2)}) copy-start(f32[8,128]{1,0:T(8,128)} %gram.10) | copy-start | bytes 12292
  154.4 0.9 copy-start
  154.4 11.5 %collective-permute-start.14 = (bf16[16,192,128]{2,1,0:T(8,128)(2,1)S(1)}, bf16[16,192,128]{2,1,0:T(8,128)(2,1)S(1)}, u32[]{:S(2)}, u32[]{:S(2)}) collective-permute-start(bf16[16,192,128]{2,1,0:T(8,128)(2,1)S(1)} %constant_dynamic-update-slice_fusion.5.chunks.lower), channel_id=1, source_target_pairs={{0,1},{1,0},{2,3},{3,2},{4,5},{5,4},{6,7},{7,6},{8,9},{9,8},{10,11... | collective-permute-start | bytes 2359304 | tf_op jit(solution)/shard_map/ppermute | solution.py:55
  155.3 10.6 %copy-start.11 = (f32[8,128]{1,0:T(8,128)S(1)}, f32[8,128]{1,0:T(8,128)}, u32[]{:S(2)}) copy-start(f32[8,128]{1,0:T(8,128)} %gram.11) | copy-start | bytes 12292
  165.9 0.6 copy-start.5
  165.9 0.9 copy-start.1
  179.2 1.5 collective-permute-start.15
  181.3 3.7 %collective-permute-start.16 = (f32[24,128]{1,0:T(8,128)S(1)}, f32[24,128]{1,0:T(8,128)S(1)}, u32[]{:S(2)}, u32[]{:S(2)}) collective-permute-start(f32[24,128]{1,0:T(8,128)S(1)} %add.51), channel_id=1, source_target_pairs={{0,2},{1,3},{2,0},{3,1},{4,6},{5,7},{6,4},{7,5},{8,10},{9,11},{10,... | collective-permute-start | bytes 36872 | tf_op jit(solution)/shard_map/ppermute | solution.py:55
  185.0 3.7 %collective-permute-start.17 = (f32[24,128]{1,0:T(8,128)S(1)}, f32[24,128]{1,0:T(8,128)S(1)}, u32[]{:S(2)}, u32[]{:S(2)}) collective-permute-start(f32[24,128]{1,0:T(8,128)S(1)} %add.52), channel_id=1, source_target_pairs={{0,4},{1,5},{2,6},{3,7},{4,0},{5,1},{6,2},{7,3},{8,12},{9,13},{10,... | collective-permute-start | bytes 36872 | tf_op jit(solution)/shard_map/ppermute | solution.py:55
  188.7 3.7 %collective-permute-start.18 = (f32[24,128]{1,0:T(8,128)S(1)}, f32[24,128]{1,0:T(8,128)S(1)}, u32[]{:S(2)}, u32[]{:S(2)}) collective-permute-start(f32[24,128]{1,0:T(8,128)S(1)} %add.53), channel_id=1, source_target_pairs={{0,8},{1,9},{2,10},{3,11},{4,12},{5,13},{6,14},{7,15},{8,0},{9,1},... | collective-permute-start | bytes 36872 | tf_op jit(solution)/shard_map/ppermute | solution.py:55
  192.4 4.6 %collective-permute-start.19 = (f32[24,128]{1,0:T(8,128)S(1)}, f32[24,128]{1,0:T(8,128)S(1)}, u32[]{:S(2)}, u32[]{:S(2)}) collective-permute-start(f32[24,128]{1,0:T(8,128)S(1)} %add.54), channel_id=1, source_target_pairs={{0,16},{1,17},{2,18},{3,19},{4,20},{5,21},{6,22},{7,23},{8,24},{9,... | collective-permute-start | bytes 36872 | tf_op jit(solution)/shard_map/ppermute | solution.py:55

commit v3 on v0

v3 whole, which is shorter than its diff:
```python
import functools
import math

import jax
import jax.numpy as jnp
from jax import lax
from jax.experimental import pallas as pl
from jax.experimental.pallas import tpu as pltpu
from jax.sharding import PartitionSpec as P

LEN = 128
LIVE = 192
GROUP = 8
LANES = 128
F32 = jnp.float32
BF16 = jnp.bfloat16


def gelu_pair(gate_pre):
    coef = math.sqrt(2.0 / math.pi)
    cube = gate_pre * gate_pre * gate_pre
    tanh_val = jnp.tanh(coef * (gate_pre + 0.044715 * cube))
    act = 0.5 * gate_pre * (1.0 + tanh_val)
    slope = 0.5 * (1.0 + tanh_val) + 0.5 * gate_pre * (1.0 - tanh_val * tanh_val) * coef * (
        1.0 + 3.0 * 0.044715 * gate_pre * gate_pre
    )
    return (act, slope)


def dot_nn(left, right):
    return jnp.dot(left, right, preferred_element_type=F32)


def dot_nt(left, right):
    return lax.dot_general(left, right, (((1,), (1,)), ((), ())), preferred_element_type=F32)


def dot_tn(left, right):
    return lax.dot_general(left, right, (((0,), (0,)), ((), ())), preferred_element_type=F32)


def total(values):
    return jnp.sum(jnp.sum(values, axis=0, keepdims=True), axis=1, keepdims=True)


def reverse_bits(value, bits):
    out = value * 0
    for bit in range(bits):
        out = out | (((value >> bit) & 1) << (bits - 1 - bit))
    return out


def exchange(block, bit):
    count = lax.axis_size("fsdp")
    return lax.ppermute(block, "fsdp", [(one, one ^ (1 << bit)) for one in range(count)])


def gather_blocks(block, bits, beside):
    for bit in reversed(range(bits)):
        other = exchange(block, bit)
        if bit in beside:
            work, done = beside[bit]
            other, extra = lax.optimization_barrier((other, work(block)))
            done(extra)
        if bit:
            block = jnp.concatenate([block, other], axis=0)
    return block, other


def after(value, earlier):
    return lax.optimization_barrier((value, earlier))[0]


def stacked(krylov):
    basis, rows, width = krylov.shape
    if rows % 16:
        return krylov.astype(F32).reshape(basis * rows, width).astype(BF16)
    return krylov.reshape(basis * rows, width)


def params(mib):
    return pltpu.CompilerParams(vmem_limit_bytes=mib << 20)


def cost(flops, read, transcendentals=0):
    return pl.CostEstimate(flops=flops, bytes_accessed=read, transcendentals=transcendentals)


FAST = pl.BlockSpec(memory_space=pltpu.VMEM)
SMALL = pl.BlockSpec(memory_space=pltpu.SMEM)
FAR = pl.BlockSpec(memory_space=pltpu.HBM)


def block_rows(rows):
    return 64 if rows % 64 == 0 else rows


def half_start(flip, devices, width, other):
    top = lax.div(flip, devices // 2) ^ other
    return pl.multiple_of(top * (width // 2), width // 2)


def live_tokens(info, lower, upper, gain, normed, spots):
    spare = info[1] - (LIVE - LEN)
    shift = lax.rem(spare, GROUP)
    half = (LIVE - LEN) // GROUP
    per = LEN // GROUP
    scale = gain[...].astype(F32)
    row_ids = lax.broadcasted_iota(jnp.int32, (GROUP, 1), 0)

    half_groups = lower.shape[0]

    def load(group):
        spot = spots(info[0], group)
        place = lax.rem(spot, half_groups)
        return jnp.where(spot < half_groups, lower[place], upper[place]).astype(F32)

    def tokens(slot):
        if slot < half:
            return load(slot)
        if slot < 2 * half:
            at = slot - half
            first = load(half + at)
            second = pltpu.roll(load(per + 2 * half - 1 - at), shift, 0)
            return jnp.where(GROUP * at + row_ids < spare, first, second)
        return load(per + slot - 2 * half)

    def norm(wide):
        mean = jnp.mean(wide * wide, axis=1, keepdims=True)
        return wide * lax.rsqrt(mean + 1e-06) * scale

    for pair in range(LIVE // (2 * GROUP)):
        both = [norm(tokens(2 * pair + side)) for side in range(2)]
        normed[2 * GROUP * pair : 2 * GROUP * (pair + 1), :] = jnp.concatenate(both, 0).astype(BF16)


def jvp_half(info, tangent_t, hidden_t, down, probe, out, inv_ff, splits):
    rows = LIVE // splits
    places = out.shape[0]
    width = down.shape[1]
    step = min(512, width)
    each = step // LANES
    for at in range(width // step):
        here = slice(at * step, (at + 1) * step)
        values = dot_nn(tangent_t, down[:, here]) + dot_nn(hidden_t, probe[:, here]) * inv_ff
        for column in range(each):
            for part in range(splits):
                piece = values[
                    part * rows : (part + 1) * rows, column * LANES : (column + 1) * LANES
                ]
                chunk = (at * each + column) * splits + part
                out[chunk ^ (info[0] & (places - 1))] = piece.astype(out.dtype)


def down_copies(info, devices, other, sources, held, sems):
    width = held.shape[2]
    start = half_start(info[0], devices, 2 * width, other)
    return [
        pltpu.make_async_copy(source.at[:, pl.ds(start, width)], held.at[at], sems.at[at])
        for at, source in enumerate(sources)
    ]


def forward_kernel(
    devices, inv_d, inv_ff, spots, splits,
    info, lower, upper, gain, gate, up, krylov_gate, krylov_up, down, krylov_down,
    normed, hidden, tangent_t, hidden_t, weight, act_out, send,
    held, held_down, tangent, sems, down_sems,
):
    basis = krylov_gate.shape[0]
    count, _, lines, width = held.shape
    sources = (gate, up, krylov_gate.at[basis - 1], krylov_up.at[basis - 1])
    copies = [
        [
            pltpu.make_async_copy(
                source.at[at * lines : (at + 1) * lines], held.at[at, one], sems.at[at, one]
            )
            for one, source in enumerate(sources)
        ]
        for at in range(count)
    ]
    last = down_copies(
        info, devices, 1, (down, krylov_down.at[basis - 1]), held_down, down_sems
    )
    for copy in sum(copies, []) + last:
        copy.start()
    live_tokens(info, lower, upper, gain, normed, spots)
    for at in range(count):
        for copy in copies[at]:
            copy.wait()
        made = dot_nt(stacked(held[at]), normed[...])
        gate_pre, up_pre, tan_gate, tan_up = (
            made[one * lines : (one + 1) * lines] for one in range(4)
        )
        act, slope = gelu_pair(gate_pre)
        here = slice(at * lines, (at + 1) * lines)
        hidden[here, :] = (act * up_pre).astype(BF16)
        tangent[here, :] = (
            slope * (tan_gate * inv_d) * up_pre + act * (tan_up * inv_d)
        ).astype(BF16)
        weight[here, :] = up_pre * slope
        act_out[here, :] = act
    tangent_t[...] = tangent[...].T
    hidden_t[...] = hidden[...].T
    for copy in last:
        copy.wait()
    jvp_half(
        info, tangent_t[...], hidden_t[...], held_down.at[0], held_down.at[1], send, inv_ff, splits
    )


def keep_kernel(
    devices, inv_ff, splits,
    info, tangent_t, hidden_t, down, krylov_down, keep, held_down, sems,
):
    basis = krylov_down.shape[0]
    copies = down_copies(info, devices, 0, (down, krylov_down.at[basis - 1]), held_down, sems)
    for copy in copies:
        copy.start()
    for copy in copies:
        copy.wait()
    jvp_half(
        info, tangent_t[...], hidden_t[...], held_down.at[0], held_down.at[1], keep, inv_ff, splits
    )


def row_copies(krylov, first, held, sems):
    count, _, lines, _ = held.shape

    def copy(at):
        start = (first + at) * lines
        if not isinstance(at, int):
            start = pl.multiple_of(start, lines)
        return pltpu.make_async_copy(
            krylov.at[:, pl.ds(start, lines), :], held.at[at], sems.at[at]
        )

    for at in range(count):
        copy(at).start()
    return copy


def gram_kernel(first, start, fold, krylov, earlier, out, held, sums, sems):
    count, basis, lines, _ = held.shape
    copy = row_copies(krylov, first, held, sems)
    sums[...] = jnp.zeros_like(sums) if start else earlier[...]

    def body(at, carry):
        copy(at).wait()
        stack = stacked(held[at])
        sums[...] += dot_nt(stack, stack)
        return carry

    lax.fori_loop(0, count, body, 0)
    if not fold:
        out[...] = sums[...]
        return
    size = basis * lines
    own = lax.broadcasted_iota(jnp.int32, (size, size), 0)
    other = lax.broadcasted_iota(jnp.int32, (size, size), 1)
    if lines & (lines - 1) == 0:
        same = (own & (lines - 1)) == (other & (lines - 1))
    else:
        same = lax.rem(own, lines) == lax.rem(other, lines)
    kept = jnp.where(same, sums[...], 0.0)
    rows = [
        jnp.sum(kept[one * lines : (one + 1) * lines], axis=0, keepdims=True)
        for one in range(basis)
    ]
    place = lax.broadcasted_iota(jnp.int32, (size, LANES), 0)
    lane = lax.broadcasted_iota(jnp.int32, (size, LANES), 1) * lines
    picks = jnp.where((place >= lane) & (place < lane + lines), 1.0, 0.0).astype(F32)
    out[...] = jnp.dot(
        jnp.concatenate(rows, axis=0), picks,
        precision=lax.Precision.HIGHEST, preferred_element_type=F32,
    )


def product_kernel(krylov, normed, out, square, held, sems):
    count, basis, lines, _ = held.shape
    copy = row_copies(krylov, 0, held, sems)
    square[...] = dot_nt(normed[...], normed[...])

    def body(at, carry):
        copy(at).wait()
        made = dot_nt(stacked(held[at]), normed[...])
        here = pl.ds(pl.multiple_of(at * lines, lines), lines)
        for one in range(basis):
            out[one, here, :] = made[one * lines : (one + 1) * lines]
        return carry

    lax.fori_loop(0, count, body, 0)


def loss_columns(flip, load, places, splits):
    made = []
    for column in range(places // splits):
        pieces = [
            load((column * splits + part) ^ (flip & (places - 1))) for part in range(splits)
        ]
        if splits > 1:
            pieces = [jnp.concatenate([one.astype(F32) for one in pieces], 0).astype(BF16)]
        made.append(pieces[0])
    return jnp.concatenate(made, axis=1)


def back_copies(info, devices, other, down, krylov, held_down, held, sems):
    count, _, lines, width = held.shape
    start = half_start(info[0], devices, 2 * width, other)
    columns = pl.ds(start, width)
    copies = [
        pltpu.make_async_copy(
            krylov.at[:, at * lines : (at + 1) * lines, columns], held.at[at], sems.at[at]
        )
        for at in range(count)
    ]
    return copies, pltpu.make_async_copy(down.at[:, columns], held_down, sems.at[count])


def back_half_kernel(
    devices, splits,
    info, chunks, down, krylov, sums, back_sum, square,
    loss, held_down, held, sems,
):
    count, basis, lines, _ = held.shape
    copies, first = back_copies(info, devices, 0, down, krylov, held_down, held, sems)
    for copy in [first] + copies:
        copy.start()
    loss[...] = loss_columns(info[0], lambda at: chunks[at], chunks.shape[0], splits)
    square[...] = dot_nt(loss[...], loss[...])
    first.wait()
    back_sum[...] = dot_nt(held_down[...], loss[...])
    for at in range(count):
        copies[at].wait()
        made = dot_nt(stacked(held[at]), loss[...])
        for one in range(basis):
            sums[one, at * lines : (at + 1) * lines, :] = made[one * lines : (one + 1) * lines]


def back_kernel(
    devices, inv_d, inv_ff, splits,
    info, chunks, down, krylov, hidden, weight, act, square, loss_square_half, back_half, grams,
    sums_half, prod_gate, prod_up,
    s_out, r_out, stats,
    loss, held_down, held, half_held, gate_held, up_held, sems, more_sems,
):
    count, basis, lines, _ = held.shape
    copies, first = back_copies(info, devices, 1, down, krylov, held_down, held, sems)
    more = [
        pltpu.make_async_copy(source, target, more_sems.at[at])
        for at, (source, target) in enumerate(
            ((prod_gate, gate_held), (prod_up, up_held), (sums_half, half_held))
        )
    ]
    for copy in [first] + more + copies:
        copy.start()
    loss[...] = loss_columns(info[0], lambda at: chunks[at], chunks.shape[0], splits)
    first.wait()
    back = dot_nt(held_down[...], loss[...]) + back_half[...]
    s_term = (back * weight[...]).astype(BF16)
    r_term = (back * act[...]).astype(BF16)
    s_out[...] = s_term
    r_out[...] = r_term
    wide = hidden[...]
    squares = inv_d * inv_d * ((dot_tn(s_term, s_term) + dot_tn(r_term, r_term)) * square[...])
    other = dot_nt(loss[...], loss[...]) + loss_square_half[...]
    squares = total(squares + inv_ff * inv_ff * (dot_tn(wide, wide) * other))
    stats[basis : 2 * basis, :] = jnp.broadcast_to(squares, (basis, LANES))
    stats[2 * basis : 3 * basis, :] = grams[...]
    for copy in more:
        copy.wait()
    wide_s = s_term.astype(F32) * inv_d
    wide_r = r_term.astype(F32) * inv_d
    wide_h = wide.astype(F32) * inv_ff
    values = []
    for one in range(basis):
        value = wide_s * gate_held[one] + wide_r * up_held[one] + wide_h * half_held[one]
        values.append(jnp.sum(value, axis=0, keepdims=True))
    for at in range(count):
        copies[at].wait()
        made = dot_nt(stacked(held[at]), loss[...])
        part = wide_h[at * lines : (at + 1) * lines]
        for one in range(basis):
            value = part * made[one * lines : (one + 1) * lines]
            values[one] = values[one] + jnp.sum(value, axis=0, keepdims=True)
    lined = jnp.sum(jnp.concatenate(values, axis=0), axis=1, keepdims=True)
    stats[0:basis, :] = jnp.broadcast_to(lined, (basis, LANES))


def split_three(value):
    first = value.astype(BF16)
    rest = value - first.astype(F32)
    second = rest.astype(BF16)
    return first, second, (rest - second.astype(F32)).astype(BF16)


def new_kernel(
    basis, count, inv_d, inv_ff, splits,
    info, stats, s_term, r_term, hidden, normed, lower, upper,
    krylov_gate, krylov_up, krylov_down,
    new_gate, new_up, new_down, coefficients,
    loss, wide, held, outs, sems, out_sems,
):
    depth, _, lines, width = held.shape
    outs_depth = outs.shape[0]
    rows = s_term.shape[0]
    number = rows // lines
    size = basis * lines
    sources = (krylov_gate, krylov_up, krylov_down)
    targets = (new_gate, new_up, new_down)

    def rows_at(at):
        return pl.ds(pl.multiple_of(at * lines, lines), lines)

    def copy_in(part, at):
        slot = lax.rem(part * number + at, depth)
        return pltpu.make_async_copy(
            sources[part].at[:, rows_at(at), :], held.at[slot], sems.at[slot]
        )

    def copy_out(part, at):
        slot = lax.rem(part * number + at, outs_depth)
        return pltpu.make_async_copy(
            outs.at[slot], targets[part].at[rows_at(at), :], out_sems.at[slot]
        )

    def fetch(turn):
        for part in range(3):
            @pl.when((turn >= part * number) & (turn < (part + 1) * number))
            def _(part=part):
                copy_in(part, turn - part * number).start()

    for turn in range(min(depth - 1, 3 * number)):
        copy_in(turn // number, turn % number).start()

    half_places = lower.shape[0]

    def load(place):
        at = place & (half_places - 1)
        return jnp.where(place < half_places, lower[at], upper[at])

    loss[...] = loss_columns(info[0], load, 2 * half_places, splits)
    proj = [stats[one, 0] / count for one in range(basis)]
    squares = stats[basis, 0]
    for one in range(basis):
        line = stats[2 * basis + one, 0] * proj[0]
        for two in range(1, basis):
            line = line + stats[2 * basis + one, two] * proj[two]
        squares = squares + proj[one] * (line - 2.0 * stats[one, 0])
    mean = jnp.maximum(jnp.full((8, LANES), squares / count, F32), 0.0)
    norm = jnp.sqrt(mean + 1e-06)
    inverse = jnp.max(1.0 / norm)
    for one in range(basis):
        coefficients[one] = proj[one]
    coefficients[basis] = jnp.max(norm)
    lane = lax.broadcasted_iota(jnp.int32, (lines, size), 1)
    row = lax.broadcasted_iota(jnp.int32, (lines, size), 0)
    values = jnp.zeros((lines, size), F32)
    for one in range(basis):
        values = jnp.where(lane == one * lines + row, proj[one] * inverse, values)
    terms = [term.astype(F32) for term in split_three(values)]
    mix = jnp.concatenate(terms, axis=0).astype(BF16)

    for part, (left, right, scale) in enumerate(
        ((s_term, normed, inv_d), (r_term, normed, inv_d), (hidden, loss, inv_ff))
    ):
        wide[...] = dot_nn(left[...], right[...]) * (scale * inverse)

        def body(at, carry, part=part):
            turn = part * number + at
            fetch(turn + depth - 1)
            copy_in(part, at).wait()

            @pl.when(turn >= outs_depth)
            def _():
                copy_out(part, at).wait()

            mixed = dot_nn(mix, stacked(held[lax.rem(turn, depth)]))
            mixed = mixed[:lines] + (mixed[lines : 2 * lines] + mixed[2 * lines :])
            outs[lax.rem(turn, outs_depth)] = (wide[rows_at(at), :] - mixed).astype(BF16)
            copy_out(part, at).start()
            return carry

        lax.fori_loop(0, number, body, 0)
    for turn in range(max(0, 3 * number - outs_depth), 3 * number):
        copy_out(turn // number, turn % number).wait()


def per_device(
    inputs, norm_gain, lengths, gate_rows, up_rows, down_rows, krylov_gate, krylov_up, krylov_down
):
    basis, rows, width = krylov_gate.shape
    devices = lax.axis_size("fsdp")
    bits = devices.bit_length() - 1
    hidden_all = rows * devices
    count = 3.0 * width * hidden_all
    inv_d = 1.0 / math.sqrt(width)
    inv_ff = 1.0 / math.sqrt(hidden_all)
    me = lax.axis_index("fsdp").astype(jnp.int32)
    mirror = reverse_bits(me, bits)
    info = jnp.stack([mirror, lengths[0]])

    splits = devices // (width // LANES)
    chunk_rows = LIVE // splits
    lines = 32 if rows % 32 == 0 else rows
    pieces = rows // lines
    long = block_rows(rows)
    halved = width // 2
    product_flops = 2 * rows * width * LIVE

    def gram(krylov, first, number, fold, earlier, before):
        size = basis * lines
        start = earlier is None
        if start:
            earlier = jnp.zeros((8, LANES), F32)
        krylov = krylov if before is None else after(krylov, before)
        out = (basis, LANES) if fold else (size, size)
        return pl.pallas_call(
            functools.partial(gram_kernel, first, start, fold),
            in_specs=[FAR, FAST],
            out_specs=FAST,
            out_shape=jax.ShapeDtypeStruct(out, F32),
            scratch_shapes=[
                pltpu.VMEM((number, basis, lines, width), BF16),
                pltpu.VMEM((size, size), F32),
                pltpu.SemaphoreType.DMA((number,)),
            ],
            compiler_params=params(46),
            cost_estimate=cost(2 * size * size * width * number, 2 * size * width * number),
            name="gram",
        )(krylov, earlier)

    cut = (pieces + 1) // 2
    spans = [
        (krylov, first, number)
        for krylov in (krylov_gate, krylov_up, krylov_down)
        for first, number in ((0, cut), (cut, pieces - cut))
        if number
    ]
    gram_sums = []

    def next_gram(before):
        krylov, first, number = spans[len(gram_sums)]
        fold = len(gram_sums) == len(spans) - 1
        earlier = gram_sums[-1] if gram_sums else None
        gram_sums.append(gram(krylov, first, number, fold, earlier, before))
        return gram_sums[-1]

    def done_gram(value):
        gram_sums[-1] = value

    own_tokens = inputs.shape[0]
    tokens = own_tokens * devices
    if own_tokens % GROUP == 0:
        sub = own_tokens // GROUP
        lower, upper = gather_blocks(
            inputs.reshape(sub, GROUP, width),
            bits,
            {bit: (next_gram, done_gram) for bit in range(min(bits, len(spans) - 1))},
        )

        def spots(flip, group):
            return (reverse_bits(group // sub, bits) ^ flip) * sub + group % sub

    else:
        gathered = lax.all_gather(inputs, "fsdp", axis=0, tiled=True)
        gathered = gathered.reshape(tokens // GROUP, GROUP, width)
        lower, upper = jnp.split(gathered, 2)

        def spots(flip, group):
            return group

    normed, hidden, tangent_t, hidden_t, weight, act, send = pl.pallas_call(
        functools.partial(forward_kernel, devices, inv_d, inv_ff, spots, splits),
        in_specs=[SMALL] + [FAST] * 3 + [FAR] * 6,
        out_specs=[FAST] * 7,
        out_shape=[
            jax.ShapeDtypeStruct((LIVE, width), BF16),
            jax.ShapeDtypeStruct((rows, LIVE), BF16),
            jax.ShapeDtypeStruct((LIVE, rows), BF16),
            jax.ShapeDtypeStruct((LIVE, rows), BF16),
            jax.ShapeDtypeStruct((rows, LIVE), F32),
            jax.ShapeDtypeStruct((rows, LIVE), F32),
            jax.ShapeDtypeStruct((devices // 2, chunk_rows, LANES), BF16),
        ],
        scratch_shapes=[
            pltpu.VMEM((rows // long, 4, long, width), BF16),
            pltpu.VMEM((2, rows, halved), BF16),
            pltpu.VMEM((rows, LIVE), BF16),
            pltpu.SemaphoreType.DMA((rows // long, 4)),
            pltpu.SemaphoreType.DMA((2,)),
        ],
        compiler_params=params(46),
        cost_estimate=cost(5 * product_flops, 10 * rows * width + 6 * LIVE * width, rows * LIVE),
        name="forward",
    )(
        info, lower, upper, norm_gain.reshape(1, width), gate_rows, up_rows, krylov_gate,
        krylov_up, down_rows, krylov_down,
    )

    def product(krylov, before):
        return pl.pallas_call(
            product_kernel,
            in_specs=[FAR, FAST],
            out_specs=[FAST, FAST],
            out_shape=[
                jax.ShapeDtypeStruct((basis, rows, LIVE), F32),
                jax.ShapeDtypeStruct((LIVE, LIVE), F32),
            ],
            scratch_shapes=[
                pltpu.VMEM((pieces, basis, lines, width), BF16),
                pltpu.SemaphoreType.DMA((pieces,)),
            ],
            compiler_params=params(46),
            cost_estimate=cost(
                basis * product_flops, 2 * basis * rows * width + 4 * basis * rows * LIVE
            ),
            name="product",
        )(after(krylov, before), normed)

    got = exchange(send, 0)
    keep = pl.pallas_call(
        functools.partial(keep_kernel, devices, inv_ff, splits),
        in_specs=[SMALL, FAST, FAST, FAR, FAR],
        out_specs=FAST,
        out_shape=jax.ShapeDtypeStruct((devices // 2, chunk_rows, LANES), F32),
        scratch_shapes=[
            pltpu.VMEM((2, rows, halved), BF16),
            pltpu.SemaphoreType.DMA((2,)),
        ],
        compiler_params=params(46),
        cost_estimate=cost(product_flops, 2 * rows * width + 2 * LIVE * width),
        name="keep",
    )(info, tangent_t, hidden_t, down_rows, krylov_down)

    plan = {1: krylov_gate, 2: krylov_up}
    prods = []
    for bit in range(1, bits):
        part = keep.shape[0] // 2
        send = (keep[part:] + got[part:].astype(F32)).astype(BF16)
        keep = keep[:part] + got[:part].astype(F32)
        got = exchange(send, bit)
        if bit in plan:
            got, made = lax.optimization_barrier((got, product(plan[bit], send)))
            prods.append(made)
    (prod_gate, square), (prod_up, _) = prods
    loss_own = (keep + got.astype(F32)).astype(BF16)

    def half_call(lower):
        return pl.pallas_call(
            functools.partial(back_half_kernel, devices, splits),
            in_specs=[SMALL, FAST, FAR, FAR],
            out_specs=[FAST] * 3,
            out_shape=[
                jax.ShapeDtypeStruct((basis, rows, LIVE), F32),
                jax.ShapeDtypeStruct((rows, LIVE), F32),
                jax.ShapeDtypeStruct((LIVE, LIVE), F32),
            ],
            scratch_shapes=[
                pltpu.VMEM((LIVE, halved), BF16),
                pltpu.VMEM((rows, halved), BF16),
                pltpu.VMEM((rows // long, basis, long, halved), BF16),
                pltpu.SemaphoreType.DMA((rows // long + 1,)),
            ],
            compiler_params=params(46),
            cost_estimate=cost(
                (basis + 1) * product_flops // 2,
                (basis + 1) * rows * width + 4 * basis * rows * LIVE,
            ),
            name="back_half",
        )(info, lower, down_rows, krylov_down)

    halves = []
    beside = {0: (half_call, halves.extend)}
    if 0 < len(gram_sums) < len(spans):
        beside[1] = (next_gram, done_gram)
    lower, upper = gather_blocks(loss_own, bits, beside)
    while len(gram_sums) < len(spans):
        next_gram(None)
    sums_half, back_half, loss_square_half = halves

    s_term, r_term, stats = pl.pallas_call(
        functools.partial(back_kernel, devices, inv_d, inv_ff, splits),
        in_specs=[SMALL, FAST, FAR, FAR] + [FAST] * 7 + [pl.BlockSpec(memory_space=pl.ANY)] * 3,
        out_specs=[FAST] * 3,
        out_shape=[
            jax.ShapeDtypeStruct((rows, LIVE), BF16),
            jax.ShapeDtypeStruct((rows, LIVE), BF16),
            jax.ShapeDtypeStruct((3 * basis, LANES), F32),
        ],
        scratch_shapes=[
            pltpu.VMEM((LIVE, halved), BF16),
            pltpu.VMEM((rows, halved), BF16),
            pltpu.VMEM((rows // long, basis, long, halved), BF16),
            pltpu.VMEM((basis, rows, LIVE), F32),
            pltpu.VMEM((basis, rows, LIVE), F32),
            pltpu.VMEM((basis, rows, LIVE), F32),
            pltpu.SemaphoreType.DMA((rows // long + 1,)),
            pltpu.SemaphoreType.DMA((3,)),
        ],
        compiler_params=params(46),
        cost_estimate=cost(
            (basis + 1) * product_flops // 2,
            (basis + 1) * rows * width + 12 * basis * rows * LIVE,
        ),
        name="back",
    )(
        info, upper, down_rows, krylov_down, hidden, weight, act, square, loss_square_half,
        back_half, gram_sums[-1], sums_half, prod_gate, prod_up,
    )

    for bit in range(bits):
        stats = stats + exchange(stats, bit)

    depth, outs_depth = min(8, 3 * pieces), min(4, 3 * pieces)
    out_shape = jax.ShapeDtypeStruct((rows, width), BF16)
    new_gate, new_up, new_down, coefficients = pl.pallas_call(
        functools.partial(new_kernel, basis, count, inv_d, inv_ff, splits),
        in_specs=[SMALL, SMALL] + [FAST] * 6 + [FAR] * 3,
        out_specs=[FAR] * 3 + [SMALL],
        out_shape=[out_shape, out_shape, out_shape, jax.ShapeDtypeStruct((basis + 1,), F32)],
        scratch_shapes=[
            pltpu.VMEM((LIVE, width), BF16),
            pltpu.VMEM((rows, width), F32),
            pltpu.VMEM((depth, basis, lines, width), BF16),
            pltpu.VMEM((outs_depth, lines, width), BF16),
            pltpu.SemaphoreType.DMA((depth,)),
            pltpu.SemaphoreType.DMA((outs_depth,)),
        ],
        compiler_params=params(46),
        cost_estimate=cost(3 * product_flops, 6 * (basis + 1) * rows * width),
        name="new",
    )(
        info, stats, s_term, r_term, hidden, normed, lower, upper, krylov_gate, krylov_up,
        krylov_down,
    )
    return (new_gate, new_up, new_down, coefficients)


def solution(mesh):
    placed = (
        P("fsdp", None),
        P(),
        P(),
        P("fsdp", None),
        P("fsdp", None),
        P("fsdp", None),
        P(None, "fsdp", None),
        P(None, "fsdp", None),
        P(None, "fsdp", None),
    )
    return jax.shard_map(
        per_device,
        mesh=mesh,
        in_specs=placed,
        out_specs=(P("fsdp", None), P("fsdp", None), P("fsdp", None), P()),
        check_vma=False,
    )
```

time: 824 us -> 177 us (0.21)
  matrix products: 417 us -> 0 us
  waiting for transfers between devices: 250 us -> 47 us
  Pallas kernels: 0 us -> 108 us
  blocking collectives: 79.3 us -> 0 us
  other arithmetic: 51.8 us -> 0.62 us
  starting transfers between devices: 0.3 us -> 17.9 us
  between operations: 16.9 us -> 1.18 us
    dot_general x15 -> x0, matrix products: 417 us -> none  [the longest x3 241 us: local_dots(): jnp.einsum('jfd,fd->j', krylov.astype(jnp.float32), grad, precision=lax.P...]
    reduce_scatter x1 -> x0, waiting for transfers between devices: 139 us -> none  [per_device(): lax.psum_scatter(contract_first(down_rows, tangent) + contract_first(prob...]
    all_gather x2 -> x0, waiting for transfers between devices: 111 us -> none  [the longest x1 59.8 us: per_device(): normed = lax.all_gather(normed_own, 'fsdp', axis=0, tiled=True)]
    pallas_call x0 -> x13, Pallas kernels: none -> 108 us  [the longest x6 32.5 us: gram(): pl.pallas_call(functools.partial(gram_kernel, first, start, fold), in_spe...]
    psum x2 -> x0, blocking collectives: 79.3 us -> none  [the longest x1 39.7 us: per_device(): squares = lax.psum(own_left, 'fsdp') / count]
    ppermute x0 -> x20, waiting for transfers between devices: none -> 47 us  [exchange(): lax.ppermute(block, 'fsdp', [(one, one ^ 1 << bit) for one in range(count)])]
    convert_element_type x7 -> x4, other arithmetic: 26.9 us -> 0.3 us  [per_device(): send = (keep[part:] + got[part:].astype(F32)).astype(BF16)]
    reduce_sum x4 -> x0, other arithmetic: 24.3 us -> none  [the longest x1 13.1 us: per_device(): jnp.sum(residuals[1] * residuals[1])]
  transfers between devices with their start and end apart: 3 -> 20, of which waited for: 3 -> 14; matrix products, arithmetic and copies ran while one was open for 0% -> 1% of each run, Pallas kernels for 0% -> 35%
where the time goes in v3:
time: 177 us
  Pallas kernels  108 us (61%)
  waiting for transfers between devices  47 us (27%)
  starting transfers between devices  17.9 us (10%)
  local copies, waits for them, and re-layouts  2.58 us (1%)
    ppermute x20, waiting for transfers between devices, exchange(): lax.ppermute(block, 'fsdp', [(one, one ^ 1 << bit) for one in range(count)])  47 us
    pallas_call x6, Pallas kernels, gram(): pl.pallas_call(functools.partial(gram_kernel, first, start, fold), in_spe...  32.5 us
    pallas_call x1, Pallas kernels, per_device(): pl.pallas_call(functools.partial(new_kernel, basis, count, inv_d, inv_ff,...  25.6 us
    pallas_call x2, Pallas kernels, product(): pl.pallas_call(product_kernel, in_specs=[FAR, FAST], out_specs=[FAST, FAS...  18.1 us
    ppermute x20, starting transfers between devices, exchange(): lax.ppermute(block, 'fsdp', [(one, one ^ 1 << bit) for one in range(count)])  17.9 us
    pallas_call x1, Pallas kernels, per_device(): pl.pallas_call(functools.partial(forward_kernel, devices, inv_d, inv_ff,...  10.2 us
    pallas_call x1, Pallas kernels, per_device(): pl.pallas_call(functools.partial(back_kernel, devices, inv_d, inv_ff, spl...  10.1 us
    pallas_call x1, Pallas kernels, half_call(): pl.pallas_call(functools.partial(back_half_kernel, devices, splits), in_s...  8.12 us
  transfers between devices with their start and end apart: 20, of which 14 were waited for; matrix products, arithmetic and copies ran while one was open for 1% of the time, Pallas kernels for 35%

profile of v3, /device:TPU:0, one launch (start us, length us, event | category | flops | bytes accessed | tf_op | source)
XLA Modules:
  0.0 176.9 jit_solution(10853638684218775976)
XLA Ops:
  0.6 4.1 %collective-permute-start = (bf16[1,8,4096]{2,1,0:T(8,128)(2,1)}, bf16[1,8,4096]{2,1,0:T(8,128)(2,1)S(1)}, u32[]{:S(2)}, u32[]{:S(2)}) collective-permute-start(bf16[1,8,4096]{2,1,0:T(8,128)(2,1)} %bitcast.4), channel_id=1, source_target_pairs={{0,16},{1,17},{2,18},{3,19},{4,20},{5,21},{6,22},{7,23},{8,24},{9,... | collective-permute-start | bytes 196616 | tf_op jit(solution)/shard_map/ppermute | solution.py:55
  4.7 0.9 constant_dynamic-update-slice_fusion.4
  5.6 5.4 %gram.6.earlier = f32[256,256]{1,0:T(8,128)S(1)} custom-call(bf16[8,320,4096]{2,1,0:T(8,128)(2,1)} %krylov_gate.3, f32[8,128]{1,0:T(8,128)S(1)} %broadcast_in_dim.3.earlier), custom_call_target="tpu_custom_call" | custom-call | flops 2684354560 | bytes 10485760 | tf_op jit(solution)/shard_map/gram/pallas_call | solution.py:518
  11.1 1.6 collective-permute-start.1
  12.7 5.3 %gram.7.earlier = f32[256,256]{1,0:T(8,128)S(1)} custom-call(bf16[8,320,4096]{2,1,0:T(8,128)(2,1)} %krylov_gate.3, f32[256,256]{1,0:T(8,128)S(1)} %gram.6.earlier), custom_call_target="tpu_custom_call" | custom-call | flops 2684354560 | bytes 10485760 | tf_op jit(solution)/shard_map/gram/pallas_call | solution.py:518
  18.1 1.6 collective-permute-start.2
  19.7 5.4 %gram.8.earlier = f32[256,256]{1,0:T(8,128)S(1)} custom-call(bf16[8,320,4096]{2,1,0:T(8,128)(2,1)} %krylov_up.3, f32[256,256]{1,0:T(8,128)S(1)} %gram.7.earlier), custom_call_target="tpu_custom_call" | custom-call | flops 2684354560 | bytes 10485760 | tf_op jit(solution)/shard_map/gram/pallas_call | solution.py:518
  25.1 0.6 collective-permute-done.2
  25.7 1.6 collective-permute-start.3
  27.3 5.4 %gram.9.earlier = f32[256,256]{1,0:T(8,128)S(1)} custom-call(bf16[8,320,4096]{2,1,0:T(8,128)(2,1)} %krylov_up.3, f32[256,256]{1,0:T(8,128)S(1)} %gram.8.earlier), custom_call_target="tpu_custom_call" | custom-call | flops 2684354560 | bytes 10485760 | tf_op jit(solution)/shard_map/gram/pallas_call | solution.py:518
  32.7 5.4 %collective-permute-done.3 = bf16[8,8,4096]{2,1,0:T(8,128)(2,1)S(1)} collective-permute-done((bf16[8,8,4096]{2,1,0:T(8,128)(2,1)S(1)}, bf16[8,8,4096]{2,1,0:T(8,128)(2,1)S(1)}, u32[]{:S(2)}, u32[]{:S(2)}) %collective-permute-start.3) | collective-permute-done | bytes 524320 | tf_op jit(solution)/shard_map/ppermute | solution.py:55
  38.1 0.1 collective-permute-start.4
  38.2 0.1 pad_add_fusion.info
  38.4 5.5 %gram.10.earlier = f32[256,256]{1,0:T(8,128)S(1)} custom-call(bf16[8,320,4096]{2,1,0:T(8,128)(2,1)} %krylov_down.5, f32[256,256]{1,0:T(8,128)S(1)} %gram.9.earlier), custom_call_target="tpu_custom_call" | custom-call | flops 2684354560 | bytes 10485760 | tf_op jit(solution)/shard_map/gram/pallas_call | solution.py:518
  43.9 10.2 %forward.1 = (bf16[192,4096]{1,0:T(8,128)(2,1)S(1)}, bf16[320,192]{1,0:T(8,128)(2,1)S(1)}, bf16[192,320]{1,0:T(8,128)(2,1)S(1)}, bf16[192,320]{1,0:T(8,128)(2,1)...) custom-call(s32[2]{0:T(128)S(1)} %pad_add_fusion.info, ...), custom_call_target="tpu_custom_call" | custom-call | flops 2516582400 | bytes 17825792 | tf_op jit(solution)/shard_map/forward/pallas_call | solution.py:573
  54.1 0.5 collective-permute-start.5
  54.6 3.1 %keep.1 = f32[16,192,128]{2,1,0:T(8,128)S(1)} custom-call(s32[2]{0:T(128)S(1)} %pad_add_fusion.info, bf16[192,320]{1,0:T(8,128)(2,1)S(1)} %get-tuple-element.63.tangent_t, bf16[192,320]{1,0:T(8,128)(2,1)S(1)} %get-tuple-element.64.hidden_t, bf16[320,4096]{1,0:T(8,128)(2,1)S(1)} %copy-done, bf16[8,320,4096]{2,1,0:T(8,128)(2,1)} %krylov_down.5), custom_call_target="tpu_custom_call" | custom-call | flops 503316480 | bytes 4194304 | tf_op jit(solution)/shard_map/keep/pallas_call | solution.py:622
  57.7 0.2 fusion
  57.9 1.6 collective-permute-start.6
  59.4 8.9 %product.2 = (f32[8,320,192]{2,1,0:T(8,128)S(1)}, f32[192,192]{1,0:T(8,128)S(1)}) custom-call(bf16[8,320,4096]{2,1,0:T(8,128)(2,1)} %krylov_gate.3, bf16[192,4096]{1,0:T(8,128)(2,1)S(1)} %get-tuple-element.67.normed), custom_call_target="tpu_custom_call" | custom-call | flops 4026531840 | bytes 22937600 | tf_op jit(solution)/shard_map/product/pallas_call | solution.py:602
  68.4 0.6 collective-permute-done.6
  69.1 1.5 collective-permute-start.7
  70.6 9.1 %product.3 = (f32[8,320,192]{2,1,0:T(8,128)S(1)}, f32[192,192]{1,0:T(8,128)}) custom-call(bf16[8,320,4096]{2,1,0:T(8,128)(2,1)} %krylov_up.3, bf16[192,4096]{1,0:T(8,128)(2,1)S(1)} %get-tuple-element.67.normed), custom_call_target="tpu_custom_call" | custom-call | flops 4026531840 | bytes 22937600 | tf_op jit(solution)/shard_map/product/pallas_call | solution.py:602
  79.8 1.5 copy-done.3
  81.3 0.5 collective-permute-start.8
  81.8 4.2 %collective-permute-done.8 = bf16[2,192,128]{2,1,0:T(8,128)(2,1)S(1)} collective-permute-done((bf16[2,192,128]{2,1,0:T(8,128)(2,1)S(1)}, bf16[2,192,128]{2,1,0:T(8,128)(2,1)S(1)}, u32[]{:S(2)}, u32[]{:S(2)}) %collective-permute-start.8) | collective-permute-done | bytes 98336 | tf_op jit(solution)/shard_map/ppermute | solution.py:55
  86.0 0.4 collective-permute-start.9
  86.4 5.9 %collective-permute-done.9 = bf16[1,192,128]{2,1,0:T(8,128)(2,1)S(1)} collective-permute-done((bf16[1,192,128]{2,1,0:T(8,128)(2,1)S(1)}, bf16[1,192,128]{2,1,0:T(8,128)(2,1)S(1)}, u32[]{:S(2)}, u32[]{:S(2)}) %collective-permute-start.9) | collective-permute-done | bytes 49184 | tf_op jit(solution)/shard_map/ppermute | solution.py:55
  92.3 0.1 collective-permute-start.10
  92.4 5.0 %collective-permute-done.10 = bf16[1,192,128]{2,1,0:T(8,128)(2,1)S(1)} collective-permute-done((bf16[1,192,128]{2,1,0:T(8,128)(2,1)S(1)}, bf16[1,192,128]{2,1,0:T(8,128)(2,1)S(1)}, u32[]{:S(2)}, u32[]{:S(2)}) %collective-permute-start.10) | collective-permute-done | bytes 49184 | tf_op jit(solution)/shard_map/ppermute | solution.py:55
  97.4 0.1 collective-permute-start.11
  97.4 4.6 %collective-permute-done.11 = bf16[2,192,128]{2,1,0:T(8,128)(2,1)S(1)} collective-permute-done((bf16[2,192,128]{2,1,0:T(8,128)(2,1)S(1)}, bf16[2,192,128]{2,1,0:T(8,128)(2,1)S(1)}, u32[]{:S(2)}, u32[]{:S(2)}) %collective-permute-start.11) | collective-permute-done | bytes 98336 | tf_op jit(solution)/shard_map/ppermute | solution.py:55
  102.1 0.1 collective-permute-start.12
  102.2 5.6 %collective-permute-done.12 = bf16[4,192,128]{2,1,0:T(8,128)(2,1)S(1)} collective-permute-done((bf16[4,192,128]{2,1,0:T(8,128)(2,1)S(1)}, bf16[4,192,128]{2,1,0:T(8,128)(2,1)S(1)}, u32[]{:S(2)}, u32[]{:S(2)}) %collective-permute-start.12) | collective-permute-done | bytes 196640 | tf_op jit(solution)/shard_map/ppermute | solution.py:55
  107.8 1.6 collective-permute-start.13
  109.5 5.6 %gram.11.grams = f32[8,128]{1,0:T(8,128)S(1)} custom-call(bf16[8,320,4096]{2,1,0:T(8,128)(2,1)} %krylov_down.5, f32[256,256]{1,0:T(8,128)S(1)} %gram.10.earlier), custom_call_target="tpu_custom_call" | custom-call | flops 2684354560 | bytes 10485760 | tf_op jit(solution)/shard_map/gram/pallas_call | solution.py:518
  115.0 0.6 collective-permute-done.13
  115.8 8.1 %back_half.1 = (f32[8,320,192]{2,1,0:T(8,128)S(1)}, f32[320,192]{1,0:T(8,128)S(1)}, f32[192,192]{1,0:T(8,128)S(1)}) custom-call(s32[2]{0:T(128)S(1)} %pad_add_fusion.info, bf16[16,192,128]{2,1,0:T(8,128)(2,1)S(1)} %constant_dynamic-update-slice_fusion.5.chunks.lower, bf16[320,4096]{1,0:T(8,128)(2,1)S(1)} %copy-done, bf16[8,320,4096]{2,1,0:T(8,128)(2,1)} %krylov_down.5), custom_call_target="tpu_custom_call" | custom-call | flops 2264924160 | bytes 13762560 | tf_op jit(solution)/shard_map/back_half/pallas_call | solution.py:650
  124.0 10.1 %back.1 = (bf16[320,192]{1,0:T(8,128)(2,1)S(1)}, bf16[320,192]{1,0:T(8,128)(2,1)S(1)}, f32[24,128]{1,0:T(8,128)S(1)}) custom-call(s32[2]{0:T(128)S(1)} %pad_add_fusion.info, bf16[16,192,128]{2,1,0:T(8,128)(2,1)S(1)} %collective-permute-done.14.chunks.upper, bf16[320,4096]{1,0:T(8,128)(2,1)S(1)} %copy-done, bf16[8,320,4096]{2,1,0:T(8,128)(2,1)} %krylov_down.5, ...), custom_call_target="tpu_custom_call" | custom-call | flops 2264924160 | bytes 17694720 | tf_op jit(solution)/shard_map/back/pallas_call | solution.py:682
  134.1 0.6 collective-permute-start.15
  134.7 0.8 collective-permute-done.15
  135.5 1.5 collective-permute-start.16
  137.0 2.2 %collective-permute-done.16 = f32[24,128]{1,0:T(8,128)S(1)} collective-permute-done((f32[24,128]{1,0:T(8,128)S(1)}, f32[24,128]{1,0:T(8,128)S(1)}, u32[]{:S(2)}, u32[]{:S(2)}) %collective-permute-start.16) | collective-permute-done | bytes 12320 | tf_op jit(solution)/shard_map/ppermute | solution.py:55
  139.2 3.6 %collective-permute-done.17 = f32[24,128]{1,0:T(8,128)S(1)} collective-permute-done((f32[24,128]{1,0:T(8,128)S(1)}, f32[24,128]{1,0:T(8,128)S(1)}, u32[]{:S(2)}, u32[]{:S(2)}) %collective-permute-start.17) | collective-permute-done | bytes 12320 | tf_op jit(solution)/shard_map/ppermute | solution.py:55
  142.9 3.7 %collective-permute-done.18 = f32[24,128]{1,0:T(8,128)S(1)} collective-permute-done((f32[24,128]{1,0:T(8,128)S(1)}, f32[24,128]{1,0:T(8,128)S(1)}, u32[]{:S(2)}, u32[]{:S(2)}) %collective-permute-start.18) | collective-permute-done | bytes 12320 | tf_op jit(solution)/shard_map/ppermute | solution.py:55
  146.6 0.5 collective-permute-start.19
  147.1 4.1 %collective-permute-done.19 = f32[24,128]{1,0:T(8,128)S(1)} collective-permute-done((f32[24,128]{1,0:T(8,128)S(1)}, f32[24,128]{1,0:T(8,128)S(1)}, u32[]{:S(2)}, u32[]{:S(2)}) %collective-permute-start.19) | collective-permute-done | bytes 12320 | tf_op jit(solution)/shard_map/ppermute | solution.py:55
  151.2 25.6 %new.1 = (bf16[320,4096]{1,0:T(8,128)(2,1)}, bf16[320,4096]{1,0:T(8,128)(2,1)}, bf16[320,4096]{1,0:T(8,128)(2,1)}, f32[9]{0:T(128)}) custom-call(s32[2]{0:T(128)S(1)} %pad_add_fusion.info, f32[24,128]{1,0:T(8,128)S(1)} %add.55.stats, bf16[320,192]{1,0:T(8,128)(2,1)S(1)} %get-tuple-element.92.s_term, bf16[320,192]{1,0:T(8,128)(2,1)S(1)} %get-tuple-element.93.r_term, ...), custom_call_target="tpu_custom_call" | custom-call | flops 1509949440 | bytes 70778880 | tf_op jit(solution)/shard_map/new/pallas_call | solution.py:717
  (47 shorter events, 0.7 us)
Async XLA Ops:
  0.6 10.4 %collective-permute-start = (bf16[1,8,4096]{2,1,0:T(8,128)(2,1)}, bf16[1,8,4096]{2,1,0:T(8,128)(2,1)S(1)}, u32[]{:S(2)}, u32[]{:S(2)}) collective-permute-start(bf16[1,8,4096]{2,1,0:T(8,128)(2,1)} %bitcast.4), channel_id=1, source_target_pairs={{0,16},{1,17},{2,18},{3,19},{4,20},{5,21},{6,22},{7,23},{8,24},{9,... | collective-permute-start | bytes 196616 | tf_op jit(solution)/shard_map/ppermute | solution.py:55
  5.6 5.4 %copy-start.4 = (bf16[8,4096]{1,0:T(8,128)(2,1)S(1)}, bf16[8,4096]{1,0:T(8,128)(2,1)}, u32[]{:S(2)}) copy-start(bf16[8,4096]{1,0:T(8,128)(2,1)} %param.9) | copy-start | bytes 196612
  11.1 7.0 %collective-permute-start.1 = (bf16[2,8,4096]{2,1,0:T(8,128)(2,1)S(1)}, bf16[2,8,4096]{2,1,0:T(8,128)(2,1)S(1)}, u32[]{:S(2)}, u32[]{:S(2)}) collective-permute-start(bf16[2,8,4096]{2,1,0:T(8,128)(2,1)S(1)} %pad_maximum_fusion.4), channel_id=1, source_target_pairs={{0,8},{1,9},{2,10},{3,11},{4,12},{5,13},{6,14},{7,15},{8,0},{9,1},... | collective-permute-start | bytes 393224 | tf_op jit(solution)/shard_map/ppermute | solution.py:55
  18.1 7.6 %collective-permute-start.2 = (bf16[4,8,4096]{2,1,0:T(8,128)(2,1)S(1)}, bf16[4,8,4096]{2,1,0:T(8,128)(2,1)S(1)}, u32[]{:S(2)}, u32[]{:S(2)}) collective-permute-start(bf16[4,8,4096]{2,1,0:T(8,128)(2,1)S(1)} %pad_maximum_fusion.2), channel_id=1, source_target_pairs={{0,4},{1,5},{2,6},{3,7},{4,0},{5,1},{6,2},{7,3},{8,12},{9,13},{10,... | collective-permute-start | bytes 786440 | tf_op jit(solution)/shard_map/ppermute | solution.py:55
  25.7 12.5 %copy-start.5 = (bf16[4096]{0:T(1024)(128)(2,1)S(1)}, bf16[4096]{0:T(1024)(128)(2,1)}, u32[]{:S(2)}) copy-start(bf16[4096]{0:T(1024)(128)(2,1)} %param.10) | copy-start | bytes 24580
  25.7 12.5 %copy-start.6 = (s32[2]{0:T(128)S(1)}, s32[2]{0:T(128)}, u32[]{:S(2)}) copy-start(s32[2]{0:T(128)} %param.11) | copy-start | bytes 28
  25.7 12.3 %collective-permute-start.3 = (bf16[8,8,4096]{2,1,0:T(8,128)(2,1)S(1)}, bf16[8,8,4096]{2,1,0:T(8,128)(2,1)S(1)}, u32[]{:S(2)}, u32[]{:S(2)}) collective-permute-start(bf16[8,8,4096]{2,1,0:T(8,128)(2,1)S(1)} %pad_maximum_fusion), channel_id=1, source_target_pairs={{0,2},{1,3},{2,0},{3,1},{4,6},{5,7},{6,4},{7,5},{8,10},{9,11},{10,... | collective-permute-start | bytes 1572872 | tf_op jit(solution)/shard_map/ppermute | solution.py:55
  38.1 5.8 %collective-permute-start.4 = (bf16[16,8,4096]{2,1,0:T(8,128)(2,1)S(1)}, bf16[16,8,4096]{2,1,0:T(8,128)(2,1)S(1)}, u32[]{:S(2)}, u32[]{:S(2)}) collective-permute-start(bf16[16,8,4096]{2,1,0:T(8,128)(2,1)S(1)} %constant_dynamic-update-slice_fusion.lower), channel_id=1, source_target_pairs={{0,1},{1,0},{2,3},{3,2},{4,5},{5,4},{6,7},{7,6},{8,9},{9,8},{10,11... | collective-permute-start | bytes 3145736 | tf_op jit(solution)/shard_map/ppermute | solution.py:55
  38.4 5.5 %copy-start.1 = (bf16[320,4096]{1,0:T(8,128)(2,1)S(1)}, bf16[320,4096]{1,0:T(8,128)(2,1)}, u32[]{:S(2)}) copy-start(bf16[320,4096]{1,0:T(8,128)(2,1)} %gate.1) | copy-start | bytes 7864324
  43.9 10.8 %copy-start = (bf16[320,4096]{1,0:T(8,128)(2,1)S(1)}, bf16[320,4096]{1,0:T(8,128)(2,1)}, u32[]{:S(2)}) copy-start(bf16[320,4096]{1,0:T(8,128)(2,1)} %down.7) | copy-start | bytes 7864324
  54.1 3.6 %collective-permute-start.5 = (bf16[16,192,128]{2,1,0:T(8,128)(2,1)S(1)}, bf16[16,192,128]{2,1,0:T(8,128)(2,1)S(1)}, u32[]{:S(2)}, u32[]{:S(2)}) collective-permute-start(bf16[16,192,128]{2,1,0:T(8,128)(2,1)S(1)} %get-tuple-element.65), channel_id=1, source_target_pairs={{0,1},{1,0},{2,3},{3,2},{4,5},{5,4},{6,7},{7,6},{8,9},{9,8},{10,11... | collective-permute-start | bytes 2359304 | tf_op jit(solution)/shard_map/ppermute | solution.py:55
  57.9 11.1 %collective-permute-start.6 = (bf16[8,192,128]{2,1,0:T(8,128)(2,1)S(1)}, bf16[8,192,128]{2,1,0:T(8,128)(2,1)S(1)}, u32[]{:S(2)}, u32[]{:S(2)}) collective-permute-start(bf16[8,192,128]{2,1,0:T(8,128)(2,1)S(1)} %get-tuple-element.96), channel_id=1, source_target_pairs={{0,2},{1,3},{2,0},{3,1},{4,6},{5,7},{6,4},{7,5},{8,10},{9,11},{10,... | collective-permute-start | bytes 1179656 | tf_op jit(solution)/shard_map/ppermute | solution.py:55
  68.4 11.3 %copy-start.2 = (f32[8,320,192]{2,1,0:T(8,128)}, f32[8,320,192]{2,1,0:T(8,128)S(1)}, u32[]{:S(2)}) copy-start(f32[8,320,192]{2,1,0:T(8,128)S(1)} %get-tuple-element.89.prod_gate) | copy-start | bytes 5898244
  69.1 12.2 %collective-permute-start.7 = (bf16[4,192,128]{2,1,0:T(8,128)(2,1)S(1)}, bf16[4,192,128]{2,1,0:T(8,128)(2,1)S(1)}, u32[]{:S(2)}, u32[]{:S(2)}) collective-permute-start(bf16[4,192,128]{2,1,0:T(8,128)(2,1)S(1)} %get-tuple-element.98), channel_id=1, source_target_pairs={{0,4},{1,5},{2,6},{3,7},{4,0},{5,1},{6,2},{7,3},{8,12},{9,13},{10,... | collective-permute-start | bytes 589832 | tf_op jit(solution)/shard_map/ppermute | solution.py:55
  79.7 1.5 copy-start.3
  81.3 4.7 %collective-permute-start.8 = (bf16[2,192,128]{2,1,0:T(8,128)(2,1)S(1)}, bf16[2,192,128]{2,1,0:T(8,128)(2,1)S(1)}, u32[]{:S(2)}, u32[]{:S(2)}) collective-permute-start(bf16[2,192,128]{2,1,0:T(8,128)(2,1)S(1)} %get-tuple-element.100), channel_id=1, source_target_pairs={{0,8},{1,9},{2,10},{3,11},{4,12},{5,13},{6,14},{7,15},{8,0},{9,1},... | collective-permute-start | bytes 294920 | tf_op jit(solution)/shard_map/ppermute | solution.py:55
  86.0 6.3 %collective-permute-start.9 = (bf16[1,192,128]{2,1,0:T(8,128)(2,1)S(1)}, bf16[1,192,128]{2,1,0:T(8,128)(2,1)S(1)}, u32[]{:S(2)}, u32[]{:S(2)}) collective-permute-start(bf16[1,192,128]{2,1,0:T(8,128)(2,1)S(1)} %fusion.3), channel_id=1, source_target_pairs={{0,16},{1,17},{2,18},{3,19},{4,20},{5,21},{6,22},{7,23},{8,24},{9,... | collective-permute-start | bytes 147464 | tf_op jit(solution)/shard_map/ppermute | solution.py:55
  92.3 5.1 %collective-permute-start.10 = (bf16[1,192,128]{2,1,0:T(8,128)(2,1)S(1)}, bf16[1,192,128]{2,1,0:T(8,128)(2,1)S(1)}, u32[]{:S(2)}, u32[]{:S(2)}) collective-permute-start(bf16[1,192,128]{2,1,0:T(8,128)(2,1)S(1)} %get-tuple-element.95), channel_id=1, source_target_pairs={{0,16},{1,17},{2,18},{3,19},{4,20},{5,21},{6,22},{7,23},{8,24},{9,... | collective-permute-start | bytes 147464 | tf_op jit(solution)/shard_map/ppermute | solution.py:55
  97.4 4.7 %collective-permute-start.11 = (bf16[2,192,128]{2,1,0:T(8,128)(2,1)S(1)}, bf16[2,192,128]{2,1,0:T(8,128)(2,1)S(1)}, u32[]{:S(2)}, u32[]{:S(2)}) collective-permute-start(bf16[2,192,128]{2,1,0:T(8,128)(2,1)S(1)} %pad_maximum_fusion.5), channel_id=1, source_target_pairs={{0,8},{1,9},{2,10},{3,11},{4,12},{5,13},{6,14},{7,15},{8,0},{9,1},... | collective-permute-start | bytes 294920 | tf_op jit(solution)/shard_map/ppermute | solution.py:55
  102.1 5.7 %collective-permute-start.12 = (bf16[4,192,128]{2,1,0:T(8,128)(2,1)S(1)}, bf16[4,192,128]{2,1,0:T(8,128)(2,1)S(1)}, u32[]{:S(2)}, u32[]{:S(2)}) collective-permute-start(bf16[4,192,128]{2,1,0:T(8,128)(2,1)S(1)} %pad_maximum_fusion.3), channel_id=1, source_target_pairs={{0,4},{1,5},{2,6},{3,7},{4,0},{5,1},{6,2},{7,3},{8,12},{9,13},{10,... | collective-permute-start | bytes 589832 | tf_op jit(solution)/shard_map/ppermute | solution.py:55
  107.8 7.8 %collective-permute-start.13 = (bf16[8,192,128]{2,1,0:T(8,128)(2,1)S(1)}, bf16[8,192,128]{2,1,0:T(8,128)(2,1)S(1)}, u32[]{:S(2)}, u32[]{:S(2)}) collective-permute-start(bf16[8,192,128]{2,1,0:T(8,128)(2,1)S(1)} %pad_maximum_fusion.1), channel_id=1, source_target_pairs={{0,2},{1,3},{2,0},{3,1},{4,6},{5,7},{6,4},{7,5},{8,10},{9,11},{10,... | collective-permute-start | bytes 1179656 | tf_op jit(solution)/shard_map/ppermute | solution.py:55
  115.7 8.2 %collective-permute-start.14 = (bf16[16,192,128]{2,1,0:T(8,128)(2,1)S(1)}, bf16[16,192,128]{2,1,0:T(8,128)(2,1)S(1)}, u32[]{:S(2)}, u32[]{:S(2)}) collective-permute-start(bf16[16,192,128]{2,1,0:T(8,128)(2,1)S(1)} %constant_dynamic-update-slice_fusion.5.chunks.lower), channel_id=1, source_target_pairs={{0,1},{1,0},{2,3},{3,2},{4,5},{5,4},{6,7},{7,6},{8,9},{9,8},{10,11... | collective-permute-start | bytes 2359304 | tf_op jit(solution)/shard_map/ppermute | solution.py:55
  134.1 1.4 collective-permute-start.15
  135.5 3.7 %collective-permute-start.16 = (f32[24,128]{1,0:T(8,128)S(1)}, f32[24,128]{1,0:T(8,128)S(1)}, u32[]{:S(2)}, u32[]{:S(2)}) collective-permute-start(f32[24,128]{1,0:T(8,128)S(1)} %add.51), channel_id=1, source_target_pairs={{0,2},{1,3},{2,0},{3,1},{4,6},{5,7},{6,4},{7,5},{8,10},{9,11},{10,... | collective-permute-start | bytes 36872 | tf_op jit(solution)/shard_map/ppermute | solution.py:55
  139.2 3.7 %collective-permute-start.17 = (f32[24,128]{1,0:T(8,128)S(1)}, f32[24,128]{1,0:T(8,128)S(1)}, u32[]{:S(2)}, u32[]{:S(2)}) collective-permute-start(f32[24,128]{1,0:T(8,128)S(1)} %add.52), channel_id=1, source_target_pairs={{0,4},{1,5},{2,6},{3,7},{4,0},{5,1},{6,2},{7,3},{8,12},{9,13},{10,... | collective-permute-start | bytes 36872 | tf_op jit(solution)/shard_map/ppermute | solution.py:55
  142.9 3.7 %collective-permute-start.18 = (f32[24,128]{1,0:T(8,128)S(1)}, f32[24,128]{1,0:T(8,128)S(1)}, u32[]{:S(2)}, u32[]{:S(2)}) collective-permute-start(f32[24,128]{1,0:T(8,128)S(1)} %add.53), channel_id=1, source_target_pairs={{0,8},{1,9},{2,10},{3,11},{4,12},{5,13},{6,14},{7,15},{8,0},{9,1},... | collective-permute-start | bytes 36872 | tf_op jit(solution)/shard_map/ppermute | solution.py:55
  146.6 4.6 %collective-permute-start.19 = (f32[24,128]{1,0:T(8,128)S(1)}, f32[24,128]{1,0:T(8,128)S(1)}, u32[]{:S(2)}, u32[]{:S(2)}) collective-permute-start(f32[24,128]{1,0:T(8,128)S(1)} %add.54), channel_id=1, source_target_pairs={{0,16},{1,17},{2,18},{3,19},{4,20},{5,21},{6,22},{7,23},{8,24},{9,... | collective-permute-start | bytes 36872 | tf_op jit(solution)/shard_map/ppermute | solution.py:55

commit v4 on v3

--- a/solution.py
+++ b/solution.py
@@ -50,21 +50,41 @@
     return out
 
 
-def exchange(block, bit):
+def exchange(block, flip):
     count = lax.axis_size("fsdp")
-    return lax.ppermute(block, "fsdp", [(one, one ^ (1 << bit)) for one in range(count)])
-
-
-def gather_blocks(block, bits, beside):
-    for bit in reversed(range(bits)):
-        other = exchange(block, bit)
-        if bit in beside:
-            work, done = beside[bit]
-            other, extra = lax.optimization_barrier((other, work(block)))
-            done(extra)
-        if bit:
-            block = jnp.concatenate([block, other], axis=0)
-    return block, other
+    return lax.ppermute(block, "fsdp", [(one, one ^ flip) for one in range(count)])
+
+
+def bit_groups(bits):
+    return [(0, 1)] + [(low, min(2, bits - low)) for low in range(1, bits, 2)]
+
+
+def flips(group):
+    low, size = group
+    return [reverse_bits(part, size) << low for part in range(1, 1 << size)]
+
+
+def gather_blocks(block, groups, beside):
+    for group in reversed(groups):
+        others = [exchange(block, flip) for flip in flips(group)]
+        job = beside(group, block)
+        if job is not None:
+            work, done = job
+            others, made = lax.optimization_barrier((others, work))
+            done(made)
+        if group[0]:
+            block = jnp.concatenate([block] + others, axis=0)
+    return block, others[0]
+
+
+def add_up(values):
+    while len(values) > 1:
+        values = [one + two for one, two in zip(values[0::2], values[1::2])]
+    return values[0]
+
+
+def far(value):
+    return pltpu.with_memory_space_constraint(value, pltpu.HBM)
 
 
 def after(value, earlier):
@@ -240,21 +260,7 @@
     return copy
 
 
-def gram_kernel(first, start, fold, krylov, earlier, out, held, sums, sems):
-    count, basis, lines, _ = held.shape
-    copy = row_copies(krylov, first, held, sems)
-    sums[...] = jnp.zeros_like(sums) if start else earlier[...]
-
-    def body(at, carry):
-        copy(at).wait()
-        stack = stacked(held[at])
-        sums[...] += dot_nt(stack, stack)
-        return carry
-
-    lax.fori_loop(0, count, body, 0)
-    if not fold:
-        out[...] = sums[...]
-        return
+def fold_gram(sums, basis, lines):
     size = basis * lines
     own = lax.broadcasted_iota(jnp.int32, (size, size), 0)
     other = lax.broadcasted_iota(jnp.int32, (size, size), 1)
@@ -262,7 +268,7 @@
         same = (own & (lines - 1)) == (other & (lines - 1))
     else:
         same = lax.rem(own, lines) == lax.rem(other, lines)
-    kept = jnp.where(same, sums[...], 0.0)
+    kept = jnp.where(same, sums, 0.0)
     rows = [
         jnp.sum(kept[one * lines : (one + 1) * lines], axis=0, keepdims=True)
         for one in range(basis)
@@ -270,10 +276,24 @@
     place = lax.broadcasted_iota(jnp.int32, (size, LANES), 0)
     lane = lax.broadcasted_iota(jnp.int32, (size, LANES), 1) * lines
     picks = jnp.where((place >= lane) & (place < lane + lines), 1.0, 0.0).astype(F32)
-    out[...] = jnp.dot(
+    return jnp.dot(
         jnp.concatenate(rows, axis=0), picks,
         precision=lax.Precision.HIGHEST, preferred_element_type=F32,
     )
+
+
+def gram_kernel(first, start, krylov, earlier, out, held, sems):
+    count, _, _, _ = held.shape
+    copy = row_copies(krylov, first, held, sems)
+    out[...] = jnp.zeros_like(out) if start else earlier[...]
+
+    def body(at, carry):
+        copy(at).wait()
+        stack = stacked(held[at])
+        out[...] += dot_nt(stack, stack)
+        return carry
+
+    lax.fori_loop(0, count, body, 0)
 
 
 def product_kernel(krylov, normed, out, square, held, sems):
@@ -290,6 +310,25 @@
         return carry
 
     lax.fori_loop(0, count, body, 0)
+
+
+def both_kernel(first, fold, krylov, normed, earlier, out, gram_out, held, sums, sems):
+    count, basis, lines, _ = held.shape
+    copy = row_copies(krylov, first, held, sems)
+    sums[...] = earlier[...]
+
+    def body(at, carry):
+        copy(at).wait()
+        stack = stacked(held[at])
+        sums[...] += dot_nt(stack, stack)
+        made = dot_nt(stack, normed[...])
+        here = pl.ds(pl.multiple_of(at * lines, lines), lines)
+        for one in range(basis):
+            out[one, here, :] = made[one * lines : (one + 1) * lines]
+        return carry
+
+    lax.fori_loop(0, count, body, 0)
+    gram_out[...] = fold_gram(sums[...], basis, lines) if fold else sums[...]
 
 
 def loss_columns(flip, load, places, splits):
@@ -338,23 +377,18 @@
 
 
 def back_kernel(
-    devices, inv_d, inv_ff, splits,
+    devices, inv_d, inv_ff, splits, spans,
     info, chunks, down, krylov, hidden, weight, act, square, loss_square_half, back_half, grams,
-    sums_half, prod_gate, prod_up,
-    s_out, r_out, stats,
-    loss, held_down, held, half_held, gate_held, up_held, sems, more_sems,
+    sums_half, prod_gate, *rest,
 ):
+    prods_up = rest[: len(spans)]
+    s_out, r_out, stats, held, loss, held_down, sems = rest[len(spans) :]
     count, basis, lines, _ = held.shape
     copies, first = back_copies(info, devices, 1, down, krylov, held_down, held, sems)
-    more = [
-        pltpu.make_async_copy(source, target, more_sems.at[at])
-        for at, (source, target) in enumerate(
-            ((prod_gate, gate_held), (prod_up, up_held), (sums_half, half_held))
-        )
-    ]
-    for copy in [first] + more + copies:
+    for copy in [first] + copies:
         copy.start()
     loss[...] = loss_columns(info[0], lambda at: chunks[at], chunks.shape[0], splits)
+    other = dot_nt(loss[...], loss[...]) + loss_square_half[...]
     first.wait()
     back = dot_nt(held_down[...], loss[...]) + back_half[...]
     s_term = (back * weight[...]).astype(BF16)
@@ -363,19 +397,20 @@
     r_out[...] = r_term
     wide = hidden[...]
     squares = inv_d * inv_d * ((dot_tn(s_term, s_term) + dot_tn(r_term, r_term)) * square[...])
-    other = dot_nt(loss[...], loss[...]) + loss_square_half[...]
     squares = total(squares + inv_ff * inv_ff * (dot_tn(wide, wide) * other))
     stats[basis : 2 * basis, :] = jnp.broadcast_to(squares, (basis, LANES))
     stats[2 * basis : 3 * basis, :] = grams[...]
-    for copy in more:
-        copy.wait()
     wide_s = s_term.astype(F32) * inv_d
     wide_r = r_term.astype(F32) * inv_d
     wide_h = wide.astype(F32) * inv_ff
     values = []
     for one in range(basis):
-        value = wide_s * gate_held[one] + wide_r * up_held[one] + wide_h * half_held[one]
-        values.append(jnp.sum(value, axis=0, keepdims=True))
+        value = wide_s * prod_gate[one] + wide_h * sums_half[one]
+        value = jnp.sum(value, axis=0, keepdims=True)
+        for (start, number), prod in zip(spans, prods_up):
+            part = wide_r[start : start + number] * prod[one]
+            value = value + jnp.sum(part, axis=0, keepdims=True)
+        values.append(value)
     for at in range(count):
         copies[at].wait()
         made = dot_nt(stacked(held[at]), loss[...])
@@ -395,51 +430,47 @@
 
 
 def new_kernel(
-    basis, count, inv_d, inv_ff, splits,
-    info, stats, s_term, r_term, hidden, normed, lower, upper,
-    krylov_gate, krylov_up, krylov_down,
-    new_gate, new_up, new_down, coefficients,
-    loss, wide, held, outs, sems, out_sems,
+    devices, count, inv_d, inv_ff, splits, long, number_up,
+    info, stats, s_term, r_term, hidden, normed, lower, upper, krylov_gate, krylov_down,
+    down_high, *rest,
 ):
-    depth, _, lines, width = held.shape
-    outs_depth = outs.shape[0]
-    rows = s_term.shape[0]
-    number = rows // lines
+    ups = rest[:number_up]
+    new_gate, new_up, new_down, coefficients = rest[number_up : number_up + 4]
+    loss, mixer, held, held_low, outs, sems, out_sems = rest[number_up + 4 :]
+    depth, basis, lines, width = held.shape
+    per = long // lines
+    blocks = s_term.shape[0] // lines
+    halved = width // 2
     size = basis * lines
-    sources = (krylov_gate, krylov_up, krylov_down)
     targets = (new_gate, new_up, new_down)
-
-    def rows_at(at):
-        return pl.ds(pl.multiple_of(at * lines, lines), lines)
-
-    def copy_in(part, at):
-        slot = lax.rem(part * number + at, depth)
+    low_start = half_start(info[0], devices, width, 0)
+    high_start = half_start(info[0], devices, width, 1)
+
+    def copy_in(block, part):
+        here = pl.ds(pl.multiple_of(block * lines, lines), lines)
+        slot = lax.rem(block, depth)
+        if part == 0:
+            source, target = krylov_gate.at[:, here, :], held.at[slot]
+        else:
+            source = krylov_down.at[:, here, pl.ds(low_start, halved)]
+            target = held_low.at[slot]
+        return pltpu.make_async_copy(source, target, sems.at[part // 2, slot])
+
+    def copy_out(block, part):
+        start = pl.multiple_of(block * lines, lines)
+        slot = lax.rem(block, 2)
         return pltpu.make_async_copy(
-            sources[part].at[:, rows_at(at), :], held.at[slot], sems.at[slot]
+            outs.at[slot, part], targets[part].at[pl.ds(start, lines), :], out_sems.at[slot, part]
         )
 
-    def copy_out(part, at):
-        slot = lax.rem(part * number + at, outs_depth)
-        return pltpu.make_async_copy(
-            outs.at[slot], targets[part].at[rows_at(at), :], out_sems.at[slot]
+    for block in range(min(depth, blocks)):
+        for part in (0, 2):
+            copy_in(block, part).start()
+
+    for at, half in enumerate((lower, upper)):
+        loss[:, at * halved : (at + 1) * halved] = loss_columns(
+            info[0], lambda place, half=half: half[place], half.shape[0], splits
         )
-
-    def fetch(turn):
-        for part in range(3):
-            @pl.when((turn >= part * number) & (turn < (part + 1) * number))
-            def _(part=part):
-                copy_in(part, turn - part * number).start()
-
-    for turn in range(min(depth - 1, 3 * number)):
-        copy_in(turn // number, turn % number).start()
-
-    half_places = lower.shape[0]
-
-    def load(place):
-        at = place & (half_places - 1)
-        return jnp.where(place < half_places, lower[at], upper[at])
-
-    loss[...] = loss_columns(info[0], load, 2 * half_places, splits)
     proj = [stats[one, 0] / count for one in range(basis)]
     squares = stats[basis, 0]
     for one in range(basis):
@@ -459,31 +490,78 @@
     for one in range(basis):
         values = jnp.where(lane == one * lines + row, proj[one] * inverse, values)
     terms = [term.astype(F32) for term in split_three(values)]
-    mix = jnp.concatenate(terms, axis=0).astype(BF16)
-
-    for part, (left, right, scale) in enumerate(
-        ((s_term, normed, inv_d), (r_term, normed, inv_d), (hidden, loss, inv_ff))
-    ):
-        wide[...] = dot_nn(left[...], right[...]) * (scale * inverse)
-
-        def body(at, carry, part=part):
-            turn = part * number + at
-            fetch(turn + depth - 1)
-            copy_in(part, at).wait()
-
-            @pl.when(turn >= outs_depth)
-            def _():
-                copy_out(part, at).wait()
-
-            mixed = dot_nn(mix, stacked(held[lax.rem(turn, depth)]))
-            mixed = mixed[:lines] + (mixed[lines : 2 * lines] + mixed[2 * lines :])
-            outs[lax.rem(turn, outs_depth)] = (wide[rows_at(at), :] - mixed).astype(BF16)
-            copy_out(part, at).start()
-            return carry
-
-        lax.fori_loop(0, number, body, 0)
-    for turn in range(max(0, 3 * number - outs_depth), 3 * number):
-        copy_out(turn // number, turn % number).wait()
+    mixer[...] = jnp.concatenate(terms, axis=0).astype(BF16)
+    chunk = min(1024, halved)
+
+    def put(part, step, left, right, scale, first, last, target, read):
+        here = pl.ds(pl.multiple_of(step * long, long), long)
+        for start in range(first, last, chunk):
+            gradient = dot_nn(left[here, :], right[:, start : start + chunk]) * (scale * inverse)
+            for sub in range(per):
+                stack = stacked(read(sub, slice(start - first, start - first + chunk)))
+                mixed = dot_nn(mixer[...], stack)
+                mixed = mixed[:lines] + (mixed[lines : 2 * lines] + mixed[2 * lines :])
+                value = gradient[sub * lines : (sub + 1) * lines] - mixed
+                columns = pl.ds(pl.multiple_of(target + (start - first), chunk), chunk)
+                slot = lax.rem(step * per + sub, 2)
+                outs[slot, part, :, columns] = value.astype(BF16)
+
+    def body(step, carry):
+        for part in range(3):
+            for sub in range(per):
+                block = step * per + sub
+
+                @pl.when(block >= 2)
+                def _(part=part, block=block):
+                    copy_out(block, part).wait()
+
+                if part != 1:
+                    copy_in(block, part).wait()
+            if part == 0:
+                put(
+                    0, step, s_term, normed, inv_d, 0, width, 0,
+                    lambda sub, columns: held[lax.rem(step * per + sub, depth), :, :, columns],
+                )
+            elif part == 1:
+                ahead = 0
+                for up in ups:
+                    steps = up.shape[0] // per
+
+                    @pl.when((step >= ahead) & (step < ahead + steps))
+                    def _(up=up, ahead=ahead):
+                        put(
+                            1, step, r_term, normed, inv_d, 0, width, 0,
+                            lambda sub, columns: up[(step - ahead) * per + sub, :, :, columns],
+                        )
+
+                    ahead += steps
+            else:
+                put(
+                    2, step, hidden, loss, inv_ff, 0, halved, low_start,
+                    lambda sub, columns: held_low[
+                        lax.rem(step * per + sub, depth), :, :, columns
+                    ],
+                )
+                put(
+                    2, step, hidden, loss, inv_ff, halved, width, high_start,
+                    lambda sub, columns: down_high[
+                        step, :, sub * lines : (sub + 1) * lines, columns
+                    ],
+                )
+            for sub in range(per):
+                block = step * per + sub
+                copy_out(block, part).start()
+                if part != 1:
+                    @pl.when(block + depth < blocks)
+                    def _(part=part, block=block):
+                        copy_in(block + depth, part).start()
+
+        return carry
+
+    lax.fori_loop(0, blocks // per, body, 0)
+    for block in range(max(0, blocks - 2), blocks):
+        for part in range(3):
+            copy_out(block, part).wait()
 
 
 def per_device(
@@ -492,6 +570,7 @@
     basis, rows, width = krylov_gate.shape
     devices = lax.axis_size("fsdp")
     bits = devices.bit_length() - 1
+    groups = bit_groups(bits)
     hidden_all = rows * devices
     count = 3.0 * width * hidden_all
     inv_d = 1.0 / math.sqrt(width)
@@ -508,56 +587,65 @@
     halved = width // 2
     product_flops = 2 * rows * width * LIVE
 
-    def gram(krylov, first, number, fold, earlier, before):
-        size = basis * lines
+    size = basis * lines
+
+    def gram(krylov, first, number, earlier, before):
         start = earlier is None
-        if start:
-            earlier = jnp.zeros((8, LANES), F32)
-        krylov = krylov if before is None else after(krylov, before)
-        out = (basis, LANES) if fold else (size, size)
         return pl.pallas_call(
-            functools.partial(gram_kernel, first, start, fold),
+            functools.partial(gram_kernel, first, start),
             in_specs=[FAR, FAST],
             out_specs=FAST,
-            out_shape=jax.ShapeDtypeStruct(out, F32),
+            out_shape=jax.ShapeDtypeStruct((size, size), F32),
             scratch_shapes=[
                 pltpu.VMEM((number, basis, lines, width), BF16),
+                pltpu.SemaphoreType.DMA((number,)),
+            ],
+            compiler_params=params(26),
+            cost_estimate=cost(2 * size * size * width * number, 2 * size * width * number),
+            name="gram",
+        )(far(after(krylov, before)), jnp.zeros((8, LANES), F32) if start else earlier)
+
+    def both(krylov, first, number, fold, earlier, normed, before):
+        return pl.pallas_call(
+            functools.partial(both_kernel, first, fold),
+            in_specs=[FAR, FAST, FAST],
+            out_specs=[FAST] * 3,
+            out_shape=[
+                jax.ShapeDtypeStruct((basis, number * lines, LIVE), F32),
+                jax.ShapeDtypeStruct((basis, LANES) if fold else (size, size), F32),
+                jax.ShapeDtypeStruct((number, basis, lines, width), BF16),
+            ],
+            scratch_shapes=[
                 pltpu.VMEM((size, size), F32),
                 pltpu.SemaphoreType.DMA((number,)),
             ],
-            compiler_params=params(46),
-            cost_estimate=cost(2 * size * size * width * number, 2 * size * width * number),
-            name="gram",
-        )(krylov, earlier)
+            compiler_params=params(8),
+            cost_estimate=cost(
+                2 * size * (size + LIVE) * width * number, 2 * size * width * number
+            ),
+            name="both",
+        )(far(after(krylov, before)), normed, earlier)
 
     cut = (pieces + 1) // 2
-    spans = [
-        (krylov, first, number)
-        for krylov in (krylov_gate, krylov_up, krylov_down)
-        for first, number in ((0, cut), (cut, pieces - cut))
-        if number
+    gram_jobs = [
+        job
+        for job in (
+            (krylov_down, 0, cut), (krylov_gate, 0, pieces), (krylov_down, cut, pieces - cut)
+        )
+        if job[2]
     ]
-    gram_sums = []
-
-    def next_gram(before):
-        krylov, first, number = spans[len(gram_sums)]
-        fold = len(gram_sums) == len(spans) - 1
-        earlier = gram_sums[-1] if gram_sums else None
-        gram_sums.append(gram(krylov, first, number, fold, earlier, before))
-        return gram_sums[-1]
-
-    def done_gram(value):
-        gram_sums[-1] = value
+    gram_sums = [None]
+
+    def next_gram(group, before):
+        if not gram_jobs:
+            return None
+        return gram(*gram_jobs.pop(0), gram_sums[-1], before), gram_sums.append
 
     own_tokens = inputs.shape[0]
     tokens = own_tokens * devices
     if own_tokens % GROUP == 0:
         sub = own_tokens // GROUP
-        lower, upper = gather_blocks(
-            inputs.reshape(sub, GROUP, width),
-            bits,
-            {bit: (next_gram, done_gram) for bit in range(min(bits, len(spans) - 1))},
-        )
+        lower, upper = gather_blocks(inputs.reshape(sub, GROUP, width), groups, next_gram)
 
         def spots(flip, group):
             return (reverse_bits(group // sub, bits) ^ flip) * sub + group % sub
@@ -569,6 +657,10 @@
 
         def spots(flip, group):
             return group
+
+    while gram_jobs:
+        made, done = next_gram(None, inputs)
+        done(made)
 
     normed, hidden, tangent_t, hidden_t, weight, act, send = pl.pallas_call(
         functools.partial(forward_kernel, devices, inv_d, inv_ff, spots, splits),
@@ -590,12 +682,12 @@
             pltpu.SemaphoreType.DMA((rows // long, 4)),
             pltpu.SemaphoreType.DMA((2,)),
         ],
-        compiler_params=params(46),
+        compiler_params=params(24),
         cost_estimate=cost(5 * product_flops, 10 * rows * width + 6 * LIVE * width, rows * LIVE),
         name="forward",
     )(
-        info, lower, upper, norm_gain.reshape(1, width), gate_rows, up_rows, krylov_gate,
-        krylov_up, down_rows, krylov_down,
+        info, lower, upper, norm_gain.reshape(1, width), far(gate_rows), far(up_rows),
+        far(krylov_gate), far(krylov_up), far(down_rows), far(krylov_down),
     )
 
     def product(krylov, before):
@@ -611,14 +703,14 @@
                 pltpu.VMEM((pieces, basis, lines, width), BF16),
                 pltpu.SemaphoreType.DMA((pieces,)),
             ],
-            compiler_params=params(46),
+            compiler_params=params(28),
             cost_estimate=cost(
                 basis * product_flops, 2 * basis * rows * width + 4 * basis * rows * LIVE
             ),
             name="product",
-        )(after(krylov, before), normed)
-
-    got = exchange(send, 0)
+        )(far(after(krylov, before)), normed)
+
+    got = exchange(send, 1)
     keep = pl.pallas_call(
         functools.partial(keep_kernel, devices, inv_ff, splits),
         in_specs=[SMALL, FAST, FAST, FAR, FAR],
@@ -628,23 +720,53 @@
             pltpu.VMEM((2, rows, halved), BF16),
             pltpu.SemaphoreType.DMA((2,)),
         ],
-        compiler_params=params(46),
+        compiler_params=params(8),
         cost_estimate=cost(product_flops, 2 * rows * width + 2 * LIVE * width),
         name="keep",
-    )(info, tangent_t, hidden_t, down_rows, krylov_down)
-
-    plan = {1: krylov_gate, 2: krylov_up}
-    prods = []
-    for bit in range(1, bits):
-        part = keep.shape[0] // 2
-        send = (keep[part:] + got[part:].astype(F32)).astype(BF16)
-        keep = keep[:part] + got[:part].astype(F32)
-        got = exchange(send, bit)
-        if bit in plan:
-            got, made = lax.optimization_barrier((got, product(plan[bit], send)))
-            prods.append(made)
-    (prod_gate, square), (prod_up, _) = prods
-    loss_own = (keep + got.astype(F32)).astype(BF16)
+    )(info, tangent_t, hidden_t, far(down_rows), far(krylov_down))
+
+    per = long // lines
+    part = (pieces // per + 2) // 3 * per
+    shares = [min(part, pieces - first) for first in range(0, pieces, part)]
+    up_jobs = [(sum(shares[:at]), number) for at, number in enumerate(shares)]
+    up_spans = [(first * lines, number * lines) for first, number in up_jobs]
+    prods_up, kept_up = [], []
+
+    def next_both(before):
+        if not up_jobs:
+            return None
+        first, number = up_jobs.pop(0)
+        made = both(
+            krylov_up, first, number, not up_jobs, gram_sums[-1], normed, before
+        )
+
+        def done(made):
+            prods_up.append(made[0])
+            gram_sums.append(made[1])
+            kept_up.append(made[2])
+
+        return made, done
+
+    got = [got]
+    for at, group in enumerate(groups[1:]):
+        parts = flips(group)
+        part = keep.shape[0] // (len(parts) + 1)
+        sends = [
+            add_up([one[turn * part : (turn + 1) * part].astype(F32) for one in [keep] + got])
+            for turn in range(1, len(parts) + 1)
+        ]
+        keep = add_up([one[:part].astype(F32) for one in [keep] + got])
+        sends = [one.astype(BF16) for one in sends]
+        got = [exchange(one, flip) for one, flip in zip(sends, parts)]
+        if at == 0:
+            got, (prod_gate, square) = lax.optimization_barrier(
+                (got, product(krylov_gate, sends[0]))
+            )
+        elif up_jobs:
+            made, done = next_both(sends[0])
+            got, made = lax.optimization_barrier((got, made))
+            done(made)
+    loss_own = add_up([one.astype(F32) for one in [keep] + got]).astype(BF16)
 
     def half_call(lower):
         return pl.pallas_call(
@@ -662,77 +784,75 @@
                 pltpu.VMEM((rows // long, basis, long, halved), BF16),
                 pltpu.SemaphoreType.DMA((rows // long + 1,)),
             ],
-            compiler_params=params(46),
+            compiler_params=params(18),
             cost_estimate=cost(
                 (basis + 1) * product_flops // 2,
                 (basis + 1) * rows * width + 4 * basis * rows * LIVE,
             ),
             name="back_half",
-        )(info, lower, down_rows, krylov_down)
+        )(info, lower, far(down_rows), far(krylov_down))
 
     halves = []
-    beside = {0: (half_call, halves.extend)}
-    if 0 < len(gram_sums) < len(spans):
-        beside[1] = (next_gram, done_gram)
-    lower, upper = gather_blocks(loss_own, bits, beside)
-    while len(gram_sums) < len(spans):
-        next_gram(None)
+
+    def beside(group, block):
+        if group[0] == 0:
+            return half_call(block), halves.extend
+        return next_both(block)
+
+    lower, upper = gather_blocks(loss_own, groups, beside)
     sums_half, back_half, loss_square_half = halves
 
-    s_term, r_term, stats = pl.pallas_call(
-        functools.partial(back_kernel, devices, inv_d, inv_ff, splits),
-        in_specs=[SMALL, FAST, FAR, FAR] + [FAST] * 7 + [pl.BlockSpec(memory_space=pl.ANY)] * 3,
-        out_specs=[FAST] * 3,
+    s_term, r_term, stats, down_high = pl.pallas_call(
+        functools.partial(back_kernel, devices, inv_d, inv_ff, splits, up_spans),
+        in_specs=[SMALL, FAST, FAR, FAR] + [FAST] * (9 + len(prods_up)),
+        out_specs=[FAST] * 4,
         out_shape=[
             jax.ShapeDtypeStruct((rows, LIVE), BF16),
             jax.ShapeDtypeStruct((rows, LIVE), BF16),
             jax.ShapeDtypeStruct((3 * basis, LANES), F32),
+            jax.ShapeDtypeStruct((rows // long, basis, long, halved), BF16),
         ],
         scratch_shapes=[
             pltpu.VMEM((LIVE, halved), BF16),
             pltpu.VMEM((rows, halved), BF16),
-            pltpu.VMEM((rows // long, basis, long, halved), BF16),
-            pltpu.VMEM((basis, rows, LIVE), F32),
-            pltpu.VMEM((basis, rows, LIVE), F32),
-            pltpu.VMEM((basis, rows, LIVE), F32),
             pltpu.SemaphoreType.DMA((rows // long + 1,)),
-            pltpu.SemaphoreType.DMA((3,)),
         ],
-        compiler_params=params(46),
+        compiler_params=params(8),
         cost_estimate=cost(
             (basis + 1) * product_flops // 2,
             (basis + 1) * rows * width + 12 * basis * rows * LIVE,
         ),
         name="back",
     )(
-        info, upper, down_rows, krylov_down, hidden, weight, act, square, loss_square_half,
-        back_half, gram_sums[-1], sums_half, prod_gate, prod_up,
-    )
-
-    for bit in range(bits):
-        stats = stats + exchange(stats, bit)
-
-    depth, outs_depth = min(8, 3 * pieces), min(4, 3 * pieces)
+        info, upper, far(down_rows), far(krylov_down), hidden, weight, act, square,
+        loss_square_half, back_half, gram_sums[-1], sums_half, prod_gate, *prods_up,
+    )
+
+    for group in groups:
+        stats = add_up([stats] + [exchange(stats, flip) for flip in flips(group)])
+
+    depth = min(3, pieces)
     out_shape = jax.ShapeDtypeStruct((rows, width), BF16)
     new_gate, new_up, new_down, coefficients = pl.pallas_call(
-        functools.partial(new_kernel, basis, count, inv_d, inv_ff, splits),
-        in_specs=[SMALL, SMALL] + [FAST] * 6 + [FAR] * 3,
+        functools.partial(new_kernel, devices, count, inv_d, inv_ff, splits, long, len(kept_up)),
+        in_specs=[SMALL, SMALL] + [FAST] * 6 + [FAR] * 2 + [FAST] * (1 + len(kept_up)),
         out_specs=[FAR] * 3 + [SMALL],
         out_shape=[out_shape, out_shape, out_shape, jax.ShapeDtypeStruct((basis + 1,), F32)],
         scratch_shapes=[
             pltpu.VMEM((LIVE, width), BF16),
-            pltpu.VMEM((rows, width), F32),
+            pltpu.VMEM((3 * lines, size), BF16),
             pltpu.VMEM((depth, basis, lines, width), BF16),
-            pltpu.VMEM((outs_depth, lines, width), BF16),
-            pltpu.SemaphoreType.DMA((depth,)),
-            pltpu.SemaphoreType.DMA((outs_depth,)),
+            pltpu.VMEM((depth, basis, lines, halved), BF16),
+            pltpu.VMEM((2, 3, lines, width), BF16),
+            pltpu.SemaphoreType.DMA((2, depth)),
+            pltpu.SemaphoreType.DMA((2, 3)),
         ],
-        compiler_params=params(46),
+        compiler_params=params(20),
         cost_estimate=cost(3 * product_flops, 6 * (basis + 1) * rows * width),
         name="new",
     )(
-        info, stats, s_term, r_term, hidden, normed, lower, upper, krylov_gate, krylov_up,
-        krylov_down,
+        info, stats, s_term, r_term, hidden, normed, lower, upper, far(krylov_gate),
+        far(krylov_down), down_high, *kept_up,
     )
     return (new_gate, new_up, new_down, coefficients)
 

time: 177 us -> 148 us (0.84)
  waiting for transfers between devices: 47 us -> 10 us
  starting transfers between devices: 17.9 us -> 34.1 us
  Pallas kernels: 108 us -> 100 us
    ppermute x20 -> x28, waiting for transfers between devices: 47 us -> 10 us  [exchange(): lax.ppermute(block, 'fsdp', [(one, one ^ flip) for one in range(count)])]
    ppermute x20 -> x28, starting transfers between devices: 17.9 us -> 34.1 us  [exchange(): lax.ppermute(block, 'fsdp', [(one, one ^ flip) for one in range(count)])]
    pallas_call x2 -> x1, Pallas kernels: 18.1 us -> 8.94 us  [product(): pl.pallas_call(product_kernel, in_specs=[FAR, FAST], out_specs=[FAST, FAS...]
  transfers between devices with their start and end apart: 20 -> 28, of which waited for: 14 -> 9; matrix products, arithmetic and copies ran while one was open for 1% -> 1% of each run, Pallas kernels for 35% -> 40%
where the time goes in v4:
time: 148 us; the launch traced here: 147 us
  Pallas kernels  100 us (68%)
  starting transfers between devices  34.1 us (23%)
  waiting for transfers between devices  10 us (7%)
    ppermute x28, starting transfers between devices, exchange(): lax.ppermute(block, 'fsdp', [(one, one ^ flip) for one in range(count)])  34.1 us
    pallas_call x1, Pallas kernels, per_device(): pl.pallas_call(functools.partial(new_kernel, devices, count, inv_d, inv_f...  21.4 us
    pallas_call x3, Pallas kernels, gram(): pl.pallas_call(functools.partial(gram_kernel, first, start), in_specs=[FA...  19.8 us
    pallas_call x3, Pallas kernels, both(): pl.pallas_call(functools.partial(both_kernel, first, fold), in_specs=[FAR...  17.9 us
    pallas_call x1, Pallas kernels, per_device(): pl.pallas_call(functools.partial(forward_kernel, devices, inv_d, inv_ff,...  10.6 us
    ppermute x28, waiting for transfers between devices, exchange(): lax.ppermute(block, 'fsdp', [(one, one ^ flip) for one in range(count)])  10 us
    pallas_call x1, Pallas kernels, per_device(): pl.pallas_call(functools.partial(back_kernel, devices, inv_d, inv_ff, spl...  9.77 us
    pallas_call x1, Pallas kernels, product(): pl.pallas_call(product_kernel, in_specs=[FAR, FAST], out_specs=[FAST, FAS...  8.94 us
  transfers between devices with their start and end apart: 28, of which 9 were waited for; matrix products, arithmetic and copies ran while one was open for 1% of the time, Pallas kernels for 40%

profile of v4, /device:TPU:0, one launch (start us, length us, event | category | flops | bytes accessed | tf_op | source)
XLA Modules:
  0.0 147.3 jit_solution(9906967173068202430)
XLA Ops:
  0.6 5.1 %collective-permute-start.2 = (bf16[1,8,4096]{2,1,0:T(8,128)(2,1)}, bf16[1,8,4096]{2,1,0:T(8,128)(2,1)S(1)}, u32[]{:S(2)}, u32[]{:S(2)}) collective-permute-start(bf16[1,8,4096]{2,1,0:T(8,128)(2,1)} %bitcast.4), channel_id=1, source_target_pairs={{0,24},{1,25},{2,26},{3,27},{4,28},{5,29},{6,30},{7,31},{8,16},{9,... | collective-permute-start | bytes 196616 | tf_op jit(solution)/shard_map/ppermute | solution.py:55
  5.7 0.6 collective-permute-start
  6.4 0.9 constant_dynamic-update-slice_fusion.6
  7.3 5.4 %gram.3.earlier = f32[256,256]{1,0:T(8,128)S(1)} custom-call(bf16[8,320,4096]{2,1,0:T(8,128)(2,1)} %krylov_down.5, f32[8,128]{1,0:T(8,128)S(1)} %broadcast_in_dim.3.earlier), custom_call_target="tpu_custom_call" | custom-call | flops 2684354560 | bytes 10485760 | tf_op jit(solution)/shard_map/gram/pallas_call | solution.py:594
  12.8 2.7 %collective-permute-start.5 = (bf16[4,8,4096]{2,1,0:T(8,128)(2,1)S(1)}, bf16[4,8,4096]{2,1,0:T(8,128)(2,1)S(1)}, u32[]{:S(2)}, u32[]{:S(2)}) collective-permute-start(bf16[4,8,4096]{2,1,0:T(8,128)(2,1)S(1)} %pad_maximum_fusion), channel_id=1, source_target_pairs={{0,6},{1,7},{2,4},{3,5},{4,2},{5,3},{6,0},{7,1},{8,14},{9,15},{10,... | collective-permute-start | bytes 786440 | tf_op jit(solution)/shard_map/ppermute | solution.py:55
  15.4 0.5 collective-permute-start.4
  16.0 0.4 collective-permute-start.3
  16.4 9.1 %gram.4.earlier = f32[256,256]{1,0:T(8,128)S(1)} custom-call(bf16[8,320,4096]{2,1,0:T(8,128)(2,1)} %krylov_gate.3, f32[256,256]{1,0:T(8,128)S(1)} %gram.3.earlier), custom_call_target="tpu_custom_call" | custom-call | flops 5368709120 | bytes 20971520 | tf_op jit(solution)/shard_map/gram/pallas_call | solution.py:594
  25.5 1.4 collective-permute-done.4
  27.2 0.1 pad_add_fusion.info
  27.3 5.3 %gram.5.earlier = f32[256,256]{1,0:T(8,128)S(1)} custom-call(bf16[8,320,4096]{2,1,0:T(8,128)(2,1)} %krylov_down.5, f32[256,256]{1,0:T(8,128)S(1)} %gram.4.earlier), custom_call_target="tpu_custom_call" | custom-call | flops 2684354560 | bytes 10485760 | tf_op jit(solution)/shard_map/gram/pallas_call | solution.py:594
  32.6 10.6 %forward.1 = (bf16[192,4096]{1,0:T(8,128)(2,1)S(1)}, bf16[320,192]{1,0:T(8,128)(2,1)S(1)}, bf16[192,320]{1,0:T(8,128)(2,1)S(1)}, bf16[192,320]{1,0:T(8,128)(2,1)...) custom-call(s32[2]{0:T(128)S(1)} %pad_add_fusion.info, ...), custom_call_target="tpu_custom_call" | custom-call | flops 2516582400 | bytes 17825792 | tf_op jit(solution)/shard_map/forward/pallas_call | solution.py:665
  43.2 0.5 collective-permute-start.7
  43.8 3.3 %keep.1 = f32[16,192,128]{2,1,0:T(8,128)S(1)} custom-call(s32[2]{0:T(128)S(1)} %pad_add_fusion.info, bf16[192,320]{1,0:T(8,128)(2,1)S(1)} %get-tuple-element.85.tangent_t, bf16[192,320]{1,0:T(8,128)(2,1)S(1)} %get-tuple-element.86.hidden_t, bf16[320,4096]{1,0:T(8,128)(2,1)} %down.7, bf16[8,320,4096]{2,1,0:T(8,128)(2,1)} %krylov_down.5), custom_call_target="tpu_custom_call" | custom-call | flops 503316480 | bytes 4194304 | tf_op jit(solution)/shard_map/keep/pallas_call | solution.py:714
  47.1 0.2 fusion
  47.3 1.5 %collective-permute-start.8 = (bf16[4,192,128]{2,1,0:T(8,128)(2,1)S(1)}, bf16[4,192,128]{2,1,0:T(8,128)(2,1)S(1)}, u32[]{:S(2)}, u32[]{:S(2)}) collective-permute-start(bf16[4,192,128]{2,1,0:T(8,128)(2,1)S(1)} %get-tuple-element.146), channel_id=1, source_target_pairs={{0,4},{1,5},{2,6},{3,7},{4,0},{5,1},{6,2},{7,3},{8,12},{9,13},{10,... | collective-permute-start | bytes 589832 | tf_op jit(solution)/shard_map/ppermute | solution.py:55
  48.8 1.5 %collective-permute-start.10 = (bf16[4,192,128]{2,1,0:T(8,128)(2,1)S(1)}, bf16[4,192,128]{2,1,0:T(8,128)(2,1)S(1)}, u32[]{:S(2)}, u32[]{:S(2)}) collective-permute-start(bf16[4,192,128]{2,1,0:T(8,128)(2,1)S(1)} %get-tuple-element.144), channel_id=1, source_target_pairs={{0,6},{1,7},{2,4},{3,5},{4,2},{5,3},{6,0},{7,1},{8,14},{9,15},{10,... | collective-permute-start | bytes 589832 | tf_op jit(solution)/shard_map/ppermute | solution.py:55
  50.4 0.5 collective-permute-start.9
  50.9 8.9 %product.1 = (f32[8,320,192]{2,1,0:T(8,128)S(1)}, f32[192,192]{1,0:T(8,128)S(1)}) custom-call(bf16[8,320,4096]{2,1,0:T(8,128)(2,1)} %krylov_gate.3, bf16[192,4096]{1,0:T(8,128)(2,1)S(1)} %get-tuple-element.89.normed), custom_call_target="tpu_custom_call" | custom-call | flops 4026531840 | bytes 22937600 | tf_op jit(solution)/shard_map/product/pallas_call | solution.py:694
  60.0 2.4 %collective-permute-start.11 = (bf16[1,192,128]{2,1,0:T(8,128)(2,1)S(1)}, bf16[1,192,128]{2,1,0:T(8,128)(2,1)S(1)}, u32[]{:S(2)}, u32[]{:S(2)}) collective-permute-start(bf16[1,192,128]{2,1,0:T(8,128)(2,1)S(1)} %get-tuple-element.150), channel_id=1, source_target_pairs={{0,16},{1,17},{2,18},{3,19},{4,20},{5,21},{6,22},{7,23},{8,24},{9,... | collective-permute-start | bytes 147464 | tf_op jit(solution)/shard_map/ppermute | solution.py:55
  62.3 1.5 %collective-permute-start.13 = (bf16[1,192,128]{2,1,0:T(8,128)(2,1)S(1)}, bf16[1,192,128]{2,1,0:T(8,128)(2,1)S(1)}, u32[]{:S(2)}, u32[]{:S(2)}) collective-permute-start(bf16[1,192,128]{2,1,0:T(8,128)(2,1)S(1)} %get-tuple-element.148), channel_id=1, source_target_pairs={{0,24},{1,25},{2,26},{3,27},{4,28},{5,29},{6,30},{7,31},{8,16},{9,... | collective-permute-start | bytes 147464 | tf_op jit(solution)/shard_map/ppermute | solution.py:55
  63.8 0.2 collective-permute-start.12
  64.1 6.7 %both.3 = (f32[8,128,192]{2,1,0:T(8,128)S(1)}, f32[256,256]{1,0:T(8,128)S(1)}, bf16[4,8,32,4096]{3,2,1,0:T(8,128)(2,1)S(1)}) custom-call(bf16[8,320,4096]{2,1,0:T(8,128)(2,1)} %krylov.8, bf16[192,4096]{1,0:T(8,128)(2,1)S(1)} %get-tuple-element.89.normed, f32[256,256]{1,0:T(8,128)S(1)} %gram.5.earlier), custom_call_target="tpu_custom_call" | custom-call | flops 3758096384 | bytes 8388608 | tf_op jit(solution)/shard_map/both/pallas_call | solution.py:609
  70.9 3.0 %collective-permute-start.16 = (bf16[1,192,128]{2,1,0:T(8,128)(2,1)S(1)}, bf16[1,192,128]{2,1,0:T(8,128)(2,1)S(1)}, u32[]{:S(2)}, u32[]{:S(2)}) collective-permute-start(bf16[1,192,128]{2,1,0:T(8,128)(2,1)S(1)} %get-tuple-element.143), channel_id=1, source_target_pairs={{0,24},{1,25},{2,26},{3,27},{4,28},{5,29},{6,30},{7,31},{8,16},{9,... | collective-permute-start | bytes 147464 | tf_op jit(solution)/shard_map/ppermute | solution.py:55
  73.9 0.3 collective-permute-start.15
  74.2 1.2 collective-permute-start.14
  75.3 6.7 %both.4 = (f32[8,128,192]{2,1,0:T(8,128)S(1)}, f32[256,256]{1,0:T(8,128)S(1)}, bf16[4,8,32,4096]{3,2,1,0:T(8,128)(2,1)S(1)}) custom-call(bf16[8,320,4096]{2,1,0:T(8,128)(2,1)} %krylov.8, bf16[192,4096]{1,0:T(8,128)(2,1)S(1)} %get-tuple-element.89.normed, f32[256,256]{1,0:T(8,128)S(1)} %get-tuple-element.104.earlier), custom_call_target="tpu_custom_call" | custom-call | flops 3758096384 | bytes 8388608 | tf_op jit(solution)/shard_map/both/pallas_call | solution.py:609
  82.1 2.4 %collective-permute-start.19 = (bf16[4,192,128]{2,1,0:T(8,128)(2,1)S(1)}, bf16[4,192,128]{2,1,0:T(8,128)(2,1)S(1)}, u32[]{:S(2)}, u32[]{:S(2)}) collective-permute-start(bf16[4,192,128]{2,1,0:T(8,128)(2,1)S(1)} %pad_maximum_fusion.1), channel_id=1, source_target_pairs={{0,6},{1,7},{2,4},{3,5},{4,2},{5,3},{6,0},{7,1},{8,14},{9,15},{10,... | collective-permute-start | bytes 589832 | tf_op jit(solution)/shard_map/ppermute | solution.py:55
  84.6 0.5 collective-permute-start.18
  85.1 0.6 collective-permute-start.17
  85.7 4.4 %both.5 = (f32[8,64,192]{2,1,0:T(8,128)S(1)}, f32[8,128]{1,0:T(8,128)S(1)}, bf16[2,8,32,4096]{3,2,1,0:T(8,128)(2,1)S(1)}) custom-call(bf16[8,320,4096]{2,1,0:T(8,128)(2,1)} %krylov.8, bf16[192,4096]{1,0:T(8,128)(2,1)S(1)} %get-tuple-element.89.normed, f32[256,256]{1,0:T(8,128)S(1)} %get-tuple-element.112.earlier), custom_call_target="tpu_custom_call" | custom-call | flops 1879048192 | bytes 4194304 | tf_op jit(solution)/shard_map/both/pallas_call | solution.py:609
  90.2 1.8 %collective-permute-done.18 = bf16[4,192,128]{2,1,0:T(8,128)(2,1)S(1)} collective-permute-done((bf16[4,192,128]{2,1,0:T(8,128)(2,1)S(1)}, bf16[4,192,128]{2,1,0:T(8,128)(2,1)S(1)}, u32[]{:S(2)}, u32[]{:S(2)}) %collective-permute-start.18) | collective-permute-done | bytes 196640 | tf_op jit(solution)/shard_map/ppermute | solution.py:55
  92.1 8.6 %back_half.1 = (f32[8,320,192]{2,1,0:T(8,128)S(1)}, f32[320,192]{1,0:T(8,128)S(1)}, f32[192,192]{1,0:T(8,128)S(1)}) custom-call(s32[2]{0:T(128)S(1)} %pad_add_fusion.info, bf16[16,192,128]{2,1,0:T(8,128)(2,1)S(1)} %constant_dynamic-update-slice_fusion.7.chunks.lower, bf16[320,4096]{1,0:T(8,128)(2,1)} %down.7, bf16[8,320,4096]{2,1,0:T(8,128)(2,1)} %krylov_down.5), custom_call_target="tpu_custom_call" | custom-call | flops 2264924160 | bytes 13762560 | tf_op jit(solution)/shard_map/back_half/pallas_call | solution.py:772
  100.7 9.8 %back.1 = (bf16[320,192]{1,0:T(8,128)(2,1)S(1)}, bf16[320,192]{1,0:T(8,128)(2,1)S(1)}, f32[24,128]{1,0:T(8,128)S(1)}, bf16[5,8,64,2048]{3,2,1,0:T(8,128)(2,1)S(1)}) custom-call(s32[2]{0:T(128)S(1)} %pad_add_fusion.info, bf16[16,192,128]{2,1,0:T(8,128)(2,1)S(1)} %collective-permute-done.20.chunks.upper, bf16[320,4096]{1,0:T(8,128)(2,1)} %down.7, ...), custom_call_target="tpu_custom_call" | custom-call | flops 2264924160 | bytes 17694720 | tf_op jit(solution)/shard_map/back/pallas_call | solution.py:805
  110.5 0.6 collective-permute-start.21
  111.1 0.8 collective-permute-done.21
  111.9 2.4 %collective-permute-start.24 = (f32[24,128]{1,0:T(8,128)S(1)}, f32[24,128]{1,0:T(8,128)S(1)}, u32[]{:S(2)}, u32[]{:S(2)}) collective-permute-start(f32[24,128]{1,0:T(8,128)S(1)} %add.97), channel_id=1, source_target_pairs={{0,6},{1,7},{2,4},{3,5},{4,2},{5,3},{6,0},{7,1},{8,14},{9,15},{10,... | collective-permute-start | bytes 36872 | tf_op jit(solution)/shard_map/ppermute | solution.py:55
  114.2 0.5 collective-permute-start.23
  114.8 0.6 collective-permute-start.22
  115.4 1.1 collective-permute-done.24
  116.5 1.5 collective-permute-done.23
  117.9 0.5 collective-permute-done.22
  118.5 2.6 %collective-permute-start.27 = (f32[24,128]{1,0:T(8,128)S(1)}, f32[24,128]{1,0:T(8,128)S(1)}, u32[]{:S(2)}, u32[]{:S(2)}) collective-permute-start(f32[24,128]{1,0:T(8,128)S(1)} %add_add_fusion.1), channel_id=1, source_target_pairs={{0,24},{1,25},{2,26},{3,27},{4,28},{5,29},{6,30},{7,31},{8,16},{9,... | collective-permute-start | bytes 36872 | tf_op jit(solution)/shard_map/ppermute | solution.py:55
  121.1 1.7 %collective-permute-start.25 = (f32[24,128]{1,0:T(8,128)S(1)}, f32[24,128]{1,0:T(8,128)S(1)}, u32[]{:S(2)}, u32[]{:S(2)}) collective-permute-start(f32[24,128]{1,0:T(8,128)S(1)} %add_add_fusion.1), channel_id=1, source_target_pairs={{0,16},{1,17},{2,18},{3,19},{4,20},{5,21},{6,22},{7,23},{8,24},{9,... | collective-permute-start | bytes 36872 | tf_op jit(solution)/shard_map/ppermute | solution.py:55
  122.9 1.1 collective-permute-done.27
  124.0 0.8 collective-permute-done.26
  124.8 0.9 collective-permute-done.25
  125.7 21.4 %new.1 = (bf16[320,4096]{1,0:T(8,128)(2,1)}, bf16[320,4096]{1,0:T(8,128)(2,1)}, bf16[320,4096]{1,0:T(8,128)(2,1)}, f32[9]{0:T(128)}) custom-call(s32[2]{0:T(128)S(1)} %pad_add_fusion.info, f32[24,128]{1,0:T(8,128)S(1)} %add_add_fusion.stats, bf16[320,192]{1,0:T(8,128)(2,1)S(1)} %get-tuple-element.136.s_term, bf16[320,192]{1,0:T(8,128)(2,1)S(1)} %get-tuple-element.137.r_term, ...), custom_call_target="tpu_custom_call" | custom-call | flops 1509949440 | bytes 70778880 | tf_op jit(solution)/shard_map/new/pallas_call | solution.py:836
  (50 shorter events, 0.6 us)
Async XLA Ops:
  0.6 12.0 %collective-permute-start.2 = (bf16[1,8,4096]{2,1,0:T(8,128)(2,1)}, bf16[1,8,4096]{2,1,0:T(8,128)(2,1)S(1)}, u32[]{:S(2)}, u32[]{:S(2)}) collective-permute-start(bf16[1,8,4096]{2,1,0:T(8,128)(2,1)} %bitcast.4), channel_id=1, source_target_pairs={{0,24},{1,25},{2,26},{3,27},{4,28},{5,29},{6,30},{7,31},{8,16},{9,... | collective-permute-start | bytes 196616 | tf_op jit(solution)/shard_map/ppermute | solution.py:55
  5.7 6.9 %collective-permute-start.1 = (bf16[1,8,4096]{2,1,0:T(8,128)(2,1)}, bf16[1,8,4096]{2,1,0:T(8,128)(2,1)S(1)}, u32[]{:S(2)}, u32[]{:S(2)}) collective-permute-start(bf16[1,8,4096]{2,1,0:T(8,128)(2,1)} %bitcast.5), channel_id=1, source_target_pairs={{0,8},{1,9},{2,10},{3,11},{4,12},{5,13},{6,14},{7,15},{8,0},{9,1},... | collective-permute-start | bytes 196616 | tf_op jit(solution)/shard_map/ppermute | solution.py:55
  5.7 6.9 %collective-permute-start = (bf16[1,8,4096]{2,1,0:T(8,128)(2,1)}, bf16[1,8,4096]{2,1,0:T(8,128)(2,1)S(1)}, u32[]{:S(2)}, u32[]{:S(2)}) collective-permute-start(bf16[1,8,4096]{2,1,0:T(8,128)(2,1)} %bitcast.6), channel_id=1, source_target_pairs={{0,16},{1,17},{2,18},{3,19},{4,20},{5,21},{6,22},{7,23},{8,24},{9,... | collective-permute-start | bytes 196616 | tf_op jit(solution)/shard_map/ppermute | solution.py:55
  7.3 5.4 %copy-start = (bf16[8,4096]{1,0:T(8,128)(2,1)S(1)}, bf16[8,4096]{1,0:T(8,128)(2,1)}, u32[]{:S(2)}) copy-start(bf16[8,4096]{1,0:T(8,128)(2,1)} %param.9) | copy-start | bytes 196612
  12.8 12.7 %collective-permute-start.5 = (bf16[4,8,4096]{2,1,0:T(8,128)(2,1)S(1)}, bf16[4,8,4096]{2,1,0:T(8,128)(2,1)S(1)}, u32[]{:S(2)}, u32[]{:S(2)}) collective-permute-start(bf16[4,8,4096]{2,1,0:T(8,128)(2,1)S(1)} %pad_maximum_fusion), channel_id=1, source_target_pairs={{0,6},{1,7},{2,4},{3,5},{4,2},{5,3},{6,0},{7,1},{8,14},{9,15},{10,... | collective-permute-start | bytes 786440 | tf_op jit(solution)/shard_map/ppermute | solution.py:55
  15.4 11.5 %collective-permute-start.4 = (bf16[4,8,4096]{2,1,0:T(8,128)(2,1)S(1)}, bf16[4,8,4096]{2,1,0:T(8,128)(2,1)S(1)}, u32[]{:S(2)}, u32[]{:S(2)}) collective-permute-start(bf16[4,8,4096]{2,1,0:T(8,128)(2,1)S(1)} %pad_maximum_fusion), channel_id=1, source_target_pairs={{0,2},{1,3},{2,0},{3,1},{4,6},{5,7},{6,4},{7,5},{8,10},{9,11},{10,... | collective-permute-start | bytes 786440 | tf_op jit(solution)/shard_map/ppermute | solution.py:55
  16.0 11.0 %collective-permute-start.3 = (bf16[4,8,4096]{2,1,0:T(8,128)(2,1)S(1)}, bf16[4,8,4096]{2,1,0:T(8,128)(2,1)S(1)}, u32[]{:S(2)}, u32[]{:S(2)}) collective-permute-start(bf16[4,8,4096]{2,1,0:T(8,128)(2,1)S(1)} %pad_maximum_fusion), channel_id=1, source_target_pairs={{0,4},{1,5},{2,6},{3,7},{4,0},{5,1},{6,2},{7,3},{8,12},{9,13},{10,... | collective-permute-start | bytes 786440 | tf_op jit(solution)/shard_map/ppermute | solution.py:55
  16.3 10.8 %copy-start.1 = (bf16[4096]{0:T(1024)(128)(2,1)S(1)}, bf16[4096]{0:T(1024)(128)(2,1)}, u32[]{:S(2)}) copy-start(bf16[4096]{0:T(1024)(128)(2,1)} %param.10) | copy-start | bytes 24580
  16.3 10.8 %copy-start.2 = (s32[2]{0:T(128)S(1)}, s32[2]{0:T(128)}, u32[]{:S(2)}) copy-start(s32[2]{0:T(128)} %param.11) | copy-start | bytes 28
  27.0 5.6 %collective-permute-start.6 = (bf16[16,8,4096]{2,1,0:T(8,128)(2,1)S(1)}, bf16[16,8,4096]{2,1,0:T(8,128)(2,1)S(1)}, u32[]{:S(2)}, u32[]{:S(2)}) collective-permute-start(bf16[16,8,4096]{2,1,0:T(8,128)(2,1)S(1)} %constant_dynamic-update-slice_fusion.lower), channel_id=1, source_target_pairs={{0,1},{1,0},{2,3},{3,2},{4,5},{5,4},{6,7},{7,6},{8,9},{9,8},{10,11... | collective-permute-start | bytes 3145736 | tf_op jit(solution)/shard_map/ppermute | solution.py:55
  43.2 3.9 %collective-permute-start.7 = (bf16[16,192,128]{2,1,0:T(8,128)(2,1)S(1)}, bf16[16,192,128]{2,1,0:T(8,128)(2,1)S(1)}, u32[]{:S(2)}, u32[]{:S(2)}) collective-permute-start(bf16[16,192,128]{2,1,0:T(8,128)(2,1)S(1)} %get-tuple-element.87), channel_id=1, source_target_pairs={{0,1},{1,0},{2,3},{3,2},{4,5},{5,4},{6,7},{7,6},{8,9},{9,8},{10,11... | collective-permute-start | bytes 2359304 | tf_op jit(solution)/shard_map/ppermute | solution.py:55
  47.3 12.5 %collective-permute-start.8 = (bf16[4,192,128]{2,1,0:T(8,128)(2,1)S(1)}, bf16[4,192,128]{2,1,0:T(8,128)(2,1)S(1)}, u32[]{:S(2)}, u32[]{:S(2)}) collective-permute-start(bf16[4,192,128]{2,1,0:T(8,128)(2,1)S(1)} %get-tuple-element.146), channel_id=1, source_target_pairs={{0,4},{1,5},{2,6},{3,7},{4,0},{5,1},{6,2},{7,3},{8,12},{9,13},{10,... | collective-permute-start | bytes 589832 | tf_op jit(solution)/shard_map/ppermute | solution.py:55
  48.8 11.0 %collective-permute-start.10 = (bf16[4,192,128]{2,1,0:T(8,128)(2,1)S(1)}, bf16[4,192,128]{2,1,0:T(8,128)(2,1)S(1)}, u32[]{:S(2)}, u32[]{:S(2)}) collective-permute-start(bf16[4,192,128]{2,1,0:T(8,128)(2,1)S(1)} %get-tuple-element.144), channel_id=1, source_target_pairs={{0,6},{1,7},{2,4},{3,5},{4,2},{5,3},{6,0},{7,1},{8,14},{9,15},{10,... | collective-permute-start | bytes 589832 | tf_op jit(solution)/shard_map/ppermute | solution.py:55
  50.4 9.5 %collective-permute-start.9 = (bf16[4,192,128]{2,1,0:T(8,128)(2,1)S(1)}, bf16[4,192,128]{2,1,0:T(8,128)(2,1)S(1)}, u32[]{:S(2)}, u32[]{:S(2)}) collective-permute-start(bf16[4,192,128]{2,1,0:T(8,128)(2,1)S(1)} %get-tuple-element.145), channel_id=1, source_target_pairs={{0,2},{1,3},{2,0},{3,1},{4,6},{5,7},{6,4},{7,5},{8,10},{9,11},{10,... | collective-permute-start | bytes 589832 | tf_op jit(solution)/shard_map/ppermute | solution.py:55
  60.0 10.9 %collective-permute-start.11 = (bf16[1,192,128]{2,1,0:T(8,128)(2,1)S(1)}, bf16[1,192,128]{2,1,0:T(8,128)(2,1)S(1)}, u32[]{:S(2)}, u32[]{:S(2)}) collective-permute-start(bf16[1,192,128]{2,1,0:T(8,128)(2,1)S(1)} %get-tuple-element.150), channel_id=1, source_target_pairs={{0,16},{1,17},{2,18},{3,19},{4,20},{5,21},{6,22},{7,23},{8,24},{9,... | collective-permute-start | bytes 147464 | tf_op jit(solution)/shard_map/ppermute | solution.py:55
  62.3 8.5 %collective-permute-start.13 = (bf16[1,192,128]{2,1,0:T(8,128)(2,1)S(1)}, bf16[1,192,128]{2,1,0:T(8,128)(2,1)S(1)}, u32[]{:S(2)}, u32[]{:S(2)}) collective-permute-start(bf16[1,192,128]{2,1,0:T(8,128)(2,1)S(1)} %get-tuple-element.148), channel_id=1, source_target_pairs={{0,24},{1,25},{2,26},{3,27},{4,28},{5,29},{6,30},{7,31},{8,16},{9,... | collective-permute-start | bytes 147464 | tf_op jit(solution)/shard_map/ppermute | solution.py:55
  63.8 7.0 %collective-permute-start.12 = (bf16[1,192,128]{2,1,0:T(8,128)(2,1)S(1)}, bf16[1,192,128]{2,1,0:T(8,128)(2,1)S(1)}, u32[]{:S(2)}, u32[]{:S(2)}) collective-permute-start(bf16[1,192,128]{2,1,0:T(8,128)(2,1)S(1)} %get-tuple-element.149), channel_id=1, source_target_pairs={{0,8},{1,9},{2,10},{3,11},{4,12},{5,13},{6,14},{7,15},{8,0},{9,1},... | collective-permute-start | bytes 147464 | tf_op jit(solution)/shard_map/ppermute | solution.py:55
  70.9 11.2 %collective-permute-start.16 = (bf16[1,192,128]{2,1,0:T(8,128)(2,1)S(1)}, bf16[1,192,128]{2,1,0:T(8,128)(2,1)S(1)}, u32[]{:S(2)}, u32[]{:S(2)}) collective-permute-start(bf16[1,192,128]{2,1,0:T(8,128)(2,1)S(1)} %get-tuple-element.143), channel_id=1, source_target_pairs={{0,24},{1,25},{2,26},{3,27},{4,28},{5,29},{6,30},{7,31},{8,16},{9,... | collective-permute-start | bytes 147464 | tf_op jit(solution)/shard_map/ppermute | solution.py:55
  73.9 8.2 %collective-permute-start.15 = (bf16[1,192,128]{2,1,0:T(8,128)(2,1)S(1)}, bf16[1,192,128]{2,1,0:T(8,128)(2,1)S(1)}, u32[]{:S(2)}, u32[]{:S(2)}) collective-permute-start(bf16[1,192,128]{2,1,0:T(8,128)(2,1)S(1)} %get-tuple-element.143), channel_id=1, source_target_pairs={{0,8},{1,9},{2,10},{3,11},{4,12},{5,13},{6,14},{7,15},{8,0},{9,1},... | collective-permute-start | bytes 147464 | tf_op jit(solution)/shard_map/ppermute | solution.py:55
  74.2 7.9 %collective-permute-start.14 = (bf16[1,192,128]{2,1,0:T(8,128)(2,1)S(1)}, bf16[1,192,128]{2,1,0:T(8,128)(2,1)S(1)}, u32[]{:S(2)}, u32[]{:S(2)}) collective-permute-start(bf16[1,192,128]{2,1,0:T(8,128)(2,1)S(1)} %get-tuple-element.143), channel_id=1, source_target_pairs={{0,16},{1,17},{2,18},{3,19},{4,20},{5,21},{6,22},{7,23},{8,24},{9,... | collective-permute-start | bytes 147464 | tf_op jit(solution)/shard_map/ppermute | solution.py:55
  82.1 8.0 %collective-permute-start.19 = (bf16[4,192,128]{2,1,0:T(8,128)(2,1)S(1)}, bf16[4,192,128]{2,1,0:T(8,128)(2,1)S(1)}, u32[]{:S(2)}, u32[]{:S(2)}) collective-permute-start(bf16[4,192,128]{2,1,0:T(8,128)(2,1)S(1)} %pad_maximum_fusion.1), channel_id=1, source_target_pairs={{0,6},{1,7},{2,4},{3,5},{4,2},{5,3},{6,0},{7,1},{8,14},{9,15},{10,... | collective-permute-start | bytes 589832 | tf_op jit(solution)/shard_map/ppermute | solution.py:55
  84.6 7.4 %collective-permute-start.18 = (bf16[4,192,128]{2,1,0:T(8,128)(2,1)S(1)}, bf16[4,192,128]{2,1,0:T(8,128)(2,1)S(1)}, u32[]{:S(2)}, u32[]{:S(2)}) collective-permute-start(bf16[4,192,128]{2,1,0:T(8,128)(2,1)S(1)} %pad_maximum_fusion.1), channel_id=1, source_target_pairs={{0,2},{1,3},{2,0},{3,1},{4,6},{5,7},{6,4},{7,5},{8,10},{9,11},{10,... | collective-permute-start | bytes 589832 | tf_op jit(solution)/shard_map/ppermute | solution.py:55
  85.1 6.8 %collective-permute-start.17 = (bf16[4,192,128]{2,1,0:T(8,128)(2,1)S(1)}, bf16[4,192,128]{2,1,0:T(8,128)(2,1)S(1)}, u32[]{:S(2)}, u32[]{:S(2)}) collective-permute-start(bf16[4,192,128]{2,1,0:T(8,128)(2,1)S(1)} %pad_maximum_fusion.1), channel_id=1, source_target_pairs={{0,4},{1,5},{2,6},{3,7},{4,0},{5,1},{6,2},{7,3},{8,12},{9,13},{10,... | collective-permute-start | bytes 589832 | tf_op jit(solution)/shard_map/ppermute | solution.py:55
  92.0 8.7 %collective-permute-start.20 = (bf16[16,192,128]{2,1,0:T(8,128)(2,1)S(1)}, bf16[16,192,128]{2,1,0:T(8,128)(2,1)S(1)}, u32[]{:S(2)}, u32[]{:S(2)}) collective-permute-start(bf16[16,192,128]{2,1,0:T(8,128)(2,1)S(1)} %constant_dynamic-update-slice_fusion.7.chunks.lower), channel_id=1, source_target_pairs={{0,1},{1,0},{2,3},{3,2},{4,5},{5,4},{6,7},{7,6},{8,9},{9,8},{10,11... | collective-permute-start | bytes 2359304 | tf_op jit(solution)/shard_map/ppermute | solution.py:55
  110.5 1.4 collective-permute-start.21
  111.9 4.6 %collective-permute-start.24 = (f32[24,128]{1,0:T(8,128)S(1)}, f32[24,128]{1,0:T(8,128)S(1)}, u32[]{:S(2)}, u32[]{:S(2)}) collective-permute-start(f32[24,128]{1,0:T(8,128)S(1)} %add.97), channel_id=1, source_target_pairs={{0,6},{1,7},{2,4},{3,5},{4,2},{5,3},{6,0},{7,1},{8,14},{9,15},{10,... | collective-permute-start | bytes 36872 | tf_op jit(solution)/shard_map/ppermute | solution.py:55
  114.2 3.7 %collective-permute-start.23 = (f32[24,128]{1,0:T(8,128)S(1)}, f32[24,128]{1,0:T(8,128)S(1)}, u32[]{:S(2)}, u32[]{:S(2)}) collective-permute-start(f32[24,128]{1,0:T(8,128)S(1)} %add.97), channel_id=1, source_target_pairs={{0,2},{1,3},{2,0},{3,1},{4,6},{5,7},{6,4},{7,5},{8,10},{9,11},{10,... | collective-permute-start | bytes 36872 | tf_op jit(solution)/shard_map/ppermute | solution.py:55
  114.8 3.7 %collective-permute-start.22 = (f32[24,128]{1,0:T(8,128)S(1)}, f32[24,128]{1,0:T(8,128)S(1)}, u32[]{:S(2)}, u32[]{:S(2)}) collective-permute-start(f32[24,128]{1,0:T(8,128)S(1)} %add.97), channel_id=1, source_target_pairs={{0,4},{1,5},{2,6},{3,7},{4,0},{5,1},{6,2},{7,3},{8,12},{9,13},{10,... | collective-permute-start | bytes 36872 | tf_op jit(solution)/shard_map/ppermute | solution.py:55
  118.5 5.5 %collective-permute-start.27 = (f32[24,128]{1,0:T(8,128)S(1)}, f32[24,128]{1,0:T(8,128)S(1)}, u32[]{:S(2)}, u32[]{:S(2)}) collective-permute-start(f32[24,128]{1,0:T(8,128)S(1)} %add_add_fusion.1), channel_id=1, source_target_pairs={{0,24},{1,25},{2,26},{3,27},{4,28},{5,29},{6,30},{7,31},{8,16},{9,... | collective-permute-start | bytes 36872 | tf_op jit(solution)/shard_map/ppermute | solution.py:55
  121.1 3.7 %collective-permute-start.26 = (f32[24,128]{1,0:T(8,128)S(1)}, f32[24,128]{1,0:T(8,128)S(1)}, u32[]{:S(2)}, u32[]{:S(2)}) collective-permute-start(f32[24,128]{1,0:T(8,128)S(1)} %add_add_fusion.1), channel_id=1, source_target_pairs={{0,8},{1,9},{2,10},{3,11},{4,12},{5,13},{6,14},{7,15},{8,0},{9,1},... | collective-permute-start | bytes 36872 | tf_op jit(solution)/shard_map/ppermute | solution.py:55
  121.1 4.6 %collective-permute-start.25 = (f32[24,128]{1,0:T(8,128)S(1)}, f32[24,128]{1,0:T(8,128)S(1)}, u32[]{:S(2)}, u32[]{:S(2)}) collective-permute-start(f32[24,128]{1,0:T(8,128)S(1)} %add_add_fusion.1), channel_id=1, source_target_pairs={{0,16},{1,17},{2,18},{3,19},{4,20},{5,21},{6,22},{7,23},{8,24},{9,... | collective-permute-start | bytes 36872 | tf_op jit(solution)/shard_map/ppermute | solution.py:55

commit v5 on v4

--- a/solution.py
+++ b/solution.py
@@ -244,7 +244,7 @@
     )
 
 
-def row_copies(krylov, first, held, sems):
+def row_copies(krylov, first, held, sems, sem=0):
     count, _, lines, _ = held.shape
 
     def copy(at):
@@ -252,7 +252,7 @@
         if not isinstance(at, int):
             start = pl.multiple_of(start, lines)
         return pltpu.make_async_copy(
-            krylov.at[:, pl.ds(start, lines), :], held.at[at], sems.at[at]
+            krylov.at[:, pl.ds(start, lines), :], held.at[at], sems.at[sem + at]
         )
 
     for at in range(count):
@@ -312,35 +312,40 @@
     lax.fori_loop(0, count, body, 0)
 
 
-def both_kernel(first, fold, krylov, normed, earlier, out, gram_out, held, sums, sems):
-    count, basis, lines, _ = held.shape
-    copy = row_copies(krylov, first, held, sems)
+def both_kernel(first, krylov, normed, earlier, out, sums, *rest):
+    pieces, sems = rest[:-1], rest[-1]
+    ahead, copies = 0, []
+    for held in pieces:
+        copies.append(row_copies(krylov, first + ahead, held, sems, ahead))
+        ahead += held.shape[0]
     sums[...] = earlier[...]
-
-    def body(at, carry):
-        copy(at).wait()
-        stack = stacked(held[at])
-        sums[...] += dot_nt(stack, stack)
-        made = dot_nt(stack, normed[...])
-        here = pl.ds(pl.multiple_of(at * lines, lines), lines)
-        for one in range(basis):
-            out[one, here, :] = made[one * lines : (one + 1) * lines]
-        return carry
-
-    lax.fori_loop(0, count, body, 0)
-    gram_out[...] = fold_gram(sums[...], basis, lines) if fold else sums[...]
-
-
-def loss_columns(flip, load, places, splits):
-    made = []
+    ahead = 0
+    for held, copy in zip(pieces, copies):
+        count, basis, lines, _ = held.shape
+
+        def body(at, carry, held=held, copy=copy, ahead=ahead):
+            copy(at).wait()
+            stack = stacked(held[at])
+            sums[...] += dot_nt(stack, stack)
+            made = dot_nt(stack, normed[...])
+            here = pl.ds(pl.multiple_of((ahead + at) * lines, lines), lines)
+            for one in range(basis):
+                out[one, here, :] = made[one * lines : (one + 1) * lines]
+            return carry
+
+        lax.fori_loop(0, count, body, 0)
+        ahead += count
+
+
+def put_loss(loss, first, flip, chunks, splits):
+    places = chunks.shape[0]
     for column in range(places // splits):
         pieces = [
-            load((column * splits + part) ^ (flip & (places - 1))) for part in range(splits)
+            chunks[(column * splits + part) ^ (flip & (places - 1))] for part in range(splits)
         ]
         if splits > 1:
             pieces = [jnp.concatenate([one.astype(F32) for one in pieces], 0).astype(BF16)]
-        made.append(pieces[0])
-    return jnp.concatenate(made, axis=1)
+        loss[:, first + column * LANES : first + (column + 1) * LANES] = pieces[0]
 
 
 def back_copies(info, devices, other, down, krylov, held_down, held, sems):
@@ -356,70 +361,79 @@
     return copies, pltpu.make_async_copy(down.at[:, columns], held_down, sems.at[count])
 
 
+def down_products(copies, held, loss, wide, values, grams):
+    count, basis, lines, _ = held.shape
+    for at in range(count):
+        copies[at].wait()
+        stack = stacked(held[at])
+        grams[...] += dot_nt(stack, stack)
+        made = dot_nt(stack, loss[...])
+        part = wide[at * lines : (at + 1) * lines]
+        for one in range(basis):
+            value = part * made[one * lines : (one + 1) * lines]
+            values[one] = values[one] + jnp.sum(value, axis=0, keepdims=True)
+    return jnp.concatenate(values, axis=0)
+
+
 def back_half_kernel(
-    devices, splits,
-    info, chunks, down, krylov, sums, back_sum, square,
+    devices, inv_ff, splits,
+    info, chunks, down, krylov, hidden, earlier, grams, back_sum, squares, values,
     loss, held_down, held, sems,
 ):
-    count, basis, lines, _ = held.shape
+    basis = held.shape[1]
     copies, first = back_copies(info, devices, 0, down, krylov, held_down, held, sems)
     for copy in [first] + copies:
         copy.start()
-    loss[...] = loss_columns(info[0], lambda at: chunks[at], chunks.shape[0], splits)
-    square[...] = dot_nt(loss[...], loss[...])
+    grams[...] = earlier[...]
+    put_loss(loss, 0, info[0], chunks, splits)
+    squares[0] = dot_nt(loss[...], loss[...])
+    squares[1] = dot_tn(hidden[...], hidden[...]) * (inv_ff * inv_ff)
     first.wait()
     back_sum[...] = dot_nt(held_down[...], loss[...])
-    for at in range(count):
-        copies[at].wait()
-        made = dot_nt(stacked(held[at]), loss[...])
-        for one in range(basis):
-            sums[one, at * lines : (at + 1) * lines, :] = made[one * lines : (one + 1) * lines]
+    wide = hidden[...].astype(F32) * inv_ff
+    zeros = [jnp.zeros((1, LIVE), F32) for _ in range(basis)]
+    values[...] = down_products(copies, held, loss, wide, zeros, grams)
 
 
 def back_kernel(
     devices, inv_d, inv_ff, splits, spans,
-    info, chunks, down, krylov, hidden, weight, act, square, loss_square_half, back_half, grams,
-    sums_half, prod_gate, *rest,
+    info, chunks, down, krylov, hidden, weight, act, square, squares_half, back_half, earlier,
+    values_half, prod_gate, *rest,
 ):
     prods_up = rest[: len(spans)]
-    s_out, r_out, stats, held, loss, held_down, sems = rest[len(spans) :]
-    count, basis, lines, _ = held.shape
+    s_out, r_out, stats, held, loss, held_down, grams, sems = rest[len(spans) :]
+    basis, lines = held.shape[1:3]
     copies, first = back_copies(info, devices, 1, down, krylov, held_down, held, sems)
     for copy in [first] + copies:
         copy.start()
-    loss[...] = loss_columns(info[0], lambda at: chunks[at], chunks.shape[0], splits)
-    other = dot_nt(loss[...], loss[...]) + loss_square_half[...]
+    grams[...] = earlier[...]
+    put_loss(loss, 0, info[0], chunks, splits)
     first.wait()
     back = dot_nt(held_down[...], loss[...]) + back_half[...]
     s_term = (back * weight[...]).astype(BF16)
     r_term = (back * act[...]).astype(BF16)
     s_out[...] = s_term
     r_out[...] = r_term
-    wide = hidden[...]
     squares = inv_d * inv_d * ((dot_tn(s_term, s_term) + dot_tn(r_term, r_term)) * square[...])
-    squares = total(squares + inv_ff * inv_ff * (dot_tn(wide, wide) * other))
-    stats[basis : 2 * basis, :] = jnp.broadcast_to(squares, (basis, LANES))
-    stats[2 * basis : 3 * basis, :] = grams[...]
+    other = dot_nt(loss[...], loss[...]) + squares_half[0]
+    squares = total(squares + squares_half[1] * other)
     wide_s = s_term.astype(F32) * inv_d
     wide_r = r_term.astype(F32) * inv_d
-    wide_h = wide.astype(F32) * inv_ff
     values = []
     for one in range(basis):
-        value = wide_s * prod_gate[one] + wide_h * sums_half[one]
-        value = jnp.sum(value, axis=0, keepdims=True)
+        value = jnp.sum(wide_s * prod_gate[one], axis=0, keepdims=True)
         for (start, number), prod in zip(spans, prods_up):
             part = wide_r[start : start + number] * prod[one]
             value = value + jnp.sum(part, axis=0, keepdims=True)
-        values.append(value)
-    for at in range(count):
-        copies[at].wait()
-        made = dot_nt(stacked(held[at]), loss[...])
-        part = wide_h[at * lines : (at + 1) * lines]
-        for one in range(basis):
-            value = part * made[one * lines : (one + 1) * lines]
-            values[one] = values[one] + jnp.sum(value, axis=0, keepdims=True)
-    lined = jnp.sum(jnp.concatenate(values, axis=0), axis=1, keepdims=True)
-    stats[0:basis, :] = jnp.broadcast_to(lined, (basis, LANES))
+        values.append(value + values_half[one : one + 1, :])
+    wide = hidden[...].astype(F32) * inv_ff
+    lined = down_products(copies, held, loss, wide, values, grams)
+    lined = jnp.sum(lined, axis=1, keepdims=True)
+    lane = lax.broadcasted_iota(jnp.int32, (basis, LANES), 1)
+    made = fold_gram(grams[...], basis, lines)
+    stats[...] = made + jnp.where(lane == basis, lined, 0.0) + jnp.where(
+        lane == basis + 1, squares, 0.0
+    )
 
 
 def split_three(value):
@@ -430,18 +444,22 @@
 
 
 def new_kernel(
-    devices, count, inv_d, inv_ff, splits, long, number_up,
+    devices, count, inv_d, inv_ff, splits, per, number_up,
     info, stats, s_term, r_term, hidden, normed, lower, upper, krylov_gate, krylov_down,
     down_high, *rest,
 ):
     ups = rest[:number_up]
     new_gate, new_up, new_down, coefficients = rest[number_up : number_up + 4]
-    loss, mixer, held, held_low, outs, sems, out_sems = rest[number_up + 4 :]
+    loss, mixer, wide, held, held_low, outs, sems, out_sems = rest[number_up + 4 :]
     depth, basis, lines, width = held.shape
-    per = long // lines
+    long = per * lines
     blocks = s_term.shape[0] // lines
+    steps = blocks // per
     halved = width // 2
-    size = basis * lines
+    shared = basis // 2
+    size = per * shared * lines
+    narrow = min(256, halved)
+    group = min(1024, halved)
     targets = (new_gate, new_up, new_down)
     low_start = half_start(info[0], devices, width, 0)
     high_start = half_start(info[0], devices, width, 1)
@@ -456,112 +474,146 @@
             target = held_low.at[slot]
         return pltpu.make_async_copy(source, target, sems.at[part // 2, slot])
 
-    def copy_out(block, part):
-        start = pl.multiple_of(block * lines, lines)
-        slot = lax.rem(block, 2)
+    def copy_out(turn, step, part):
+        start = pl.multiple_of(step * long, long)
+        slot = lax.rem(turn, 2)
         return pltpu.make_async_copy(
-            outs.at[slot, part], targets[part].at[pl.ds(start, lines), :], out_sems.at[slot, part]
+            outs.at[slot], targets[part].at[pl.ds(start, long), :], out_sems.at[slot]
         )
 
-    for block in range(min(depth, blocks)):
-        for part in (0, 2):
+    for part in (2, 0):
+        for block in range(min(depth, blocks)):
             copy_in(block, part).start()
 
     for at, half in enumerate((lower, upper)):
-        loss[:, at * halved : (at + 1) * halved] = loss_columns(
-            info[0], lambda place, half=half: half[place], half.shape[0], splits
-        )
-    proj = [stats[one, 0] / count for one in range(basis)]
-    squares = stats[basis, 0]
+        put_loss(loss, at * halved, info[0], half, splits)
+    sums = stats[0]
+    for one in range(1, devices):
+        sums = sums + stats[one]
+    lane = lax.broadcasted_iota(jnp.int32, sums.shape, 1)
+    row = lax.broadcasted_iota(jnp.int32, sums.shape, 0)
+
+    def pick(where):
+        return jnp.sum(jnp.where(where, sums, 0.0))
+
+    proj = [pick((lane == basis) & (row == one)) / count for one in range(basis)]
+    squares = pick((lane == basis + 1) & (row == 0))
     for one in range(basis):
-        line = stats[2 * basis + one, 0] * proj[0]
-        for two in range(1, basis):
-            line = line + stats[2 * basis + one, two] * proj[two]
-        squares = squares + proj[one] * (line - 2.0 * stats[one, 0])
+        line = jnp.zeros((1, LANES), F32)
+        for two in range(basis):
+            line = line + proj[two] * sums[two : two + 1, :]
+        dots = pick((lane == basis) & (row == one))
+        mixed = jnp.sum(jnp.where(lane[0:1] == one, line, 0.0))
+        squares = squares + proj[one] * (mixed - 2.0 * dots)
     mean = jnp.maximum(jnp.full((8, LANES), squares / count, F32), 0.0)
     norm = jnp.sqrt(mean + 1e-06)
     inverse = jnp.max(1.0 / norm)
     for one in range(basis):
         coefficients[one] = proj[one]
     coefficients[basis] = jnp.max(norm)
-    lane = lax.broadcasted_iota(jnp.int32, (lines, size), 1)
-    row = lax.broadcasted_iota(jnp.int32, (lines, size), 0)
-    values = jnp.zeros((lines, size), F32)
-    for one in range(basis):
-        values = jnp.where(lane == one * lines + row, proj[one] * inverse, values)
+    scales = [one * inverse for one in proj]
+
+    lane = lax.broadcasted_iota(jnp.int32, (long, size), 1)
+    row = lax.broadcasted_iota(jnp.int32, (long, size), 0)
+    values = jnp.zeros((long, size), F32)
+    for sub in range(per):
+        inside = (row >= sub * lines) & (row < (sub + 1) * lines)
+        for one in range(shared):
+            place = (sub * shared + one - sub) * lines + row
+            values = jnp.where(inside & (lane == place), scales[one], values)
     terms = [term.astype(F32) for term in split_three(values)]
     mixer[...] = jnp.concatenate(terms, axis=0).astype(BF16)
-    chunk = min(1024, halved)
-
-    def put(part, step, left, right, scale, first, last, target, read):
+
+    def put(turn, step, part, pieces):
+        slot = lax.rem(turn, 2)
         here = pl.ds(pl.multiple_of(step * long, long), long)
-        for start in range(first, last, chunk):
-            gradient = dot_nn(left[here, :], right[:, start : start + chunk]) * (scale * inverse)
+
+        @pl.when(turn >= 2)
+        def _():
+            copy_out(turn, step, part).wait()
+
+        for first, last, target, read in pieces:
+
+            def body(at, carry, first=first, target=target, read=read):
+                for sub in range(group // narrow):
+                    start = pl.multiple_of(at * group + sub * narrow, narrow)
+                    columns = pl.ds(start, narrow)
+                    stack = jnp.concatenate(
+                        [stacked(read(block, slice(0, shared), columns)) for block in range(per)],
+                        axis=0,
+                    )
+                    mixed = dot_nn(mixer[...], stack)
+                    value = wide[here, pl.ds(pl.multiple_of(first + start, narrow), narrow)]
+                    value = value - (mixed[:long] + (mixed[long : 2 * long] + mixed[2 * long :]))
+                    goal = pl.ds(pl.multiple_of(target + start, narrow), narrow)
+                    for block in range(per):
+                        inside = slice(block * lines, (block + 1) * lines)
+                        rest = value[inside]
+                        others = read(block, slice(shared, basis), columns)
+                        for one in range(basis - shared):
+                            rest = rest - scales[shared + one] * others[one].astype(F32)
+                        outs[slot, inside, goal] = rest.astype(BF16)
+                return carry
+
+            lax.fori_loop(0, (last - first) // group, body, 0)
+        copy_out(turn, step, part).start()
+
+    def refill(step, part):
+        for sub in range(per):
+            block = step * per + sub + depth
+
+            @pl.when(block < blocks)
+            def _(block=block):
+                copy_in(block, part).start()
+
+    for turn, part in enumerate((1, 2, 0)):
+        left, right, scale = (
+            (s_term, normed, inv_d), (r_term, normed, inv_d), (hidden, loss, inv_ff)
+        )[part]
+
+        def gradient(at, carry, left=left, right=right, scale=scale):
+            columns = pl.ds(pl.multiple_of(at * narrow, narrow), narrow)
+            wide[:, columns] = dot_nn(left[...], right[:, columns]) * (scale * inverse)
+            return carry
+
+        lax.fori_loop(0, width // narrow, gradient, 0)
+        if part == 1:
+            ahead = 0
+            for up in ups:
+
+                def up_body(step, carry, up=up, ahead=ahead):
+                    def read(block, vectors, columns):
+                        return up[(step - ahead) * per + block, vectors, :, columns]
+
+                    put(step, step, 1, [(0, width, 0, read)])
+                    return carry
+
+                lax.fori_loop(ahead, ahead + up.shape[0] // per, up_body, 0)
+                ahead += up.shape[0] // per
+            continue
+
+        def body(step, carry, turn=turn, part=part):
             for sub in range(per):
-                stack = stacked(read(sub, slice(start - first, start - first + chunk)))
-                mixed = dot_nn(mixer[...], stack)
-                mixed = mixed[:lines] + (mixed[lines : 2 * lines] + mixed[2 * lines :])
-                value = gradient[sub * lines : (sub + 1) * lines] - mixed
-                columns = pl.ds(pl.multiple_of(target + (start - first), chunk), chunk)
-                slot = lax.rem(step * per + sub, 2)
-                outs[slot, part, :, columns] = value.astype(BF16)
-
-    def body(step, carry):
-        for part in range(3):
-            for sub in range(per):
-                block = step * per + sub
-
-                @pl.when(block >= 2)
-                def _(part=part, block=block):
-                    copy_out(block, part).wait()
-
-                if part != 1:
-                    copy_in(block, part).wait()
+                copy_in(step * per + sub, part).wait()
+
+            def read(block, vectors, columns):
+                source = held if part == 0 else held_low
+                return source[lax.rem(step * per + block, depth), vectors, :, columns]
+
+            def read_high(block, vectors, columns):
+                return down_high[step * per + block, vectors, :, columns]
+
             if part == 0:
-                put(
-                    0, step, s_term, normed, inv_d, 0, width, 0,
-                    lambda sub, columns: held[lax.rem(step * per + sub, depth), :, :, columns],
-                )
-            elif part == 1:
-                ahead = 0
-                for up in ups:
-                    steps = up.shape[0] // per
-
-                    @pl.when((step >= ahead) & (step < ahead + steps))
-                    def _(up=up, ahead=ahead):
-                        put(
-                            1, step, r_term, normed, inv_d, 0, width, 0,
-                            lambda sub, columns: up[(step - ahead) * per + sub, :, :, columns],
-                        )
-
-                    ahead += steps
+                pieces = [(0, width, 0, read)]
             else:
-                put(
-                    2, step, hidden, loss, inv_ff, 0, halved, low_start,
-                    lambda sub, columns: held_low[
-                        lax.rem(step * per + sub, depth), :, :, columns
-                    ],
-                )
-                put(
-                    2, step, hidden, loss, inv_ff, halved, width, high_start,
-                    lambda sub, columns: down_high[
-                        step, :, sub * lines : (sub + 1) * lines, columns
-                    ],
-                )
-            for sub in range(per):
-                block = step * per + sub
-                copy_out(block, part).start()
-                if part != 1:
-                    @pl.when(block + depth < blocks)
-                    def _(part=part, block=block):
-                        copy_in(block + depth, part).start()
-
-        return carry
-
-    lax.fori_loop(0, blocks // per, body, 0)
-    for block in range(max(0, blocks - 2), blocks):
-        for part in range(3):
-            copy_out(block, part).wait()
+                pieces = [(0, halved, low_start, read), (halved, width, high_start, read_high)]
+            put(turn * steps + step, step, part, pieces)
+            refill(step, part)
+            return carry
+
+        lax.fori_loop(0, steps, body, 0)
+    for turn in range(max(0, 3 * steps - 2), 3 * steps):
+        copy_out(turn, turn % steps, 0).wait()
 
 
 def per_device(
@@ -605,20 +657,18 @@
             name="gram",
         )(far(after(krylov, before)), jnp.zeros((8, LANES), F32) if start else earlier)
 
-    def both(krylov, first, number, fold, earlier, normed, before):
+    def both(krylov, first, number, earlier, normed, before):
+        split = [min(4, number - at) for at in range(0, number, 4)]
         return pl.pallas_call(
-            functools.partial(both_kernel, first, fold),
+            functools.partial(both_kernel, first),
             in_specs=[FAR, FAST, FAST],
-            out_specs=[FAST] * 3,
+            out_specs=[FAST] * (2 + len(split)),
             out_shape=[
                 jax.ShapeDtypeStruct((basis, number * lines, LIVE), F32),
-                jax.ShapeDtypeStruct((basis, LANES) if fold else (size, size), F32),
-                jax.ShapeDtypeStruct((number, basis, lines, width), BF16),
-            ],
-            scratch_shapes=[
-                pltpu.VMEM((size, size), F32),
-                pltpu.SemaphoreType.DMA((number,)),
-            ],
+                jax.ShapeDtypeStruct((size, size), F32),
+            ]
+            + [jax.ShapeDtypeStruct((one, basis, lines, width), BF16) for one in split],
+            scratch_shapes=[pltpu.SemaphoreType.DMA((number,))],
             compiler_params=params(8),
             cost_estimate=cost(
                 2 * size * (size + LIVE) * width * number, 2 * size * width * number
@@ -630,14 +680,14 @@
     gram_jobs = [
         job
         for job in (
-            (krylov_down, 0, cut), (krylov_gate, 0, pieces), (krylov_down, cut, pieces - cut)
+            (krylov_gate, 0, cut), (krylov_gate, cut, pieces - cut)
         )
         if job[2]
     ]
     gram_sums = [None]
 
     def next_gram(group, before):
-        if not gram_jobs:
+        if not gram_jobs or group == groups[-1]:
             return None
         return gram(*gram_jobs.pop(0), gram_sums[-1], before), gram_sums.append
 
@@ -726,8 +776,8 @@
     )(info, tangent_t, hidden_t, far(down_rows), far(krylov_down))
 
     per = long // lines
-    part = (pieces // per + 2) // 3 * per
-    shares = [min(part, pieces - first) for first in range(0, pieces, part)]
+    part = pieces // per // 2 * per
+    shares = [number for number in (part, pieces - part) if number]
     up_jobs = [(sum(shares[:at]), number) for at, number in enumerate(shares)]
     up_spans = [(first * lines, number * lines) for first, number in up_jobs]
     prods_up, kept_up = [], []
@@ -736,14 +786,12 @@
         if not up_jobs:
             return None
         first, number = up_jobs.pop(0)
-        made = both(
-            krylov_up, first, number, not up_jobs, gram_sums[-1], normed, before
-        )
+        made = both(krylov_up, first, number, gram_sums[-1], normed, before)
 
         def done(made):
             prods_up.append(made[0])
             gram_sums.append(made[1])
-            kept_up.append(made[2])
+            kept_up.extend(made[2:])
 
         return made, done
 
@@ -768,39 +816,39 @@
             done(made)
     loss_own = add_up([one.astype(F32) for one in [keep] + got]).astype(BF16)
 
+    back_flops = (basis + 1) * product_flops // 2 + size * size * width * pieces
+
     def half_call(lower):
         return pl.pallas_call(
-            functools.partial(back_half_kernel, devices, splits),
-            in_specs=[SMALL, FAST, FAR, FAR],
-            out_specs=[FAST] * 3,
+            functools.partial(back_half_kernel, devices, inv_ff, splits),
+            in_specs=[SMALL, FAST, FAR, FAR, FAST, FAST],
+            out_specs=[FAST] * 4,
             out_shape=[
-                jax.ShapeDtypeStruct((basis, rows, LIVE), F32),
+                jax.ShapeDtypeStruct((size, size), F32),
                 jax.ShapeDtypeStruct((rows, LIVE), F32),
-                jax.ShapeDtypeStruct((LIVE, LIVE), F32),
+                jax.ShapeDtypeStruct((2, LIVE, LIVE), F32),
+                jax.ShapeDtypeStruct((basis, LIVE), F32),
             ],
             scratch_shapes=[
                 pltpu.VMEM((LIVE, halved), BF16),
                 pltpu.VMEM((rows, halved), BF16),
-                pltpu.VMEM((rows // long, basis, long, halved), BF16),
-                pltpu.SemaphoreType.DMA((rows // long + 1,)),
+                pltpu.VMEM((pieces, basis, lines, halved), BF16),
+                pltpu.SemaphoreType.DMA((pieces + 1,)),
             ],
             compiler_params=params(18),
-            cost_estimate=cost(
-                (basis + 1) * product_flops // 2,
-                (basis + 1) * rows * width + 4 * basis * rows * LIVE,
-            ),
+            cost_estimate=cost(back_flops, (basis + 1) * rows * width),
             name="back_half",
-        )(info, lower, far(down_rows), far(krylov_down))
+        )(info, lower, far(down_rows), far(krylov_down), hidden, gram_sums[-1])
 
     halves = []
 
     def beside(group, block):
         if group[0] == 0:
             return half_call(block), halves.extend
-        return next_both(block)
+        return next_both(block) if group == groups[1] else None
 
     lower, upper = gather_blocks(loss_own, groups, beside)
-    sums_half, back_half, loss_square_half = halves
+    gram_sum, back_half, squares_half, values_half = halves
 
     s_term, r_term, stats, down_high = pl.pallas_call(
         functools.partial(back_kernel, devices, inv_d, inv_ff, splits, up_spans),
@@ -809,45 +857,46 @@
         out_shape=[
             jax.ShapeDtypeStruct((rows, LIVE), BF16),
             jax.ShapeDtypeStruct((rows, LIVE), BF16),
-            jax.ShapeDtypeStruct((3 * basis, LANES), F32),
-            jax.ShapeDtypeStruct((rows // long, basis, long, halved), BF16),
+            jax.ShapeDtypeStruct((basis, LANES), F32),
+            jax.ShapeDtypeStruct((pieces, basis, lines, halved), BF16),
         ],
         scratch_shapes=[
             pltpu.VMEM((LIVE, halved), BF16),
             pltpu.VMEM((rows, halved), BF16),
-            pltpu.SemaphoreType.DMA((rows // long + 1,)),
+            pltpu.VMEM((size, size), F32),
+            pltpu.SemaphoreType.DMA((pieces + 1,)),
         ],
         compiler_params=params(8),
         cost_estimate=cost(
-            (basis + 1) * product_flops // 2,
-            (basis + 1) * rows * width + 12 * basis * rows * LIVE,
+            back_flops, (basis + 1) * rows * width + 8 * basis * rows * LIVE
         ),
         name="back",
     )(
         info, upper, far(down_rows), far(krylov_down), hidden, weight, act, square,
-        loss_square_half, back_half, gram_sums[-1], sums_half, prod_gate, *prods_up,
-    )
-
-    for group in groups:
-        stats = add_up([stats] + [exchange(stats, flip) for flip in flips(group)])
-
-    depth = min(3, pieces)
+        squares_half, back_half, gram_sum, values_half, prod_gate, *prods_up,
+    )
+
+    stats = jnp.broadcast_to(stats[None], (devices, basis, LANES))
+    stats = lax.all_to_all(stats, "fsdp", 0, 0, tiled=True)
+
+    depth = min(per + 1, pieces)
     out_shape = jax.ShapeDtypeStruct((rows, width), BF16)
     new_gate, new_up, new_down, coefficients = pl.pallas_call(
-        functools.partial(new_kernel, devices, count, inv_d, inv_ff, splits, long, len(kept_up)),
-        in_specs=[SMALL, SMALL] + [FAST] * 6 + [FAR] * 2 + [FAST] * (1 + len(kept_up)),
+        functools.partial(new_kernel, devices, count, inv_d, inv_ff, splits, per, len(kept_up)),
+        in_specs=[SMALL] + [FAST] * 7 + [FAR] * 2 + [FAST] * (1 + len(kept_up)),
         out_specs=[FAR] * 3 + [SMALL],
         out_shape=[out_shape, out_shape, out_shape, jax.ShapeDtypeStruct((basis + 1,), F32)],
         scratch_shapes=[
             pltpu.VMEM((LIVE, width), BF16),
-            pltpu.VMEM((3 * lines, size), BF16),
+            pltpu.VMEM((3 * long, basis // 2 * long), BF16),
+            pltpu.VMEM((rows, width), F32),
             pltpu.VMEM((depth, basis, lines, width), BF16),
             pltpu.VMEM((depth, basis, lines, halved), BF16),
-            pltpu.VMEM((2, 3, lines, width), BF16),
+            pltpu.VMEM((2, long, width), BF16),
             pltpu.SemaphoreType.DMA((2, depth)),
-            pltpu.SemaphoreType.DMA((2, 3)),
+            pltpu.SemaphoreType.DMA((2,)),
         ],
-        compiler_params=params(20),
+        compiler_params=params(18),
         cost_estimate=cost(3 * product_flops, 6 * (basis + 1) * rows * width),
         name="new",
     )(

time: 148 us -> 168 us (1.14)
  Pallas kernels: 100 us -> 114 us
  blocking collectives: 0 us -> 11.8 us
  starting transfers between devices: 34.1 us -> 25.1 us
  waiting for transfers between devices: 10 us -> 12.9 us
    pallas_call x1, Pallas kernels: 21.4 us -> 43 us  [per_device(): pl.pallas_call(functools.partial(new_kernel, devices, count, inv_d, inv_f...]
    all_to_all x0 -> x1, blocking collectives: none -> 11.8 us  [per_device(): stats = lax.all_to_all(stats, 'fsdp', 0, 0, tiled=True)]
    pallas_call x3 -> x2, Pallas kernels: 19.8 us -> 10.7 us  [gram(): pl.pallas_call(functools.partial(gram_kernel, first, start), in_specs=[FA...]
    ppermute x28 -> x21, starting transfers between devices: 34.1 us -> 25.1 us  [exchange(): lax.ppermute(block, 'fsdp', [(one, one ^ flip) for one in range(count)])]
    ppermute x28 -> x21, waiting for transfers between devices: 10 us -> 12.9 us  [exchange(): lax.ppermute(block, 'fsdp', [(one, one ^ flip) for one in range(count)])]
    pallas_call x1, Pallas kernels: 9.77 us -> 11.8 us  [per_device(): pl.pallas_call(functools.partial(back_kernel, devices, inv_d, inv_ff, spl...]
    pallas_call x4 -> x3, Pallas kernels: 26.4 us -> 26 us  [the longest x2 16.2 us: both(): pl.pallas_call(functools.partial(both_kernel, first), in_specs=[FAR, FAST...]
  transfers between devices with their start and end apart: 28 -> 21, of which waited for: 9 -> 8; matrix products, arithmetic and copies ran while one was open for 1% -> 1% of each run, Pallas kernels for 40% -> 29%
where the time goes in v5:
time: 168 us
  Pallas kernels  114 us (68%)
  starting transfers between devices  25.1 us (15%)
  waiting for transfers between devices  12.9 us (8%)
  blocking collectives  11.8 us (7%)
    pallas_call x1, Pallas kernels, per_device(): pl.pallas_call(functools.partial(new_kernel, devices, count, inv_d, inv_f...  43 us
    ppermute x21, starting transfers between devices, exchange(): lax.ppermute(block, 'fsdp', [(one, one ^ flip) for one in range(count)])  25.1 us
    pallas_call x2, Pallas kernels, both(): pl.pallas_call(functools.partial(both_kernel, first), in_specs=[FAR, FAST...  16.2 us
    ppermute x21, waiting for transfers between devices, exchange(): lax.ppermute(block, 'fsdp', [(one, one ^ flip) for one in range(count)])  12.9 us
    all_to_all x1, blocking collectives, per_device(): stats = lax.all_to_all(stats, 'fsdp', 0, 0, tiled=True)  11.8 us
    pallas_call x1, Pallas kernels, per_device(): pl.pallas_call(functools.partial(back_kernel, devices, inv_d, inv_ff, spl...  11.8 us
    pallas_call x2, Pallas kernels, gram(): pl.pallas_call(functools.partial(gram_kernel, first, start), in_specs=[FA...  10.7 us
    pallas_call x1, Pallas kernels, per_device(): pl.pallas_call(functools.partial(forward_kernel, devices, inv_d, inv_ff,...  10.6 us
  transfers between devices with their start and end apart: 21, of which 8 were waited for; matrix products, arithmetic and copies ran while one was open for 1% of the time, Pallas kernels for 29%

profile of v5, /device:TPU:0, one launch (start us, length us, event | category | flops | bytes accessed | tf_op | source)
XLA Modules:
  0.0 167.8 jit_solution(495630063725454502)
XLA Ops:
  0.6 5.1 %collective-permute-start.2 = (bf16[1,8,4096]{2,1,0:T(8,128)(2,1)}, bf16[1,8,4096]{2,1,0:T(8,128)(2,1)S(1)}, u32[]{:S(2)}, u32[]{:S(2)}) collective-permute-start(bf16[1,8,4096]{2,1,0:T(8,128)(2,1)} %bitcast.4), channel_id=1, source_target_pairs={{0,24},{1,25},{2,26},{3,27},{4,28},{5,29},{6,30},{7,31},{8,16},{9,... | collective-permute-start | bytes 196616 | tf_op jit(solution)/shard_map/ppermute | solution.py:55
  5.7 0.0 collective-permute-start.1
  5.7 0.6 collective-permute-start
  6.4 0.9 constant_dynamic-update-slice_fusion.6
  7.3 1.6 collective-permute-done.2
  8.9 1.8 %collective-permute-done.1 = bf16[1,8,4096]{2,1,0:T(8,128)(2,1)S(1)} collective-permute-done((bf16[1,8,4096]{2,1,0:T(8,128)(2,1)}, bf16[1,8,4096]{2,1,0:T(8,128)(2,1)S(1)}, u32[]{:S(2)}, u32[]{:S(2)}) %collective-permute-start.1) | collective-permute-done | bytes 65568 | tf_op jit(solution)/shard_map/ppermute | solution.py:55
  10.6 1.0 collective-permute-done
  11.6 0.9 pad_maximum_fusion
  12.5 2.5 %collective-permute-start.5 = (bf16[4,8,4096]{2,1,0:T(8,128)(2,1)S(1)}, bf16[4,8,4096]{2,1,0:T(8,128)(2,1)S(1)}, u32[]{:S(2)}, u32[]{:S(2)}) collective-permute-start(bf16[4,8,4096]{2,1,0:T(8,128)(2,1)S(1)} %pad_maximum_fusion), channel_id=1, source_target_pairs={{0,6},{1,7},{2,4},{3,5},{4,2},{5,3},{6,0},{7,1},{8,14},{9,15},{10,... | collective-permute-start | bytes 786440 | tf_op jit(solution)/shard_map/ppermute | solution.py:55
  15.0 0.5 collective-permute-start.4
  15.5 0.5 collective-permute-start.3
  16.1 0.0 copy-start
  16.1 0.0 copy-start.1
  16.1 5.4 %gram.2.earlier = f32[256,256]{1,0:T(8,128)S(1)} custom-call(bf16[8,320,4096]{2,1,0:T(8,128)(2,1)} %krylov_gate.3, f32[8,128]{1,0:T(8,128)S(1)} %broadcast_in_dim.4.earlier), custom_call_target="tpu_custom_call" | custom-call | flops 2684354560 | bytes 10485760 | tf_op jit(solution)/shard_map/gram/pallas_call | solution.py:646
  21.5 1.2 collective-permute-done.5
  22.7 3.4 %collective-permute-done.4 = bf16[4,8,4096]{2,1,0:T(8,128)(2,1)S(1)} collective-permute-done((bf16[4,8,4096]{2,1,0:T(8,128)(2,1)S(1)}, bf16[4,8,4096]{2,1,0:T(8,128)(2,1)S(1)}, u32[]{:S(2)}, u32[]{:S(2)}) %collective-permute-start.4) | collective-permute-done | bytes 262176 | tf_op jit(solution)/shard_map/ppermute | solution.py:55
  26.2 0.1 collective-permute-start.6
  26.3 0.1 pad_add_fusion.info
  26.4 5.3 %gram.3.earlier = f32[256,256]{1,0:T(8,128)S(1)} custom-call(bf16[8,320,4096]{2,1,0:T(8,128)(2,1)} %krylov_gate.3, f32[256,256]{1,0:T(8,128)S(1)} %gram.2.earlier), custom_call_target="tpu_custom_call" | custom-call | flops 2684354560 | bytes 10485760 | tf_op jit(solution)/shard_map/gram/pallas_call | solution.py:646
  31.8 10.6 %forward.1 = (bf16[192,4096]{1,0:T(8,128)(2,1)S(1)}, bf16[320,192]{1,0:T(8,128)(2,1)S(1)}, bf16[192,320]{1,0:T(8,128)(2,1)S(1)}, bf16[192,320]{1,0:T(8,128)(2,1)...) custom-call(s32[2]{0:T(128)S(1)} %pad_add_fusion.info, ...), custom_call_target="tpu_custom_call" | custom-call | flops 2516582400 | bytes 17825792 | tf_op jit(solution)/shard_map/forward/pallas_call | solution.py:715
  42.4 0.5 collective-permute-start.7
  43.0 3.3 %keep.1 = f32[16,192,128]{2,1,0:T(8,128)S(1)} custom-call(s32[2]{0:T(128)S(1)} %pad_add_fusion.info, bf16[192,320]{1,0:T(8,128)(2,1)S(1)} %get-tuple-element.69.tangent_t, bf16[192,320]{1,0:T(8,128)(2,1)S(1)} %get-tuple-element.70.hidden_t, bf16[320,4096]{1,0:T(8,128)(2,1)} %down.7, bf16[8,320,4096]{2,1,0:T(8,128)(2,1)} %krylov_down.5), custom_call_target="tpu_custom_call" | custom-call | flops 503316480 | bytes 4194304 | tf_op jit(solution)/shard_map/keep/pallas_call | solution.py:764
  46.3 0.2 fusion
  46.5 1.5 collective-permute-start.8
  48.0 1.5 collective-permute-start.10
  49.6 0.5 collective-permute-start.9
  50.1 8.9 %product.1 = (f32[8,320,192]{2,1,0:T(8,128)S(1)}, f32[192,192]{1,0:T(8,128)S(1)}) custom-call(bf16[8,320,4096]{2,1,0:T(8,128)(2,1)} %krylov_gate.3, bf16[192,4096]{1,0:T(8,128)(2,1)S(1)} %get-tuple-element.73.normed), custom_call_target="tpu_custom_call" | custom-call | flops 4026531840 | bytes 22937600 | tf_op jit(solution)/shard_map/product/pallas_call | solution.py:744
  59.1 0.1 fusion.4
  59.2 1.9 %collective-permute-start.11 = (bf16[1,192,128]{2,1,0:T(8,128)(2,1)S(1)}, bf16[1,192,128]{2,1,0:T(8,128)(2,1)S(1)}, u32[]{:S(2)}, u32[]{:S(2)}) collective-permute-start(bf16[1,192,128]{2,1,0:T(8,128)(2,1)S(1)} %get-tuple-element.128), channel_id=1, source_target_pairs={{0,16},{1,17},{2,18},{3,19},{4,20},{5,21},{6,22},{7,23},{8,24},{9,... | collective-permute-start | bytes 147464 | tf_op jit(solution)/shard_map/ppermute | solution.py:55
  61.0 1.5 collective-permute-start.13
  62.6 0.1 collective-permute-start.12
  62.7 6.7 %both.2 = (f32[8,128,192]{2,1,0:T(8,128)S(1)}, f32[256,256]{1,0:T(8,128)S(1)}, bf16[4,8,32,4096]{3,2,1,0:T(8,128)(2,1)S(1)}) custom-call(bf16[8,320,4096]{2,1,0:T(8,128)(2,1)} %krylov.6, bf16[192,4096]{1,0:T(8,128)(2,1)S(1)} %get-tuple-element.73.normed, f32[256,256]{1,0:T(8,128)S(1)} %gram.3.earlier), custom_call_target="tpu_custom_call" | custom-call | flops 3758096384 | bytes 8388608 | tf_op jit(solution)/shard_map/both/pallas_call | solution.py:662
  69.5 0.1 constant_dynamic-update-slice_fusion.13
  69.5 2.6 %collective-permute-start.16 = (bf16[1,192,128]{2,1,0:T(8,128)(2,1)S(1)}, bf16[1,192,128]{2,1,0:T(8,128)(2,1)S(1)}, u32[]{:S(2)}, u32[]{:S(2)}) collective-permute-start(bf16[1,192,128]{2,1,0:T(8,128)(2,1)S(1)} %get-tuple-element.121), channel_id=1, source_target_pairs={{0,24},{1,25},{2,26},{3,27},{4,28},{5,29},{6,30},{7,31},{8,16},{9,... | collective-permute-start | bytes 147464 | tf_op jit(solution)/shard_map/ppermute | solution.py:55
  72.1 0.8 collective-permute-start.15
  72.9 1.1 collective-permute-start.14
  74.0 2.1 %collective-permute-done.16 = bf16[1,192,128]{2,1,0:T(8,128)(2,1)S(1)} collective-permute-done((bf16[1,192,128]{2,1,0:T(8,128)(2,1)S(1)}, bf16[1,192,128]{2,1,0:T(8,128)(2,1)S(1)}, u32[]{:S(2)}, u32[]{:S(2)}) %collective-permute-start.16) | collective-permute-done | bytes 49184 | tf_op jit(solution)/shard_map/ppermute | solution.py:55
  76.1 0.3 collective-permute-done.15
  76.4 1.5 collective-permute-done.14
  77.9 2.4 %collective-permute-start.19 = (bf16[4,192,128]{2,1,0:T(8,128)(2,1)S(1)}, bf16[4,192,128]{2,1,0:T(8,128)(2,1)S(1)}, u32[]{:S(2)}, u32[]{:S(2)}) collective-permute-start(bf16[4,192,128]{2,1,0:T(8,128)(2,1)S(1)} %pad_maximum_fusion.1), channel_id=1, source_target_pairs={{0,6},{1,7},{2,4},{3,5},{4,2},{5,3},{6,0},{7,1},{8,14},{9,15},{10,... | collective-permute-start | bytes 589832 | tf_op jit(solution)/shard_map/ppermute | solution.py:55
  80.3 0.5 collective-permute-start.18
  80.8 0.6 collective-permute-start.17
  81.4 9.4 %both.3 = (f32[8,192,192]{2,1,0:T(8,128)S(1)}, f32[256,256]{1,0:T(8,128)S(1)}, bf16[4,8,32,4096]{3,2,1,0:T(8,128)(2,1)S(1)}, bf16[2,8,32,4096]{3,2,1,0:T(8,128)(2,1)S(1)}) custom-call(bf16[8,320,4096]{2,1,0:T(8,128)(2,1)} %krylov.6, bf16[192,4096]{1,0:T(8,128)(2,1)S(1)} %get-tuple-element.73.normed, f32[256,256]{1,0:T(8,128)S(1)} %get-tuple-element.88.earlier), custom_call_target="tpu_custom_call" | custom-call | flops 5637144576 | bytes 12582912 | tf_op jit(solution)/shard_map/both/pallas_call | solution.py:662
  91.1 0.1 collective-permute-start.20
  91.2 9.9 %back_half.1 = (f32[256,256]{1,0:T(8,128)S(1)}, f32[320,192]{1,0:T(8,128)S(1)}, f32[2,192,192]{2,1,0:T(8,128)S(1)}, f32[8,192]{1,0:T(8,128)S(1)}) custom-call(s32[2]{0:T(128)S(1)} %pad_add_fusion.info, bf16[16,192,128]{2,1,0:T(8,128)(2,1)S(1)} %constant_dynamic-update-slice_fusion.7.chunks.lower, bf16[320,4096]{1,0:T(8,128)(2,1)} %down.7, ...), custom_call_target="tpu_custom_call" | custom-call | flops 4949278720 | bytes 11796480 | tf_op jit(solution)/shard_map/back_half/pallas_call | solution.py:822
  101.1 11.8 %back.1 = (bf16[320,192]{1,0:T(8,128)(2,1)S(1)}, bf16[320,192]{1,0:T(8,128)(2,1)S(1)}, f32[8,128]{1,0:T(8,128)S(1)}, bf16[10,8,32,2048]{3,2,1,0:T(8,128)(2,1)S(1)}) custom-call(s32[2]{0:T(128)S(1)} %pad_add_fusion.info, bf16[16,192,128]{2,1,0:T(8,128)(2,1)S(1)} %collective-permute-done.20.chunks.upper, bf16[320,4096]{1,0:T(8,128)(2,1)} %down.7, ...), custom_call_target="tpu_custom_call" | custom-call | flops 4949278720 | bytes 15728640 | tf_op jit(solution)/shard_map/back/pallas_call | solution.py:853
  112.9 11.8 %all_to_all.5.stats = f32[32,8,128]{2,1,0:T(8,128)S(1)} all-to-all(f32[32,8,128]{2,1,0:T(8,128)S(1)} %broadcast_in_dim.10), channel_id=1, replica_groups=mesh['fsdp'=32] {'fsdp'}, dimensions={0} | all-to-all | bytes 262144 | tf_op jit(solution)/shard_map/all_to_all | solution.py:880
  124.7 43.0 %new.1 = (bf16[320,4096]{1,0:T(8,128)(2,1)}, bf16[320,4096]{1,0:T(8,128)(2,1)}, bf16[320,4096]{1,0:T(8,128)(2,1)}, f32[9]{0:T(128)}) custom-call(s32[2]{0:T(128)S(1)} %pad_add_fusion.info, f32[32,8,128]{2,1,0:T(8,128)S(1)} %all_to_all.5.stats, bf16[320,192]{1,0:T(8,128)(2,1)S(1)} %get-tuple-element.114.s_term, ...), custom_call_target="tpu_custom_call" | custom-call | flops 1509949440 | bytes 70778880 | tf_op jit(solution)/shard_map/new/pallas_call | solution.py:884
  (31 shorter events, 0.3 us)
Async XLA Ops:
  0.6 8.2 %collective-permute-start.2 = (bf16[1,8,4096]{2,1,0:T(8,128)(2,1)}, bf16[1,8,4096]{2,1,0:T(8,128)(2,1)S(1)}, u32[]{:S(2)}, u32[]{:S(2)}) collective-permute-start(bf16[1,8,4096]{2,1,0:T(8,128)(2,1)} %bitcast.4), channel_id=1, source_target_pairs={{0,24},{1,25},{2,26},{3,27},{4,28},{5,29},{6,30},{7,31},{8,16},{9,... | collective-permute-start | bytes 196616 | tf_op jit(solution)/shard_map/ppermute | solution.py:55
  5.7 4.9 %collective-permute-start.1 = (bf16[1,8,4096]{2,1,0:T(8,128)(2,1)}, bf16[1,8,4096]{2,1,0:T(8,128)(2,1)S(1)}, u32[]{:S(2)}, u32[]{:S(2)}) collective-permute-start(bf16[1,8,4096]{2,1,0:T(8,128)(2,1)} %bitcast.5), channel_id=1, source_target_pairs={{0,8},{1,9},{2,10},{3,11},{4,12},{5,13},{6,14},{7,15},{8,0},{9,1},... | collective-permute-start | bytes 196616 | tf_op jit(solution)/shard_map/ppermute | solution.py:55
  5.7 5.8 %collective-permute-start = (bf16[1,8,4096]{2,1,0:T(8,128)(2,1)}, bf16[1,8,4096]{2,1,0:T(8,128)(2,1)S(1)}, u32[]{:S(2)}, u32[]{:S(2)}) collective-permute-start(bf16[1,8,4096]{2,1,0:T(8,128)(2,1)} %bitcast.6), channel_id=1, source_target_pairs={{0,16},{1,17},{2,18},{3,19},{4,20},{5,21},{6,22},{7,23},{8,24},{9,... | collective-permute-start | bytes 196616 | tf_op jit(solution)/shard_map/ppermute | solution.py:55
  12.5 10.2 %collective-permute-start.5 = (bf16[4,8,4096]{2,1,0:T(8,128)(2,1)S(1)}, bf16[4,8,4096]{2,1,0:T(8,128)(2,1)S(1)}, u32[]{:S(2)}, u32[]{:S(2)}) collective-permute-start(bf16[4,8,4096]{2,1,0:T(8,128)(2,1)S(1)} %pad_maximum_fusion), channel_id=1, source_target_pairs={{0,6},{1,7},{2,4},{3,5},{4,2},{5,3},{6,0},{7,1},{8,14},{9,15},{10,... | collective-permute-start | bytes 786440 | tf_op jit(solution)/shard_map/ppermute | solution.py:55
  15.0 11.1 %collective-permute-start.4 = (bf16[4,8,4096]{2,1,0:T(8,128)(2,1)S(1)}, bf16[4,8,4096]{2,1,0:T(8,128)(2,1)S(1)}, u32[]{:S(2)}, u32[]{:S(2)}) collective-permute-start(bf16[4,8,4096]{2,1,0:T(8,128)(2,1)S(1)} %pad_maximum_fusion), channel_id=1, source_target_pairs={{0,2},{1,3},{2,0},{3,1},{4,6},{5,7},{6,4},{7,5},{8,10},{9,11},{10,... | collective-permute-start | bytes 786440 | tf_op jit(solution)/shard_map/ppermute | solution.py:55
  15.5 10.6 %collective-permute-start.3 = (bf16[4,8,4096]{2,1,0:T(8,128)(2,1)S(1)}, bf16[4,8,4096]{2,1,0:T(8,128)(2,1)S(1)}, u32[]{:S(2)}, u32[]{:S(2)}) collective-permute-start(bf16[4,8,4096]{2,1,0:T(8,128)(2,1)S(1)} %pad_maximum_fusion), channel_id=1, source_target_pairs={{0,4},{1,5},{2,6},{3,7},{4,0},{5,1},{6,2},{7,3},{8,12},{9,13},{10,... | collective-permute-start | bytes 786440 | tf_op jit(solution)/shard_map/ppermute | solution.py:55
  16.1 10.2 %copy-start = (bf16[4096]{0:T(1024)(128)(2,1)S(1)}, bf16[4096]{0:T(1024)(128)(2,1)}, u32[]{:S(2)}) copy-start(bf16[4096]{0:T(1024)(128)(2,1)} %param.10) | copy-start | bytes 24580
  16.1 10.3 %copy-start.1 = (s32[2]{0:T(128)S(1)}, s32[2]{0:T(128)}, u32[]{:S(2)}) copy-start(s32[2]{0:T(128)} %param.11) | copy-start | bytes 28
  26.2 5.6 %collective-permute-start.6 = (bf16[16,8,4096]{2,1,0:T(8,128)(2,1)S(1)}, bf16[16,8,4096]{2,1,0:T(8,128)(2,1)S(1)}, u32[]{:S(2)}, u32[]{:S(2)}) collective-permute-start(bf16[16,8,4096]{2,1,0:T(8,128)(2,1)S(1)} %constant_dynamic-update-slice_fusion.lower), channel_id=1, source_target_pairs={{0,1},{1,0},{2,3},{3,2},{4,5},{5,4},{6,7},{7,6},{8,9},{9,8},{10,11... | collective-permute-start | bytes 3145736 | tf_op jit(solution)/shard_map/ppermute | solution.py:55
  42.4 3.9 %collective-permute-start.7 = (bf16[16,192,128]{2,1,0:T(8,128)(2,1)S(1)}, bf16[16,192,128]{2,1,0:T(8,128)(2,1)S(1)}, u32[]{:S(2)}, u32[]{:S(2)}) collective-permute-start(bf16[16,192,128]{2,1,0:T(8,128)(2,1)S(1)} %get-tuple-element.71), channel_id=1, source_target_pairs={{0,1},{1,0},{2,3},{3,2},{4,5},{5,4},{6,7},{7,6},{8,9},{9,8},{10,11... | collective-permute-start | bytes 2359304 | tf_op jit(solution)/shard_map/ppermute | solution.py:55
  46.5 12.5 %collective-permute-start.8 = (bf16[4,192,128]{2,1,0:T(8,128)(2,1)S(1)}, bf16[4,192,128]{2,1,0:T(8,128)(2,1)S(1)}, u32[]{:S(2)}, u32[]{:S(2)}) collective-permute-start(bf16[4,192,128]{2,1,0:T(8,128)(2,1)S(1)} %get-tuple-element.124), channel_id=1, source_target_pairs={{0,4},{1,5},{2,6},{3,7},{4,0},{5,1},{6,2},{7,3},{8,12},{9,13},{10,... | collective-permute-start | bytes 589832 | tf_op jit(solution)/shard_map/ppermute | solution.py:55
  48.0 11.0 %collective-permute-start.10 = (bf16[4,192,128]{2,1,0:T(8,128)(2,1)S(1)}, bf16[4,192,128]{2,1,0:T(8,128)(2,1)S(1)}, u32[]{:S(2)}, u32[]{:S(2)}) collective-permute-start(bf16[4,192,128]{2,1,0:T(8,128)(2,1)S(1)} %get-tuple-element.122), channel_id=1, source_target_pairs={{0,6},{1,7},{2,4},{3,5},{4,2},{5,3},{6,0},{7,1},{8,14},{9,15},{10,... | collective-permute-start | bytes 589832 | tf_op jit(solution)/shard_map/ppermute | solution.py:55
  49.6 9.5 %collective-permute-start.9 = (bf16[4,192,128]{2,1,0:T(8,128)(2,1)S(1)}, bf16[4,192,128]{2,1,0:T(8,128)(2,1)S(1)}, u32[]{:S(2)}, u32[]{:S(2)}) collective-permute-start(bf16[4,192,128]{2,1,0:T(8,128)(2,1)S(1)} %get-tuple-element.123), channel_id=1, source_target_pairs={{0,2},{1,3},{2,0},{3,1},{4,6},{5,7},{6,4},{7,5},{8,10},{9,11},{10,... | collective-permute-start | bytes 589832 | tf_op jit(solution)/shard_map/ppermute | solution.py:55
  59.2 10.3 %collective-permute-start.11 = (bf16[1,192,128]{2,1,0:T(8,128)(2,1)S(1)}, bf16[1,192,128]{2,1,0:T(8,128)(2,1)S(1)}, u32[]{:S(2)}, u32[]{:S(2)}) collective-permute-start(bf16[1,192,128]{2,1,0:T(8,128)(2,1)S(1)} %get-tuple-element.128), channel_id=1, source_target_pairs={{0,16},{1,17},{2,18},{3,19},{4,20},{5,21},{6,22},{7,23},{8,24},{9,... | collective-permute-start | bytes 147464 | tf_op jit(solution)/shard_map/ppermute | solution.py:55
  61.0 8.4 %collective-permute-start.13 = (bf16[1,192,128]{2,1,0:T(8,128)(2,1)S(1)}, bf16[1,192,128]{2,1,0:T(8,128)(2,1)S(1)}, u32[]{:S(2)}, u32[]{:S(2)}) collective-permute-start(bf16[1,192,128]{2,1,0:T(8,128)(2,1)S(1)} %get-tuple-element.126), channel_id=1, source_target_pairs={{0,24},{1,25},{2,26},{3,27},{4,28},{5,29},{6,30},{7,31},{8,16},{9,... | collective-permute-start | bytes 147464 | tf_op jit(solution)/shard_map/ppermute | solution.py:55
  62.6 6.9 %collective-permute-start.12 = (bf16[1,192,128]{2,1,0:T(8,128)(2,1)S(1)}, bf16[1,192,128]{2,1,0:T(8,128)(2,1)S(1)}, u32[]{:S(2)}, u32[]{:S(2)}) collective-permute-start(bf16[1,192,128]{2,1,0:T(8,128)(2,1)S(1)} %get-tuple-element.127), channel_id=1, source_target_pairs={{0,8},{1,9},{2,10},{3,11},{4,12},{5,13},{6,14},{7,15},{8,0},{9,1},... | collective-permute-start | bytes 147464 | tf_op jit(solution)/shard_map/ppermute | solution.py:55
  69.5 6.6 %collective-permute-start.16 = (bf16[1,192,128]{2,1,0:T(8,128)(2,1)S(1)}, bf16[1,192,128]{2,1,0:T(8,128)(2,1)S(1)}, u32[]{:S(2)}, u32[]{:S(2)}) collective-permute-start(bf16[1,192,128]{2,1,0:T(8,128)(2,1)S(1)} %get-tuple-element.121), channel_id=1, source_target_pairs={{0,24},{1,25},{2,26},{3,27},{4,28},{5,29},{6,30},{7,31},{8,16},{9,... | collective-permute-start | bytes 147464 | tf_op jit(solution)/shard_map/ppermute | solution.py:55
  72.1 4.3 %collective-permute-start.15 = (bf16[1,192,128]{2,1,0:T(8,128)(2,1)S(1)}, bf16[1,192,128]{2,1,0:T(8,128)(2,1)S(1)}, u32[]{:S(2)}, u32[]{:S(2)}) collective-permute-start(bf16[1,192,128]{2,1,0:T(8,128)(2,1)S(1)} %get-tuple-element.121), channel_id=1, source_target_pairs={{0,8},{1,9},{2,10},{3,11},{4,12},{5,13},{6,14},{7,15},{8,0},{9,1},... | collective-permute-start | bytes 147464 | tf_op jit(solution)/shard_map/ppermute | solution.py:55
  72.9 5.0 %collective-permute-start.14 = (bf16[1,192,128]{2,1,0:T(8,128)(2,1)S(1)}, bf16[1,192,128]{2,1,0:T(8,128)(2,1)S(1)}, u32[]{:S(2)}, u32[]{:S(2)}) collective-permute-start(bf16[1,192,128]{2,1,0:T(8,128)(2,1)S(1)} %get-tuple-element.121), channel_id=1, source_target_pairs={{0,16},{1,17},{2,18},{3,19},{4,20},{5,21},{6,22},{7,23},{8,24},{9,... | collective-permute-start | bytes 147464 | tf_op jit(solution)/shard_map/ppermute | solution.py:55
  77.9 13.1 %collective-permute-start.19 = (bf16[4,192,128]{2,1,0:T(8,128)(2,1)S(1)}, bf16[4,192,128]{2,1,0:T(8,128)(2,1)S(1)}, u32[]{:S(2)}, u32[]{:S(2)}) collective-permute-start(bf16[4,192,128]{2,1,0:T(8,128)(2,1)S(1)} %pad_maximum_fusion.1), channel_id=1, source_target_pairs={{0,6},{1,7},{2,4},{3,5},{4,2},{5,3},{6,0},{7,1},{8,14},{9,15},{10,... | collective-permute-start | bytes 589832 | tf_op jit(solution)/shard_map/ppermute | solution.py:55
  80.3 10.7 %collective-permute-start.18 = (bf16[4,192,128]{2,1,0:T(8,128)(2,1)S(1)}, bf16[4,192,128]{2,1,0:T(8,128)(2,1)S(1)}, u32[]{:S(2)}, u32[]{:S(2)}) collective-permute-start(bf16[4,192,128]{2,1,0:T(8,128)(2,1)S(1)} %pad_maximum_fusion.1), channel_id=1, source_target_pairs={{0,2},{1,3},{2,0},{3,1},{4,6},{5,7},{6,4},{7,5},{8,10},{9,11},{10,... | collective-permute-start | bytes 589832 | tf_op jit(solution)/shard_map/ppermute | solution.py:55
  80.8 10.1 %collective-permute-start.17 = (bf16[4,192,128]{2,1,0:T(8,128)(2,1)S(1)}, bf16[4,192,128]{2,1,0:T(8,128)(2,1)S(1)}, u32[]{:S(2)}, u32[]{:S(2)}) collective-permute-start(bf16[4,192,128]{2,1,0:T(8,128)(2,1)S(1)} %pad_maximum_fusion.1), channel_id=1, source_target_pairs={{0,4},{1,5},{2,6},{3,7},{4,0},{5,1},{6,2},{7,3},{8,12},{9,13},{10,... | collective-permute-start | bytes 589832 | tf_op jit(solution)/shard_map/ppermute | solution.py:55
  91.1 10.0 %collective-permute-start.20 = (bf16[16,192,128]{2,1,0:T(8,128)(2,1)S(1)}, bf16[16,192,128]{2,1,0:T(8,128)(2,1)S(1)}, u32[]{:S(2)}, u32[]{:S(2)}) collective-permute-start(bf16[16,192,128]{2,1,0:T(8,128)(2,1)S(1)} %constant_dynamic-update-slice_fusion.7.chunks.lower), channel_id=1, source_target_pairs={{0,1},{1,0},{2,3},{3,2},{4,5},{5,4},{6,7},{7,6},{8,9},{9,8},{10,11... | collective-permute-start | bytes 2359304 | tf_op jit(solution)/shard_map/ppermute | solution.py:55

commit v6 on v5

v6 whole, which is shorter than its diff:
```python
import functools
import math

import jax
import jax.numpy as jnp
from jax import lax
from jax.experimental import pallas as pl
from jax.experimental.pallas import tpu as pltpu
from jax.sharding import PartitionSpec as P

LEN = 128
LIVE = 192
GROUP = 8
LANES = 128
F32 = jnp.float32
BF16 = jnp.bfloat16


def gelu_pair(gate_pre):
    coef = math.sqrt(2.0 / math.pi)
    cube = gate_pre * gate_pre * gate_pre
    tanh_val = jnp.tanh(coef * (gate_pre + 0.044715 * cube))
    act = 0.5 * gate_pre * (1.0 + tanh_val)
    slope = 0.5 * (1.0 + tanh_val) + 0.5 * gate_pre * (1.0 - tanh_val * tanh_val) * coef * (
        1.0 + 3.0 * 0.044715 * gate_pre * gate_pre
    )
    return (act, slope)


def dot_nn(left, right):
    return jnp.dot(left, right, preferred_element_type=F32)


def dot_nt(left, right):
    return lax.dot_general(left, right, (((1,), (1,)), ((), ())), preferred_element_type=F32)


def dot_tn(left, right):
    return lax.dot_general(left, right, (((0,), (0,)), ((), ())), preferred_element_type=F32)


def total(values):
    return jnp.sum(jnp.sum(values, axis=0, keepdims=True), axis=1, keepdims=True)


def reverse_bits(value, bits):
    out = value * 0
    for bit in range(bits):
        out = out | (((value >> bit) & 1) << (bits - 1 - bit))
    return out


def exchange(block, flip):
    count = lax.axis_size("fsdp")
    return lax.ppermute(block, "fsdp", [(one, one ^ flip) for one in range(count)])


def bit_groups(bits):
    return [(0, 1)] + [(low, min(2, bits - low)) for low in range(1, bits, 2)]


def flips(group):
    low, size = group
    return [reverse_bits(part, size) << low for part in range(1, 1 << size)]


def gather_blocks(block, groups, beside):
    for group in reversed(groups):
        others = [exchange(block, flip) for flip in flips(group)]
        job = beside(group, block)
        if job is not None:
            work, done = job
            others, made = lax.optimization_barrier((others, work))
            done(made)
        if group[0]:
            block = jnp.concatenate([block] + others, axis=0)
    return block, others[0]


def add_up(values):
    while len(values) > 1:
        values = [one + two for one, two in zip(values[0::2], values[1::2])]
    return values[0]


def far(value):
    return pltpu.with_memory_space_constraint(value, pltpu.HBM)


def after(value, earlier):
    return lax.optimization_barrier((value, earlier))[0]


def stacked(krylov):
    basis, rows, width = krylov.shape
    if rows % 16:
        return krylov.astype(F32).reshape(basis * rows, width).astype(BF16)
    return krylov.reshape(basis * rows, width)


def params(mib):
    return pltpu.CompilerParams(vmem_limit_bytes=mib << 20)


def cost(flops, read, transcendentals=0):
    return pl.CostEstimate(flops=flops, bytes_accessed=read, transcendentals=transcendentals)


FAST = pl.BlockSpec(memory_space=pltpu.VMEM)
SMALL = pl.BlockSpec(memory_space=pltpu.SMEM)
FAR = pl.BlockSpec(memory_space=pltpu.HBM)


def call(name, body, operands, results, scratch, fetches, price, mib=6):
    counts = [len(arrays) for arrays, _, _ in fetches]
    placed = [SMALL] + [FAR if one[0] else FAST for one in operands[1:]]
    values = [one[1] for one in operands]
    for arrays, _, _ in fetches:
        placed += [FAR] * len(arrays)
        values += [far(one) for one in arrays]
    made = [jax.ShapeDtypeStruct(shape, BF16) for _, shape, _ in fetches]
    number = sum(shape[0] * (len(arrays) if len(arrays) > 1 else 1) for arrays, shape, _ in fetches)

    def kernel(*refs):
        at = len(operands)
        own, refs = refs[:at], refs[at:]
        sources, refs = refs[: sum(counts)], refs[sum(counts) :]
        outs, refs = refs[: len(results)], refs[len(results) :]
        targets, refs = refs[: len(fetches)], refs[len(fetches) :]
        copies = []
        for (_, _, pairs), count, target in zip(fetches, counts, targets):
            for source, goal in pairs(own[0], sources[:count], target):
                copies.append(pltpu.make_async_copy(source, goal, refs[-1].at[len(copies)]))
            sources = sources[count:]
        for copy in copies:
            copy.start()
        body(*own, *outs, *refs[: len(scratch)])
        for copy in copies:
            copy.wait()

    return pl.pallas_call(
        kernel,
        in_specs=placed,
        out_specs=[FAST] * (len(results) + len(fetches)),
        out_shape=list(results) + made,
        scratch_shapes=list(scratch) + [pltpu.SemaphoreType.DMA((max(1, number),))],
        compiler_params=params(mib),
        cost_estimate=price,
        name=name,
    )(*values)


def near(value):
    return (False, value)


def block_rows(rows):
    return 64 if rows % 64 == 0 else rows


def half_start(flip, devices, width, other):
    top = lax.div(flip, devices // 2) ^ other
    return pl.multiple_of(top * (width // 2), width // 2)


def live_tokens(info, lower, upper, gain, normed, spots):
    spare = info[1] - (LIVE - LEN)
    shift = lax.rem(spare, GROUP)
    half = (LIVE - LEN) // GROUP
    per = LEN // GROUP
    scale = gain[...].astype(F32)
    row_ids = lax.broadcasted_iota(jnp.int32, (GROUP, 1), 0)

    half_groups = lower.shape[0]

    def load(group):
        spot = spots(info[0], group)
        place = lax.rem(spot, half_groups)
        return jnp.where(spot < half_groups, lower[place], upper[place]).astype(F32)

    def tokens(slot):
        if slot < half:
            return load(slot)
        if slot < 2 * half:
            at = slot - half
            first = load(half + at)
            second = pltpu.roll(load(per + 2 * half - 1 - at), shift, 0)
            return jnp.where(GROUP * at + row_ids < spare, first, second)
        return load(per + slot - 2 * half)

    def norm(wide):
        mean = jnp.mean(wide * wide, axis=1, keepdims=True)
        return wide * lax.rsqrt(mean + 1e-06) * scale

    for pair in range(LIVE // (2 * GROUP)):
        both = [norm(tokens(2 * pair + side)) for side in range(2)]
        normed[2 * GROUP * pair : 2 * GROUP * (pair + 1), :] = jnp.concatenate(both, 0).astype(BF16)


def jvp_half(info, tangent_t, hidden_t, down, probe, out, inv_ff, splits):
    rows = LIVE // splits
    places = out.shape[0]
    width = down.shape[1]
    step = min(512, width)
    each = step // LANES
    for at in range(width // step):
        here = slice(at * step, (at + 1) * step)
        values = dot_nn(tangent_t, down[:, here]) + dot_nn(hidden_t, probe[:, here]) * inv_ff
        for column in range(each):
            for part in range(splits):
                piece = values[
                    part * rows : (part + 1) * rows, column * LANES : (column + 1) * LANES
                ]
                chunk = (at * each + column) * splits + part
                out[chunk ^ (info[0] & (places - 1))] = piece.astype(out.dtype)


def down_copies(info, devices, other, sources, held, sems):
    width = held.shape[2]
    start = half_start(info[0], devices, 2 * width, other)
    return [
        pltpu.make_async_copy(source.at[:, pl.ds(start, width)], held.at[at], sems.at[at])
        for at, source in enumerate(sources)
    ]


def forward_kernel(
    devices, inv_d, inv_ff, spots, splits,
    info, lower, upper, gain, gate, up, krylov_gate, krylov_up, down, krylov_down,
    normed, hidden, tangent_t, hidden_t, weight, act_out, send,
    held, held_down, tangent, row_sems, sems,
):
    basis = krylov_down.shape[0]
    count, _, lines, width = held.shape
    sources = (gate, up, krylov_gate.at[basis - 1], krylov_up.at[basis - 1])
    copies = [
        [
            pltpu.make_async_copy(
                source.at[at * lines : (at + 1) * lines], held.at[at, one], row_sems.at[at, one]
            )
            for one, source in enumerate(sources)
        ]
        for at in range(count)
    ]
    for copy in sum(copies, []):
        copy.start()
    last = down_copies(info, devices, 1, (down, krylov_down.at[basis - 1]), held_down, sems)
    for copy in last:
        copy.start()
    live_tokens(info, lower, upper, gain, normed, spots)
    for at in range(count):
        for copy in copies[at]:
            copy.wait()
        made = dot_nt(stacked(held[at]), normed[...])
        gate_pre, up_pre, tan_gate, tan_up = (
            made[one * lines : (one + 1) * lines] for one in range(4)
        )
        act, slope = gelu_pair(gate_pre)
        here = slice(at * lines, (at + 1) * lines)
        hidden[here, :] = (act * up_pre).astype(BF16)
        tangent[here, :] = (
            slope * (tan_gate * inv_d) * up_pre + act * (tan_up * inv_d)
        ).astype(BF16)
        weight[here, :] = up_pre * slope
        act_out[here, :] = act
    tangent_t[...] = tangent[...].T
    hidden_t[...] = hidden[...].T
    for copy in last:
        copy.wait()
    jvp_half(
        info, tangent_t[...], hidden_t[...], held_down.at[0], held_down.at[1], send, inv_ff, splits
    )


def keep_kernel(inv_ff, splits, info, tangent_t, hidden_t, held_down, keep):
    jvp_half(
        info, tangent_t[...], hidden_t[...], held_down.at[0], held_down.at[1], keep, inv_ff, splits
    )


def fold_gram(sums, basis, lines):
    size = basis * lines
    own = lax.broadcasted_iota(jnp.int32, (size, size), 0)
    other = lax.broadcasted_iota(jnp.int32, (size, size), 1)
    if lines & (lines - 1) == 0:
        same = (own & (lines - 1)) == (other & (lines - 1))
    else:
        same = lax.rem(own, lines) == lax.rem(other, lines)
    kept = jnp.where(same, sums, 0.0)
    rows = [
        jnp.sum(kept[one * lines : (one + 1) * lines], axis=0, keepdims=True)
        for one in range(basis)
    ]
    place = lax.broadcasted_iota(jnp.int32, (size, LANES), 0)
    lane = lax.broadcasted_iota(jnp.int32, (size, LANES), 1) * lines
    picks = jnp.where((place >= lane) & (place < lane + lines), 1.0, 0.0).astype(F32)
    return jnp.dot(
        jnp.concatenate(rows, axis=0), picks,
        precision=lax.Precision.HIGHEST, preferred_element_type=F32,
    )


def gram_kernel(start, info, held, *rest):
    out = rest[-1]
    out[...] = jnp.zeros_like(out) if start else rest[0][...]

    def body(at, carry):
        stack = stacked(held[at])
        out[...] += dot_nt(stack, stack)
        return carry

    lax.fori_loop(0, held.shape[0], body, 0)


def put_products(held, normed, out, ahead, sums):
    count, basis, lines, _ = held.shape

    def body(at, carry):
        stack = stacked(held[at])
        if sums is not None:
            sums[...] += dot_nt(stack, stack)
        made = dot_nt(stack, normed[...])
        here = pl.ds(pl.multiple_of((ahead + at) * lines, lines), lines)
        for one in range(basis):
            out[one, here, :] = made[one * lines : (one + 1) * lines]
        return carry

    lax.fori_loop(0, count, body, 0)


def product_kernel(info, normed, *rest):
    helds, (out, square) = rest[:-2], rest[-2:]
    square[...] = dot_nt(normed[...], normed[...])
    ahead = 0
    for held in helds:
        put_products(held, normed, out, ahead, None)
        ahead += held.shape[0]


def both_kernel(info, normed, earlier, held, out, sums):
    sums[...] = earlier[...]
    put_products(held, normed, out, 0, sums)


def put_loss(loss, first, flip, chunks, splits):
    places = chunks.shape[0]
    for column in range(places // splits):
        pieces = [
            chunks[(column * splits + part) ^ (flip & (places - 1))] for part in range(splits)
        ]
        if splits > 1:
            pieces = [jnp.concatenate([one.astype(F32) for one in pieces], 0).astype(BF16)]
        loss[:, first + column * LANES : first + (column + 1) * LANES] = pieces[0]


def down_products(held, ahead, loss, wide, values, grams):
    count, basis, lines, _ = held.shape
    values = list(values)
    for at in range(count):
        stack = stacked(held[at])
        grams[...] += dot_nt(stack, stack)
        made = dot_nt(stack, loss[...])
        part = wide[(ahead + at) * lines : (ahead + at + 1) * lines]
        for one in range(basis):
            value = part * made[one * lines : (one + 1) * lines]
            values[one] = values[one] + jnp.sum(value, axis=0, keepdims=True)
    return values


def back_half_kernel(
    inv_ff, splits,
    info, chunks, held, held_down, hidden, earlier, grams, back_sum, squares, values, loss,
):
    basis = held.shape[1]
    grams[...] = earlier[...]
    put_loss(loss, 0, info[0], chunks, splits)
    squares[0] = dot_nt(loss[...], loss[...])
    squares[1] = dot_tn(hidden[...], hidden[...]) * (inv_ff * inv_ff)
    back_sum[...] = dot_nt(held_down[0], loss[...])
    wide = hidden[...].astype(F32) * inv_ff
    zeros = [jnp.zeros((1, LIVE), F32) for _ in range(basis)]
    values[...] = jnp.concatenate(down_products(held, 0, loss, wide, zeros, grams), axis=0)


def back_kernel(
    devices, inv_d, inv_ff, splits, spans, more,
    info, chunks, held, held_down, hidden, weight, act, square, squares_half, back_half, earlier,
    values_half, prod_gate, *rest,
):
    prods_up, rest = rest[: len(spans)], rest[len(spans) :]
    copies, other_held = [], None
    if more:
        krylov, s_out, r_out, stats, other_held, loss, grams, sems = rest
        start = half_start(info[0], devices, krylov.shape[2], 1)
        first, lines = held.shape[0], held.shape[2]
        for at in range(more):
            here = slice((first + at) * lines, (first + at + 1) * lines)
            source = krylov.at[:, here, pl.ds(start, held.shape[3])]
            copies.append(pltpu.make_async_copy(source, other_held.at[at], sems.at[at]))
            copies[-1].start()
    else:
        s_out, r_out, stats, loss, grams = rest
    basis, lines = held.shape[1:3]
    grams[...] = earlier[...]
    put_loss(loss, 0, info[0], chunks, splits)
    back = dot_nt(held_down[0], loss[...]) + back_half[...]
    s_term = (back * weight[...]).astype(BF16)
    r_term = (back * act[...]).astype(BF16)
    s_out[...] = s_term
    r_out[...] = r_term
    squares = inv_d * inv_d * ((dot_tn(s_term, s_term) + dot_tn(r_term, r_term)) * square[...])
    other = dot_nt(loss[...], loss[...]) + squares_half[0]
    squares = total(squares + squares_half[1] * other)
    wide_s = s_term.astype(F32) * inv_d
    wide_r = r_term.astype(F32) * inv_d
    values = []
    for one in range(basis):
        value = jnp.sum(wide_s * prod_gate[one], axis=0, keepdims=True)
        for (start, number), prod in zip(spans, prods_up):
            part = wide_r[start : start + number] * prod[one]
            value = value + jnp.sum(part, axis=0, keepdims=True)
        values.append(value + values_half[one : one + 1, :])
    wide = hidden[...].astype(F32) * inv_ff
    values = down_products(held, 0, loss, wide, values, grams)
    for copy in copies:
        copy.wait()
    if copies:
        values = down_products(other_held, held.shape[0], loss, wide, values, grams)
    lined = jnp.sum(jnp.concatenate(values, axis=0), axis=1, keepdims=True)
    lane = lax.broadcasted_iota(jnp.int32, (basis, LANES), 1)
    made = fold_gram(grams[...], basis, lines)
    stats[...] = made + jnp.where(lane == basis, lined, 0.0) + jnp.where(
        lane == basis + 1, squares, 0.0
    )


def split_three(value):
    first = value.astype(BF16)
    rest = value - first.astype(F32)
    second = rest.astype(BF16)
    return first, second, (rest - second.astype(F32)).astype(BF16)


def new_kernel(
    devices, count, inv_d, inv_ff, splits, number_high,
    info, stats, s_term, r_term, hidden, normed, lower, upper, krylov_gate, krylov_up,
    krylov_down, *rest,
):
    highs, rest = rest[:number_high], rest[number_high:]
    new_gate, new_up, new_down, coefficients = rest[:4]
    loss, mixer, wide, held, held_low, outs, sems, low_sems, out_sems = rest[4:]
    depth, basis, lines, width = held.shape
    blocks = s_term.shape[0] // lines
    halved = width // 2
    size = basis * lines
    narrow = min(256, halved)
    group = min(1024, halved)
    outs_depth, low_depth = outs.shape[0], held_low.shape[0]
    targets = (new_gate, new_up, new_down)
    low_start = half_start(info[0], devices, width, 0)
    high_start = half_start(info[0], devices, width, 1)

    def copy_in(turn, part):
        block = turn - part * blocks
        here = pl.ds(pl.multiple_of(block * lines, lines), lines)
        slot = lax.rem(turn, depth)
        source = (krylov_gate, krylov_up)[part]
        return pltpu.make_async_copy(source.at[:, here, :], held.at[slot], sems.at[slot])

    def copy_low(block):
        here = pl.ds(pl.multiple_of(block * lines, lines), lines)
        slot = lax.rem(block, low_depth)
        return pltpu.make_async_copy(
            krylov_down.at[:, here, pl.ds(low_start, halved)], held_low.at[slot], low_sems.at[slot]
        )

    def copy_out(turn, block, part):
        start = pl.multiple_of(block * lines, lines)
        slot = lax.rem(turn, outs_depth)
        return pltpu.make_async_copy(
            outs.at[slot], targets[part].at[pl.ds(start, lines), :], out_sems.at[slot]
        )

    for block in range(low_depth):
        copy_low(block).start()
    for turn in range(depth):
        copy_in(turn, turn // blocks).start()

    for at, half in enumerate((lower, upper)):
        put_loss(loss, at * halved, info[0], half, splits)
    sums = stats[0]
    for one in range(1, devices):
        sums = sums + stats[one]
    lane = lax.broadcasted_iota(jnp.int32, sums.shape, 1)
    row = lax.broadcasted_iota(jnp.int32, sums.shape, 0)

    def pick(where):
        return jnp.sum(jnp.where(where, sums, 0.0))

    proj = [pick((lane == basis) & (row == one)) / count for one in range(basis)]
    squares = pick((lane == basis + 1) & (row == 0))
    for one in range(basis):
        line = jnp.zeros((1, LANES), F32)
        for two in range(basis):
            line = line + proj[two] * sums[two : two + 1, :]
        dots = pick((lane == basis) & (row == one))
        mixed = jnp.sum(jnp.where(lane[0:1] == one, line, 0.0))
        squares = squares + proj[one] * (mixed - 2.0 * dots)
    mean = jnp.maximum(jnp.full((8, LANES), squares / count, F32), 0.0)
    norm = jnp.sqrt(mean + 1e-06)
    inverse = jnp.max(1.0 / norm)
    for one in range(basis):
        coefficients[one] = proj[one]
    coefficients[basis] = jnp.max(norm)
    scales = [one * inverse for one in proj]

    lane = lax.broadcasted_iota(jnp.int32, (lines, size), 1)
    row = lax.broadcasted_iota(jnp.int32, (lines, size), 0)
    values = jnp.zeros((lines, size), F32)
    for one in range(basis):
        values = jnp.where(lane == one * lines + row, scales[one], values)
    terms = [term.astype(F32) for term in split_three(values)]
    mixer[...] = jnp.concatenate(terms, axis=0).astype(BF16)

    def put(turn, block, part, pieces):
        slot = lax.rem(turn, outs_depth)
        here = pl.ds(pl.multiple_of(block * lines, lines), lines)

        @pl.when(turn >= outs_depth)
        def _():
            copy_out(turn, block, part).wait()

        for first, last, target, read in pieces:
            for start in range(0, last - first, group):
                mixed = dot_nn(mixer[...], stacked(read(slice(start, start + group))))
                mixed = mixed[:lines] + (mixed[lines : 2 * lines] + mixed[2 * lines :])
                value = wide[here, first + start : first + start + group] - mixed
                goal = pl.ds(pl.multiple_of(target + start, group), group)
                outs[slot, :, goal] = value.astype(BF16)
        copy_out(turn, block, part).start()

    for order, part in enumerate((2, 0, 1)):
        left, right, scale = (
            (s_term, normed, inv_d), (r_term, normed, inv_d), (hidden, loss, inv_ff)
        )[part]

        def gradient(at, carry, left=left, right=right, scale=scale):
            columns = pl.ds(pl.multiple_of(at * narrow, narrow), narrow)
            wide[:, columns] = dot_nn(left[...], right[:, columns]) * (scale * inverse)
            return carry

        lax.fori_loop(0, width // narrow, gradient, 0)
        ahead = 0
        for kept in highs if part == 2 else (None,):
            number = kept.shape[0] if part == 2 else blocks

            def body(at, carry, part=part, kept=kept, ahead=ahead, order=order):
                block = ahead + at
                turn = part * blocks + block
                slot = lax.rem(turn, depth)
                low_slot = lax.rem(block, low_depth)
                if part == 2:
                    copy_low(block).wait()
                    pieces = [
                        (0, halved, low_start, lambda columns: held_low[low_slot, :, :, columns]),
                        (halved, width, high_start, lambda columns: kept[at, :, :, columns]),
                    ]
                else:
                    copy_in(turn, part).wait()
                    pieces = [(0, width, 0, lambda columns: held[slot, :, :, columns])]
                put(order * blocks + block, block, part, pieces)
                if part == 2:
                    @pl.when(block + low_depth < blocks)
                    def _():
                        copy_low(block + low_depth).start()

                else:
                    for later in range(part, 2):
                        there = (turn + depth >= later * blocks) & (
                            turn + depth < (later + 1) * blocks
                        )

                        @pl.when(there)
                        def _(later=later):
                            copy_in(turn + depth, later).start()

                return carry

            lax.fori_loop(0, number, body, 0)
            ahead += number
    for turn in range(max(0, 3 * blocks - outs_depth), 3 * blocks):
        copy_out(turn, turn % blocks, 0).wait()


def per_device(
    inputs, norm_gain, lengths, gate_rows, up_rows, down_rows, krylov_gate, krylov_up, krylov_down
):
    basis, rows, width = krylov_gate.shape
    devices = lax.axis_size("fsdp")
    bits = devices.bit_length() - 1
    groups = bit_groups(bits)
    hidden_all = rows * devices
    count = 3.0 * width * hidden_all
    inv_d = 1.0 / math.sqrt(width)
    inv_ff = 1.0 / math.sqrt(hidden_all)
    me = lax.axis_index("fsdp").astype(jnp.int32)
    mirror = reverse_bits(me, bits)
    info = jnp.stack([mirror, lengths[0]])

    splits = devices // (width // LANES)
    chunk_rows = LIVE // splits
    lines = 32 if rows % 32 == 0 else rows
    pieces = rows // lines
    long = block_rows(rows)
    halved = width // 2
    product_flops = 2 * rows * width * LIVE

    size = basis * lines

    def rows_of(krylov, first, number):
        def pairs(_, sources, target):
            return [
                (
                    sources[0].at[:, (first + at) * lines : (first + at + 1) * lines, :],
                    target.at[at],
                )
                for at in range(number)
            ]

        return ((krylov,), (number, basis, lines, width), pairs)

    def half_columns(other, before, number):
        def start(info):
            return pl.ds(half_start(info[0], devices, width, other), halved)

        def pairs(info, sources, target):
            return [
                (
                    sources[0].at[:, at * lines : (at + 1) * lines, start(info)],
                    target.at[at],
                )
                for at in range(number)
            ]

        def down_pairs(info, sources, target):
            return [(sources[0].at[:, start(info)], target.at[0])]

        krylov, down = after((krylov_down, down_rows), before)
        return [
            ((krylov,), (number, basis, lines, halved), pairs),
            ((down,), (1, rows, halved), down_pairs),
        ]

    def keep_columns():
        def pairs(info, sources, target):
            columns = pl.ds(half_start(info[0], devices, width, 0), halved)
            return [
                (sources[0].at[:, columns], target.at[0]),
                (sources[1].at[basis - 1, :, columns], target.at[1]),
            ]

        return ((down_rows, krylov_down), (2, rows, halved), pairs)

    cut = (pieces + 1) // 2
    spans = [span for span in ((0, cut), (cut, pieces - cut)) if span[1]]
    helds, gram_sums = [], []

    def gram_stage(group, before):
        at = len(gram_sums) + 1 if helds else 0
        if at > len(spans):
            return None
        operands, results, body = [near(info)], [], lambda info: None
        if at:
            operands += [near(helds[at - 1])] + [near(one) for one in gram_sums[-1:]]
            results = [jax.ShapeDtypeStruct((size, size), F32)]
            body = functools.partial(gram_kernel, not gram_sums)
        fetches = [rows_of(after(krylov_gate, before), *span) for span in spans[at : at + 1]]
        made = call(
            "gram" if at else "read", body, operands, results, [], fetches,
            cost(2 * size * size * width * (cut if at else 1), 2 * size * width * cut),
        )

        def done(made):
            gram_sums.extend(made[: len(results)])
            helds.extend(made[len(results) :])

        return made, done

    own_tokens = inputs.shape[0]
    tokens = own_tokens * devices
    if own_tokens % GROUP == 0:
        sub = own_tokens // GROUP
        lower, upper = gather_blocks(inputs.reshape(sub, GROUP, width), groups, gram_stage)

        def spots(flip, group):
            return (reverse_bits(group // sub, bits) ^ flip) * sub + group % sub

    else:
        gathered = lax.all_gather(inputs, "fsdp", axis=0, tiled=True)
        gathered = gathered.reshape(tokens // GROUP, GROUP, width)
        lower, upper = jnp.split(gathered, 2)

        def spots(flip, group):
            return group

    while len(gram_sums) < len(spans):
        made, done = gram_stage(None, inputs)
        done(made)

    normed, hidden, tangent_t, hidden_t, weight, act, send, keep_down = call(
        "forward",
        functools.partial(forward_kernel, devices, inv_d, inv_ff, spots, splits),
        [
            near(info), near(lower), near(upper), near(norm_gain.reshape(1, width)),
            *(
                (True, far(one))
                for one in (gate_rows, up_rows, krylov_gate, krylov_up, down_rows, krylov_down)
            ),
        ],
        [
            jax.ShapeDtypeStruct((LIVE, width), BF16),
            jax.ShapeDtypeStruct((rows, LIVE), BF16),
            jax.ShapeDtypeStruct((LIVE, rows), BF16),
            jax.ShapeDtypeStruct((LIVE, rows), BF16),
            jax.ShapeDtypeStruct((rows, LIVE), F32),
            jax.ShapeDtypeStruct((rows, LIVE), F32),
            jax.ShapeDtypeStruct((devices // 2, chunk_rows, LANES), BF16),
        ],
        [
            pltpu.VMEM((rows // long, 4, long, width), BF16),
            pltpu.VMEM((2, rows, halved), BF16),
            pltpu.VMEM((rows, LIVE), BF16),
            pltpu.SemaphoreType.DMA((rows // long, 4)),
            pltpu.SemaphoreType.DMA((2,)),
        ],
        [keep_columns()],
        cost(5 * product_flops, 12 * rows * width, rows * LIVE),
        24,
    )

    got = exchange(send, 1)
    (keep,) = call(
        "keep",
        functools.partial(keep_kernel, inv_ff, splits),
        [near(info), near(tangent_t), near(hidden_t), near(keep_down)],
        [jax.ShapeDtypeStruct((devices // 2, chunk_rows, LANES), F32)],
        [],
        [],
        cost(product_flops, 2 * rows * width + 2 * LIVE * width),
    )

    shares = [pieces - 2 * (pieces // 3), pieces // 3, pieces // 3]
    up_jobs = [(sum(shares[:at]), number) for at, number in enumerate(shares) if number]
    up_spans = [(first * lines, number * lines) for first, number in up_jobs]
    prods_up, ups, ahead = [], [], []

    def product(before):
        return call(
            "product",
            product_kernel,
            [near(info), near(normed)] + [near(one) for one in helds],
            [
                jax.ShapeDtypeStruct((basis, rows, LIVE), F32),
                jax.ShapeDtypeStruct((LIVE, LIVE), F32),
            ],
            [],
            [rows_of(after(krylov_up, before), *up_jobs[0])],
            cost(basis * product_flops, 2 * size * width * up_jobs[0][1]),
        )

    def next_both(before):
        at = len(prods_up)
        if at == len(up_jobs):
            return None
        number = up_jobs[at][1]
        if at + 1 < len(up_jobs):
            fetches = [rows_of(after(krylov_up, before), *up_jobs[at + 1])]
        else:
            fetches = half_columns(0, before, pieces)
        made = call(
            "both",
            both_kernel,
            [near(info), near(normed), near(gram_sums[-1]), near(ups[-1])],
            [
                jax.ShapeDtypeStruct((basis, number * lines, LIVE), F32),
                jax.ShapeDtypeStruct((size, size), F32),
            ],
            [],
            fetches,
            cost(2 * size * (size + LIVE) * width * number, 2 * size * width * number),
        )

        def done(made):
            prods_up.append(made[0])
            gram_sums.append(made[1])
            (ups if len(made) == 3 else ahead).extend(made[2:])

        return made, done

    got = [got]
    for at, group in enumerate(groups[1:]):
        parts = flips(group)
        part = keep.shape[0] // (len(parts) + 1)
        sends = [
            add_up([one[turn * part : (turn + 1) * part].astype(F32) for one in [keep] + got])
            for turn in range(1, len(parts) + 1)
        ]
        keep = add_up([one[:part].astype(F32) for one in [keep] + got])
        sends = [one.astype(BF16) for one in sends]
        got = [exchange(one, flip) for one, flip in zip(sends, parts)]
        if at == 0:
            got, (prod_gate, square, first_up) = lax.optimization_barrier((got, product(sends[0])))
            ups.append(first_up)
        elif len(prods_up) < len(up_jobs):
            made, done = next_both(sends[0])
            got, made = lax.optimization_barrier((got, made))
            done(made)
    loss_own = add_up([one.astype(F32) for one in [keep] + got]).astype(BF16)

    back_flops = (basis + 1) * product_flops // 2 + size * size * width * pieces

    def half_call(lower):
        down_low, rows_low = ahead
        return call(
            "back_half",
            functools.partial(back_half_kernel, inv_ff, splits),
            [
                near(info), near(lower), near(down_low), near(rows_low), near(hidden),
                near(gram_sums[-1]),
            ],
            [
                jax.ShapeDtypeStruct((size, size), F32),
                jax.ShapeDtypeStruct((rows, LIVE), F32),
                jax.ShapeDtypeStruct((2, LIVE, LIVE), F32),
                jax.ShapeDtypeStruct((basis, LIVE), F32),
            ],
            [pltpu.VMEM((LIVE, halved), BF16)],
            half_columns(1, lower, pieces),
            cost(back_flops, (basis + 1) * rows * width),
        )

    halves = []

    def beside(group, block):
        if group[0] == 0:
            return half_call(block), halves.extend
        return next_both(block)

    lower, upper = gather_blocks(loss_own, groups, beside)
    gram_sum, back_half, squares_half, values_half, down_high, rows_high = halves

    more = 0
    s_term, r_term, stats, *rest_high = call(
        "back",
        functools.partial(back_kernel, devices, inv_d, inv_ff, splits, up_spans, more),
        [
            near(one)
            for one in (
                info, upper, down_high, rows_high, hidden, weight, act, square, squares_half,
                back_half, gram_sum, values_half, prod_gate, *prods_up,
            )
        ]
        + ([(True, far(krylov_down))] if more else []),
        [
            jax.ShapeDtypeStruct((rows, LIVE), BF16),
            jax.ShapeDtypeStruct((rows, LIVE), BF16),
            jax.ShapeDtypeStruct((basis, LANES), F32),
        ]
        + ([jax.ShapeDtypeStruct((more, basis, lines, halved), BF16)] if more else []),
        [pltpu.VMEM((LIVE, halved), BF16), pltpu.VMEM((size, size), F32)]
        + ([pltpu.SemaphoreType.DMA((more,))] if more else []),
        [],
        cost(back_flops, 8 * basis * rows * LIVE),
    )
    highs = [down_high] + rest_high

    stats = jnp.broadcast_to(stats[None], (devices, basis, LANES))
    stats = lax.all_to_all(stats, "fsdp", 0, 0, tiled=True)

    depth, outs_depth = min(4, pieces), min(4, 3 * pieces)
    out_shape = jax.ShapeDtypeStruct((rows, width), BF16)
    new_gate, new_up, new_down, coefficients = pl.pallas_call(
        functools.partial(new_kernel, devices, count, inv_d, inv_ff, splits, len(highs)),
        in_specs=[SMALL] + [FAST] * 7 + [FAR] * 3 + [FAST] * len(highs),
        out_specs=[FAR] * 3 + [SMALL],
        out_shape=[out_shape, out_shape, out_shape, jax.ShapeDtypeStruct((basis + 1,), F32)],
        scratch_shapes=[
            pltpu.VMEM((LIVE, width), BF16),
            pltpu.VMEM((3 * lines, size), BF16),
            pltpu.VMEM((rows, width), F32),
            pltpu.VMEM((depth, basis, lines, width), BF16),
            pltpu.VMEM((depth, basis, lines, halved), BF16),
            pltpu.VMEM((outs_depth, lines, width), BF16),
            pltpu.SemaphoreType.DMA((depth,)),
            pltpu.SemaphoreType.DMA((depth,)),
            pltpu.SemaphoreType.DMA((outs_depth,)),
        ],
        compiler_params=params(22),
        cost_estimate=cost(3 * product_flops, 6 * (basis + 1) * rows * width),
        name="new",
    )(
        info, stats, s_term, r_term, hidden, normed, lower, upper, far(krylov_gate),
        far(krylov_up), far(krylov_down), *highs,
    )
    return (new_gate, new_up, new_down, coefficients)


def solution(mesh):
    placed = (
        P("fsdp", None),
        P(),
        P(),
        P("fsdp", None),
        P("fsdp", None),
        P("fsdp", None),
        P(None, "fsdp", None),
        P(None, "fsdp", None),
        P(None, "fsdp", None),
    )
    return jax.shard_map(
        per_device,
        mesh=mesh,
        in_specs=placed,
        out_specs=(P("fsdp", None), P("fsdp", None), P("fsdp", None), P()),
        check_vma=False,
    )
```

time: 168 us -> 145 us (0.86)
  Pallas kernels: 114 us -> 94.4 us
  waiting for transfers between devices: 12.9 us -> 8.09 us
    pallas_call x1, Pallas kernels: 43 us -> 29.6 us  [per_device(): pl.pallas_call(functools.partial(new_kernel, devices, count, inv_d, inv_f...]
    pallas_call x9 -> x11, Pallas kernels: 71.4 us -> 64.8 us  [call(): pl.pallas_call(kernel, in_specs=placed, out_specs=[FAST] * (len(results)...]
    ppermute x21, waiting for transfers between devices: 12.9 us -> 8.09 us  [exchange(): lax.ppermute(block, 'fsdp', [(one, one ^ flip) for one in range(count)])]
  transfers between devices with their start and end apart: 21 -> 21, of which waited for: 8 -> 5; matrix products, arithmetic and copies ran while one was open for 1% -> 1% of each run, Pallas kernels for 29% -> 32%
where the time goes in v6:
time: 145 us; the launch traced here: 144 us
  Pallas kernels  94.4 us (65%)
  starting transfers between devices  25.7 us (18%)
  blocking collectives  12.9 us (9%)
  waiting for transfers between devices  8.09 us (6%)
    pallas_call x11, Pallas kernels, call(): pl.pallas_call(kernel, in_specs=placed, out_specs=[FAST] * (len(results)...  64.8 us
    pallas_call x1, Pallas kernels, per_device(): pl.pallas_call(functools.partial(new_kernel, devices, count, inv_d, inv_f...  29.6 us
    ppermute x21, starting transfers between devices, exchange(): lax.ppermute(block, 'fsdp', [(one, one ^ flip) for one in range(count)])  25.7 us
    all_to_all x1, blocking collectives, per_device(): stats = lax.all_to_all(stats, 'fsdp', 0, 0, tiled=True)  12.9 us
    ppermute x21, waiting for transfers between devices, exchange(): lax.ppermute(block, 'fsdp', [(one, one ^ flip) for one in range(count)])  8.09 us
  transfers between devices with their start and end apart: 21, of which 5 were waited for; matrix products, arithmetic and copies ran while one was open for 1% of the time, Pallas kernels for 32%

profile of v6, /device:TPU:0, one launch (start us, length us, event | category | flops | bytes accessed | tf_op | source)
XLA Modules:
  0.0 144.4 jit_solution(3570126897546560752)
XLA Ops:
  0.6 5.1 %collective-permute-start.2 = (bf16[1,8,4096]{2,1,0:T(8,128)(2,1)}, bf16[1,8,4096]{2,1,0:T(8,128)(2,1)S(1)}, u32[]{:S(2)}, u32[]{:S(2)}) collective-permute-start(bf16[1,8,4096]{2,1,0:T(8,128)(2,1)} %bitcast.4), channel_id=1, source_target_pairs={{0,24},{1,25},{2,26},{3,27},{4,28},{5,29},{6,30},{7,31},{8,16},{9,... | collective-permute-start | bytes 196616 | tf_op jit(solution)/shard_map/ppermute | solution.py:55
  5.7 0.0 collective-permute-start.1
  5.7 0.6 collective-permute-start
  6.4 0.9 constant_dynamic-update-slice_fusion.6
  7.3 0.7 pad_add_fusion.refs_0_.info
  8.0 4.6 %read.1.refs_1_.refs_2_ = bf16[5,8,32,4096]{3,2,1,0:T(8,128)(2,1)S(1)} custom-call(s32[2]{0:T(128)S(1)} %pad_add_fusion.refs_0_.info, bf16[8,320,4096]{2,1,0:T(8,128)(2,1)} %krylov_gate.1), custom_call_target="tpu_custom_call" | custom-call | flops 536870912 | bytes 10485760 | tf_op jit(solution)/shard_map/read/pallas_call | solution.py:141
  12.6 0.0 collective-permute-done.2
  12.7 0.0 collective-permute-done.1
  12.7 2.7 %collective-permute-start.5 = (bf16[4,8,4096]{2,1,0:T(8,128)(2,1)S(1)}, bf16[4,8,4096]{2,1,0:T(8,128)(2,1)S(1)}, u32[]{:S(2)}, u32[]{:S(2)}) collective-permute-start(bf16[4,8,4096]{2,1,0:T(8,128)(2,1)S(1)} %pad_maximum_fusion), channel_id=1, source_target_pairs={{0,6},{1,7},{2,4},{3,5},{4,2},{5,3},{6,0},{7,1},{8,14},{9,15},{10,... | collective-permute-start | bytes 786440 | tf_op jit(solution)/shard_map/ppermute | solution.py:55
  15.4 0.5 collective-permute-start.4
  15.9 0.4 collective-permute-start.3
  16.3 0.0 copy-start.1
  16.3 4.7 %gram.2 = (f32[256,256]{1,0:T(8,128)S(1)}, bf16[5,8,32,4096]{3,2,1,0:T(8,128)(2,1)S(1)}) custom-call(s32[2]{0:T(128)S(1)} %pad_add_fusion.refs_0_.info, bf16[5,8,32,4096]{3,2,1,0:T(8,128)(2,1)S(1)} %read.1.refs_1_.refs_2_, bf16[8,320,4096]{2,1,0:T(8,128)(2,1)} %krylov_gate.1), custom_call_target="tpu_custom_call" | custom-call | flops 2684354560 | bytes 10485760 | tf_op jit(solution)/shard_map/gram/pallas_call | solution.py:141
  21.0 2.0 %collective-permute-done.5 = bf16[4,8,4096]{2,1,0:T(8,128)(2,1)S(1)} collective-permute-done((bf16[4,8,4096]{2,1,0:T(8,128)(2,1)S(1)}, bf16[4,8,4096]{2,1,0:T(8,128)(2,1)S(1)}, u32[]{:S(2)}, u32[]{:S(2)}) %collective-permute-start.5) | collective-permute-done | bytes 262176 | tf_op jit(solution)/shard_map/ppermute | solution.py:55
  23.0 3.9 %collective-permute-done.4 = bf16[4,8,4096]{2,1,0:T(8,128)(2,1)S(1)} collective-permute-done((bf16[4,8,4096]{2,1,0:T(8,128)(2,1)S(1)}, bf16[4,8,4096]{2,1,0:T(8,128)(2,1)S(1)}, u32[]{:S(2)}, u32[]{:S(2)}) %collective-permute-start.4) | collective-permute-done | bytes 262176 | tf_op jit(solution)/shard_map/ppermute | solution.py:55
  27.0 0.1 collective-permute-start.6
  27.1 4.3 %gram.3.refs_2_ = f32[256,256]{1,0:T(8,128)S(1)} custom-call(s32[2]{0:T(128)S(1)} %pad_add_fusion.refs_0_.info, bf16[5,8,32,4096]{3,2,1,0:T(8,128)(2,1)S(1)} %get-tuple-element.99.refs_1_.refs_3_, f32[256,256]{1,0:T(8,128)S(1)} %get-tuple-element.100.refs_2_), custom_call_target="tpu_custom_call" | custom-call | flops 2684354560 | bytes 10485760 | tf_op jit(solution)/shard_map/gram/pallas_call | solution.py:141
  31.4 10.7 %forward.1 = (bf16[192,4096]{1,0:T(8,128)(2,1)S(1)}, bf16[320,192]{1,0:T(8,128)(2,1)S(1)}, bf16[192,320]{1,0:T(8,128)(2,1)S(1)}, bf16[192,320]{1,0:T(8,128)(2,1)...) custom-call(s32[2]{0:T(128)S(1)} %pad_add_fusion.refs_0_.info, ...), custom_call_target="tpu_custom_call" | custom-call | flops 2516582400 | bytes 15728640 | tf_op jit(solution)/shard_map/forward/pallas_call | solution.py:141
  42.1 0.6 collective-permute-start.7
  42.6 1.6 %keep.1 = f32[16,192,128]{2,1,0:T(8,128)S(1)} custom-call(s32[2]{0:T(128)S(1)} %pad_add_fusion.refs_0_.info, bf16[192,320]{1,0:T(8,128)(2,1)S(1)} %get-tuple-element.102.refs_1_, bf16[192,320]{1,0:T(8,128)(2,1)S(1)} %get-tuple-element.103.refs_2_, bf16[2,320,2048]{2,1,0:T(8,128)(2,1)S(1)} %get-tuple-element.104.refs_3_), custom_call_target="tpu_custom_call" | custom-call | flops 503316480 | bytes 4194304 | tf_op jit(solution)/shard_map/keep/pallas_call | solution.py:141
  44.2 0.3 collective-permute-done.7
  44.6 0.2 fusion
  44.7 1.5 %collective-permute-start.8 = (bf16[4,192,128]{2,1,0:T(8,128)(2,1)S(1)}, bf16[4,192,128]{2,1,0:T(8,128)(2,1)S(1)}, u32[]{:S(2)}, u32[]{:S(2)}) collective-permute-start(bf16[4,192,128]{2,1,0:T(8,128)(2,1)S(1)} %get-tuple-element.176), channel_id=1, source_target_pairs={{0,4},{1,5},{2,6},{3,7},{4,0},{5,1},{6,2},{7,3},{8,12},{9,13},{10,... | collective-permute-start | bytes 589832 | tf_op jit(solution)/shard_map/ppermute | solution.py:55
  46.2 1.5 %collective-permute-start.10 = (bf16[4,192,128]{2,1,0:T(8,128)(2,1)S(1)}, bf16[4,192,128]{2,1,0:T(8,128)(2,1)S(1)}, u32[]{:S(2)}, u32[]{:S(2)}) collective-permute-start(bf16[4,192,128]{2,1,0:T(8,128)(2,1)S(1)} %get-tuple-element.174), channel_id=1, source_target_pairs={{0,6},{1,7},{2,4},{3,5},{4,2},{5,3},{6,0},{7,1},{8,14},{9,15},{10,... | collective-permute-start | bytes 589832 | tf_op jit(solution)/shard_map/ppermute | solution.py:55
  47.8 0.5 collective-permute-start.9
  48.3 8.4 %product.1 = (f32[8,320,192]{2,1,0:T(8,128)S(1)}, f32[192,192]{1,0:T(8,128)S(1)}, bf16[4,8,32,4096]{3,2,1,0:T(8,128)(2,1)S(1)}) custom-call(s32[2]{0:T(128)S(1)} %pad_add_fusion.refs_0_.info, bf16[192,4096]{1,0:T(8,128)(2,1)S(1)} %get-tuple-element.106.refs_1_.normed, bf16[5,8,32,4096]{3,2,1,0:T(8,128)(2,1)S(1)} %read.1.refs_1_.refs_2_, ...), custom_call_target="tpu_custom_call" | custom-call | flops 4026531840 | bytes 8388608 | tf_op jit(solution)/shard_map/product/pallas_call | solution.py:141
  56.7 0.7 collective-permute-done.9
  57.4 0.1 fusion.4
  57.5 2.3 %collective-permute-start.11 = (bf16[1,192,128]{2,1,0:T(8,128)(2,1)S(1)}, bf16[1,192,128]{2,1,0:T(8,128)(2,1)S(1)}, u32[]{:S(2)}, u32[]{:S(2)}) collective-permute-start(bf16[1,192,128]{2,1,0:T(8,128)(2,1)S(1)} %get-tuple-element.180), channel_id=1, source_target_pairs={{0,16},{1,17},{2,18},{3,19},{4,20},{5,21},{6,22},{7,23},{8,24},{9,... | collective-permute-start | bytes 147464 | tf_op jit(solution)/shard_map/ppermute | solution.py:55
  59.9 1.5 %collective-permute-start.13 = (bf16[1,192,128]{2,1,0:T(8,128)(2,1)S(1)}, bf16[1,192,128]{2,1,0:T(8,128)(2,1)S(1)}, u32[]{:S(2)}, u32[]{:S(2)}) collective-permute-start(bf16[1,192,128]{2,1,0:T(8,128)(2,1)S(1)} %get-tuple-element.178), channel_id=1, source_target_pairs={{0,24},{1,25},{2,26},{3,27},{4,28},{5,29},{6,30},{7,31},{8,16},{9,... | collective-permute-start | bytes 147464 | tf_op jit(solution)/shard_map/ppermute | solution.py:55
  61.3 0.3 collective-permute-start.12
  61.6 5.7 %both.3 = (f32[8,128,192]{2,1,0:T(8,128)S(1)}, f32[256,256]{1,0:T(8,128)S(1)}, bf16[3,8,32,4096]{3,2,1,0:T(8,128)(2,1)S(1)}) custom-call(s32[2]{0:T(128)S(1)} %pad_add_fusion.refs_0_.info, bf16[192,4096]{1,0:T(8,128)(2,1)S(1)} %get-tuple-element.106.refs_1_.normed, f32[256,256]{1,0:T(8,128)S(1)} %gram.3.refs_2_, ...), custom_call_target="tpu_custom_call" | custom-call | flops 3758096384 | bytes 8388608 | tf_op jit(solution)/shard_map/both/pallas_call | solution.py:141
  67.3 0.1 constant_dynamic-update-slice_fusion.13
  67.4 3.0 %collective-permute-start.16 = (bf16[1,192,128]{2,1,0:T(8,128)(2,1)S(1)}, bf16[1,192,128]{2,1,0:T(8,128)(2,1)S(1)}, u32[]{:S(2)}, u32[]{:S(2)}) collective-permute-start(bf16[1,192,128]{2,1,0:T(8,128)(2,1)S(1)} %get-tuple-element.173), channel_id=1, source_target_pairs={{0,24},{1,25},{2,26},{3,27},{4,28},{5,29},{6,30},{7,31},{8,16},{9,... | collective-permute-start | bytes 147464 | tf_op jit(solution)/shard_map/ppermute | solution.py:55
  70.4 0.3 collective-permute-start.15
  70.6 1.2 collective-permute-start.14
  71.8 4.4 %both.4 = (f32[8,96,192]{2,1,0:T(8,128)S(1)}, f32[256,256]{1,0:T(8,128)S(1)}, bf16[3,8,32,4096]{3,2,1,0:T(8,128)(2,1)S(1)}) custom-call(s32[2]{0:T(128)S(1)} %pad_add_fusion.refs_0_.info, bf16[192,4096]{1,0:T(8,128)(2,1)S(1)} %get-tuple-element.106.refs_1_.normed, f32[256,256]{1,0:T(8,128)S(1)} %get-tuple-element.123.refs_2_, ...), custom_call_target="tpu_custom_call" | custom-call | flops 2818572288 | bytes 6291456 | tf_op jit(solution)/shard_map/both/pallas_call | solution.py:141
  76.3 2.4 %collective-permute-start.19 = (bf16[4,192,128]{2,1,0:T(8,128)(2,1)S(1)}, bf16[4,192,128]{2,1,0:T(8,128)(2,1)S(1)}, u32[]{:S(2)}, u32[]{:S(2)}) collective-permute-start(bf16[4,192,128]{2,1,0:T(8,128)(2,1)S(1)} %pad_maximum_fusion.1), channel_id=1, source_target_pairs={{0,6},{1,7},{2,4},{3,5},{4,2},{5,3},{6,0},{7,1},{8,14},{9,15},{10,... | collective-permute-start | bytes 589832 | tf_op jit(solution)/shard_map/ppermute | solution.py:55
  78.7 0.5 collective-permute-start.18
  79.2 0.6 collective-permute-start.17
  79.9 5.1 %both.5 = (f32[8,96,192]{2,1,0:T(8,128)S(1)}, f32[256,256]{1,0:T(8,128)S(1)}, bf16[10,8,32,2048]{3,2,1,0:T(8,128)(2,1)S(1)}, bf16[1,320,2048]{2,1,0:T(8,128)(2,1)S(1)}) custom-call(s32[2]{0:T(128)S(1)} %pad_add_fusion.refs_0_.info, bf16[192,4096]{1,0:T(8,128)(2,1)S(1)} %get-tuple-element.106.refs_1_.normed, f32[256,256]{1,0:T(8,128)S(1)} %get-tuple-element.132.refs_2_, ...), custom_call_target="tpu_custom_call" | custom-call | flops 2818572288 | bytes 6291456 | tf_op jit(solution)/shard_map/both/pallas_call | solution.py:141
  85.0 1.1 collective-permute-done.18
  86.1 0.0 collective-permute-done.17
  86.2 0.1 collective-permute-start.20
  86.3 6.9 %back_half.1 = (f32[256,256]{1,0:T(8,128)S(1)}, f32[320,192]{1,0:T(8,128)S(1)}, f32[2,192,192]{2,1,0:T(8,128)S(1)}, f32[8,192]{1,0:T(8,128)S(1)}, bf16[10,8,32,2...) custom-call(s32[2]{0:T(128)S(1)} %pad_add_fusion.refs_0_.info, ...), custom_call_target="tpu_custom_call" | custom-call | flops 4949278720 | bytes 11796480 | tf_op jit(solution)/shard_map/back_half/pallas_call | solution.py:141
  93.3 8.4 %back.1 = (bf16[320,192]{1,0:T(8,128)(2,1)S(1)}, bf16[320,192]{1,0:T(8,128)(2,1)S(1)}, f32[8,128]{1,0:T(8,128)S(1)}) custom-call(s32[2]{0:T(128)S(1)} %pad_add_fusion.refs_0_.info, bf16[16,192,128]{2,1,0:T(8,128)(2,1)S(1)} %collective-permute-done.20.refs_1_.upper, bf16[10,8,32,2048]{3,2,1,0:T(8,128)(2,1)S(1)} %get-tuple-element.156.refs_2_.rest_0_, ...), custom_call_target="tpu_custom_call" | custom-call | flops 4949278720 | bytes 3932160 | tf_op jit(solution)/shard_map/back/pallas_call | solution.py:141
  101.7 12.9 %all_to_all.5.stats = f32[32,8,128]{2,1,0:T(8,128)S(1)} all-to-all(f32[32,8,128]{2,1,0:T(8,128)S(1)} %broadcast_in_dim.2), channel_id=1, replica_groups=mesh['fsdp'=32] {'fsdp'}, dimensions={0} | all-to-all | bytes 262144 | tf_op jit(solution)/shard_map/all_to_all | solution.py:878
  114.6 29.6 %new.1 = (bf16[320,4096]{1,0:T(8,128)(2,1)}, bf16[320,4096]{1,0:T(8,128)(2,1)}, bf16[320,4096]{1,0:T(8,128)(2,1)}, f32[9]{0:T(128)}) custom-call(s32[2]{0:T(128)S(1)} %pad_add_fusion.refs_0_.info, f32[32,8,128]{2,1,0:T(8,128)S(1)} %all_to_all.5.stats, bf16[320,192]{1,0:T(8,128)(2,1)S(1)} %get-tuple-element.170.s_term, ...), custom_call_target="tpu_custom_call" | custom-call | flops 1509949440 | bytes 70778880 | tf_op jit(solution)/shard_map/new/pallas_call | solution.py:882
  (32 shorter events, 0.3 us)
Async XLA Ops:
  0.6 12.0 %collective-permute-start.2 = (bf16[1,8,4096]{2,1,0:T(8,128)(2,1)}, bf16[1,8,4096]{2,1,0:T(8,128)(2,1)S(1)}, u32[]{:S(2)}, u32[]{:S(2)}) collective-permute-start(bf16[1,8,4096]{2,1,0:T(8,128)(2,1)} %bitcast.4), channel_id=1, source_target_pairs={{0,24},{1,25},{2,26},{3,27},{4,28},{5,29},{6,30},{7,31},{8,16},{9,... | collective-permute-start | bytes 196616 | tf_op jit(solution)/shard_map/ppermute | solution.py:55
  5.7 6.9 %collective-permute-start.1 = (bf16[1,8,4096]{2,1,0:T(8,128)(2,1)}, bf16[1,8,4096]{2,1,0:T(8,128)(2,1)S(1)}, u32[]{:S(2)}, u32[]{:S(2)}) collective-permute-start(bf16[1,8,4096]{2,1,0:T(8,128)(2,1)} %bitcast.5), channel_id=1, source_target_pairs={{0,8},{1,9},{2,10},{3,11},{4,12},{5,13},{6,14},{7,15},{8,0},{9,1},... | collective-permute-start | bytes 196616 | tf_op jit(solution)/shard_map/ppermute | solution.py:55
  5.7 6.9 %collective-permute-start = (bf16[1,8,4096]{2,1,0:T(8,128)(2,1)}, bf16[1,8,4096]{2,1,0:T(8,128)(2,1)S(1)}, u32[]{:S(2)}, u32[]{:S(2)}) collective-permute-start(bf16[1,8,4096]{2,1,0:T(8,128)(2,1)} %bitcast.6), channel_id=1, source_target_pairs={{0,16},{1,17},{2,18},{3,19},{4,20},{5,21},{6,22},{7,23},{8,24},{9,... | collective-permute-start | bytes 196616 | tf_op jit(solution)/shard_map/ppermute | solution.py:55
  8.0 4.7 %copy-start = (bf16[8,4096]{1,0:T(8,128)(2,1)S(1)}, bf16[8,4096]{1,0:T(8,128)(2,1)}, u32[]{:S(2)}) copy-start(bf16[8,4096]{1,0:T(8,128)(2,1)} %param.9) | copy-start | bytes 196612
  12.7 10.3 %collective-permute-start.5 = (bf16[4,8,4096]{2,1,0:T(8,128)(2,1)S(1)}, bf16[4,8,4096]{2,1,0:T(8,128)(2,1)S(1)}, u32[]{:S(2)}, u32[]{:S(2)}) collective-permute-start(bf16[4,8,4096]{2,1,0:T(8,128)(2,1)S(1)} %pad_maximum_fusion), channel_id=1, source_target_pairs={{0,6},{1,7},{2,4},{3,5},{4,2},{5,3},{6,0},{7,1},{8,14},{9,15},{10,... | collective-permute-start | bytes 786440 | tf_op jit(solution)/shard_map/ppermute | solution.py:55
  15.4 11.5 %collective-permute-start.4 = (bf16[4,8,4096]{2,1,0:T(8,128)(2,1)S(1)}, bf16[4,8,4096]{2,1,0:T(8,128)(2,1)S(1)}, u32[]{:S(2)}, u32[]{:S(2)}) collective-permute-start(bf16[4,8,4096]{2,1,0:T(8,128)(2,1)S(1)} %pad_maximum_fusion), channel_id=1, source_target_pairs={{0,2},{1,3},{2,0},{3,1},{4,6},{5,7},{6,4},{7,5},{8,10},{9,11},{10,... | collective-permute-start | bytes 786440 | tf_op jit(solution)/shard_map/ppermute | solution.py:55
  15.9 11.0 %collective-permute-start.3 = (bf16[4,8,4096]{2,1,0:T(8,128)(2,1)S(1)}, bf16[4,8,4096]{2,1,0:T(8,128)(2,1)S(1)}, u32[]{:S(2)}, u32[]{:S(2)}) collective-permute-start(bf16[4,8,4096]{2,1,0:T(8,128)(2,1)S(1)} %pad_maximum_fusion), channel_id=1, source_target_pairs={{0,4},{1,5},{2,6},{3,7},{4,0},{5,1},{6,2},{7,3},{8,12},{9,13},{10,... | collective-permute-start | bytes 786440 | tf_op jit(solution)/shard_map/ppermute | solution.py:55
  16.3 10.7 %copy-start.1 = (bf16[4096]{0:T(1024)(128)(2,1)S(1)}, bf16[4096]{0:T(1024)(128)(2,1)}, u32[]{:S(2)}) copy-start(bf16[4096]{0:T(1024)(128)(2,1)} %param.10) | copy-start | bytes 24580
  27.0 4.4 %collective-permute-start.6 = (bf16[16,8,4096]{2,1,0:T(8,128)(2,1)S(1)}, bf16[16,8,4096]{2,1,0:T(8,128)(2,1)S(1)}, u32[]{:S(2)}, u32[]{:S(2)}) collective-permute-start(bf16[16,8,4096]{2,1,0:T(8,128)(2,1)S(1)} %constant_dynamic-update-slice_fusion.refs_1_), channel_id=1, source_target_pairs={{0,1},{1,0},{2,3},{3,2},{4,5},{5,4},{6,7},{7,6},{8,9},{9,8},{10,11... | collective-permute-start | bytes 3145736 | tf_op jit(solution)/shard_map/ppermute | solution.py:55
  42.1 2.5 %collective-permute-start.7 = (bf16[16,192,128]{2,1,0:T(8,128)(2,1)S(1)}, bf16[16,192,128]{2,1,0:T(8,128)(2,1)S(1)}, u32[]{:S(2)}, u32[]{:S(2)}) collective-permute-start(bf16[16,192,128]{2,1,0:T(8,128)(2,1)S(1)} %get-tuple-element.105), channel_id=1, source_target_pairs={{0,1},{1,0},{2,3},{3,2},{4,5},{5,4},{6,7},{7,6},{8,9},{9,8},{10,11... | collective-permute-start | bytes 2359304 | tf_op jit(solution)/shard_map/ppermute | solution.py:55
  44.7 12.7 %collective-permute-start.8 = (bf16[4,192,128]{2,1,0:T(8,128)(2,1)S(1)}, bf16[4,192,128]{2,1,0:T(8,128)(2,1)S(1)}, u32[]{:S(2)}, u32[]{:S(2)}) collective-permute-start(bf16[4,192,128]{2,1,0:T(8,128)(2,1)S(1)} %get-tuple-element.176), channel_id=1, source_target_pairs={{0,4},{1,5},{2,6},{3,7},{4,0},{5,1},{6,2},{7,3},{8,12},{9,13},{10,... | collective-permute-start | bytes 589832 | tf_op jit(solution)/shard_map/ppermute | solution.py:55
  46.2 10.5 %collective-permute-start.10 = (bf16[4,192,128]{2,1,0:T(8,128)(2,1)S(1)}, bf16[4,192,128]{2,1,0:T(8,128)(2,1)S(1)}, u32[]{:S(2)}, u32[]{:S(2)}) collective-permute-start(bf16[4,192,128]{2,1,0:T(8,128)(2,1)S(1)} %get-tuple-element.174), channel_id=1, source_target_pairs={{0,6},{1,7},{2,4},{3,5},{4,2},{5,3},{6,0},{7,1},{8,14},{9,15},{10,... | collective-permute-start | bytes 589832 | tf_op jit(solution)/shard_map/ppermute | solution.py:55
  47.8 9.7 %collective-permute-start.9 = (bf16[4,192,128]{2,1,0:T(8,128)(2,1)S(1)}, bf16[4,192,128]{2,1,0:T(8,128)(2,1)S(1)}, u32[]{:S(2)}, u32[]{:S(2)}) collective-permute-start(bf16[4,192,128]{2,1,0:T(8,128)(2,1)S(1)} %get-tuple-element.175), channel_id=1, source_target_pairs={{0,2},{1,3},{2,0},{3,1},{4,6},{5,7},{6,4},{7,5},{8,10},{9,11},{10,... | collective-permute-start | bytes 589832 | tf_op jit(solution)/shard_map/ppermute | solution.py:55
  57.5 9.8 %collective-permute-start.11 = (bf16[1,192,128]{2,1,0:T(8,128)(2,1)S(1)}, bf16[1,192,128]{2,1,0:T(8,128)(2,1)S(1)}, u32[]{:S(2)}, u32[]{:S(2)}) collective-permute-start(bf16[1,192,128]{2,1,0:T(8,128)(2,1)S(1)} %get-tuple-element.180), channel_id=1, source_target_pairs={{0,16},{1,17},{2,18},{3,19},{4,20},{5,21},{6,22},{7,23},{8,24},{9,... | collective-permute-start | bytes 147464 | tf_op jit(solution)/shard_map/ppermute | solution.py:55
  59.9 7.4 %collective-permute-start.13 = (bf16[1,192,128]{2,1,0:T(8,128)(2,1)S(1)}, bf16[1,192,128]{2,1,0:T(8,128)(2,1)S(1)}, u32[]{:S(2)}, u32[]{:S(2)}) collective-permute-start(bf16[1,192,128]{2,1,0:T(8,128)(2,1)S(1)} %get-tuple-element.178), channel_id=1, source_target_pairs={{0,24},{1,25},{2,26},{3,27},{4,28},{5,29},{6,30},{7,31},{8,16},{9,... | collective-permute-start | bytes 147464 | tf_op jit(solution)/shard_map/ppermute | solution.py:55
  61.3 5.9 %collective-permute-start.12 = (bf16[1,192,128]{2,1,0:T(8,128)(2,1)S(1)}, bf16[1,192,128]{2,1,0:T(8,128)(2,1)S(1)}, u32[]{:S(2)}, u32[]{:S(2)}) collective-permute-start(bf16[1,192,128]{2,1,0:T(8,128)(2,1)S(1)} %get-tuple-element.179), channel_id=1, source_target_pairs={{0,8},{1,9},{2,10},{3,11},{4,12},{5,13},{6,14},{7,15},{8,0},{9,1},... | collective-permute-start | bytes 147464 | tf_op jit(solution)/shard_map/ppermute | solution.py:55
  67.4 8.9 %collective-permute-start.16 = (bf16[1,192,128]{2,1,0:T(8,128)(2,1)S(1)}, bf16[1,192,128]{2,1,0:T(8,128)(2,1)S(1)}, u32[]{:S(2)}, u32[]{:S(2)}) collective-permute-start(bf16[1,192,128]{2,1,0:T(8,128)(2,1)S(1)} %get-tuple-element.173), channel_id=1, source_target_pairs={{0,24},{1,25},{2,26},{3,27},{4,28},{5,29},{6,30},{7,31},{8,16},{9,... | collective-permute-start | bytes 147464 | tf_op jit(solution)/shard_map/ppermute | solution.py:55
  70.4 5.9 %collective-permute-start.15 = (bf16[1,192,128]{2,1,0:T(8,128)(2,1)S(1)}, bf16[1,192,128]{2,1,0:T(8,128)(2,1)S(1)}, u32[]{:S(2)}, u32[]{:S(2)}) collective-permute-start(bf16[1,192,128]{2,1,0:T(8,128)(2,1)S(1)} %get-tuple-element.173), channel_id=1, source_target_pairs={{0,8},{1,9},{2,10},{3,11},{4,12},{5,13},{6,14},{7,15},{8,0},{9,1},... | collective-permute-start | bytes 147464 | tf_op jit(solution)/shard_map/ppermute | solution.py:55
  70.6 5.6 %collective-permute-start.14 = (bf16[1,192,128]{2,1,0:T(8,128)(2,1)S(1)}, bf16[1,192,128]{2,1,0:T(8,128)(2,1)S(1)}, u32[]{:S(2)}, u32[]{:S(2)}) collective-permute-start(bf16[1,192,128]{2,1,0:T(8,128)(2,1)S(1)} %get-tuple-element.173), channel_id=1, source_target_pairs={{0,16},{1,17},{2,18},{3,19},{4,20},{5,21},{6,22},{7,23},{8,24},{9,... | collective-permute-start | bytes 147464 | tf_op jit(solution)/shard_map/ppermute | solution.py:55
  76.3 8.7 %collective-permute-start.19 = (bf16[4,192,128]{2,1,0:T(8,128)(2,1)S(1)}, bf16[4,192,128]{2,1,0:T(8,128)(2,1)S(1)}, u32[]{:S(2)}, u32[]{:S(2)}) collective-permute-start(bf16[4,192,128]{2,1,0:T(8,128)(2,1)S(1)} %pad_maximum_fusion.1), channel_id=1, source_target_pairs={{0,6},{1,7},{2,4},{3,5},{4,2},{5,3},{6,0},{7,1},{8,14},{9,15},{10,... | collective-permute-start | bytes 589832 | tf_op jit(solution)/shard_map/ppermute | solution.py:55
  78.7 7.4 %collective-permute-start.18 = (bf16[4,192,128]{2,1,0:T(8,128)(2,1)S(1)}, bf16[4,192,128]{2,1,0:T(8,128)(2,1)S(1)}, u32[]{:S(2)}, u32[]{:S(2)}) collective-permute-start(bf16[4,192,128]{2,1,0:T(8,128)(2,1)S(1)} %pad_maximum_fusion.1), channel_id=1, source_target_pairs={{0,2},{1,3},{2,0},{3,1},{4,6},{5,7},{6,4},{7,5},{8,10},{9,11},{10,... | collective-permute-start | bytes 589832 | tf_op jit(solution)/shard_map/ppermute | solution.py:55
  79.2 6.9 %collective-permute-start.17 = (bf16[4,192,128]{2,1,0:T(8,128)(2,1)S(1)}, bf16[4,192,128]{2,1,0:T(8,128)(2,1)S(1)}, u32[]{:S(2)}, u32[]{:S(2)}) collective-permute-start(bf16[4,192,128]{2,1,0:T(8,128)(2,1)S(1)} %pad_maximum_fusion.1), channel_id=1, source_target_pairs={{0,4},{1,5},{2,6},{3,7},{4,0},{5,1},{6,2},{7,3},{8,12},{9,13},{10,... | collective-permute-start | bytes 589832 | tf_op jit(solution)/shard_map/ppermute | solution.py:55
  86.2 7.0 %collective-permute-start.20 = (bf16[16,192,128]{2,1,0:T(8,128)(2,1)S(1)}, bf16[16,192,128]{2,1,0:T(8,128)(2,1)S(1)}, u32[]{:S(2)}, u32[]{:S(2)}) collective-permute-start(bf16[16,192,128]{2,1,0:T(8,128)(2,1)S(1)} %constant_dynamic-update-slice_fusion.7.refs_1_.lower), channel_id=1, source_target_pairs={{0,1},{1,0},{2,3},{3,2},{4,5},{5,4},{6,7},{7,6},{8,9},{9,8},{10,11... | collective-permute-start | bytes 2359304 | tf_op jit(solution)/shard_map/ppermute | solution.py:55

commit v7 on v6

--- a/solution.py
+++ b/solution.py
@@ -111,7 +111,7 @@
 FAR = pl.BlockSpec(memory_space=pltpu.HBM)
 
 
-def call(name, body, operands, results, scratch, fetches, price, mib=6):
+def call(name, body, operands, results, scratch, fetches, price, mib=5):
     counts = [len(arrays) for arrays, _, _ in fetches]
     placed = [SMALL] + [FAR if one[0] else FAST for one in operands[1:]]
     values = [one[1] for one in operands]
@@ -383,23 +383,12 @@
 
 
 def back_kernel(
-    devices, inv_d, inv_ff, splits, spans, more,
+    inv_d, inv_ff, splits, spans,
     info, chunks, held, held_down, hidden, weight, act, square, squares_half, back_half, earlier,
     values_half, prod_gate, *rest,
 ):
     prods_up, rest = rest[: len(spans)], rest[len(spans) :]
-    copies, other_held = [], None
-    if more:
-        krylov, s_out, r_out, stats, other_held, loss, grams, sems = rest
-        start = half_start(info[0], devices, krylov.shape[2], 1)
-        first, lines = held.shape[0], held.shape[2]
-        for at in range(more):
-            here = slice((first + at) * lines, (first + at + 1) * lines)
-            source = krylov.at[:, here, pl.ds(start, held.shape[3])]
-            copies.append(pltpu.make_async_copy(source, other_held.at[at], sems.at[at]))
-            copies[-1].start()
-    else:
-        s_out, r_out, stats, loss, grams = rest
+    s_out, r_out, stats, loss, grams = rest
     basis, lines = held.shape[1:3]
     grams[...] = earlier[...]
     put_loss(loss, 0, info[0], chunks, splits)
@@ -422,10 +411,6 @@
         values.append(value + values_half[one : one + 1, :])
     wide = hidden[...].astype(F32) * inv_ff
     values = down_products(held, 0, loss, wide, values, grams)
-    for copy in copies:
-        copy.wait()
-    if copies:
-        values = down_products(other_held, held.shape[0], loss, wide, values, grams)
     lined = jnp.sum(jnp.concatenate(values, axis=0), axis=1, keepdims=True)
     lane = lax.broadcasted_iota(jnp.int32, (basis, LANES), 1)
     made = fold_gram(grams[...], basis, lines)
@@ -442,13 +427,12 @@
 
 
 def new_kernel(
-    devices, count, inv_d, inv_ff, splits, number_high,
-    info, stats, s_term, r_term, hidden, normed, lower, upper, krylov_gate, krylov_up,
-    krylov_down, *rest,
+    devices, count, inv_d, inv_ff, splits,
+    info, stats, s_term, r_term, hidden, normed, lower, upper, gate, krylov_up,
+    krylov_down, high,
+    new_gate, new_up, new_down, coefficients,
+    loss, mixer, wide, held, held_low, outs, sems, low_sems, out_sems,
 ):
-    highs, rest = rest[:number_high], rest[number_high:]
-    new_gate, new_up, new_down, coefficients = rest[:4]
-    loss, mixer, wide, held, held_low, outs, sems, low_sems, out_sems = rest[4:]
     depth, basis, lines, width = held.shape
     blocks = s_term.shape[0] // lines
     halved = width // 2
@@ -460,12 +444,10 @@
     low_start = half_start(info[0], devices, width, 0)
     high_start = half_start(info[0], devices, width, 1)
 
-    def copy_in(turn, part):
-        block = turn - part * blocks
+    def copy_in(block):
         here = pl.ds(pl.multiple_of(block * lines, lines), lines)
-        slot = lax.rem(turn, depth)
-        source = (krylov_gate, krylov_up)[part]
-        return pltpu.make_async_copy(source.at[:, here, :], held.at[slot], sems.at[slot])
+        slot = lax.rem(block, depth)
+        return pltpu.make_async_copy(krylov_up.at[:, here, :], held.at[slot], sems.at[slot])
 
     def copy_low(block):
         here = pl.ds(pl.multiple_of(block * lines, lines), lines)
@@ -483,8 +465,8 @@
 
     for block in range(low_depth):
         copy_low(block).start()
-    for turn in range(depth):
-        copy_in(turn, turn // blocks).start()
+    for block in range(depth):
+        copy_in(block).start()
 
     for at, half in enumerate((lower, upper)):
         put_loss(loss, at * halved, info[0], half, splits)
@@ -522,9 +504,8 @@
     terms = [term.astype(F32) for term in split_three(values)]
     mixer[...] = jnp.concatenate(terms, axis=0).astype(BF16)
 
-    def put(turn, block, part, pieces):
+    def put(turn, here, block, part, pieces):
         slot = lax.rem(turn, outs_depth)
-        here = pl.ds(pl.multiple_of(block * lines, lines), lines)
 
         @pl.when(turn >= outs_depth)
         def _():
@@ -539,55 +520,49 @@
                 outs[slot, :, goal] = value.astype(BF16)
         copy_out(turn, block, part).start()
 
-    for order, part in enumerate((2, 0, 1)):
+    tall = wide.shape[0]
+    each = tall // lines
+    for order, part in enumerate((0, 2, 1)):
         left, right, scale = (
             (s_term, normed, inv_d), (r_term, normed, inv_d), (hidden, loss, inv_ff)
         )[part]
-
-        def gradient(at, carry, left=left, right=right, scale=scale):
-            columns = pl.ds(pl.multiple_of(at * narrow, narrow), narrow)
-            wide[:, columns] = dot_nn(left[...], right[:, columns]) * (scale * inverse)
-            return carry
-
-        lax.fori_loop(0, width // narrow, gradient, 0)
-        ahead = 0
-        for kept in highs if part == 2 else (None,):
-            number = kept.shape[0] if part == 2 else blocks
-
-            def body(at, carry, part=part, kept=kept, ahead=ahead, order=order):
-                block = ahead + at
-                turn = part * blocks + block
-                slot = lax.rem(turn, depth)
+        for share in range(blocks // each):
+            for start in range(0, width, group):
+                columns = slice(start, start + group)
+                rows_here = slice(share * tall, (share + 1) * tall)
+                made = dot_nn(left[rows_here, :], right[:, columns])
+                wide[:, columns] = made * (scale * inverse)
+
+            def body(at, carry, part=part, order=order, share=share):
+                block = share * each + at
+                here = pl.ds(pl.multiple_of(at * lines, lines), lines)
+                slot = lax.rem(block, depth)
                 low_slot = lax.rem(block, low_depth)
-                if part == 2:
+                if part == 0:
+                    pieces = [(0, width, 0, lambda columns: gate[block, :, :, columns])]
+                elif part == 1:
+                    copy_in(block).wait()
+                    pieces = [(0, width, 0, lambda columns: held[slot, :, :, columns])]
+                else:
                     copy_low(block).wait()
                     pieces = [
                         (0, halved, low_start, lambda columns: held_low[low_slot, :, :, columns]),
-                        (halved, width, high_start, lambda columns: kept[at, :, :, columns]),
+                        (halved, width, high_start, lambda columns: high[block, :, :, columns]),
                     ]
-                else:
-                    copy_in(turn, part).wait()
-                    pieces = [(0, width, 0, lambda columns: held[slot, :, :, columns])]
-                put(order * blocks + block, block, part, pieces)
-                if part == 2:
+                put(order * blocks + block, here, block, part, pieces)
+                if part == 1:
+                    @pl.when(block + depth < blocks)
+                    def _():
+                        copy_in(block + depth).start()
+
+                elif part == 2:
                     @pl.when(block + low_depth < blocks)
                     def _():
                         copy_low(block + low_depth).start()
 
-                else:
-                    for later in range(part, 2):
-                        there = (turn + depth >= later * blocks) & (
-                            turn + depth < (later + 1) * blocks
-                        )
-
-                        @pl.when(there)
-                        def _(later=later):
-                            copy_in(turn + depth, later).start()
-
                 return carry
 
-            lax.fori_loop(0, number, body, 0)
-            ahead += number
+            lax.fori_loop(0, each, body, 0)
     for turn in range(max(0, 3 * blocks - outs_depth), 3 * blocks):
         copy_out(turn, turn % blocks, 0).wait()
 
@@ -849,45 +824,41 @@
     lower, upper = gather_blocks(loss_own, groups, beside)
     gram_sum, back_half, squares_half, values_half, down_high, rows_high = halves
 
-    more = 0
-    s_term, r_term, stats, *rest_high = call(
+    s_term, r_term, stats, held_gate = call(
         "back",
-        functools.partial(back_kernel, devices, inv_d, inv_ff, splits, up_spans, more),
+        functools.partial(back_kernel, inv_d, inv_ff, splits, up_spans),
         [
             near(one)
             for one in (
                 info, upper, down_high, rows_high, hidden, weight, act, square, squares_half,
                 back_half, gram_sum, values_half, prod_gate, *prods_up,
             )
-        ]
-        + ([(True, far(krylov_down))] if more else []),
+        ],
         [
             jax.ShapeDtypeStruct((rows, LIVE), BF16),
             jax.ShapeDtypeStruct((rows, LIVE), BF16),
             jax.ShapeDtypeStruct((basis, LANES), F32),
-        ]
-        + ([jax.ShapeDtypeStruct((more, basis, lines, halved), BF16)] if more else []),
-        [pltpu.VMEM((LIVE, halved), BF16), pltpu.VMEM((size, size), F32)]
-        + ([pltpu.SemaphoreType.DMA((more,))] if more else []),
-        [],
+        ],
+        [pltpu.VMEM((LIVE, halved), BF16), pltpu.VMEM((size, size), F32)],
+        [rows_of(after(krylov_gate, upper), 0, pieces)],
         cost(back_flops, 8 * basis * rows * LIVE),
     )
-    highs = [down_high] + rest_high
 
     stats = jnp.broadcast_to(stats[None], (devices, basis, LANES))
     stats = lax.all_to_all(stats, "fsdp", 0, 0, tiled=True)
 
-    depth, outs_depth = min(4, pieces), min(4, 3 * pieces)
+    depth, outs_depth = min(3, pieces), min(4, 3 * pieces)
+    tall = cut * lines if pieces == 2 * cut else rows
     out_shape = jax.ShapeDtypeStruct((rows, width), BF16)
     new_gate, new_up, new_down, coefficients = pl.pallas_call(
-        functools.partial(new_kernel, devices, count, inv_d, inv_ff, splits, len(highs)),
-        in_specs=[SMALL] + [FAST] * 7 + [FAR] * 3 + [FAST] * len(highs),
+        functools.partial(new_kernel, devices, count, inv_d, inv_ff, splits),
+        in_specs=[SMALL] + [FAST] * 8 + [FAR] * 2 + [FAST],
         out_specs=[FAR] * 3 + [SMALL],
         out_shape=[out_shape, out_shape, out_shape, jax.ShapeDtypeStruct((basis + 1,), F32)],
         scratch_shapes=[
             pltpu.VMEM((LIVE, width), BF16),
             pltpu.VMEM((3 * lines, size), BF16),
-            pltpu.VMEM((rows, width), F32),
+            pltpu.VMEM((tall, width), F32),
             pltpu.VMEM((depth, basis, lines, width), BF16),
             pltpu.VMEM((depth, basis, lines, halved), BF16),
             pltpu.VMEM((outs_depth, lines, width), BF16),
@@ -895,12 +866,12 @@
             pltpu.SemaphoreType.DMA((depth,)),
             pltpu.SemaphoreType.DMA((outs_depth,)),
         ],
-        compiler_params=params(22),
+        compiler_params=params(18),
         cost_estimate=cost(3 * product_flops, 6 * (basis + 1) * rows * width),
         name="new",
     )(
-        info, stats, s_term, r_term, hidden, normed, lower, upper, far(krylov_gate),
-        far(krylov_up), far(krylov_down), *highs,
+        info, stats, s_term, r_term, hidden, normed, lower, upper, held_gate,
+        far(krylov_up), far(krylov_down), down_high,
     )
     return (new_gate, new_up, new_down, coefficients)
 

time: 145 us -> 144 us (level)
  Pallas kernels: 94.4 us -> 92.5 us
    pallas_call x1, Pallas kernels: 29.6 us -> 22.7 us  [per_device(): pl.pallas_call(functools.partial(new_kernel, devices, count, inv_d, inv_f...]
    pallas_call x11, Pallas kernels: 64.8 us -> 69.9 us  [call(): pl.pallas_call(kernel, in_specs=placed, out_specs=[FAST] * (len(results)...]
where the time goes in v7:
time: 144 us
  Pallas kernels  92.5 us (64%)
  starting transfers between devices  25.7 us (18%)
  blocking collectives  12.9 us (9%)
  waiting for transfers between devices  8.07 us (6%)
  local copies, waits for them, and re-layouts  2.34 us (2%)
    pallas_call x11, Pallas kernels, call(): pl.pallas_call(kernel, in_specs=placed, out_specs=[FAST] * (len(results)...  69.9 us
    ppermute x21, starting transfers between devices, exchange(): lax.ppermute(block, 'fsdp', [(one, one ^ flip) for one in range(count)])  25.7 us
    pallas_call x1, Pallas kernels, per_device(): pl.pallas_call(functools.partial(new_kernel, devices, count, inv_d, inv_f...  22.7 us
    all_to_all x1, blocking collectives, per_device(): stats = lax.all_to_all(stats, 'fsdp', 0, 0, tiled=True)  12.9 us
    ppermute x21, waiting for transfers between devices, exchange(): lax.ppermute(block, 'fsdp', [(one, one ^ flip) for one in range(count)])  8.07 us
  transfers between devices with their start and end apart: 21, of which 5 were waited for; matrix products, arithmetic and copies ran while one was open for 1% of the time, Pallas kernels for 32%

profile of v7, /device:TPU:0, one launch (start us, length us, event | category | flops | bytes accessed | tf_op | source)
XLA Modules:
  0.0 143.9 jit_solution(8919763034223151261)
XLA Ops:
  0.6 5.1 %collective-permute-start.2 = (bf16[1,8,4096]{2,1,0:T(8,128)(2,1)}, bf16[1,8,4096]{2,1,0:T(8,128)(2,1)S(1)}, u32[]{:S(2)}, u32[]{:S(2)}) collective-permute-start(bf16[1,8,4096]{2,1,0:T(8,128)(2,1)} %bitcast.4), channel_id=1, source_target_pairs={{0,24},{1,25},{2,26},{3,27},{4,28},{5,29},{6,30},{7,31},{8,16},{9,... | collective-permute-start | bytes 196616 | tf_op jit(solution)/shard_map/ppermute | solution.py:55
  5.7 0.6 collective-permute-start
  6.4 0.9 constant_dynamic-update-slice_fusion.6
  7.3 0.7 pad_add_fusion.refs_0_.info
  8.0 4.6 %read.1.refs_1_.refs_2_ = bf16[5,8,32,4096]{3,2,1,0:T(8,128)(2,1)S(1)} custom-call(s32[2]{0:T(128)S(1)} %pad_add_fusion.refs_0_.info, bf16[8,320,4096]{2,1,0:T(8,128)(2,1)} %refs_16_), custom_call_target="tpu_custom_call" | custom-call | flops 536870912 | bytes 10485760 | tf_op jit(solution)/shard_map/read/pallas_call | solution.py:141
  12.7 2.7 %collective-permute-start.5 = (bf16[4,8,4096]{2,1,0:T(8,128)(2,1)S(1)}, bf16[4,8,4096]{2,1,0:T(8,128)(2,1)S(1)}, u32[]{:S(2)}, u32[]{:S(2)}) collective-permute-start(bf16[4,8,4096]{2,1,0:T(8,128)(2,1)S(1)} %pad_maximum_fusion), channel_id=1, source_target_pairs={{0,6},{1,7},{2,4},{3,5},{4,2},{5,3},{6,0},{7,1},{8,14},{9,15},{10,... | collective-permute-start | bytes 786440 | tf_op jit(solution)/shard_map/ppermute | solution.py:55
  15.4 0.5 collective-permute-start.4
  15.9 0.4 collective-permute-start.3
  16.3 0.0 copy-start.5
  16.3 4.7 %gram.2 = (f32[256,256]{1,0:T(8,128)S(1)}, bf16[5,8,32,4096]{3,2,1,0:T(8,128)(2,1)S(1)}) custom-call(s32[2]{0:T(128)S(1)} %pad_add_fusion.refs_0_.info, bf16[5,8,32,4096]{3,2,1,0:T(8,128)(2,1)S(1)} %read.1.refs_1_.refs_2_, bf16[8,320,4096]{2,1,0:T(8,128)(2,1)} %refs_16_), custom_call_target="tpu_custom_call" | custom-call | flops 2684354560 | bytes 10485760 | tf_op jit(solution)/shard_map/gram/pallas_call | solution.py:141
  21.0 2.0 %collective-permute-done.5 = bf16[4,8,4096]{2,1,0:T(8,128)(2,1)S(1)} collective-permute-done((bf16[4,8,4096]{2,1,0:T(8,128)(2,1)S(1)}, bf16[4,8,4096]{2,1,0:T(8,128)(2,1)S(1)}, u32[]{:S(2)}, u32[]{:S(2)}) %collective-permute-start.5) | collective-permute-done | bytes 262176 | tf_op jit(solution)/shard_map/ppermute | solution.py:55
  23.0 3.9 %collective-permute-done.4 = bf16[4,8,4096]{2,1,0:T(8,128)(2,1)S(1)} collective-permute-done((bf16[4,8,4096]{2,1,0:T(8,128)(2,1)S(1)}, bf16[4,8,4096]{2,1,0:T(8,128)(2,1)S(1)}, u32[]{:S(2)}, u32[]{:S(2)}) %collective-permute-start.4) | collective-permute-done | bytes 262176 | tf_op jit(solution)/shard_map/ppermute | solution.py:55
  27.0 0.0 copy-start.2
  27.0 0.1 collective-permute-start.6
  27.1 4.3 %gram.3.refs_2_ = f32[256,256]{1,0:T(8,128)S(1)} custom-call(s32[2]{0:T(128)S(1)} %pad_add_fusion.refs_0_.info, bf16[5,8,32,4096]{3,2,1,0:T(8,128)(2,1)S(1)} %get-tuple-element.101.refs_1_.refs_3_, f32[256,256]{1,0:T(8,128)S(1)} %get-tuple-element.102.refs_2_), custom_call_target="tpu_custom_call" | custom-call | flops 2684354560 | bytes 10485760 | tf_op jit(solution)/shard_map/gram/pallas_call | solution.py:141
  31.4 1.2 copy-done.3
  32.6 10.6 %forward.1 = (bf16[192,4096]{1,0:T(8,128)(2,1)S(1)}, bf16[320,192]{1,0:T(8,128)(2,1)S(1)}, bf16[192,320]{1,0:T(8,128)(2,1)S(1)}, bf16[192,320]{1,0:T(8,128)(2,1)...) custom-call(s32[2]{0:T(128)S(1)} %pad_add_fusion.refs_0_.info, ...), custom_call_target="tpu_custom_call" | custom-call | flops 2516582400 | bytes 15728640 | tf_op jit(solution)/shard_map/forward/pallas_call | solution.py:141
  43.3 0.6 collective-permute-start.7
  43.8 1.6 %keep.1 = f32[16,192,128]{2,1,0:T(8,128)S(1)} custom-call(s32[2]{0:T(128)S(1)} %pad_add_fusion.refs_0_.info, bf16[192,320]{1,0:T(8,128)(2,1)S(1)} %get-tuple-element.104.refs_1_, bf16[192,320]{1,0:T(8,128)(2,1)S(1)} %get-tuple-element.105.refs_2_, bf16[2,320,2048]{2,1,0:T(8,128)(2,1)S(1)} %get-tuple-element.106.refs_3_), custom_call_target="tpu_custom_call" | custom-call | flops 503316480 | bytes 4194304 | tf_op jit(solution)/shard_map/keep/pallas_call | solution.py:141
  45.4 0.3 collective-permute-done.7
  45.7 0.2 fusion
  46.0 1.5 %collective-permute-start.8 = (bf16[4,192,128]{2,1,0:T(8,128)(2,1)S(1)}, bf16[4,192,128]{2,1,0:T(8,128)(2,1)S(1)}, u32[]{:S(2)}, u32[]{:S(2)}) collective-permute-start(bf16[4,192,128]{2,1,0:T(8,128)(2,1)S(1)} %get-tuple-element.180), channel_id=1, source_target_pairs={{0,4},{1,5},{2,6},{3,7},{4,0},{5,1},{6,2},{7,3},{8,12},{9,13},{10,... | collective-permute-start | bytes 589832 | tf_op jit(solution)/shard_map/ppermute | solution.py:55
  47.4 1.5 %collective-permute-start.10 = (bf16[4,192,128]{2,1,0:T(8,128)(2,1)S(1)}, bf16[4,192,128]{2,1,0:T(8,128)(2,1)S(1)}, u32[]{:S(2)}, u32[]{:S(2)}) collective-permute-start(bf16[4,192,128]{2,1,0:T(8,128)(2,1)S(1)} %get-tuple-element.178), channel_id=1, source_target_pairs={{0,6},{1,7},{2,4},{3,5},{4,2},{5,3},{6,0},{7,1},{8,14},{9,15},{10,... | collective-permute-start | bytes 589832 | tf_op jit(solution)/shard_map/ppermute | solution.py:55
  49.0 0.5 collective-permute-start.9
  49.5 8.4 %product.1 = (f32[8,320,192]{2,1,0:T(8,128)S(1)}, f32[192,192]{1,0:T(8,128)S(1)}, bf16[4,8,32,4096]{3,2,1,0:T(8,128)(2,1)S(1)}) custom-call(s32[2]{0:T(128)S(1)} %pad_add_fusion.refs_0_.info, bf16[192,4096]{1,0:T(8,128)(2,1)S(1)} %get-tuple-element.108.refs_1_.normed, bf16[5,8,32,4096]{3,2,1,0:T(8,128)(2,1)S(1)} %read.1.refs_1_.refs_2_, ...), custom_call_target="tpu_custom_call" | custom-call | flops 4026531840 | bytes 8388608 | tf_op jit(solution)/shard_map/product/pallas_call | solution.py:141
  57.9 0.0 copy-start
  58.0 0.7 collective-permute-done.9
  58.6 0.1 fusion.4
  58.7 2.4 %collective-permute-start.11 = (bf16[1,192,128]{2,1,0:T(8,128)(2,1)S(1)}, bf16[1,192,128]{2,1,0:T(8,128)(2,1)S(1)}, u32[]{:S(2)}, u32[]{:S(2)}) collective-permute-start(bf16[1,192,128]{2,1,0:T(8,128)(2,1)S(1)} %get-tuple-element.184), channel_id=1, source_target_pairs={{0,16},{1,17},{2,18},{3,19},{4,20},{5,21},{6,22},{7,23},{8,24},{9,... | collective-permute-start | bytes 147464 | tf_op jit(solution)/shard_map/ppermute | solution.py:55
  61.1 1.5 %collective-permute-start.13 = (bf16[1,192,128]{2,1,0:T(8,128)(2,1)S(1)}, bf16[1,192,128]{2,1,0:T(8,128)(2,1)S(1)}, u32[]{:S(2)}, u32[]{:S(2)}) collective-permute-start(bf16[1,192,128]{2,1,0:T(8,128)(2,1)S(1)} %get-tuple-element.182), channel_id=1, source_target_pairs={{0,24},{1,25},{2,26},{3,27},{4,28},{5,29},{6,30},{7,31},{8,16},{9,... | collective-permute-start | bytes 147464 | tf_op jit(solution)/shard_map/ppermute | solution.py:55
  62.6 0.2 collective-permute-start.12
  62.8 5.7 %both.3 = (f32[8,128,192]{2,1,0:T(8,128)S(1)}, f32[256,256]{1,0:T(8,128)S(1)}, bf16[3,8,32,4096]{3,2,1,0:T(8,128)(2,1)S(1)}) custom-call(s32[2]{0:T(128)S(1)} %pad_add_fusion.refs_0_.info, bf16[192,4096]{1,0:T(8,128)(2,1)S(1)} %get-tuple-element.108.refs_1_.normed, f32[256,256]{1,0:T(8,128)S(1)} %gram.3.refs_2_, ...), custom_call_target="tpu_custom_call" | custom-call | flops 3758096384 | bytes 8388608 | tf_op jit(solution)/shard_map/both/pallas_call | solution.py:141
  68.5 0.1 constant_dynamic-update-slice_fusion.13
  68.6 3.0 %collective-permute-start.16 = (bf16[1,192,128]{2,1,0:T(8,128)(2,1)S(1)}, bf16[1,192,128]{2,1,0:T(8,128)(2,1)S(1)}, u32[]{:S(2)}, u32[]{:S(2)}) collective-permute-start(bf16[1,192,128]{2,1,0:T(8,128)(2,1)S(1)} %get-tuple-element.177), channel_id=1, source_target_pairs={{0,24},{1,25},{2,26},{3,27},{4,28},{5,29},{6,30},{7,31},{8,16},{9,... | collective-permute-start | bytes 147464 | tf_op jit(solution)/shard_map/ppermute | solution.py:55
  71.6 0.3 collective-permute-start.15
  71.9 1.2 collective-permute-start.14
  73.0 4.4 %both.4 = (f32[8,96,192]{2,1,0:T(8,128)S(1)}, f32[256,256]{1,0:T(8,128)S(1)}, bf16[3,8,32,4096]{3,2,1,0:T(8,128)(2,1)S(1)}) custom-call(s32[2]{0:T(128)S(1)} %pad_add_fusion.refs_0_.info, bf16[192,4096]{1,0:T(8,128)(2,1)S(1)} %get-tuple-element.108.refs_1_.normed, f32[256,256]{1,0:T(8,128)S(1)} %get-tuple-element.125.refs_2_, ...), custom_call_target="tpu_custom_call" | custom-call | flops 2818572288 | bytes 6291456 | tf_op jit(solution)/shard_map/both/pallas_call | solution.py:141
  77.5 2.4 %collective-permute-start.19 = (bf16[4,192,128]{2,1,0:T(8,128)(2,1)S(1)}, bf16[4,192,128]{2,1,0:T(8,128)(2,1)S(1)}, u32[]{:S(2)}, u32[]{:S(2)}) collective-permute-start(bf16[4,192,128]{2,1,0:T(8,128)(2,1)S(1)} %pad_maximum_fusion.1), channel_id=1, source_target_pairs={{0,6},{1,7},{2,4},{3,5},{4,2},{5,3},{6,0},{7,1},{8,14},{9,15},{10,... | collective-permute-start | bytes 589832 | tf_op jit(solution)/shard_map/ppermute | solution.py:55
  79.9 0.5 collective-permute-start.18
  80.5 0.6 collective-permute-start.17
  81.1 5.1 %both.5 = (f32[8,96,192]{2,1,0:T(8,128)S(1)}, f32[256,256]{1,0:T(8,128)S(1)}, bf16[10,8,32,2048]{3,2,1,0:T(8,128)(2,1)S(1)}, bf16[1,320,2048]{2,1,0:T(8,128)(2,1)S(1)}) custom-call(s32[2]{0:T(128)S(1)} %pad_add_fusion.refs_0_.info, bf16[192,4096]{1,0:T(8,128)(2,1)S(1)} %get-tuple-element.108.refs_1_.normed, f32[256,256]{1,0:T(8,128)S(1)} %get-tuple-element.134.refs_2_, ...), custom_call_target="tpu_custom_call" | custom-call | flops 2818572288 | bytes 6291456 | tf_op jit(solution)/shard_map/both/pallas_call | solution.py:141
  86.2 1.1 collective-permute-done.18
  87.4 0.1 collective-permute-start.20
  87.5 0.0 copy-start.1
  87.5 6.9 %back_half.1 = (f32[256,256]{1,0:T(8,128)S(1)}, f32[320,192]{1,0:T(8,128)S(1)}, f32[2,192,192]{2,1,0:T(8,128)S(1)}, f32[8,192]{1,0:T(8,128)S(1)}, bf16[10,8,32,2...) custom-call(s32[2]{0:T(128)S(1)} %pad_add_fusion.refs_0_.info, ...), custom_call_target="tpu_custom_call" | custom-call | flops 4949278720 | bytes 11796480 | tf_op jit(solution)/shard_map/back_half/pallas_call | solution.py:141
  94.5 13.6 %back.1 = (bf16[320,192]{1,0:T(8,128)(2,1)S(1)}, bf16[320,192]{1,0:T(8,128)(2,1)S(1)}, f32[8,128]{1,0:T(8,128)S(1)}, bf16[10,8,32,4096]{3,2,1,0:T(8,128)(2,1)S(1)}) custom-call(s32[2]{0:T(128)S(1)} %pad_add_fusion.refs_0_.info, bf16[16,192,128]{2,1,0:T(8,128)(2,1)S(1)} %collective-permute-done.20.refs_1_.upper, ...), custom_call_target="tpu_custom_call" | custom-call | flops 4949278720 | bytes 3932160 | tf_op jit(solution)/shard_map/back/pallas_call | solution.py:141
  108.1 12.9 %all_to_all.5.stats = f32[32,8,128]{2,1,0:T(8,128)S(1)} all-to-all(f32[32,8,128]{2,1,0:T(8,128)S(1)} %broadcast_in_dim.2), channel_id=1, replica_groups=mesh['fsdp'=32] {'fsdp'}, dimensions={0} | all-to-all | bytes 262144 | tf_op jit(solution)/shard_map/all_to_all | solution.py:848
  121.0 22.7 %new.1 = (bf16[320,4096]{1,0:T(8,128)(2,1)}, bf16[320,4096]{1,0:T(8,128)(2,1)}, bf16[320,4096]{1,0:T(8,128)(2,1)}, f32[9]{0:T(128)}) custom-call(s32[2]{0:T(128)S(1)} %pad_add_fusion.refs_0_.info, f32[32,8,128]{2,1,0:T(8,128)S(1)} %all_to_all.5.stats, bf16[320,192]{1,0:T(8,128)(2,1)S(1)} %get-tuple-element.173.s_term, ...), custom_call_target="tpu_custom_call" | custom-call | flops 1509949440 | bytes 70778880 | tf_op jit(solution)/shard_map/new/pallas_call | solution.py:853
  (40 shorter events, 0.3 us)
Async XLA Ops:
  0.6 12.0 %collective-permute-start.2 = (bf16[1,8,4096]{2,1,0:T(8,128)(2,1)}, bf16[1,8,4096]{2,1,0:T(8,128)(2,1)S(1)}, u32[]{:S(2)}, u32[]{:S(2)}) collective-permute-start(bf16[1,8,4096]{2,1,0:T(8,128)(2,1)} %bitcast.4), channel_id=1, source_target_pairs={{0,24},{1,25},{2,26},{3,27},{4,28},{5,29},{6,30},{7,31},{8,16},{9,... | collective-permute-start | bytes 196616 | tf_op jit(solution)/shard_map/ppermute | solution.py:55
  5.7 6.9 %collective-permute-start.1 = (bf16[1,8,4096]{2,1,0:T(8,128)(2,1)}, bf16[1,8,4096]{2,1,0:T(8,128)(2,1)S(1)}, u32[]{:S(2)}, u32[]{:S(2)}) collective-permute-start(bf16[1,8,4096]{2,1,0:T(8,128)(2,1)} %bitcast.5), channel_id=1, source_target_pairs={{0,8},{1,9},{2,10},{3,11},{4,12},{5,13},{6,14},{7,15},{8,0},{9,1},... | collective-permute-start | bytes 196616 | tf_op jit(solution)/shard_map/ppermute | solution.py:55
  5.7 6.9 %collective-permute-start = (bf16[1,8,4096]{2,1,0:T(8,128)(2,1)}, bf16[1,8,4096]{2,1,0:T(8,128)(2,1)S(1)}, u32[]{:S(2)}, u32[]{:S(2)}) collective-permute-start(bf16[1,8,4096]{2,1,0:T(8,128)(2,1)} %bitcast.6), channel_id=1, source_target_pairs={{0,16},{1,17},{2,18},{3,19},{4,20},{5,21},{6,22},{7,23},{8,24},{9,... | collective-permute-start | bytes 196616 | tf_op jit(solution)/shard_map/ppermute | solution.py:55
  8.0 4.7 %copy-start.4 = (bf16[8,4096]{1,0:T(8,128)(2,1)S(1)}, bf16[8,4096]{1,0:T(8,128)(2,1)}, u32[]{:S(2)}) copy-start(bf16[8,4096]{1,0:T(8,128)(2,1)} %param.9) | copy-start | bytes 196612
  12.7 10.3 %collective-permute-start.5 = (bf16[4,8,4096]{2,1,0:T(8,128)(2,1)S(1)}, bf16[4,8,4096]{2,1,0:T(8,128)(2,1)S(1)}, u32[]{:S(2)}, u32[]{:S(2)}) collective-permute-start(bf16[4,8,4096]{2,1,0:T(8,128)(2,1)S(1)} %pad_maximum_fusion), channel_id=1, source_target_pairs={{0,6},{1,7},{2,4},{3,5},{4,2},{5,3},{6,0},{7,1},{8,14},{9,15},{10,... | collective-permute-start | bytes 786440 | tf_op jit(solution)/shard_map/ppermute | solution.py:55
  15.4 11.5 %collective-permute-start.4 = (bf16[4,8,4096]{2,1,0:T(8,128)(2,1)S(1)}, bf16[4,8,4096]{2,1,0:T(8,128)(2,1)S(1)}, u32[]{:S(2)}, u32[]{:S(2)}) collective-permute-start(bf16[4,8,4096]{2,1,0:T(8,128)(2,1)S(1)} %pad_maximum_fusion), channel_id=1, source_target_pairs={{0,2},{1,3},{2,0},{3,1},{4,6},{5,7},{6,4},{7,5},{8,10},{9,11},{10,... | collective-permute-start | bytes 786440 | tf_op jit(solution)/shard_map/ppermute | solution.py:55
  15.9 11.0 %collective-permute-start.3 = (bf16[4,8,4096]{2,1,0:T(8,128)(2,1)S(1)}, bf16[4,8,4096]{2,1,0:T(8,128)(2,1)S(1)}, u32[]{:S(2)}, u32[]{:S(2)}) collective-permute-start(bf16[4,8,4096]{2,1,0:T(8,128)(2,1)S(1)} %pad_maximum_fusion), channel_id=1, source_target_pairs={{0,4},{1,5},{2,6},{3,7},{4,0},{5,1},{6,2},{7,3},{8,12},{9,13},{10,... | collective-permute-start | bytes 786440 | tf_op jit(solution)/shard_map/ppermute | solution.py:55
  16.3 10.8 %copy-start.5 = (bf16[4096]{0:T(1024)(128)(2,1)S(1)}, bf16[4096]{0:T(1024)(128)(2,1)}, u32[]{:S(2)}) copy-start(bf16[4096]{0:T(1024)(128)(2,1)} %param.10) | copy-start | bytes 24580
  27.0 4.4 %copy-start.2 = (bf16[16,8,4096]{2,1,0:T(8,128)(2,1)}, bf16[16,8,4096]{2,1,0:T(8,128)(2,1)S(1)}, u32[]{:S(2)}) copy-start(bf16[16,8,4096]{2,1,0:T(8,128)(2,1)S(1)} %constant_dynamic-update-slice_fusion.refs_1_) | copy-start | bytes 3145732
  27.0 4.4 %collective-permute-start.6 = (bf16[16,8,4096]{2,1,0:T(8,128)(2,1)S(1)}, bf16[16,8,4096]{2,1,0:T(8,128)(2,1)S(1)}, u32[]{:S(2)}, u32[]{:S(2)}) collective-permute-start(bf16[16,8,4096]{2,1,0:T(8,128)(2,1)S(1)} %constant_dynamic-update-slice_fusion.refs_1_), channel_id=1, source_target_pairs={{0,1},{1,0},{2,3},{3,2},{4,5},{5,4},{6,7},{7,6},{8,9},{9,8},{10,11... | collective-permute-start | bytes 3145736 | tf_op jit(solution)/shard_map/ppermute | solution.py:55
  31.4 1.2 copy-start.3
  43.3 2.5 %collective-permute-start.7 = (bf16[16,192,128]{2,1,0:T(8,128)(2,1)S(1)}, bf16[16,192,128]{2,1,0:T(8,128)(2,1)S(1)}, u32[]{:S(2)}, u32[]{:S(2)}) collective-permute-start(bf16[16,192,128]{2,1,0:T(8,128)(2,1)S(1)} %get-tuple-element.107), channel_id=1, source_target_pairs={{0,1},{1,0},{2,3},{3,2},{4,5},{5,4},{6,7},{7,6},{8,9},{9,8},{10,11... | collective-permute-start | bytes 2359304 | tf_op jit(solution)/shard_map/ppermute | solution.py:55
  46.0 12.7 %collective-permute-start.8 = (bf16[4,192,128]{2,1,0:T(8,128)(2,1)S(1)}, bf16[4,192,128]{2,1,0:T(8,128)(2,1)S(1)}, u32[]{:S(2)}, u32[]{:S(2)}) collective-permute-start(bf16[4,192,128]{2,1,0:T(8,128)(2,1)S(1)} %get-tuple-element.180), channel_id=1, source_target_pairs={{0,4},{1,5},{2,6},{3,7},{4,0},{5,1},{6,2},{7,3},{8,12},{9,13},{10,... | collective-permute-start | bytes 589832 | tf_op jit(solution)/shard_map/ppermute | solution.py:55
  47.4 10.5 %collective-permute-start.10 = (bf16[4,192,128]{2,1,0:T(8,128)(2,1)S(1)}, bf16[4,192,128]{2,1,0:T(8,128)(2,1)S(1)}, u32[]{:S(2)}, u32[]{:S(2)}) collective-permute-start(bf16[4,192,128]{2,1,0:T(8,128)(2,1)S(1)} %get-tuple-element.178), channel_id=1, source_target_pairs={{0,6},{1,7},{2,4},{3,5},{4,2},{5,3},{6,0},{7,1},{8,14},{9,15},{10,... | collective-permute-start | bytes 589832 | tf_op jit(solution)/shard_map/ppermute | solution.py:55
  49.0 9.7 %collective-permute-start.9 = (bf16[4,192,128]{2,1,0:T(8,128)(2,1)S(1)}, bf16[4,192,128]{2,1,0:T(8,128)(2,1)S(1)}, u32[]{:S(2)}, u32[]{:S(2)}) collective-permute-start(bf16[4,192,128]{2,1,0:T(8,128)(2,1)S(1)} %get-tuple-element.179), channel_id=1, source_target_pairs={{0,2},{1,3},{2,0},{3,1},{4,6},{5,7},{6,4},{7,5},{8,10},{9,11},{10,... | collective-permute-start | bytes 589832 | tf_op jit(solution)/shard_map/ppermute | solution.py:55
  57.9 10.5 %copy-start = (f32[8,320,192]{2,1,0:T(8,128)}, f32[8,320,192]{2,1,0:T(8,128)S(1)}, u32[]{:S(2)}) copy-start(f32[8,320,192]{2,1,0:T(8,128)S(1)} %get-tuple-element.167.refs_12_) | copy-start | bytes 5898244
  58.7 9.8 %collective-permute-start.11 = (bf16[1,192,128]{2,1,0:T(8,128)(2,1)S(1)}, bf16[1,192,128]{2,1,0:T(8,128)(2,1)S(1)}, u32[]{:S(2)}, u32[]{:S(2)}) collective-permute-start(bf16[1,192,128]{2,1,0:T(8,128)(2,1)S(1)} %get-tuple-element.184), channel_id=1, source_target_pairs={{0,16},{1,17},{2,18},{3,19},{4,20},{5,21},{6,22},{7,23},{8,24},{9,... | collective-permute-start | bytes 147464 | tf_op jit(solution)/shard_map/ppermute | solution.py:55
  61.1 7.4 %collective-permute-start.13 = (bf16[1,192,128]{2,1,0:T(8,128)(2,1)S(1)}, bf16[1,192,128]{2,1,0:T(8,128)(2,1)S(1)}, u32[]{:S(2)}, u32[]{:S(2)}) collective-permute-start(bf16[1,192,128]{2,1,0:T(8,128)(2,1)S(1)} %get-tuple-element.182), channel_id=1, source_target_pairs={{0,24},{1,25},{2,26},{3,27},{4,28},{5,29},{6,30},{7,31},{8,16},{9,... | collective-permute-start | bytes 147464 | tf_op jit(solution)/shard_map/ppermute | solution.py:55
  62.6 5.9 %collective-permute-start.12 = (bf16[1,192,128]{2,1,0:T(8,128)(2,1)S(1)}, bf16[1,192,128]{2,1,0:T(8,128)(2,1)S(1)}, u32[]{:S(2)}, u32[]{:S(2)}) collective-permute-start(bf16[1,192,128]{2,1,0:T(8,128)(2,1)S(1)} %get-tuple-element.183), channel_id=1, source_target_pairs={{0,8},{1,9},{2,10},{3,11},{4,12},{5,13},{6,14},{7,15},{8,0},{9,1},... | collective-permute-start | bytes 147464 | tf_op jit(solution)/shard_map/ppermute | solution.py:55
  68.6 8.9 %collective-permute-start.16 = (bf16[1,192,128]{2,1,0:T(8,128)(2,1)S(1)}, bf16[1,192,128]{2,1,0:T(8,128)(2,1)S(1)}, u32[]{:S(2)}, u32[]{:S(2)}) collective-permute-start(bf16[1,192,128]{2,1,0:T(8,128)(2,1)S(1)} %get-tuple-element.177), channel_id=1, source_target_pairs={{0,24},{1,25},{2,26},{3,27},{4,28},{5,29},{6,30},{7,31},{8,16},{9,... | collective-permute-start | bytes 147464 | tf_op jit(solution)/shard_map/ppermute | solution.py:55
  71.6 5.9 %collective-permute-start.15 = (bf16[1,192,128]{2,1,0:T(8,128)(2,1)S(1)}, bf16[1,192,128]{2,1,0:T(8,128)(2,1)S(1)}, u32[]{:S(2)}, u32[]{:S(2)}) collective-permute-start(bf16[1,192,128]{2,1,0:T(8,128)(2,1)S(1)} %get-tuple-element.177), channel_id=1, source_target_pairs={{0,8},{1,9},{2,10},{3,11},{4,12},{5,13},{6,14},{7,15},{8,0},{9,1},... | collective-permute-start | bytes 147464 | tf_op jit(solution)/shard_map/ppermute | solution.py:55
  71.9 5.6 %collective-permute-start.14 = (bf16[1,192,128]{2,1,0:T(8,128)(2,1)S(1)}, bf16[1,192,128]{2,1,0:T(8,128)(2,1)S(1)}, u32[]{:S(2)}, u32[]{:S(2)}) collective-permute-start(bf16[1,192,128]{2,1,0:T(8,128)(2,1)S(1)} %get-tuple-element.177), channel_id=1, source_target_pairs={{0,16},{1,17},{2,18},{3,19},{4,20},{5,21},{6,22},{7,23},{8,24},{9,... | collective-permute-start | bytes 147464 | tf_op jit(solution)/shard_map/ppermute | solution.py:55
  77.5 8.7 %collective-permute-start.19 = (bf16[4,192,128]{2,1,0:T(8,128)(2,1)S(1)}, bf16[4,192,128]{2,1,0:T(8,128)(2,1)S(1)}, u32[]{:S(2)}, u32[]{:S(2)}) collective-permute-start(bf16[4,192,128]{2,1,0:T(8,128)(2,1)S(1)} %pad_maximum_fusion.1), channel_id=1, source_target_pairs={{0,6},{1,7},{2,4},{3,5},{4,2},{5,3},{6,0},{7,1},{8,14},{9,15},{10,... | collective-permute-start | bytes 589832 | tf_op jit(solution)/shard_map/ppermute | solution.py:55
  79.9 7.4 %collective-permute-start.18 = (bf16[4,192,128]{2,1,0:T(8,128)(2,1)S(1)}, bf16[4,192,128]{2,1,0:T(8,128)(2,1)S(1)}, u32[]{:S(2)}, u32[]{:S(2)}) collective-permute-start(bf16[4,192,128]{2,1,0:T(8,128)(2,1)S(1)} %pad_maximum_fusion.1), channel_id=1, source_target_pairs={{0,2},{1,3},{2,0},{3,1},{4,6},{5,7},{6,4},{7,5},{8,10},{9,11},{10,... | collective-permute-start | bytes 589832 | tf_op jit(solution)/shard_map/ppermute | solution.py:55
  80.5 6.9 %collective-permute-start.17 = (bf16[4,192,128]{2,1,0:T(8,128)(2,1)S(1)}, bf16[4,192,128]{2,1,0:T(8,128)(2,1)S(1)}, u32[]{:S(2)}, u32[]{:S(2)}) collective-permute-start(bf16[4,192,128]{2,1,0:T(8,128)(2,1)S(1)} %pad_maximum_fusion.1), channel_id=1, source_target_pairs={{0,4},{1,5},{2,6},{3,7},{4,0},{5,1},{6,2},{7,3},{8,12},{9,13},{10,... | collective-permute-start | bytes 589832 | tf_op jit(solution)/shard_map/ppermute | solution.py:55
  87.4 7.0 %collective-permute-start.20 = (bf16[16,192,128]{2,1,0:T(8,128)(2,1)S(1)}, bf16[16,192,128]{2,1,0:T(8,128)(2,1)S(1)}, u32[]{:S(2)}, u32[]{:S(2)}) collective-permute-start(bf16[16,192,128]{2,1,0:T(8,128)(2,1)S(1)} %constant_dynamic-update-slice_fusion.7.refs_1_.lower), channel_id=1, source_target_pairs={{0,1},{1,0},{2,3},{3,2},{4,5},{5,4},{6,7},{7,6},{8,9},{9,8},{10,11... | collective-permute-start | bytes 2359304 | tf_op jit(solution)/shard_map/ppermute | solution.py:55
  87.5 7.0 %copy-start.1 = (f32[8,320,192]{2,1,0:T(8,128)S(1)}, f32[8,320,192]{2,1,0:T(8,128)}, u32[]{:S(2)}) copy-start(f32[8,320,192]{2,1,0:T(8,128)} %copy-done) | copy-start | bytes 5898244

commit v8 on v7

--- a/solution.py
+++ b/solution.py
@@ -428,7 +428,7 @@
 
 def new_kernel(
     devices, count, inv_d, inv_ff, splits,
-    info, stats, s_term, r_term, hidden, normed, lower, upper, gate, krylov_up,
+    info, stats, s_term, r_term, hidden, normed, lower, upper, krylov_gate, krylov_up,
     krylov_down, high,
     new_gate, new_up, new_down, coefficients,
     loss, mixer, wide, held, held_low, outs, sems, low_sems, out_sems,
@@ -444,10 +444,12 @@
     low_start = half_start(info[0], devices, width, 0)
     high_start = half_start(info[0], devices, width, 1)
 
-    def copy_in(block):
+    def copy_in(turn, part):
+        block = turn - part * blocks
         here = pl.ds(pl.multiple_of(block * lines, lines), lines)
-        slot = lax.rem(block, depth)
-        return pltpu.make_async_copy(krylov_up.at[:, here, :], held.at[slot], sems.at[slot])
+        slot = lax.rem(turn, depth)
+        source = (krylov_gate, krylov_up)[part]
+        return pltpu.make_async_copy(source.at[:, here, :], held.at[slot], sems.at[slot])
 
     def copy_low(block):
         here = pl.ds(pl.multiple_of(block * lines, lines), lines)
@@ -465,8 +467,8 @@
 
     for block in range(low_depth):
         copy_low(block).start()
-    for block in range(depth):
-        copy_in(block).start()
+    for turn in range(depth):
+        copy_in(turn, 0).start()
 
     for at, half in enumerate((lower, upper)):
         put_loss(loss, at * halved, info[0], half, splits)
@@ -512,17 +514,18 @@
             copy_out(turn, block, part).wait()
 
         for first, last, target, read in pieces:
-            for start in range(0, last - first, group):
-                mixed = dot_nn(mixer[...], stacked(read(slice(start, start + group))))
+            broad = min(2048, last - first)
+            for start in range(0, last - first, broad):
+                mixed = dot_nn(mixer[...], stacked(read(slice(start, start + broad))))
                 mixed = mixed[:lines] + (mixed[lines : 2 * lines] + mixed[2 * lines :])
-                value = wide[here, first + start : first + start + group] - mixed
-                goal = pl.ds(pl.multiple_of(target + start, group), group)
+                value = wide[here, first + start : first + start + broad] - mixed
+                goal = pl.ds(pl.multiple_of(target + start, broad), broad)
                 outs[slot, :, goal] = value.astype(BF16)
         copy_out(turn, block, part).start()
 
     tall = wide.shape[0]
     each = tall // lines
-    for order, part in enumerate((0, 2, 1)):
+    for order, part in enumerate((2, 0, 1)):
         left, right, scale = (
             (s_term, normed, inv_d), (r_term, normed, inv_d), (hidden, loss, inv_ff)
         )[part]
@@ -536,12 +539,11 @@
             def body(at, carry, part=part, order=order, share=share):
                 block = share * each + at
                 here = pl.ds(pl.multiple_of(at * lines, lines), lines)
-                slot = lax.rem(block, depth)
+                turn = part * blocks + block
+                slot = lax.rem(turn, depth)
                 low_slot = lax.rem(block, low_depth)
-                if part == 0:
-                    pieces = [(0, width, 0, lambda columns: gate[block, :, :, columns])]
-                elif part == 1:
-                    copy_in(block).wait()
+                if part != 2:
+                    copy_in(turn, part).wait()
                     pieces = [(0, width, 0, lambda columns: held[slot, :, :, columns])]
                 else:
                     copy_low(block).wait()
@@ -550,12 +552,17 @@
                         (halved, width, high_start, lambda columns: high[block, :, :, columns]),
                     ]
                 put(order * blocks + block, here, block, part, pieces)
-                if part == 1:
-                    @pl.when(block + depth < blocks)
-                    def _():
-                        copy_in(block + depth).start()
-
-                elif part == 2:
+                if part != 2:
+                    for later in range(part, 2):
+                        there = (turn + depth >= later * blocks) & (
+                            turn + depth < (later + 1) * blocks
+                        )
+
+                        @pl.when(there)
+                        def _(later=later):
+                            copy_in(turn + depth, later).start()
+
+                else:
                     @pl.when(block + low_depth < blocks)
                     def _():
                         copy_low(block + low_depth).start()
@@ -824,7 +831,7 @@
     lower, upper = gather_blocks(loss_own, groups, beside)
     gram_sum, back_half, squares_half, values_half, down_high, rows_high = halves
 
-    s_term, r_term, stats, held_gate = call(
+    s_term, r_term, stats = call(
         "back",
         functools.partial(back_kernel, inv_d, inv_ff, splits, up_spans),
         [
@@ -840,19 +847,19 @@
             jax.ShapeDtypeStruct((basis, LANES), F32),
         ],
         [pltpu.VMEM((LIVE, halved), BF16), pltpu.VMEM((size, size), F32)],
-        [rows_of(after(krylov_gate, upper), 0, pieces)],
+        [],
         cost(back_flops, 8 * basis * rows * LIVE),
     )
 
     stats = jnp.broadcast_to(stats[None], (devices, basis, LANES))
     stats = lax.all_to_all(stats, "fsdp", 0, 0, tiled=True)
 
-    depth, outs_depth = min(3, pieces), min(4, 3 * pieces)
+    depth, outs_depth = min(6, pieces), min(4, 3 * pieces)
     tall = cut * lines if pieces == 2 * cut else rows
     out_shape = jax.ShapeDtypeStruct((rows, width), BF16)
     new_gate, new_up, new_down, coefficients = pl.pallas_call(
         functools.partial(new_kernel, devices, count, inv_d, inv_ff, splits),
-        in_specs=[SMALL] + [FAST] * 8 + [FAR] * 2 + [FAST],
+        in_specs=[SMALL] + [FAST] * 7 + [FAR] * 3 + [FAST],
         out_specs=[FAR] * 3 + [SMALL],
         out_shape=[out_shape, out_shape, out_shape, jax.ShapeDtypeStruct((basis + 1,), F32)],
         scratch_shapes=[
@@ -860,17 +867,17 @@
             pltpu.VMEM((3 * lines, size), BF16),
             pltpu.VMEM((tall, width), F32),
             pltpu.VMEM((depth, basis, lines, width), BF16),
-            pltpu.VMEM((depth, basis, lines, halved), BF16),
+            pltpu.VMEM((min(4, depth), basis, lines, halved), BF16),
             pltpu.VMEM((outs_depth, lines, width), BF16),
             pltpu.SemaphoreType.DMA((depth,)),
-            pltpu.SemaphoreType.DMA((depth,)),
+            pltpu.SemaphoreType.DMA((min(4, depth),)),
             pltpu.SemaphoreType.DMA((outs_depth,)),
         ],
-        compiler_params=params(18),
+        compiler_params=params(28),
         cost_estimate=cost(3 * product_flops, 6 * (basis + 1) * rows * width),
         name="new",
     )(
-        info, stats, s_term, r_term, hidden, normed, lower, upper, held_gate,
+        info, stats, s_term, r_term, hidden, normed, lower, upper, far(krylov_gate),
         far(krylov_up), far(krylov_down), down_high,
     )
     return (new_gate, new_up, new_down, coefficients)

time: 144 us -> 140 us (0.972)
  Pallas kernels: 92.5 us -> 89.3 us
    pallas_call x11, Pallas kernels: 69.9 us -> 64.8 us  [call(): pl.pallas_call(kernel, in_specs=placed, out_specs=[FAST] * (len(results)...]
    pallas_call x1, Pallas kernels: 22.7 us -> 24.5 us  [per_device(): pl.pallas_call(functools.partial(new_kernel, devices, count, inv_d, inv_f...]
  transfers between devices with their start and end apart: 21 -> 21, of which waited for: 5 -> 5; matrix products, arithmetic and copies ran while one was open for 1% -> 1% of each run, Pallas kernels for 32% -> 33%
where the time goes in v8:
time: 140 us; the launch traced here: 139 us
  Pallas kernels  89.3 us (64%)
  starting transfers between devices  25.7 us (18%)
  blocking collectives  12.9 us (9%)
  waiting for transfers between devices  8.09 us (6%)
    pallas_call x11, Pallas kernels, call(): pl.pallas_call(kernel, in_specs=placed, out_specs=[FAST] * (len(results)...  64.8 us
    ppermute x21, starting transfers between devices, exchange(): lax.ppermute(block, 'fsdp', [(one, one ^ flip) for one in range(count)])  25.7 us
    pallas_call x1, Pallas kernels, per_device(): pl.pallas_call(functools.partial(new_kernel, devices, count, inv_d, inv_f...  24.5 us
    all_to_all x1, blocking collectives, per_device(): stats = lax.all_to_all(stats, 'fsdp', 0, 0, tiled=True)  12.9 us
    ppermute x21, waiting for transfers between devices, exchange(): lax.ppermute(block, 'fsdp', [(one, one ^ flip) for one in range(count)])  8.09 us
  transfers between devices with their start and end apart: 21, of which 5 were waited for; matrix products, arithmetic and copies ran while one was open for 1% of the time, Pallas kernels for 33%

profile of v8, /device:TPU:0, one launch (start us, length us, event | category | flops | bytes accessed | tf_op | source)
XLA Modules:
  0.0 139.3 jit_solution(16893834444267023235)
XLA Ops:
  0.6 5.1 %collective-permute-start.2 = (bf16[1,8,4096]{2,1,0:T(8,128)(2,1)}, bf16[1,8,4096]{2,1,0:T(8,128)(2,1)S(1)}, u32[]{:S(2)}, u32[]{:S(2)}) collective-permute-start(bf16[1,8,4096]{2,1,0:T(8,128)(2,1)} %bitcast.4), channel_id=1, source_target_pairs={{0,24},{1,25},{2,26},{3,27},{4,28},{5,29},{6,30},{7,31},{8,16},{9,... | collective-permute-start | bytes 196616 | tf_op jit(solution)/shard_map/ppermute | solution.py:55
  5.7 0.0 collective-permute-start.1
  5.7 0.6 collective-permute-start
  6.4 0.9 constant_dynamic-update-slice_fusion.6
  7.3 0.7 pad_add_fusion.refs_0_.info
  8.0 4.6 %read.1.refs_1_.refs_2_ = bf16[5,8,32,4096]{3,2,1,0:T(8,128)(2,1)S(1)} custom-call(s32[2]{0:T(128)S(1)} %pad_add_fusion.refs_0_.info, bf16[8,320,4096]{2,1,0:T(8,128)(2,1)} %krylov_gate.1), custom_call_target="tpu_custom_call" | custom-call | flops 536870912 | bytes 10485760 | tf_op jit(solution)/shard_map/read/pallas_call | solution.py:141
  12.6 0.0 collective-permute-done.2
  12.7 0.0 collective-permute-done.1
  12.7 2.7 %collective-permute-start.5 = (bf16[4,8,4096]{2,1,0:T(8,128)(2,1)S(1)}, bf16[4,8,4096]{2,1,0:T(8,128)(2,1)S(1)}, u32[]{:S(2)}, u32[]{:S(2)}) collective-permute-start(bf16[4,8,4096]{2,1,0:T(8,128)(2,1)S(1)} %pad_maximum_fusion), channel_id=1, source_target_pairs={{0,6},{1,7},{2,4},{3,5},{4,2},{5,3},{6,0},{7,1},{8,14},{9,15},{10,... | collective-permute-start | bytes 786440 | tf_op jit(solution)/shard_map/ppermute | solution.py:55
  15.4 0.5 collective-permute-start.4
  15.9 0.4 collective-permute-start.3
  16.3 0.0 copy-start.1
  16.3 4.7 %gram.2 = (f32[256,256]{1,0:T(8,128)S(1)}, bf16[5,8,32,4096]{3,2,1,0:T(8,128)(2,1)S(1)}) custom-call(s32[2]{0:T(128)S(1)} %pad_add_fusion.refs_0_.info, bf16[5,8,32,4096]{3,2,1,0:T(8,128)(2,1)S(1)} %read.1.refs_1_.refs_2_, bf16[8,320,4096]{2,1,0:T(8,128)(2,1)} %krylov_gate.1), custom_call_target="tpu_custom_call" | custom-call | flops 2684354560 | bytes 10485760 | tf_op jit(solution)/shard_map/gram/pallas_call | solution.py:141
  21.0 2.0 %collective-permute-done.5 = bf16[4,8,4096]{2,1,0:T(8,128)(2,1)S(1)} collective-permute-done((bf16[4,8,4096]{2,1,0:T(8,128)(2,1)S(1)}, bf16[4,8,4096]{2,1,0:T(8,128)(2,1)S(1)}, u32[]{:S(2)}, u32[]{:S(2)}) %collective-permute-start.5) | collective-permute-done | bytes 262176 | tf_op jit(solution)/shard_map/ppermute | solution.py:55
  23.0 3.9 %collective-permute-done.4 = bf16[4,8,4096]{2,1,0:T(8,128)(2,1)S(1)} collective-permute-done((bf16[4,8,4096]{2,1,0:T(8,128)(2,1)S(1)}, bf16[4,8,4096]{2,1,0:T(8,128)(2,1)S(1)}, u32[]{:S(2)}, u32[]{:S(2)}) %collective-permute-start.4) | collective-permute-done | bytes 262176 | tf_op jit(solution)/shard_map/ppermute | solution.py:55
  27.0 0.1 collective-permute-start.6
  27.1 4.3 %gram.3.refs_2_ = f32[256,256]{1,0:T(8,128)S(1)} custom-call(s32[2]{0:T(128)S(1)} %pad_add_fusion.refs_0_.info, bf16[5,8,32,4096]{3,2,1,0:T(8,128)(2,1)S(1)} %get-tuple-element.99.refs_1_.refs_3_, f32[256,256]{1,0:T(8,128)S(1)} %get-tuple-element.100.refs_2_), custom_call_target="tpu_custom_call" | custom-call | flops 2684354560 | bytes 10485760 | tf_op jit(solution)/shard_map/gram/pallas_call | solution.py:141
  31.4 10.7 %forward.1 = (bf16[192,4096]{1,0:T(8,128)(2,1)S(1)}, bf16[320,192]{1,0:T(8,128)(2,1)S(1)}, bf16[192,320]{1,0:T(8,128)(2,1)S(1)}, bf16[192,320]{1,0:T(8,128)(2,1)...) custom-call(s32[2]{0:T(128)S(1)} %pad_add_fusion.refs_0_.info, ...), custom_call_target="tpu_custom_call" | custom-call | flops 2516582400 | bytes 15728640 | tf_op jit(solution)/shard_map/forward/pallas_call | solution.py:141
  42.1 0.6 collective-permute-start.7
  42.6 1.6 %keep.1 = f32[16,192,128]{2,1,0:T(8,128)S(1)} custom-call(s32[2]{0:T(128)S(1)} %pad_add_fusion.refs_0_.info, bf16[192,320]{1,0:T(8,128)(2,1)S(1)} %get-tuple-element.102.refs_1_, bf16[192,320]{1,0:T(8,128)(2,1)S(1)} %get-tuple-element.103.refs_2_, bf16[2,320,2048]{2,1,0:T(8,128)(2,1)S(1)} %get-tuple-element.104.refs_3_), custom_call_target="tpu_custom_call" | custom-call | flops 503316480 | bytes 4194304 | tf_op jit(solution)/shard_map/keep/pallas_call | solution.py:141
  44.2 0.3 collective-permute-done.7
  44.6 0.2 fusion
  44.8 1.5 %collective-permute-start.8 = (bf16[4,192,128]{2,1,0:T(8,128)(2,1)S(1)}, bf16[4,192,128]{2,1,0:T(8,128)(2,1)S(1)}, u32[]{:S(2)}, u32[]{:S(2)}) collective-permute-start(bf16[4,192,128]{2,1,0:T(8,128)(2,1)S(1)} %get-tuple-element.176), channel_id=1, source_target_pairs={{0,4},{1,5},{2,6},{3,7},{4,0},{5,1},{6,2},{7,3},{8,12},{9,13},{10,... | collective-permute-start | bytes 589832 | tf_op jit(solution)/shard_map/ppermute | solution.py:55
  46.3 1.5 %collective-permute-start.10 = (bf16[4,192,128]{2,1,0:T(8,128)(2,1)S(1)}, bf16[4,192,128]{2,1,0:T(8,128)(2,1)S(1)}, u32[]{:S(2)}, u32[]{:S(2)}) collective-permute-start(bf16[4,192,128]{2,1,0:T(8,128)(2,1)S(1)} %get-tuple-element.174), channel_id=1, source_target_pairs={{0,6},{1,7},{2,4},{3,5},{4,2},{5,3},{6,0},{7,1},{8,14},{9,15},{10,... | collective-permute-start | bytes 589832 | tf_op jit(solution)/shard_map/ppermute | solution.py:55
  47.8 0.5 collective-permute-start.9
  48.3 8.4 %product.1 = (f32[8,320,192]{2,1,0:T(8,128)S(1)}, f32[192,192]{1,0:T(8,128)S(1)}, bf16[4,8,32,4096]{3,2,1,0:T(8,128)(2,1)S(1)}) custom-call(s32[2]{0:T(128)S(1)} %pad_add_fusion.refs_0_.info, bf16[192,4096]{1,0:T(8,128)(2,1)S(1)} %get-tuple-element.106.refs_1_.normed, bf16[5,8,32,4096]{3,2,1,0:T(8,128)(2,1)S(1)} %read.1.refs_1_.refs_2_, ...), custom_call_target="tpu_custom_call" | custom-call | flops 4026531840 | bytes 8388608 | tf_op jit(solution)/shard_map/product/pallas_call | solution.py:141
  56.8 0.7 collective-permute-done.9
  57.5 0.1 fusion.4
  57.5 2.3 %collective-permute-start.11 = (bf16[1,192,128]{2,1,0:T(8,128)(2,1)S(1)}, bf16[1,192,128]{2,1,0:T(8,128)(2,1)S(1)}, u32[]{:S(2)}, u32[]{:S(2)}) collective-permute-start(bf16[1,192,128]{2,1,0:T(8,128)(2,1)S(1)} %get-tuple-element.180), channel_id=1, source_target_pairs={{0,16},{1,17},{2,18},{3,19},{4,20},{5,21},{6,22},{7,23},{8,24},{9,... | collective-permute-start | bytes 147464 | tf_op jit(solution)/shard_map/ppermute | solution.py:55
  59.9 1.5 %collective-permute-start.13 = (bf16[1,192,128]{2,1,0:T(8,128)(2,1)S(1)}, bf16[1,192,128]{2,1,0:T(8,128)(2,1)S(1)}, u32[]{:S(2)}, u32[]{:S(2)}) collective-permute-start(bf16[1,192,128]{2,1,0:T(8,128)(2,1)S(1)} %get-tuple-element.178), channel_id=1, source_target_pairs={{0,24},{1,25},{2,26},{3,27},{4,28},{5,29},{6,30},{7,31},{8,16},{9,... | collective-permute-start | bytes 147464 | tf_op jit(solution)/shard_map/ppermute | solution.py:55
  61.4 0.3 collective-permute-start.12
  61.6 5.7 %both.3 = (f32[8,128,192]{2,1,0:T(8,128)S(1)}, f32[256,256]{1,0:T(8,128)S(1)}, bf16[3,8,32,4096]{3,2,1,0:T(8,128)(2,1)S(1)}) custom-call(s32[2]{0:T(128)S(1)} %pad_add_fusion.refs_0_.info, bf16[192,4096]{1,0:T(8,128)(2,1)S(1)} %get-tuple-element.106.refs_1_.normed, f32[256,256]{1,0:T(8,128)S(1)} %gram.3.refs_2_, ...), custom_call_target="tpu_custom_call" | custom-call | flops 3758096384 | bytes 8388608 | tf_op jit(solution)/shard_map/both/pallas_call | solution.py:141
  67.3 0.1 constant_dynamic-update-slice_fusion.13
  67.4 3.0 %collective-permute-start.16 = (bf16[1,192,128]{2,1,0:T(8,128)(2,1)S(1)}, bf16[1,192,128]{2,1,0:T(8,128)(2,1)S(1)}, u32[]{:S(2)}, u32[]{:S(2)}) collective-permute-start(bf16[1,192,128]{2,1,0:T(8,128)(2,1)S(1)} %get-tuple-element.173), channel_id=1, source_target_pairs={{0,24},{1,25},{2,26},{3,27},{4,28},{5,29},{6,30},{7,31},{8,16},{9,... | collective-permute-start | bytes 147464 | tf_op jit(solution)/shard_map/ppermute | solution.py:55
  70.4 0.3 collective-permute-start.15
  70.7 1.2 collective-permute-start.14
  71.8 4.4 %both.4 = (f32[8,96,192]{2,1,0:T(8,128)S(1)}, f32[256,256]{1,0:T(8,128)S(1)}, bf16[3,8,32,4096]{3,2,1,0:T(8,128)(2,1)S(1)}) custom-call(s32[2]{0:T(128)S(1)} %pad_add_fusion.refs_0_.info, bf16[192,4096]{1,0:T(8,128)(2,1)S(1)} %get-tuple-element.106.refs_1_.normed, f32[256,256]{1,0:T(8,128)S(1)} %get-tuple-element.123.refs_2_, ...), custom_call_target="tpu_custom_call" | custom-call | flops 2818572288 | bytes 6291456 | tf_op jit(solution)/shard_map/both/pallas_call | solution.py:141
  76.3 2.4 %collective-permute-start.19 = (bf16[4,192,128]{2,1,0:T(8,128)(2,1)S(1)}, bf16[4,192,128]{2,1,0:T(8,128)(2,1)S(1)}, u32[]{:S(2)}, u32[]{:S(2)}) collective-permute-start(bf16[4,192,128]{2,1,0:T(8,128)(2,1)S(1)} %pad_maximum_fusion.1), channel_id=1, source_target_pairs={{0,6},{1,7},{2,4},{3,5},{4,2},{5,3},{6,0},{7,1},{8,14},{9,15},{10,... | collective-permute-start | bytes 589832 | tf_op jit(solution)/shard_map/ppermute | solution.py:55
  78.7 0.5 collective-permute-start.18
  79.3 0.6 collective-permute-start.17
  79.9 5.1 %both.5 = (f32[8,96,192]{2,1,0:T(8,128)S(1)}, f32[256,256]{1,0:T(8,128)S(1)}, bf16[10,8,32,2048]{3,2,1,0:T(8,128)(2,1)S(1)}, bf16[1,320,2048]{2,1,0:T(8,128)(2,1)S(1)}) custom-call(s32[2]{0:T(128)S(1)} %pad_add_fusion.refs_0_.info, bf16[192,4096]{1,0:T(8,128)(2,1)S(1)} %get-tuple-element.106.refs_1_.normed, f32[256,256]{1,0:T(8,128)S(1)} %get-tuple-element.132.refs_2_, ...), custom_call_target="tpu_custom_call" | custom-call | flops 2818572288 | bytes 6291456 | tf_op jit(solution)/shard_map/both/pallas_call | solution.py:141
  85.0 1.1 collective-permute-done.18
  86.1 0.0 collective-permute-done.17
  86.2 0.1 collective-permute-start.20
  86.3 7.0 %back_half.1 = (f32[256,256]{1,0:T(8,128)S(1)}, f32[320,192]{1,0:T(8,128)S(1)}, f32[2,192,192]{2,1,0:T(8,128)S(1)}, f32[8,192]{1,0:T(8,128)S(1)}, bf16[10,8,32,2...) custom-call(s32[2]{0:T(128)S(1)} %pad_add_fusion.refs_0_.info, ...), custom_call_target="tpu_custom_call" | custom-call | flops 4949278720 | bytes 11796480 | tf_op jit(solution)/shard_map/back_half/pallas_call | solution.py:141
  93.3 8.4 %back.1 = (bf16[320,192]{1,0:T(8,128)(2,1)S(1)}, bf16[320,192]{1,0:T(8,128)(2,1)S(1)}, f32[8,128]{1,0:T(8,128)S(1)}) custom-call(s32[2]{0:T(128)S(1)} %pad_add_fusion.refs_0_.info, bf16[16,192,128]{2,1,0:T(8,128)(2,1)S(1)} %collective-permute-done.20.refs_1_.upper, bf16[10,8,32,2048]{3,2,1,0:T(8,128)(2,1)S(1)} %get-tuple-element.156.refs_2_.high, ...), custom_call_target="tpu_custom_call" | custom-call | flops 4949278720 | bytes 3932160 | tf_op jit(solution)/shard_map/back/pallas_call | solution.py:141
  101.8 12.9 %all_to_all.5.stats = f32[32,8,128]{2,1,0:T(8,128)S(1)} all-to-all(f32[32,8,128]{2,1,0:T(8,128)S(1)} %broadcast_in_dim.2), channel_id=1, replica_groups=mesh['fsdp'=32] {'fsdp'}, dimensions={0} | all-to-all | bytes 262144 | tf_op jit(solution)/shard_map/all_to_all | solution.py:855
  114.7 24.5 %new.1 = (bf16[320,4096]{1,0:T(8,128)(2,1)}, bf16[320,4096]{1,0:T(8,128)(2,1)}, bf16[320,4096]{1,0:T(8,128)(2,1)}, f32[9]{0:T(128)}) custom-call(s32[2]{0:T(128)S(1)} %pad_add_fusion.refs_0_.info, f32[32,8,128]{2,1,0:T(8,128)S(1)} %all_to_all.5.stats, bf16[320,192]{1,0:T(8,128)(2,1)S(1)} %get-tuple-element.170.s_term, ...), custom_call_target="tpu_custom_call" | custom-call | flops 1509949440 | bytes 70778880 | tf_op jit(solution)/shard_map/new/pallas_call | solution.py:860
  (32 shorter events, 0.3 us)
Async XLA Ops:
  0.6 12.0 %collective-permute-start.2 = (bf16[1,8,4096]{2,1,0:T(8,128)(2,1)}, bf16[1,8,4096]{2,1,0:T(8,128)(2,1)S(1)}, u32[]{:S(2)}, u32[]{:S(2)}) collective-permute-start(bf16[1,8,4096]{2,1,0:T(8,128)(2,1)} %bitcast.4), channel_id=1, source_target_pairs={{0,24},{1,25},{2,26},{3,27},{4,28},{5,29},{6,30},{7,31},{8,16},{9,... | collective-permute-start | bytes 196616 | tf_op jit(solution)/shard_map/ppermute | solution.py:55
  5.7 6.9 %collective-permute-start.1 = (bf16[1,8,4096]{2,1,0:T(8,128)(2,1)}, bf16[1,8,4096]{2,1,0:T(8,128)(2,1)S(1)}, u32[]{:S(2)}, u32[]{:S(2)}) collective-permute-start(bf16[1,8,4096]{2,1,0:T(8,128)(2,1)} %bitcast.5), channel_id=1, source_target_pairs={{0,8},{1,9},{2,10},{3,11},{4,12},{5,13},{6,14},{7,15},{8,0},{9,1},... | collective-permute-start | bytes 196616 | tf_op jit(solution)/shard_map/ppermute | solution.py:55
  5.7 6.9 %collective-permute-start = (bf16[1,8,4096]{2,1,0:T(8,128)(2,1)}, bf16[1,8,4096]{2,1,0:T(8,128)(2,1)S(1)}, u32[]{:S(2)}, u32[]{:S(2)}) collective-permute-start(bf16[1,8,4096]{2,1,0:T(8,128)(2,1)} %bitcast.6), channel_id=1, source_target_pairs={{0,16},{1,17},{2,18},{3,19},{4,20},{5,21},{6,22},{7,23},{8,24},{9,... | collective-permute-start | bytes 196616 | tf_op jit(solution)/shard_map/ppermute | solution.py:55
  8.0 4.7 %copy-start = (bf16[8,4096]{1,0:T(8,128)(2,1)S(1)}, bf16[8,4096]{1,0:T(8,128)(2,1)}, u32[]{:S(2)}) copy-start(bf16[8,4096]{1,0:T(8,128)(2,1)} %param.9) | copy-start | bytes 196612
  12.7 10.3 %collective-permute-start.5 = (bf16[4,8,4096]{2,1,0:T(8,128)(2,1)S(1)}, bf16[4,8,4096]{2,1,0:T(8,128)(2,1)S(1)}, u32[]{:S(2)}, u32[]{:S(2)}) collective-permute-start(bf16[4,8,4096]{2,1,0:T(8,128)(2,1)S(1)} %pad_maximum_fusion), channel_id=1, source_target_pairs={{0,6},{1,7},{2,4},{3,5},{4,2},{5,3},{6,0},{7,1},{8,14},{9,15},{10,... | collective-permute-start | bytes 786440 | tf_op jit(solution)/shard_map/ppermute | solution.py:55
  15.4 11.5 %collective-permute-start.4 = (bf16[4,8,4096]{2,1,0:T(8,128)(2,1)S(1)}, bf16[4,8,4096]{2,1,0:T(8,128)(2,1)S(1)}, u32[]{:S(2)}, u32[]{:S(2)}) collective-permute-start(bf16[4,8,4096]{2,1,0:T(8,128)(2,1)S(1)} %pad_maximum_fusion), channel_id=1, source_target_pairs={{0,2},{1,3},{2,0},{3,1},{4,6},{5,7},{6,4},{7,5},{8,10},{9,11},{10,... | collective-permute-start | bytes 786440 | tf_op jit(solution)/shard_map/ppermute | solution.py:55
  15.9 11.0 %collective-permute-start.3 = (bf16[4,8,4096]{2,1,0:T(8,128)(2,1)S(1)}, bf16[4,8,4096]{2,1,0:T(8,128)(2,1)S(1)}, u32[]{:S(2)}, u32[]{:S(2)}) collective-permute-start(bf16[4,8,4096]{2,1,0:T(8,128)(2,1)S(1)} %pad_maximum_fusion), channel_id=1, source_target_pairs={{0,4},{1,5},{2,6},{3,7},{4,0},{5,1},{6,2},{7,3},{8,12},{9,13},{10,... | collective-permute-start | bytes 786440 | tf_op jit(solution)/shard_map/ppermute | solution.py:55
  16.3 10.7 %copy-start.1 = (bf16[4096]{0:T(1024)(128)(2,1)S(1)}, bf16[4096]{0:T(1024)(128)(2,1)}, u32[]{:S(2)}) copy-start(bf16[4096]{0:T(1024)(128)(2,1)} %param.10) | copy-start | bytes 24580
  27.0 4.4 %collective-permute-start.6 = (bf16[16,8,4096]{2,1,0:T(8,128)(2,1)S(1)}, bf16[16,8,4096]{2,1,0:T(8,128)(2,1)S(1)}, u32[]{:S(2)}, u32[]{:S(2)}) collective-permute-start(bf16[16,8,4096]{2,1,0:T(8,128)(2,1)S(1)} %constant_dynamic-update-slice_fusion.refs_1_), channel_id=1, source_target_pairs={{0,1},{1,0},{2,3},{3,2},{4,5},{5,4},{6,7},{7,6},{8,9},{9,8},{10,11... | collective-permute-start | bytes 3145736 | tf_op jit(solution)/shard_map/ppermute | solution.py:55
  42.1 2.5 %collective-permute-start.7 = (bf16[16,192,128]{2,1,0:T(8,128)(2,1)S(1)}, bf16[16,192,128]{2,1,0:T(8,128)(2,1)S(1)}, u32[]{:S(2)}, u32[]{:S(2)}) collective-permute-start(bf16[16,192,128]{2,1,0:T(8,128)(2,1)S(1)} %get-tuple-element.105), channel_id=1, source_target_pairs={{0,1},{1,0},{2,3},{3,2},{4,5},{5,4},{6,7},{7,6},{8,9},{9,8},{10,11... | collective-permute-start | bytes 2359304 | tf_op jit(solution)/shard_map/ppermute | solution.py:55
  44.8 12.7 %collective-permute-start.8 = (bf16[4,192,128]{2,1,0:T(8,128)(2,1)S(1)}, bf16[4,192,128]{2,1,0:T(8,128)(2,1)S(1)}, u32[]{:S(2)}, u32[]{:S(2)}) collective-permute-start(bf16[4,192,128]{2,1,0:T(8,128)(2,1)S(1)} %get-tuple-element.176), channel_id=1, source_target_pairs={{0,4},{1,5},{2,6},{3,7},{4,0},{5,1},{6,2},{7,3},{8,12},{9,13},{10,... | collective-permute-start | bytes 589832 | tf_op jit(solution)/shard_map/ppermute | solution.py:55
  46.3 10.5 %collective-permute-start.10 = (bf16[4,192,128]{2,1,0:T(8,128)(2,1)S(1)}, bf16[4,192,128]{2,1,0:T(8,128)(2,1)S(1)}, u32[]{:S(2)}, u32[]{:S(2)}) collective-permute-start(bf16[4,192,128]{2,1,0:T(8,128)(2,1)S(1)} %get-tuple-element.174), channel_id=1, source_target_pairs={{0,6},{1,7},{2,4},{3,5},{4,2},{5,3},{6,0},{7,1},{8,14},{9,15},{10,... | collective-permute-start | bytes 589832 | tf_op jit(solution)/shard_map/ppermute | solution.py:55
  47.8 9.7 %collective-permute-start.9 = (bf16[4,192,128]{2,1,0:T(8,128)(2,1)S(1)}, bf16[4,192,128]{2,1,0:T(8,128)(2,1)S(1)}, u32[]{:S(2)}, u32[]{:S(2)}) collective-permute-start(bf16[4,192,128]{2,1,0:T(8,128)(2,1)S(1)} %get-tuple-element.175), channel_id=1, source_target_pairs={{0,2},{1,3},{2,0},{3,1},{4,6},{5,7},{6,4},{7,5},{8,10},{9,11},{10,... | collective-permute-start | bytes 589832 | tf_op jit(solution)/shard_map/ppermute | solution.py:55
  57.5 9.8 %collective-permute-start.11 = (bf16[1,192,128]{2,1,0:T(8,128)(2,1)S(1)}, bf16[1,192,128]{2,1,0:T(8,128)(2,1)S(1)}, u32[]{:S(2)}, u32[]{:S(2)}) collective-permute-start(bf16[1,192,128]{2,1,0:T(8,128)(2,1)S(1)} %get-tuple-element.180), channel_id=1, source_target_pairs={{0,16},{1,17},{2,18},{3,19},{4,20},{5,21},{6,22},{7,23},{8,24},{9,... | collective-permute-start | bytes 147464 | tf_op jit(solution)/shard_map/ppermute | solution.py:55
  59.9 7.4 %collective-permute-start.13 = (bf16[1,192,128]{2,1,0:T(8,128)(2,1)S(1)}, bf16[1,192,128]{2,1,0:T(8,128)(2,1)S(1)}, u32[]{:S(2)}, u32[]{:S(2)}) collective-permute-start(bf16[1,192,128]{2,1,0:T(8,128)(2,1)S(1)} %get-tuple-element.178), channel_id=1, source_target_pairs={{0,24},{1,25},{2,26},{3,27},{4,28},{5,29},{6,30},{7,31},{8,16},{9,... | collective-permute-start | bytes 147464 | tf_op jit(solution)/shard_map/ppermute | solution.py:55
  61.4 5.9 %collective-permute-start.12 = (bf16[1,192,128]{2,1,0:T(8,128)(2,1)S(1)}, bf16[1,192,128]{2,1,0:T(8,128)(2,1)S(1)}, u32[]{:S(2)}, u32[]{:S(2)}) collective-permute-start(bf16[1,192,128]{2,1,0:T(8,128)(2,1)S(1)} %get-tuple-element.179), channel_id=1, source_target_pairs={{0,8},{1,9},{2,10},{3,11},{4,12},{5,13},{6,14},{7,15},{8,0},{9,1},... | collective-permute-start | bytes 147464 | tf_op jit(solution)/shard_map/ppermute | solution.py:55
  67.4 8.9 %collective-permute-start.16 = (bf16[1,192,128]{2,1,0:T(8,128)(2,1)S(1)}, bf16[1,192,128]{2,1,0:T(8,128)(2,1)S(1)}, u32[]{:S(2)}, u32[]{:S(2)}) collective-permute-start(bf16[1,192,128]{2,1,0:T(8,128)(2,1)S(1)} %get-tuple-element.173), channel_id=1, source_target_pairs={{0,24},{1,25},{2,26},{3,27},{4,28},{5,29},{6,30},{7,31},{8,16},{9,... | collective-permute-start | bytes 147464 | tf_op jit(solution)/shard_map/ppermute | solution.py:55
  70.4 5.9 %collective-permute-start.15 = (bf16[1,192,128]{2,1,0:T(8,128)(2,1)S(1)}, bf16[1,192,128]{2,1,0:T(8,128)(2,1)S(1)}, u32[]{:S(2)}, u32[]{:S(2)}) collective-permute-start(bf16[1,192,128]{2,1,0:T(8,128)(2,1)S(1)} %get-tuple-element.173), channel_id=1, source_target_pairs={{0,8},{1,9},{2,10},{3,11},{4,12},{5,13},{6,14},{7,15},{8,0},{9,1},... | collective-permute-start | bytes 147464 | tf_op jit(solution)/shard_map/ppermute | solution.py:55
  70.7 5.6 %collective-permute-start.14 = (bf16[1,192,128]{2,1,0:T(8,128)(2,1)S(1)}, bf16[1,192,128]{2,1,0:T(8,128)(2,1)S(1)}, u32[]{:S(2)}, u32[]{:S(2)}) collective-permute-start(bf16[1,192,128]{2,1,0:T(8,128)(2,1)S(1)} %get-tuple-element.173), channel_id=1, source_target_pairs={{0,16},{1,17},{2,18},{3,19},{4,20},{5,21},{6,22},{7,23},{8,24},{9,... | collective-permute-start | bytes 147464 | tf_op jit(solution)/shard_map/ppermute | solution.py:55
  76.3 8.7 %collective-permute-start.19 = (bf16[4,192,128]{2,1,0:T(8,128)(2,1)S(1)}, bf16[4,192,128]{2,1,0:T(8,128)(2,1)S(1)}, u32[]{:S(2)}, u32[]{:S(2)}) collective-permute-start(bf16[4,192,128]{2,1,0:T(8,128)(2,1)S(1)} %pad_maximum_fusion.1), channel_id=1, source_target_pairs={{0,6},{1,7},{2,4},{3,5},{4,2},{5,3},{6,0},{7,1},{8,14},{9,15},{10,... | collective-permute-start | bytes 589832 | tf_op jit(solution)/shard_map/ppermute | solution.py:55
  78.7 7.4 %collective-permute-start.18 = (bf16[4,192,128]{2,1,0:T(8,128)(2,1)S(1)}, bf16[4,192,128]{2,1,0:T(8,128)(2,1)S(1)}, u32[]{:S(2)}, u32[]{:S(2)}) collective-permute-start(bf16[4,192,128]{2,1,0:T(8,128)(2,1)S(1)} %pad_maximum_fusion.1), channel_id=1, source_target_pairs={{0,2},{1,3},{2,0},{3,1},{4,6},{5,7},{6,4},{7,5},{8,10},{9,11},{10,... | collective-permute-start | bytes 589832 | tf_op jit(solution)/shard_map/ppermute | solution.py:55
  79.3 6.9 %collective-permute-start.17 = (bf16[4,192,128]{2,1,0:T(8,128)(2,1)S(1)}, bf16[4,192,128]{2,1,0:T(8,128)(2,1)S(1)}, u32[]{:S(2)}, u32[]{:S(2)}) collective-permute-start(bf16[4,192,128]{2,1,0:T(8,128)(2,1)S(1)} %pad_maximum_fusion.1), channel_id=1, source_target_pairs={{0,4},{1,5},{2,6},{3,7},{4,0},{5,1},{6,2},{7,3},{8,12},{9,13},{10,... | collective-permute-start | bytes 589832 | tf_op jit(solution)/shard_map/ppermute | solution.py:55
  86.2 7.0 %collective-permute-start.20 = (bf16[16,192,128]{2,1,0:T(8,128)(2,1)S(1)}, bf16[16,192,128]{2,1,0:T(8,128)(2,1)S(1)}, u32[]{:S(2)}, u32[]{:S(2)}) collective-permute-start(bf16[16,192,128]{2,1,0:T(8,128)(2,1)S(1)} %constant_dynamic-update-slice_fusion.7.refs_1_.lower), channel_id=1, source_target_pairs={{0,1},{1,0},{2,3},{3,2},{4,5},{5,4},{6,7},{7,6},{8,9},{9,8},{10,11... | collective-permute-start | bytes 2359304 | tf_op jit(solution)/shard_map/ppermute | solution.py:55
